TPU v7x, 128 devices: a whole 4x4x4 slice. The times are simulated.
128 devices in a mesh: dp: 32 (over z, x, core), rep: 4 (over y).
Axes of the slice: x: 4, y: 4, z: 4, core: 2. Of those that a mesh axis runs over, the one named last changes fastest.
Arguments:
- features: bfloat16 [65536, 2048], P(('dp', 'rep'))
- head_weight: bfloat16 [2048, 512], replicated
- slot_of_image: int32 [65536], P(('dp', 'rep')), may hold values from 0 to 65535, as said below
- candidates: int32 [512, 8], replicated, may hold values from 0 to 511, as said below
- positives: int32 [65536], P('dp'), may hold values from 0 to 1023
Outputs:
- anchor_row_loss: float32 [65536], P('dp')
- weight_grad: float32 [2048, 512], P(('dp', 'rep'))
Inputs may be any that keep to these rules, and one draw needn't show every extreme that they name: `slot_of_image`: every block row holds exactly one image. The images of one device go to the owners (dp index slot // 2048) as 32 images to each of a quarter of the owners, 16 to each of another quarter and 8 to each of the rest. `candidates`: in the rows of one owner's 16 blocks and one group of 2 consecutive columns (group r is columns r * 2 to r * 2 + 1), the blocks of every owner (block // 16) are named exactly 1 times. Repeats may occur.
All inputs are finite; a program needn't handle non-finite values.
Results may differ from a plain program's by a relative error of at most 0.0035.
Values may be sent and summed in bfloat16 or wider, within the bound.
No kernel may reach another device: no remote copies, remote signals or barrier semaphores. Data moves between devices by JAX's collectives and lax.ppermute only.
A program may use at most 64 MiB of HBM per device.

v0:
```python
import math

import jax
import jax.numpy as jnp
from jax import lax
from jax.sharding import PartitionSpec as P

BR = 128
PAIRS_REP = 2


logit_sharpness = 0.05
objective_factor = 32.0
norm_eps = 1e-06


def owner_ranks(owners, bucket_count):
    onehot = (owners[..., None] == jnp.arange(bucket_count, dtype=jnp.int32)).astype(jnp.int32)
    before = jnp.cumsum(onehot, axis=-2) - onehot
    return jnp.sum(before * onehot, axis=-1)


def shards(features, head_weight, slot_of_image, candidates, positives):
    dp_count = lax.axis_size("dp")
    rep_count = lax.axis_size("rep")
    dp_index = lax.axis_index("dp")
    rep_index = lax.axis_index("rep")
    image_count = features.shape[0]
    desc_width = head_weight.shape[1]
    slot_number_count = image_count * rep_count
    block_count = slot_number_count // BR
    capacity = 2 * image_count // dp_count
    pictures_overall = image_count * dp_count * rep_count
    derivative_factor = objective_factor / (logit_sharpness * math.sqrt(pictures_overall))
    projected = jnp.dot(features, head_weight, preferred_element_type=jnp.float32)
    row_norms = jnp.sqrt(jnp.sum(projected * projected, axis=1, keepdims=True) + norm_eps)
    unit_rows = projected / row_norms
    descriptor = unit_rows.astype(jnp.bfloat16)
    owners = slot_of_image // slot_number_count
    local_slot = slot_of_image % slot_number_count
    bucket_rank = owner_ranks(owners, dp_count)
    position = owners * capacity + bucket_rank
    send_rows = (
        jnp.zeros((dp_count * capacity, desc_width), jnp.bfloat16).at[position].set(descriptor)
    )
    send_slots = (
        jnp.full((dp_count * capacity,), slot_number_count, jnp.int32).at[position].set(local_slot)
    )
    wide_rows = jnp.broadcast_to(
        send_rows.reshape(dp_count, 1, capacity, desc_width),
        (dp_count, rep_count, capacity, desc_width),
    )
    wide_slots = jnp.broadcast_to(
        send_slots.reshape(dp_count, 1, capacity), (dp_count, rep_count, capacity)
    )
    arrived_rows, arrived_slots = (
        lax.all_to_all(
            wide_rows.reshape(dp_count * rep_count, capacity, desc_width),
            ("dp", "rep"),
            split_axis=0,
            concat_axis=0,
            tiled=True,
        ),
        lax.all_to_all(
            wide_slots.reshape(dp_count * rep_count, capacity),
            ("dp", "rep"),
            split_axis=0,
            concat_axis=0,
            tiled=True,
        ),
    )
    by_rep_rows = jnp.transpose(
        arrived_rows.reshape(dp_count, rep_count, capacity, desc_width), (1, 0, 2, 3)
    )
    by_rep_slots = jnp.transpose(arrived_slots.reshape(dp_count, rep_count, capacity), (1, 0, 2))
    flat_slots = by_rep_slots.reshape(rep_count * dp_count * capacity)
    anchors = (
        jnp.zeros((slot_number_count, desc_width), jnp.bfloat16)
        .at[flat_slots]
        .set(by_rep_rows.reshape(rep_count * dp_count * capacity, desc_width), mode="drop")
    )
    anchor_blocks = anchors.reshape(block_count, BR, desc_width)
    pair_table = candidates.reshape(dp_count, block_count, rep_count, PAIRS_REP)
    share_list = lax.dynamic_index_in_dim(pair_table, rep_index, axis=2, keepdims=False)
    share_list = share_list.reshape(dp_count, block_count * PAIRS_REP)
    partner_owner = share_list // block_count
    partner_local = share_list % block_count
    partner_rank = owner_ranks(partner_owner, dp_count)
    fetch_quota = block_count * PAIRS_REP // dp_count
    wanted = partner_owner == dp_index
    requester = jnp.broadcast_to(
        jnp.arange(dp_count, dtype=jnp.int32)[:, None], partner_owner.shape
    )
    flat_index = jnp.where(wanted, requester * fetch_quota + partner_rank, dp_count * fetch_quota)
    serve_index = (
        jnp.zeros((dp_count * fetch_quota,), jnp.int32)
        .at[flat_index.reshape(-1)]
        .set(partner_local.reshape(-1), mode="drop")
    )
    served = anchor_blocks[serve_index].reshape(dp_count, fetch_quota, BR, desc_width)
    fetched = lax.all_to_all(served, "dp", split_axis=0, concat_axis=0, tiled=True)
    need_owner = lax.dynamic_index_in_dim(partner_owner, dp_index, axis=0, keepdims=False)
    need_rank = lax.dynamic_index_in_dim(partner_rank, dp_index, axis=0, keepdims=False)
    partners = fetched.reshape(dp_count * fetch_quota, BR, desc_width)[
        need_owner * fetch_quota + need_rank
    ]
    partners = partners.reshape(block_count, PAIRS_REP * BR, desc_width)
    cosine_logits = (
        jnp.einsum("bre,bce->brc", anchor_blocks, partners, preferred_element_type=jnp.float32)
        / logit_sharpness
    )
    linear_head_matrix = jnp.exp(cosine_logits - 1.0 / logit_sharpness)
    positive_index = positives.reshape(block_count, BR)
    positive_pair = positive_index // BR
    in_share = positive_pair // PAIRS_REP == rep_index
    positive_column = (positive_pair - rep_index * PAIRS_REP) * BR + positive_index % BR
    column_ids = jnp.arange(PAIRS_REP * BR, dtype=jnp.int32)
    is_positive = (column_ids[None, None, :] == positive_column[..., None]) & in_share[..., None]
    share_total = jnp.sum(linear_head_matrix, axis=2)
    share_positive = jnp.sum(jnp.where(is_positive, cosine_logits, 0.0), axis=2)
    normalizer_sum, matching_logit = lax.psum((share_total, share_positive), "rep")
    anchor_row_loss = (jnp.log(normalizer_sum) + 1.0 / logit_sharpness - matching_logit).reshape(
        slot_number_count
    )
    coefficient = (
        linear_head_matrix / normalizer_sum[..., None] - is_positive.astype(jnp.float32)
    ).astype(jnp.bfloat16)
    share_grad = (
        jnp.einsum("brc,bce->bre", coefficient, partners, preferred_element_type=jnp.float32)
        * derivative_factor
    )
    share_grad = share_grad.astype(jnp.bfloat16).reshape(slot_number_count, desc_width)
    safe_slots = jnp.minimum(by_rep_slots, slot_number_count - 1)
    back_rows = share_grad[jnp.transpose(safe_slots, (1, 0, 2))]
    back_rows = back_rows.reshape(dp_count * rep_count, capacity, desc_width)
    returned = lax.all_to_all(back_rows, ("dp", "rep"), split_axis=0, concat_axis=0, tiled=True)
    summed = jnp.sum(
        returned.reshape(dp_count, rep_count, capacity, desc_width), axis=1, dtype=jnp.float32
    )
    unit_grad = summed.reshape(dp_count * capacity, desc_width)[position]
    radial = jnp.sum(unit_rows * unit_grad, axis=1, keepdims=True)
    grad_projected = ((unit_grad - unit_rows * radial) / row_norms).astype(jnp.bfloat16)
    weight_grad = lax.psum_scatter(
        lax.dot_general(
            features, grad_projected, (((0,), (0,)), ((), ())), preferred_element_type=jnp.float32
        ),
        ("dp", "rep"),
        scatter_dimension=0,
        tiled=True,
    )
    return (anchor_row_loss, weight_grad)


def solution(mesh):
    placed = (P(("dp", "rep"), None), P(), P(("dp", "rep")), P(), P("dp"))
    return jax.shard_map(
        shards,
        mesh=mesh,
        in_specs=placed,
        out_specs=(P("dp"), P(("dp", "rep"), None)),
        check_vma=False,
    )
```

profile of v0, /device:TPU:0, one launch (start us, length us, event | category | flops | bytes accessed | tf_op | source)
XLA Modules:
  0.0 961.2 jit_solution(12106018923085776402)
XLA Ops:
  8.0 1.2 reduce-window.6
  9.6 2.4 scatter_custom_fusion
  12.7 11.1 %all-to-all-start = ((s32[128,1,32]{2,1,0:T(1,128)}), s32[128,1,32]{2,1,0:T(1,128)S(1)}, u32[]{:S(2)}, u32[]{:S(2)}) async-start(s32[128,1,32]{2,1,0:T(1,128)} %bitcast.2), calls=%async_computation | async-start | bytes 131072 | tf_op jit(solution)/shard_map/all_to_all | solution.py:64
  23.9 2.9 multiply_reduce_fusion.1
  26.8 1.0 copy-done.1
  27.9 1.0 copy.34
  28.9 3.2 scatter_custom_fusion.1
  32.1 1.1 all-to-all-done
  33.2 2.6 broadcast_in_dim.66
  35.8 9.2 all-to-all-start.1
  45.9 1.0 fusion.39
  47.1 4.5 scatter_custom_fusion.3
  51.8 44.7 %all-to-all-done.1 = bf16[128,32,512]{2,1,0:T(8,128)(2,1)} async-done(((bf16[128,32,512]{2,1,0:T(8,128)(2,1)}), bf16[128,32,512]{2,1,0:T(8,128)(2,1)}, u32[]{:S(2)}, u32[]{:S(2)}) %all-to-all-start.1) | async-done | bytes 4194336 | tf_op jit(solution)/shard_map/all_to_all | solution.py:57
  96.5 4.7 copy.35
  101.3 20.2 %scatter_custom_fusion.2 = bf16[2048,512]{1,0:T(8,128)(2,1)} fusion(s32[4096]{0:T(1024)S(1)} %bitcast.120, bf16[4096,512]{1,0:T(8,128)(2,1)} %bitcast.115, bf16[]{:T(256)} %constant.126.clone.1), kind=kCustom, calls=%fused_computation.24 | custom fusion | bytes 2097664 | tf_op jit(solution)/shard_map/scatter | solution.py:80
  121.5 4.3 gather_fusion
  125.8 5.0 all-to-all-start.2
  131.3 53.0 %all-to-all-done.2 = bf16[32,1,128,512]{3,2,1,0:T(8,128)(2,1)} async-done(((bf16[32,1,128,512]{3,2,1,0:T(8,128)(2,1)}), bf16[32,1,128,512]{3,2,1,0:T(8,128)(2,1)}, u32[]{:S(2)}, u32[]{:S(2)}) %all-to-all-start.2) | async-done | bytes 4194336 | tf_op jit(solution)/shard_map/all_to_all | solution.py:101
  184.3 4.9 gather_fusion.1
  189.2 5.8 fusion.1
  195.0 16.1 %all-reduce = (f32[16,128]{1,0:T(8,128)S(1)}, f32[16,128]{1,0:T(8,128)S(1)}) all-reduce(f32[16,128]{1,0:T(8,128)S(1)} %get-tuple-element.11, f32[16,128]{1,0:T(8,128)S(1)} %get-tuple-element.10), channel_id=1, replica_groups=mesh['dp'=32,'rep'=4] {'rep'}, use_global_device_ids=true, to_apply=%region_13.14 | all-reduce | flops 4096 | bytes 32768 | tf_op jit(solution)/shard_map/psum | solution.py:121
  211.2 5.2 multiply_convert_fusion
  216.4 19.3 %gather_fusion.2 = bf16[4096,512]{1,0:T(8,128)(2,1)} fusion(bf16[2048,512]{1,0:T(8,128)(2,1)} %bitcast.105, s32[4096]{0:T(1024)S(1)} %broadcast_clamp_fusion), kind=kCustom, calls=%fused_computation.2 | custom fusion | bytes 8404992 | tf_op jit(solution)/shard_map/gather | solution.py:134
  235.7 5.8 all-to-all-start.3
  241.8 51.2 %all-to-all-done.3 = bf16[128,32,512]{2,1,0:T(8,128)(2,1)} async-done(((bf16[128,32,512]{2,1,0:T(8,128)(2,1)}), bf16[128,32,512]{2,1,0:T(8,128)(2,1)}, u32[]{:S(2)}, u32[]{:S(2)}) %all-to-all-start.3) | async-done | bytes 4194336 | tf_op jit(solution)/shard_map/all_to_all | solution.py:136
  293.0 4.5 convert_reduce_fusion
  297.5 3.6 gather_fusion.3
  301.1 1.3 copy.41
  302.5 1.9 multiply_reduce_fusion
  304.6 3.2 convolution_bitcast_fusion
  307.8 5.3 copy.43
  313.8 640.5 %reduce-scatter.4.cloned.1.call-done = f32[16,512]{1,0:T(8,128)} async-done(((f32[2048,512]{1,0:T(8,128)}), f32[16,512]{1,0:T(8,128)}) %reduce-scatter.4.cloned.1.call-update) | async-done | bytes 32784
  (52 shorter events, 4.8 us)
Async XLA Ops:
  7.2 16.7 %copy-start = (bf16[512,2048]{1,0:T(8,128)(2,1)S(1)}, bf16[512,2048]{1,0:T(8,128)(2,1)}, u32[]{:S(2)}) copy-start(bf16[512,2048]{1,0:T(8,128)(2,1)} %param.5) | copy-start | bytes 6291460
  12.7 20.5 %all-to-all-start = ((s32[128,1,32]{2,1,0:T(1,128)}), s32[128,1,32]{2,1,0:T(1,128)S(1)}, u32[]{:S(2)}, u32[]{:S(2)}) async-start(s32[128,1,32]{2,1,0:T(1,128)} %bitcast.2), calls=%async_computation | async-start | bytes 131072 | tf_op jit(solution)/shard_map/all_to_all | solution.py:64
  26.8 1.0 copy-start.1
  35.8 9.3 copy-start.5
  35.8 60.8 %all-to-all-start.1 = ((bf16[128,32,512]{2,1,0:T(8,128)(2,1)}), bf16[128,32,512]{2,1,0:T(8,128)(2,1)}, u32[]{:S(2)}, u32[]{:S(2)}) async-start(bf16[128,32,512]{2,1,0:T(8,128)(2,1)} %bitcast.110), calls=%async_computation.1 | async-start | bytes 8388608 | tf_op jit(solution)/shard_map/all_to_all | solution.py:57
  125.8 5.2 copy-start.4
  125.8 58.5 %all-to-all-start.2 = ((bf16[32,1,128,512]{3,2,1,0:T(8,128)(2,1)}), bf16[32,1,128,512]{3,2,1,0:T(8,128)(2,1)}, u32[]{:S(2)}, u32[]{:S(2)}) async-start(bf16[32,1,128,512]{3,2,1,0:T(8,128)(2,1)} %bitcast.111), calls=%async_computation.2 | async-start | bytes 8388608 | tf_op jit(solution)/shard_map/all_to_all | solution.py:101
  235.7 57.3 %all-to-all-start.3 = ((bf16[128,32,512]{2,1,0:T(8,128)(2,1)}), bf16[128,32,512]{2,1,0:T(8,128)(2,1)}, u32[]{:S(2)}, u32[]{:S(2)}) async-start(bf16[128,32,512]{2,1,0:T(8,128)(2,1)} %bitcast.109), calls=%async_computation.3 | async-start | bytes 8388608 | tf_op jit(solution)/shard_map/all_to_all | solution.py:136
  241.5 712.8 %reduce-scatter.4.cloned.1.call-start = ((), (), s32[]{:S(2)}) async-start(), calls=%async_computation.5 | async-start | bytes 4227072
  302.5 1.9 copy-start.2
  302.5 2.2 copy-start.3
Sparse Core Ops, SparseCore 0:
  313.3 640.9 reduce-scatter.3
where the time goes:
time: 962 us; the launch traced here: 961 us
  waiting for transfers between devices  791 us (82%)
  local copies, waits for them, and re-layouts  80.8 us (8%)
  starting transfers between devices  31.5 us (3%)
  matrix products  17.2 us (2%)
  blocking collectives  16.1 us (2%)
  between operations  14.3 us (1%)
  other arithmetic  10.7 us (1%)
    unnamed x2, waiting for transfers between devices  641 us
    all_to_all x1, waiting for transfers between devices, shards(): lax.all_to_all(served, 'dp', split_axis=0, concat_axis=0, tiled=True)  53 us
    all_to_all x1, waiting for transfers between devices, shards(): lax.all_to_all(back_rows, ('dp', 'rep'), split_axis=0, concat_axis=0, til...  51.2 us
    all_to_all x1, waiting for transfers between devices, shards(): lax.all_to_all(wide_rows.reshape(dp_count * rep_count, capacity, desc_wid...  44.7 us
    scatter x1, local copies, waits for them, and re-layouts, shards(): anchors = jnp.zeros((slot_number_count, desc_width), jnp.bfloat16).at[fla...  20.2 us
    gather x1, local copies, waits for them, and re-layouts, shards(): back_rows = share_grad[jnp.transpose(safe_slots, (1, 0, 2))]  19.3 us
  transfers between devices with their start and end apart: 5, of which 5 were waited for; matrix products, arithmetic and copies ran while one was open for 2% of the time, Pallas kernels for 0%

commit v1 on v0

v1 whole, which is shorter than its diff:
```python
import math

import jax
import jax.numpy as jnp
from jax import lax
from jax.experimental import pallas as pl
from jax.experimental.pallas import tpu as pltpu
from jax.sharding import PartitionSpec as P

BR = 128
PAIRS_REP = 2
REPS = 4

logit_sharpness = 0.05
objective_factor = 32.0
norm_eps = 1e-06

BF = jnp.bfloat16
F32 = jnp.float32
I32 = jnp.int32
VMEM_BYTES = 56 * 1024 * 1024


def params():
    return pltpu.CompilerParams(vmem_limit_bytes=VMEM_BYTES)


def iota(shape, dim):
    return lax.broadcasted_iota(I32, shape, dim)


def hot(mask):
    return jnp.where(mask, 1.0, 0.0).astype(BF)


def dot(a, b, ca=1, cb=0):
    return lax.dot_general(a, b, (((ca,), (cb,)), ((), ())), preferred_element_type=F32)


def sds(shape, dtype):
    return jax.ShapeDtypeStruct(shape, dtype)


def project_kernel(owner_slots, owners, cap, slot, feat, head, send, unit, norm, place):
    n = feat.shape[0]
    e = head.shape[1]
    projected = dot(feat[...], head[...])
    length = jnp.sqrt(jnp.sum(projected * projected, axis=1, keepdims=True) + norm_eps)
    rows = projected / length
    unit[...] = rows
    norm[...] = jnp.broadcast_to(length, norm.shape)
    descriptor = rows.astype(BF)
    s = slot[...]
    owner = s // owner_slots
    local = s - owner * owner_slots
    mine = iota((owners, n), 0) == owner
    before = dot(hot(mine), hot(iota((n, n), 0) < iota((n, n), 1)))
    rank = jnp.sum(jnp.where(mine, before, 0.0), axis=0, keepdims=True).astype(I32)
    p = (owner * REPS + (rank & (REPS - 1))) * cap + rank // REPS
    place[...] = jnp.broadcast_to(p.astype(F32), place.shape)
    count = send.shape[0]
    scatter = hot(iota((count, n), 0) == p)
    send[:, :e] = dot(scatter, descriptor).astype(BF)
    high = local // BR
    low = local - high * BR
    row = iota((BR, n), 0)
    tags = jnp.where(row == 0, high, jnp.where(row == 1, low, jnp.where(row == 2, 1, 0)))
    send[:, e:] = dot(scatter, tags.astype(F32).astype(BF), 1, 1).astype(BF)


def compact_kernel(got, packed, place):
    count = got.shape[0]
    e = packed.shape[1]
    rows = packed.shape[0] - 16
    tags = got[:, e:].astype(F32).T
    valid = tags[2:3, :]
    upper = hot(iota((count, count), 0) < iota((count, count), 1))
    before = dot(jnp.broadcast_to(valid, (16, count)).astype(BF), upper)[0:1, :]
    pos = jnp.where(valid > 0.5, before, -1.0)
    place[...] = jnp.broadcast_to(pos, place.shape)
    pick = hot(iota((rows, count), 0) == pos.astype(I32))
    packed[:rows, :] = dot(pick, got[:, :e]).astype(BF)
    packed[rows:, :] = dot(tags[:16, :].astype(BF), pick, 1, 1).astype(BF)


def anchors_kernel(serve, own, left, right, far_a, far_b, anchors, served, slots, sems):
    rows = own.shape[0] - 16
    half = rows // 2

    def slot_row(ref, base):
        tag = ref[base : base + 16, :].astype(F32)
        return (tag[0:1, :] * BR + tag[1:2, :]).astype(I32)

    ids = (
        slot_row(own, rows),
        slot_row(left, rows),
        slot_row(right, rows),
        slot_row(far_b, half),
    )
    for k in range(4):
        slots[k, :, :] = jnp.broadcast_to(ids[k].astype(F32), slots.shape[1:])
    step = 256

    def body(i, carry):
        base = pl.multiple_of(i * step, step)
        at = iota((step, rows), 0) + base
        total = dot(hot(at == ids[0]), own[:rows, :])
        total += dot(hot(at == ids[1]), left[:rows, :])
        total += dot(hot(at == ids[2]), right[:rows, :])
        far = hot(at == ids[3])
        total += dot(far[:, :half], far_a[...])
        total += dot(far[:, half:], far_b[:half, :])
        anchors[pl.ds(base, step), :] = total.astype(BF)
        return carry

    lax.fori_loop(0, anchors.shape[0] // step, body, 0)
    copies = []
    for d in range(served.shape[0]):
        start = pl.multiple_of(serve[d] * BR, BR)
        copies.append(
            pltpu.make_async_copy(anchors.at[pl.ds(start, BR), :], served.at[d], sems.at[d])
        )
    for c in copies:
        c.start()
    for c in copies:
        c.wait()


def scores_kernel(need, column, anchors, fetched, weights, stats):
    blocks = weights.shape[0]

    def body(i, carry):
        for j in range(4):
            b = i * 4 + j
            q = anchors[pl.ds(pl.multiple_of(b * BR, BR), BR), :]
            total = jnp.zeros((1, BR), F32)
            positive = jnp.zeros((1, BR), F32)
            want = column[pl.ds(b, 1), :]
            for k in range(PAIRS_REP):
                logits = dot(fetched[need[b * PAIRS_REP + k]], q, 1, 1) / logit_sharpness
                w = jnp.exp(logits - 1.0 / logit_sharpness)
                weights[b, k * BR : (k + 1) * BR, :] = w
                total += jnp.sum(w, axis=0, keepdims=True)
                hit = iota((BR, BR), 0) + k * BR == want
                positive += jnp.sum(jnp.where(hit, logits, 0.0), axis=0, keepdims=True)
            stats[pl.ds(b, 1), :] = total
            stats[pl.ds(blocks + b, 1), :] = positive
        return carry

    lax.fori_loop(0, blocks // 4, body, 0)


def grads_kernel(factor, need, column, stats, weights, fetched, slots, y0, y1, y2, y3, share):
    blocks = weights.shape[0]

    def body(i, carry):
        for j in range(4):
            b = i * 4 + j
            want = column[pl.ds(b, 1), :]
            total = stats[pl.ds(b, 1), :]
            grad = jnp.zeros((BR, share.shape[1]), F32)
            for k in range(PAIRS_REP):
                hit = iota((BR, BR), 0) + k * BR == want
                c = weights[b, k * BR : (k + 1) * BR, :] / total - jnp.where(hit, 1.0, 0.0)
                grad += dot(c.astype(BF).T, fetched[need[b * PAIRS_REP + k]])
            share[pl.ds(pl.multiple_of(b * BR, BR), BR), :] = (grad * factor).astype(BF)
        return carry

    lax.fori_loop(0, blocks // 4, body, 0)
    step = 256
    total_slots = share.shape[0]
    for k, out in enumerate((y0, y1, y2, y3)):
        ids = slots[k, :, :].T[:, 0:1].astype(I32)
        for h in range(out.shape[0] // step):
            pick = hot(iota((step, total_slots), 1) == ids[h * step : (h + 1) * step, :])
            out[h * step : (h + 1) * step, :] = dot(pick, share[...]).astype(BF)


def back_kernel(a, b, c, d, place, back):
    total = a[...].astype(F32) + b[...].astype(F32) + c[...].astype(F32) + d[...].astype(F32)
    rows = a.shape[0]
    pos = place[...].T[:, 0:1].astype(I32)
    back[...] = dot(hot(iota((back.shape[0], rows), 1) == pos), total.astype(BF)).astype(BF)


def head_grad_kernel(returned, place, unit, norm, feat, out):
    n = unit.shape[0]
    pos = place[...].T[:, 0:1].astype(I32)
    grad = dot(hot(iota((n, returned.shape[0]), 1) == pos), returned[...])
    rows = unit[...]
    radial = jnp.sum(rows * grad, axis=1, keepdims=True)
    g = ((grad - rows * radial) / norm[:, 0:1]).astype(BF)
    step = 512
    for i in range(feat.shape[1] // step):
        out[i * step : (i + 1) * step, :] = dot(feat[:, i * step : (i + 1) * step], g, 0, 0).astype(BF)


def sum_kernel(parts, out):
    out[...] = jnp.sum(parts[...].astype(F32), axis=0)


def turn(x, k):
    return lax.ppermute(x, "rep", [(i, (i + k) % REPS) for i in range(REPS)])


def shards(features, head_weight, slot_of_image, candidates, positives):
    dp = lax.axis_size("dp")
    me = lax.axis_index("dp")
    rep = lax.axis_index("rep")
    n, width = features.shape
    e = head_weight.shape[1]
    devices = dp * REPS
    owner_slots = n * REPS
    blocks = owner_slots // BR
    cap = 2 * n // devices
    count = devices * cap
    factor = objective_factor / (logit_sharpness * math.sqrt(n * devices))
    both = ("dp", "rep")
    vmem = pl.BlockSpec(memory_space=pltpu.VMEM)
    smem = pl.BlockSpec(memory_space=pltpu.SMEM)

    send, unit, norm, place = pl.pallas_call(
        lambda *r: project_kernel(owner_slots, dp, cap, *r),
        out_shape=(
            sds((count, e + BR), BF),
            sds((n, e), F32),
            sds((n, BR), F32),
            sds((BR, n), F32),
        ),
        compiler_params=params(),
        name="project",
    )(slot_of_image.reshape(1, n), features, head_weight)

    got = lax.all_to_all(send.reshape(devices, cap, e + BR), both, 0, 0, tiled=True)
    packed, back_place = pl.pallas_call(
        compact_kernel,
        out_shape=(sds((n + 16, e), BF), sds((BR, count), F32)),
        compiler_params=params(),
        name="compact",
    )(got.reshape(count, e + BR))

    left, right = turn(packed, 1), turn(packed, 3)
    half = n // 2
    far_a, far_b = turn(left[:half], 1), turn(right[half:], 3)

    table = candidates.reshape(dp, blocks, REPS, PAIRS_REP)
    table = lax.dynamic_index_in_dim(table, rep, axis=2, keepdims=False)
    table = table.reshape(dp, blocks * PAIRS_REP)
    owner = table // blocks
    serve = jnp.sum(jnp.where(owner == me, table - owner * blocks, 0), axis=1)
    need = lax.dynamic_index_in_dim(owner, me, axis=0, keepdims=False)
    column = positives.reshape(blocks, BR) - rep * (PAIRS_REP * BR)

    anchors, served, slots = pl.pallas_call(
        anchors_kernel,
        out_shape=(
            sds((owner_slots, e), BF),
            sds((dp, BR, e), BF),
            sds((4, BR, n), F32),
        ),
        in_specs=[smem] + [vmem] * 5,
        out_specs=(vmem, pl.BlockSpec(memory_space=pl.ANY), vmem),
        scratch_shapes=[pltpu.SemaphoreType.DMA((dp,))],
        compiler_params=params(),
        name="anchors",
    )(serve, packed, left, right, far_a, far_b)

    fetched = lax.all_to_all(served, "dp", 0, 0, tiled=True)

    weights, stats = pl.pallas_call(
        scores_kernel,
        out_shape=(sds((blocks, PAIRS_REP * BR, BR), F32), sds((2 * blocks, BR), F32)),
        in_specs=[smem] + [vmem] * 3,
        compiler_params=params(),
        name="scores",
    )(need, column, anchors, fetched)
    stats = lax.psum(stats, "rep")
    total, matching = stats[:blocks], stats[blocks:]
    anchor_row_loss = (jnp.log(total) + 1.0 / logit_sharpness - matching).reshape(owner_slots)

    y = pl.pallas_call(
        lambda *r: grads_kernel(factor, *r),
        out_shape=(sds((n, e), BF),) * 4,
        in_specs=[smem] + [vmem] * 5,
        scratch_shapes=[pltpu.VMEM((owner_slots, e), BF)],
        compiler_params=params(),
        name="grads",
    )(need, column, stats, weights, fetched, slots)
    shares = (y[0], turn(y[1], 3), turn(y[2], 1), turn(y[3], 2))
    back = pl.pallas_call(
        back_kernel,
        out_shape=sds((count, e), BF),
        compiler_params=params(),
        name="back",
    )(*shares, back_place)
    returned = lax.all_to_all(back.reshape(devices, cap, e), both, 0, 0, tiled=True)
    partial = pl.pallas_call(
        head_grad_kernel,
        out_shape=sds((width, e), BF),
        compiler_params=params(),
        name="head_grad",
    )(returned.reshape(count, e), place, unit, norm, features)
    parts = lax.all_to_all(partial.reshape(devices, width // devices, e), both, 0, 0, tiled=True)
    weight_grad = pl.pallas_call(
        sum_kernel,
        out_shape=sds((width // devices, e), F32),
        compiler_params=params(),
        name="add",
    )(parts)
    return (anchor_row_loss, weight_grad)


def solution(mesh):
    placed = (P(("dp", "rep"), None), P(), P(("dp", "rep")), P(), P("dp"))
    return jax.shard_map(
        shards,
        mesh=mesh,
        in_specs=placed,
        out_specs=(P("dp"), P(("dp", "rep"), None)),
        check_vma=False,
    )
```

time: 962 us -> 268 us (0.28)
  waiting for transfers between devices: 791 us -> 119 us
  local copies, waits for them, and re-layouts: 80.8 us -> 3.34 us
  blocking collectives: 16.1 us -> 74.1 us
  Pallas kernels: 0 us -> 49.9 us
  matrix products: 17.2 us -> 0 us
  starting transfers between devices: 31.5 us -> 17.3 us
  between operations: 14.3 us -> 0.75 us
    unnamed x2 -> x0, waiting for transfers between devices: 641 us -> none
    all_to_all x4 -> x2, waiting for transfers between devices: 150 us -> 81.2 us  [the longest x1 52 us: shards(): fetched = lax.all_to_all(served, 'dp', 0, 0, tiled=True)]
    all_to_all x0 -> x2, blocking collectives: none -> 58.3 us  [the longest x1 32.8 us: shards(): lax.all_to_all(send.reshape(devices, cap, e + BR), both, 0, 0, tiled=True)]
    pallas_call x0 -> x8, Pallas kernels: none -> 49.9 us  [the longest x1 11.2 us: shards(): pl.pallas_call(anchors_kernel, out_shape=(sds((owner_slots, e), BF), sds(...]
    ppermute x0 -> x7, waiting for transfers between devices: none -> 37.5 us  [turn(): return lax.ppermute(x, 'rep', [(i, (i + k) % REPS) for i in range(REPS)])]
    gather x5 -> x0, local copies, waits for them, and re-layouts: 33.5 us -> none  [the longest x1 19.3 us: shards(): back_rows = share_grad[jnp.transpose(safe_slots, (1, 0, 2))]]
    scatter x4 -> x0, local copies, waits for them, and re-layouts: 30.4 us -> none  [the longest x1 20.2 us: shards(): anchors = jnp.zeros((slot_number_count, desc_width), jnp.bfloat16).at[fla...]
    all_to_all x4 -> x2, starting transfers between devices: 31.2 us -> 10.2 us  [the longest x1 5.38 us: shards(): fetched = lax.all_to_all(served, 'dp', 0, 0, tiled=True)]
  transfers between devices with their start and end apart: 5 -> 9, of which waited for: 5 -> 6; matrix products, arithmetic and copies ran while one was open for 2% -> 1% of each run, Pallas kernels for 0% -> 0%
where the time goes in v1:
time: 268 us; the launch traced here: 267 us
  waiting for transfers between devices  119 us (44%)
  blocking collectives  74.1 us (28%)
  Pallas kernels  49.9 us (19%)
  starting transfers between devices  17.3 us (6%)
  local copies, waits for them, and re-layouts  3.34 us (1%)
    all_to_all x1, waiting for transfers between devices, shards(): fetched = lax.all_to_all(served, 'dp', 0, 0, tiled=True)  52 us
    ppermute x7, waiting for transfers between devices, turn(): return lax.ppermute(x, 'rep', [(i, (i + k) % REPS) for i in range(REPS)])  37.5 us
    all_to_all x1, blocking collectives, shards(): lax.all_to_all(send.reshape(devices, cap, e + BR), both, 0, 0, tiled=True)  32.8 us
    all_to_all x1, waiting for transfers between devices, shards(): lax.all_to_all(partial.reshape(devices, width // devices, e), both, 0, 0,...  29.2 us
    all_to_all x1, blocking collectives, shards(): lax.all_to_all(back.reshape(devices, cap, e), both, 0, 0, tiled=True)  25.5 us
    psum x1, blocking collectives, shards(): stats = lax.psum(stats, 'rep')  15.8 us
    pallas_call x1, Pallas kernels, shards(): pl.pallas_call(anchors_kernel, out_shape=(sds((owner_slots, e), BF), sds(...  11.2 us
    pallas_call x1, Pallas kernels, shards(): pl.pallas_call(lambda *r: grads_kernel(factor, *r), out_shape=(sds((n, e)...  11.2 us
  transfers between devices with their start and end apart: 9, of which 6 were waited for; matrix products, arithmetic and copies ran while one was open for 1% of the time, Pallas kernels for 0%

profile of v1, /device:TPU:0, one launch (start us, length us, event | category | flops | bytes accessed | tf_op | source)
XLA Modules:
  0.0 266.7 jit_solution(4348806280759563104)
XLA Ops:
  0.6 5.7 %project.1 = (bf16[1024,640]{1,0:T(8,128)(2,1)}, f32[512,512]{1,0:T(8,128)}, f32[512,128]{1,0:T(8,128)}, f32[128,512]{1,0:T(8,128)}) custom-call(s32[1,512]{1,0:T(1,128)} %bitcast.21, bf16[512,2048]{1,0:T(8,128)(2,1)} %feat.1, bf16[2048,512]{1,0:T(8,128)(2,1)} %r_2_.1), custom_call_target="tpu_custom_call" | custom-call | tf_op jit(solution)/shard_map/project/pallas_call | solution.py:222
  6.3 32.8 %all_to_all.20 = bf16[128,8,640]{2,1,0:T(8,128)(2,1)} all-to-all(bf16[128,8,640]{2,1,0:T(8,128)(2,1)} %bitcast.17), channel_id=1, replica_groups=mesh['dp'=32,'rep'=4] {'dp','rep'}, dimensions={0} | all-to-all | bytes 2621440 | tf_op jit(solution)/shard_map/all_to_all | solution.py:234
  39.1 3.3 %compact.1 = (bf16[528,512]{1,0:T(8,128)(2,1)}, f32[128,1024]{1,0:T(8,128)}) custom-call(bf16[1024,640]{1,0:T(8,128)(2,1)} %bitcast.14), custom_call_target="tpu_custom_call" | custom-call | tf_op jit(solution)/shard_map/compact/pallas_call | solution.py:235
  42.5 1.2 collective-permute-start.1
  43.7 0.8 collective-permute-start
  44.5 12.5 %collective-permute-done.1.right = bf16[528,512]{1,0:T(8,128)(2,1)S(1)} collective-permute-done((bf16[528,512]{1,0:T(8,128)(2,1)}, bf16[528,512]{1,0:T(8,128)(2,1)S(1)}, u32[]{:S(2)}, u32[]{:S(2)}) %collective-permute-start.1) | collective-permute-done | bytes 540704 | tf_op jit(solution)/shard_map/ppermute | solution.py:203
  57.0 2.2 collective-permute-start.3
  59.4 0.7 select_reduce_fusion
  60.0 7.3 %collective-permute-done.2.far_a = bf16[256,512]{1,0:T(8,128)(2,1)S(1)} collective-permute-done((bf16[256,512]{1,0:T(8,128)(2,1)S(1)}, bf16[256,512]{1,0:T(8,128)(2,1)S(1)}, u32[]{:S(2)}, u32[]{:S(2)}) %collective-permute-start.2) | collective-permute-done | bytes 262176 | tf_op jit(solution)/shard_map/ppermute | solution.py:203
  67.3 0.7 copy-done.7
  68.1 11.2 %anchors.1 = (bf16[2048,512]{1,0:T(8,128)(2,1)}, bf16[32,128,512]{2,1,0:T(8,128)(2,1)}, f32[4,128,512]{2,1,0:T(8,128)}) custom-call(s32[32]{0:T(128)} %get-tuple-element.32.serve, bf16[528,512]{1,0:T(8,128)(2,1)} %get-tuple-element.18.own, bf16[528,512]{1,0:T(8,128)(2,1)} %copy-done.2, bf16[528,512]{1,0:T(8,128)(2,1)} %copy-done.1, ...), custom_call_target="tpu_custom_call" | custom-call | tf_op jit(solution)/shard_map/anchors/pallas_call | solution.py:254
  79.3 5.4 %all-to-all-start.1 = ((bf16[32,128,512]{2,1,0:T(8,128)(2,1)}), bf16[32,128,512]{2,1,0:T(8,128)(2,1)}, u32[]{:S(2)}, u32[]{:S(2)}) async-start(bf16[32,128,512]{2,1,0:T(8,128)(2,1)} %get-tuple-element.20), calls=%async_computation.1 | async-start | bytes 8388608 | tf_op jit(solution)/shard_map/all_to_all | solution.py:268
  84.8 0.7 fusion.3.need.r_0_
  85.5 0.6 subtract_bitcast_fusion.column.r_1_
  86.1 52.0 %all-to-all-done.1.fetched.r_4_ = bf16[32,128,512]{2,1,0:T(8,128)(2,1)} async-done(((bf16[32,128,512]{2,1,0:T(8,128)(2,1)}), bf16[32,128,512]{2,1,0:T(8,128)(2,1)}, u32[]{:S(2)}, u32[]{:S(2)}) %all-to-all-start.1) | async-done | bytes 4194336 | tf_op jit(solution)/shard_map/all_to_all | solution.py:268
  138.2 6.0 %scores.1 = (f32[16,256,128]{2,1,0:T(8,128)}, f32[32,128]{1,0:T(8,128)}) custom-call(s32[32]{0:T(128)} %fusion.3.need.r_0_, s32[16,128]{1,0:T(8,128)} %subtract_bitcast_fusion.column.r_1_, bf16[2048,512]{1,0:T(8,128)(2,1)} %get-tuple-element.19.anchors, bf16[32,128,512]{2,1,0:T(8,128)(2,1)} %all-to-all-done.1.fetched.r_4_), custom_call_target="tpu_custom_call" | custom-call | tf_op jit(solution)/shard_map/scores/pallas_call | solution.py:270
  144.2 15.8 %psum.7.r_2_ = f32[32,128]{1,0:T(8,128)} all-reduce(f32[32,128]{1,0:T(8,128)} %get-tuple-element.21), channel_id=1, replica_groups=mesh['dp'=32,'rep'=4] {'rep'}, use_global_device_ids=true, to_apply=%region_1.2 | all-reduce | flops 4096 | bytes 32768 | tf_op jit(solution)/shard_map/psum | solution.py:277
  160.0 11.2 %grads.1 = (bf16[512,512]{1,0:T(8,128)(2,1)}, bf16[512,512]{1,0:T(8,128)(2,1)}, bf16[512,512]{1,0:T(8,128)(2,1)}, bf16[512,512]{1,0:T(8,128)(2,1)}) custom-call(s32[32]{0:T(128)} %fusion.3.need.r_0_, s32[16,128]{1,0:T(8,128)} %subtract_bitcast_fusion.column.r_1_, f32[32,128]{1,0:T(8,128)} %psum.7.r_2_, f32[16,256,128]{2,1,0:T(8,128)} %get-tuple-element.22.r_3_, ...), custom_call_target="tpu_custom_call" | custom-call | tf_op jit(solution)/shard_map/grads/pallas_call | solution.py:281
  171.2 1.0 collective-permute-start.4
  172.2 1.0 collective-permute-start.5
  173.2 0.8 collective-permute-start.6
  174.1 10.1 %collective-permute-done.4.b = bf16[512,512]{1,0:T(8,128)(2,1)S(1)} collective-permute-done((bf16[512,512]{1,0:T(8,128)(2,1)}, bf16[512,512]{1,0:T(8,128)(2,1)S(1)}, u32[]{:S(2)}, u32[]{:S(2)}) %collective-permute-start.4) | collective-permute-done | bytes 524320 | tf_op jit(solution)/shard_map/ppermute | solution.py:203
  184.1 7.7 %collective-permute-done.5.c = bf16[512,512]{1,0:T(8,128)(2,1)S(1)} collective-permute-done((bf16[512,512]{1,0:T(8,128)(2,1)}, bf16[512,512]{1,0:T(8,128)(2,1)S(1)}, u32[]{:S(2)}, u32[]{:S(2)}) %collective-permute-start.5) | collective-permute-done | bytes 524320 | tf_op jit(solution)/shard_map/ppermute | solution.py:203
  191.8 0.8 copy-done.4
  192.8 3.8 %back.1 = bf16[1024,512]{1,0:T(8,128)(2,1)} custom-call(bf16[512,512]{1,0:T(8,128)(2,1)} %get-tuple-element.24.a, bf16[512,512]{1,0:T(8,128)(2,1)} %copy-done.3, bf16[512,512]{1,0:T(8,128)(2,1)} %copy-done.4, bf16[512,512]{1,0:T(8,128)(2,1)} %copy-done.5, f32[128,1024]{1,0:T(8,128)} %get-tuple-element.28.place), custom_call_target="tpu_custom_call" | custom-call | tf_op jit(solution)/shard_map/back/pallas_call | solution.py:290
  196.6 25.5 %all_to_all.21 = bf16[128,8,512]{2,1,0:T(8,128)(2,1)} all-to-all(bf16[128,8,512]{2,1,0:T(8,128)(2,1)} %bitcast.15), channel_id=1, replica_groups=mesh['dp'=32,'rep'=4] {'dp','rep'}, dimensions={0} | all-to-all | bytes 2097152 | tf_op jit(solution)/shard_map/all_to_all | solution.py:296
  222.1 6.1 %head_grad.1 = bf16[2048,512]{1,0:T(8,128)(2,1)} custom-call(bf16[1024,512]{1,0:T(8,128)(2,1)} %bitcast.16, f32[128,512]{1,0:T(8,128)} %get-tuple-element.29.place, f32[512,512]{1,0:T(8,128)} %get-tuple-element.30.unit, f32[512,128]{1,0:T(8,128)} %get-tuple-element.31.norm, bf16[512,2048]{1,0:T(8,128)(2,1)} %feat.1), custom_call_target="tpu_custom_call" | custom-call | tf_op jit(solution)/shard_map/head_grad/pallas_call | solution.py:297
  228.2 4.8 %all-to-all-start.3 = ((bf16[128,16,512]{2,1,0:T(8,128)(2,1)}), bf16[128,16,512]{2,1,0:T(8,128)(2,1)S(1)}, u32[]{:S(2)}, u32[]{:S(2)}) async-start(bf16[128,16,512]{2,1,0:T(8,128)(2,1)} %bitcast.13), calls=%async_computation.3 | async-start | bytes 4194304 | tf_op jit(solution)/shard_map/all_to_all | solution.py:303
  233.0 0.6 fusion.6
  233.6 29.2 %all-to-all-done.3.parts = bf16[128,16,512]{2,1,0:T(8,128)(2,1)S(1)} async-done(((bf16[128,16,512]{2,1,0:T(8,128)(2,1)}), bf16[128,16,512]{2,1,0:T(8,128)(2,1)S(1)}, u32[]{:S(2)}, u32[]{:S(2)}) %all-to-all-start.3) | async-done | bytes 2097184 | tf_op jit(solution)/shard_map/all_to_all | solution.py:303
  262.8 1.3 copy-done
  264.1 2.6 add.28
  (29 shorter events, 0.6 us)
Async XLA Ops:
  6.3 52.9 %copy-start.9 = (s32[512,8]{0,1:T(8,128)S(1)}, s32[512,8]{0,1:T(8,128)}, u32[]{:S(2)}) copy-start(s32[512,8]{0,1:T(8,128)} %param.8) | copy-start | bytes 49156
  42.5 14.5 %collective-permute-start.1 = (bf16[528,512]{1,0:T(8,128)(2,1)}, bf16[528,512]{1,0:T(8,128)(2,1)S(1)}, u32[]{:S(2)}, u32[]{:S(2)}) collective-permute-start(bf16[528,512]{1,0:T(8,128)(2,1)} %get-tuple-element.18.own), channel_id=1, source_target_pairs={{0,3},{1,0},{2,1},{3,2},{4,7},{5,4},{6,5},{7,6},{8,11},{9,8},{10,9... | collective-permute-start | bytes 1622024 | tf_op jit(solution)/shard_map/ppermute | solution.py:203
  43.7 15.5 %collective-permute-start = (bf16[528,512]{1,0:T(8,128)(2,1)}, bf16[528,512]{1,0:T(8,128)(2,1)S(1)}, u32[]{:S(2)}, u32[]{:S(2)}) collective-permute-start(bf16[528,512]{1,0:T(8,128)(2,1)} %get-tuple-element.18.own), channel_id=1, source_target_pairs={{0,1},{1,2},{2,3},{3,0},{4,5},{5,6},{6,7},{7,4},{8,9},{9,10},{10,1... | collective-permute-start | bytes 1622024 | tf_op jit(solution)/shard_map/ppermute | solution.py:203
  57.0 10.3 %copy-start.1 = (bf16[528,512]{1,0:T(8,128)(2,1)}, bf16[528,512]{1,0:T(8,128)(2,1)S(1)}, u32[]{:S(2)}) copy-start(bf16[528,512]{1,0:T(8,128)(2,1)S(1)} %collective-permute-done.1.right) | copy-start | bytes 1622020
  57.0 10.3 %collective-permute-start.3 = (bf16[272,512]{1,0:T(8,128)(2,1)S(1)}, bf16[272,512]{1,0:T(8,128)(2,1)S(1)}, u32[]{:S(2)}, u32[]{:S(2)}) collective-permute-start(bf16[272,512]{1,0:T(8,128)(2,1)S(1)} %slice.17), channel_id=1, source_target_pairs={{0,3},{1,0},{2,1},{3,2},{4,7},{5,4},{6,5},{7,6},{8,11},{9,8},{10,9... | collective-permute-start | bytes 835592 | tf_op jit(solution)/shard_map/ppermute | solution.py:203
  59.1 8.2 %copy-start.2 = (bf16[528,512]{1,0:T(8,128)(2,1)}, bf16[528,512]{1,0:T(8,128)(2,1)S(1)}, u32[]{:S(2)}) copy-start(bf16[528,512]{1,0:T(8,128)(2,1)S(1)} %collective-permute-done.left) | copy-start | bytes 1622020
  59.2 8.1 %collective-permute-start.2 = (bf16[256,512]{1,0:T(8,128)(2,1)S(1)}, bf16[256,512]{1,0:T(8,128)(2,1)S(1)}, u32[]{:S(2)}, u32[]{:S(2)}) collective-permute-start(bf16[256,512]{1,0:T(8,128)(2,1)S(1)} %slice.16), channel_id=1, source_target_pairs={{0,1},{1,2},{2,3},{3,0},{4,5},{5,6},{6,7},{7,4},{8,9},{9,10},{10,1... | collective-permute-start | bytes 786440 | tf_op jit(solution)/shard_map/ppermute | solution.py:203
  67.3 0.7 copy-start.7
  67.3 0.8 copy-start.6
  79.3 6.2 %copy-start.10 = (s32[2048]{0:T(1024)S(1)}, s32[2048]{0:T(1024)}, u32[]{:S(2)}) copy-start(s32[2048]{0:T(1024)} %param.9) | copy-start | bytes 24580
  79.3 58.9 %all-to-all-start.1 = ((bf16[32,128,512]{2,1,0:T(8,128)(2,1)}), bf16[32,128,512]{2,1,0:T(8,128)(2,1)}, u32[]{:S(2)}, u32[]{:S(2)}) async-start(bf16[32,128,512]{2,1,0:T(8,128)(2,1)} %get-tuple-element.20), calls=%async_computation.1 | async-start | bytes 8388608 | tf_op jit(solution)/shard_map/all_to_all | solution.py:268
  171.2 12.9 %collective-permute-start.4 = (bf16[512,512]{1,0:T(8,128)(2,1)}, bf16[512,512]{1,0:T(8,128)(2,1)S(1)}, u32[]{:S(2)}, u32[]{:S(2)}) collective-permute-start(bf16[512,512]{1,0:T(8,128)(2,1)} %get-tuple-element.25), channel_id=1, source_target_pairs={{0,3},{1,0},{2,1},{3,2},{4,7},{5,4},{6,5},{7,6},{8,11},{9,8},{10,9... | collective-permute-start | bytes 1572872 | tf_op jit(solution)/shard_map/ppermute | solution.py:203
  172.2 19.6 %collective-permute-start.5 = (bf16[512,512]{1,0:T(8,128)(2,1)}, bf16[512,512]{1,0:T(8,128)(2,1)S(1)}, u32[]{:S(2)}, u32[]{:S(2)}) collective-permute-start(bf16[512,512]{1,0:T(8,128)(2,1)} %get-tuple-element.26), channel_id=1, source_target_pairs={{0,1},{1,2},{2,3},{3,0},{4,5},{5,6},{6,7},{7,4},{8,9},{9,10},{10,1... | collective-permute-start | bytes 1572872 | tf_op jit(solution)/shard_map/ppermute | solution.py:203
  173.2 18.6 %collective-permute-start.6 = (bf16[512,512]{1,0:T(8,128)(2,1)}, bf16[512,512]{1,0:T(8,128)(2,1)S(1)}, u32[]{:S(2)}, u32[]{:S(2)}) collective-permute-start(bf16[512,512]{1,0:T(8,128)(2,1)} %get-tuple-element.27), channel_id=1, source_target_pairs={{0,2},{1,3},{2,0},{3,1},{4,6},{5,7},{6,4},{7,5},{8,10},{9,11},{10,... | collective-permute-start | bytes 1572872 | tf_op jit(solution)/shard_map/ppermute | solution.py:203
  184.1 7.7 %copy-start.3 = (bf16[512,512]{1,0:T(8,128)(2,1)}, bf16[512,512]{1,0:T(8,128)(2,1)S(1)}, u32[]{:S(2)}) copy-start(bf16[512,512]{1,0:T(8,128)(2,1)S(1)} %collective-permute-done.4.b) | copy-start | bytes 1572868
  191.8 0.8 copy-start.4
  191.8 1.0 copy-start.5
  228.2 4.8 %copy-start.8 = (f32[32,128]{1,0:T(8,128)S(1)}, f32[32,128]{1,0:T(8,128)}, u32[]{:S(2)}) copy-start(f32[32,128]{1,0:T(8,128)} %psum.7.r_2_) | copy-start | bytes 49156
  228.2 34.6 %all-to-all-start.3 = ((bf16[128,16,512]{2,1,0:T(8,128)(2,1)}), bf16[128,16,512]{2,1,0:T(8,128)(2,1)S(1)}, u32[]{:S(2)}, u32[]{:S(2)}) async-start(bf16[128,16,512]{2,1,0:T(8,128)(2,1)} %bitcast.13), calls=%async_computation.3 | async-start | bytes 4194304 | tf_op jit(solution)/shard_map/all_to_all | solution.py:303
  262.8 1.3 copy-start

commit v2 on v1

v2 whole, which is shorter than its diff:
```python
import math

import jax
import jax.numpy as jnp
from jax import lax
from jax.experimental import pallas as pl
from jax.experimental.pallas import tpu as pltpu
from jax.sharding import PartitionSpec as P

BR = 128
PAIRS_REP = 2
REPS = 4

logit_sharpness = 0.05
objective_factor = 32.0
norm_eps = 1e-06

BF = jnp.bfloat16
F32 = jnp.float32
I32 = jnp.int32
VMEM_BYTES = 56 * 1024 * 1024


def params():
    return pltpu.CompilerParams(vmem_limit_bytes=VMEM_BYTES)


def iota(shape, dim):
    return lax.broadcasted_iota(I32, shape, dim)


def hot(mask):
    return jnp.where(mask, 1.0, 0.0).astype(BF)


def dot(a, b, ca=1, cb=0):
    return lax.dot_general(a, b, (((ca,), (cb,)), ((), ())), preferred_element_type=F32)


def sds(shape, dtype):
    return jax.ShapeDtypeStruct(shape, dtype)


def column_of(rows):
    wide = jnp.concatenate([rows] * (BR // rows.shape[0]), axis=0)
    return wide.T[:, 0:1].astype(I32)


def project_kernel(owner_slots, owners, cap, slot, feat, head, send0, send1, unit, norm, place):
    n = feat.shape[0]
    h = head.shape[1] // 2
    projected = dot(feat[...], head[...])
    length = jnp.sqrt(jnp.sum(projected * projected, axis=1, keepdims=True) + norm_eps)
    rows = projected / length
    unit[...] = rows
    norm[...] = jnp.broadcast_to(length, norm.shape)
    descriptor = rows.astype(BF)
    s = slot[...]
    owner = s // owner_slots
    local = s - owner * owner_slots
    mine = iota((owners, n), 0) == owner
    before = dot(hot(mine), hot(iota((n, n), 0) < iota((n, n), 1)))
    rank = jnp.sum(jnp.where(mine, before, 0.0), axis=0, keepdims=True).astype(I32)
    p = (owner * REPS + (rank & (REPS - 1))) * cap + rank // REPS
    place[...] = jnp.broadcast_to(p.astype(F32), place.shape)
    scatter = hot(iota((send0.shape[0], n), 0) == p)
    send0[:, :h] = dot(scatter, descriptor[:, :h]).astype(BF)
    send1[...] = dot(scatter, descriptor[:, h:]).astype(BF)
    high = local // BR
    low = local - high * BR
    row = iota((BR, n), 0)
    tags = jnp.where(row == 0, high, jnp.where(row == 1, low, jnp.where(row == 2, 1, 0)))
    send0[:, h:] = dot(scatter, tags.astype(F32).astype(BF), 1, 1).astype(BF)


def stripes_kernel(core, feat, mine, other):
    n = feat.shape[0]
    first = core[0] == 0
    half = BR // 2
    for z in range(feat.shape[1] // BR):
        t = feat[:, z * BR : (z + 1) * BR].astype(F32).T
        a, b = t[:half, :], t[half:, :]
        mine[z * half : (z + 1) * half, :] = jnp.where(first, a, b).astype(BF)
        other[z * half : (z + 1) * half, :] = jnp.where(first, b, a).astype(BF)


def compact0_kernel(got, packed, place):
    count = got.shape[0]
    h = packed.shape[1]
    rows = packed.shape[0] - 32
    tags = got[:, h:].astype(F32).T
    valid = tags[2:3, :]
    upper = hot(iota((count, count), 0) < iota((count, count), 1))
    before = dot(jnp.broadcast_to(valid, (16, count)).astype(BF), upper)[0:1, :]
    pos = jnp.where(valid > 0.5, before, -1.0)
    place[...] = jnp.broadcast_to(pos, place.shape)
    pick = hot(iota((rows, count), 0) == pos.astype(I32))
    packed[:rows, :] = dot(pick, got[:, :h]).astype(BF)
    tag = dot(tags[:16, :].astype(BF), pick, 1, 1).astype(BF)
    packed[rows : rows + 16, :] = tag[:, :h]
    packed[rows + 16 :, :] = tag[:, h:]


def compact1_kernel(got, place, packed):
    rows, count = packed.shape[0], got.shape[0]
    pick = hot(iota((rows, count), 0) == place[0:1, :].astype(I32))
    packed[...] = dot(pick, got[...]).astype(BF)


def near0_kernel(own, left, right, partial, slots):
    n = own.shape[0] - 32
    ids = []
    for k, ref in enumerate((own, left, right)):
        tag = ref[n:, :].astype(F32)
        row = jnp.concatenate(
            [tag[0:1, :] * BR + tag[1:2, :], tag[16:17, :] * BR + tag[17:18, :]], axis=1
        )
        slots[k, :, :] = jnp.broadcast_to(row, slots.shape[1:])
        ids.append(row.astype(I32))
    place_rows(partial, [(ids[k], ref[:n, :]) for k, ref in enumerate((own, left, right))], None)


def near1_kernel(own, left, right, slots, partial):
    ids = [slots[k, 0:1, :].astype(I32) for k in range(3)]
    place_rows(partial, [(ids[k], ref[...]) for k, ref in enumerate((own, left, right))], None)


def place_rows(out, pieces, start):
    step = 256

    def body(i, carry):
        base = pl.multiple_of(i * step, step)
        total = None if start is None else start[pl.ds(base, step), :].astype(F32)
        for ids, rows in pieces:
            at = iota((step, rows.shape[0]), 0) + base
            part = dot(hot(at == ids), rows)
            total = part if total is None else total + part
        out[pl.ds(base, step), :] = total.astype(BF)
        return carry

    lax.fori_loop(0, out.shape[0] // step, body, 0)


def serve_blocks(serve, anchors, served, sems):
    copies = []
    for d in range(served.shape[0]):
        start = pl.multiple_of(serve[d] * BR, BR)
        copies.append(
            pltpu.make_async_copy(anchors.at[pl.ds(start, BR), :], served.at[d], sems.at[d])
        )
    for c in copies:
        c.start()
    for c in copies:
        c.wait()


def far0_kernel(serve, partial, far_a, far_b, anchors, served, slots, sems):
    q = far_a.shape[0]
    tag = far_b[q:, :].astype(F32)
    row = jnp.concatenate(
        [tag[0:1, :] * BR + tag[1:2, :], tag[16:17, :] * BR + tag[17:18, :]], axis=1
    )
    slots[...] = jnp.broadcast_to(row, slots.shape)
    ids = row.astype(I32)
    place_rows(anchors, [(ids[:, :q], far_a[...]), (ids[:, q:], far_b[:q, :])], partial)
    serve_blocks(serve, anchors, served, sems)


def far1_kernel(serve, partial, far_a, far_b, slots, anchors, served, sems):
    q = far_a.shape[0]
    ids = slots[0:1, :].astype(I32)
    place_rows(anchors, [(ids[:, :q], far_a[...]), (ids[:, q:], far_b[...])], partial)
    serve_blocks(serve, anchors, served, sems)


def logits_kernel(need, anchors, fetched, out):
    blocks = out.shape[0]

    def body(i, carry):
        for j in range(4):
            b = i * 4 + j
            q = anchors[pl.ds(pl.multiple_of(b * BR, BR), BR), :]
            for k in range(PAIRS_REP):
                out[b, k * BR : (k + 1) * BR, :] = dot(fetched[need[b * PAIRS_REP + k]], q, 1, 1)
        return carry

    lax.fori_loop(0, blocks // 4, body, 0)


def scores_kernel(need, column, begun, anchors, fetched, weights, stats):
    blocks = weights.shape[0]

    def body(i, carry):
        for j in range(4):
            b = i * 4 + j
            q = anchors[pl.ds(pl.multiple_of(b * BR, BR), BR), :]
            total = jnp.zeros((1, BR), F32)
            positive = jnp.zeros((1, BR), F32)
            want = column[pl.ds(b, 1), :]
            for k in range(PAIRS_REP):
                raw = begun[b, k * BR : (k + 1) * BR, :] + dot(fetched[need[b * PAIRS_REP + k]], q, 1, 1)
                logits = raw / logit_sharpness
                w = jnp.exp(logits - 1.0 / logit_sharpness)
                weights[b, k * BR : (k + 1) * BR, :] = w
                total += jnp.sum(w, axis=0, keepdims=True)
                hit = iota((BR, BR), 0) + k * BR == want
                positive += jnp.sum(jnp.where(hit, logits, 0.0), axis=0, keepdims=True)
            stats[pl.ds(b, 1), :] = total
            stats[pl.ds(blocks + b, 1), :] = positive
        return carry

    lax.fori_loop(0, blocks // 4, body, 0)


def grads_kernel(factor, need, column, stats, weights, fetched, slots, far, y0, y1, y2, y3, share):
    blocks = weights.shape[0]

    def body(i, carry):
        for j in range(4):
            b = i * 4 + j
            want = column[pl.ds(b, 1), :]
            total = stats[pl.ds(b, 1), :]
            grad = jnp.zeros((BR, share.shape[1]), F32)
            for k in range(PAIRS_REP):
                hit = iota((BR, BR), 0) + k * BR == want
                c = weights[b, k * BR : (k + 1) * BR, :] / total - jnp.where(hit, 1.0, 0.0)
                grad += dot(c.astype(BF).T, fetched[need[b * PAIRS_REP + k]])
            share[pl.ds(pl.multiple_of(b * BR, BR), BR), :] = (grad * factor).astype(BF)
        return carry

    lax.fori_loop(0, blocks // 4, body, 0)
    step = 256
    total_slots = share.shape[0]
    ids = [column_of(slots[k, :, :]) for k in range(3)] + [column_of(far[...])]
    for k, out in enumerate((y0, y1, y2, y3)):
        for h in range(out.shape[0] // step):
            pick = hot(iota((step, total_slots), 1) == ids[k][h * step : (h + 1) * step, :])
            out[h * step : (h + 1) * step, :] = dot(pick, share[...]).astype(BF)


def back_kernel(a, b, c, d, place, back):
    total = a[...].astype(F32) + b[...].astype(F32) + c[...].astype(F32) + d[...].astype(F32)
    rows = a.shape[0]
    pos = column_of(place[...])
    back[...] = dot(hot(iota((back.shape[0], rows), 1) == pos), total.astype(BF)).astype(BF)


def unit_grad_kernel(got0, got1, place, unit, norm, out):
    n, e = unit.shape
    h = e // 2
    pick = hot(iota((n, got0.shape[0]), 1) == column_of(place[...]))
    grad0 = dot(pick, got0[...])
    grad1 = dot(pick, got1[...])
    rows0, rows1 = unit[:, :h], unit[:, h:]
    radial = jnp.sum(rows0 * grad0, axis=1, keepdims=True)
    radial += jnp.sum(rows1 * grad1, axis=1, keepdims=True)
    length = norm[:, 0:1]
    out[:, :h] = ((grad0 - rows0 * radial) / length).astype(BF)
    out[:, h:] = ((grad1 - rows1 * radial) / length).astype(BF)


def head_grad_kernel(mine, theirs, grad, partner, out):
    step = 256
    for i in range(out.shape[0] // step):
        at = slice(i * step, (i + 1) * step)
        out[at, :] = (dot(mine[at, :], grad[...]) + dot(theirs[at, :], partner[...])).astype(BF)


def sum_kernel(parts, out):
    out[...] = jnp.sum(parts[...].astype(F32), axis=0)


def turn(x, k):
    return lax.ppermute(x, "rep", [(i, (i + k) % REPS) for i in range(REPS)])


def swap(x):
    return lax.ppermute(x, "core", [(0, 1), (1, 0)])


def gather_rep(x):
    half = x.shape[0] // 2 if x.shape[0] % 64 == 0 else (x.shape[0] - 32) // 2
    left, right = turn(x, 1), turn(x, 3)
    return left, right, turn(left[:half], 1), turn(right[half:], 3)


def exchange(x, axes):
    return lax.all_to_all(x, axes, 0, 0, tiled=True)


def shards(features, head_weight, slot_of_image, candidates, positives):
    owners_axes = ("zx", "core")
    everyone = ("zx", "core", "rep")
    dp = lax.axis_size(owners_axes)
    me = lax.axis_index(owners_axes)
    core = lax.axis_index("core")
    rep = lax.axis_index("rep")
    n, width = features.shape
    e = head_weight.shape[1]
    h = e // 2
    devices = dp * REPS
    owner_slots = n * REPS
    blocks = owner_slots // BR
    cap = 2 * n // devices
    count = devices * cap
    factor = objective_factor / (logit_sharpness * math.sqrt(n * devices))
    vmem = pl.BlockSpec(memory_space=pltpu.VMEM)
    smem = pl.BlockSpec(memory_space=pltpu.SMEM)
    far_away = pl.BlockSpec(memory_space=pl.ANY)

    def call(kernel, name, shapes, args, **more):
        return pl.pallas_call(
            kernel, out_shape=shapes, compiler_params=params(), name=name, **more
        )(*args)

    send0, send1, unit, norm, place = call(
        lambda *r: project_kernel(owner_slots, dp, cap, *r),
        "project",
        (
            sds((count, h + BR), BF),
            sds((count, h), BF),
            sds((n, e), F32),
            sds((n, BR), F32),
            sds((8, n), F32),
        ),
        (slot_of_image.reshape(1, n), features, head_weight),
    )
    got0 = exchange(send0.reshape(devices, cap, h + BR), everyone).reshape(count, h + BR)
    got1 = exchange(send1.reshape(devices, cap, h), everyone).reshape(count, h)

    mine, other = call(
        stripes_kernel,
        "stripes",
        (sds((width // 2, n), BF),) * 2,
        (core.reshape(1), features),
        in_specs=[smem, vmem],
    )
    theirs = swap(other)

    packed0, back_place = call(
        compact0_kernel, "compact0", (sds((n + 32, h), BF), sds((8, count), F32)), (got0,)
    )
    left0, right0, far_a0, far_b0 = gather_rep(packed0)
    packed1 = call(compact1_kernel, "compact1", sds((n, h), BF), (got1, back_place))
    left1, right1, far_a1, far_b1 = gather_rep(packed1)

    table = candidates.reshape(dp, blocks, REPS, PAIRS_REP)
    table = lax.dynamic_index_in_dim(table, rep, axis=2, keepdims=False)
    table = table.reshape(dp, blocks * PAIRS_REP)
    owner = table // blocks
    serve = jnp.sum(jnp.where(owner == me, table - owner * blocks, 0), axis=1)
    need = lax.dynamic_index_in_dim(owner, me, axis=0, keepdims=False)
    column = positives.reshape(blocks, BR) - rep * (PAIRS_REP * BR)

    partial0, slots = call(
        near0_kernel,
        "near0",
        (sds((owner_slots, h), BF), sds((3, 8, n), F32)),
        (packed0, left0, right0),
    )
    served_shape = sds((dp, BR, h), BF)
    sems = [pltpu.SemaphoreType.DMA((dp,))]
    anchors0, served0, far = call(
        far0_kernel,
        "far0",
        (sds((owner_slots, h), BF), served_shape, sds((8, n), F32)),
        (serve, partial0, far_a0, far_b0),
        in_specs=[smem] + [vmem] * 3,
        out_specs=(vmem, far_away, vmem),
        scratch_shapes=sems,
    )
    fetched0 = exchange(served0, owners_axes)
    partial1 = call(
        near1_kernel, "near1", sds((owner_slots, h), BF), (packed1, left1, right1, slots)
    )
    anchors1, served1 = call(
        far1_kernel,
        "far1",
        (sds((owner_slots, h), BF), served_shape),
        (serve, partial1, far_a1, far_b1, far),
        in_specs=[smem] + [vmem] * 4,
        out_specs=(vmem, far_away),
        scratch_shapes=sems,
    )
    fetched1 = exchange(served1, owners_axes)

    begun = call(
        logits_kernel,
        "logits",
        sds((blocks, PAIRS_REP * BR, BR), F32),
        (need, anchors0, fetched0),
        in_specs=[smem] + [vmem] * 2,
    )
    weights, stats = call(
        scores_kernel,
        "scores",
        (sds((blocks, PAIRS_REP * BR, BR), F32), sds((2 * blocks, BR), F32)),
        (need, column, begun, anchors1, fetched1),
        in_specs=[smem] + [vmem] * 4,
    )
    stats = lax.psum(stats, "rep")
    total, matching = stats[:blocks], stats[blocks:]
    anchor_row_loss = (jnp.log(total) + 1.0 / logit_sharpness - matching).reshape(owner_slots)

    returned = []
    for i, fetched in enumerate((fetched0, fetched1)):
        y = call(
            lambda *r: grads_kernel(factor, *r),
            f"grads{i}",
            (sds((n, h), BF),) * 4,
            (need, column, stats, weights, fetched, slots, far),
            in_specs=[smem] + [vmem] * 6,
            scratch_shapes=[pltpu.VMEM((owner_slots, h), BF)],
        )
        shares = (y[0], turn(y[1], 3), turn(y[2], 1), turn(y[3], 2))
        back = call(back_kernel, f"back{i}", sds((count, h), BF), (*shares, back_place))
        returned.append(exchange(back.reshape(devices, cap, h), everyone).reshape(count, h))

    grad = call(
        unit_grad_kernel, "unit_grad", sds((n, e), BF), (*returned, place, unit, norm)
    )
    partner = swap(grad)
    partial = call(
        head_grad_kernel, "head_grad", sds((width // 2, e), BF), (mine, theirs, grad, partner)
    )
    parts = exchange(partial.reshape(devices // 2, width // devices, e), ("zx", "rep"))
    weight_grad = call(sum_kernel, "add", sds((width // devices, e), F32), (parts,))
    return (anchor_row_loss, weight_grad)


def solution(mesh):
    dp, rep = mesh.devices.shape
    split = jax.sharding.Mesh(mesh.devices.reshape(dp // 2, 2, rep), ("zx", "core", "rep"))
    everyone = ("zx", "core", "rep")
    owners = ("zx", "core")
    placed = (P(everyone, None), P(), P(everyone), P(), P(owners))
    return jax.shard_map(
        shards,
        mesh=split,
        in_specs=placed,
        out_specs=(P(owners), P(everyone, None)),
        check_vma=False,
    )
```

time: 268 us -> 281 us (1.049)
  waiting for transfers between devices: 119 us -> 77.7 us
  starting transfers between devices: 17.3 us -> 47 us
  Pallas kernels: 49.9 us -> 75.6 us
  blocking collectives: 74.1 us -> 68.7 us
  local copies, waits for them, and re-layouts: 3.34 us -> 7.19 us
    all_to_all x2 -> x5, waiting for transfers between devices: 81.2 us -> 45.2 us  [exchange(): return lax.all_to_all(x, axes, 0, 0, tiled=True)]
    pallas_call x8 -> x17, Pallas kernels: 49.9 us -> 75.6 us  [call(): pl.pallas_call(kernel, out_shape=shapes, compiler_params=params(), name=n...]
    all_to_all x2 -> x5, starting transfers between devices: 10.2 us -> 27.4 us  [exchange(): return lax.all_to_all(x, axes, 0, 0, tiled=True)]
    ppermute x7 -> x14, starting transfers between devices: 7.13 us -> 19.6 us  [turn(): return lax.ppermute(x, 'rep', [(i, (i + k) % REPS) for i in range(REPS)])]
    all_to_all x2, blocking collectives: 58.3 us -> 50.4 us  [exchange(): return lax.all_to_all(x, axes, 0, 0, tiled=True)]
    ppermute x7 -> x14, waiting for transfers between devices: 37.5 us -> 30.3 us  [turn(): return lax.ppermute(x, 'rep', [(i, (i + k) % REPS) for i in range(REPS)])]
    unnamed x22 -> x46, local copies, waits for them, and re-layouts: 3.14 us -> 6.98 us
  transfers between devices with their start and end apart: 9 -> 21, of which waited for: 6 -> 11; matrix products, arithmetic and copies ran while one was open for 1% -> 1% of each run, Pallas kernels for 0% -> 17%
where the time goes in v2:
time: 281 us; the launch traced here: 280 us
  waiting for transfers between devices  77.7 us (28%)
  Pallas kernels  75.6 us (27%)
  blocking collectives  68.7 us (24%)
  starting transfers between devices  47 us (17%)
  local copies, waits for them, and re-layouts  7.19 us (3%)
    pallas_call x17, Pallas kernels, call(): pl.pallas_call(kernel, out_shape=shapes, compiler_params=params(), name=n...  75.6 us
    all_to_all x2, blocking collectives, exchange(): return lax.all_to_all(x, axes, 0, 0, tiled=True)  50.4 us
    all_to_all x5, waiting for transfers between devices, exchange(): return lax.all_to_all(x, axes, 0, 0, tiled=True)  45.2 us
    ppermute x14, waiting for transfers between devices, turn(): return lax.ppermute(x, 'rep', [(i, (i + k) % REPS) for i in range(REPS)])  30.3 us
    all_to_all x5, starting transfers between devices, exchange(): return lax.all_to_all(x, axes, 0, 0, tiled=True)  27.4 us
    ppermute x14, starting transfers between devices, turn(): return lax.ppermute(x, 'rep', [(i, (i + k) % REPS) for i in range(REPS)])  19.6 us
    psum x1, blocking collectives, shards(): stats = lax.psum(stats, 'rep')  18.3 us
    unnamed x46, local copies, waits for them, and re-layouts  6.98 us
  transfers between devices with their start and end apart: 21, of which 11 were waited for; matrix products, arithmetic and copies ran while one was open for 1% of the time, Pallas kernels for 17%

profile of v2, /device:TPU:0, one launch (start us, length us, event | category | flops | bytes accessed | tf_op | source)
XLA Modules:
  0.0 279.5 jit_solution(18006305658416416351)
XLA Ops:
  0.6 6.0 %project.1 = (bf16[1024,384]{1,0:T(8,128)(2,1)}, bf16[1024,256]{1,0:T(8,128)(2,1)}, f32[512,512]{1,0:T(8,128)}, f32[512,128]{1,0:T(8,128)}, f32[8,512]{1,0:T(8,128)}) custom-call(s32[1,512]{1,0:T(1,128)} %bitcast.30, bf16[512,2048]{1,0:T(8,128)(2,1)} %feat.1, bf16[2048,512]{1,0:T(8,128)(2,1)} %r_2_.1), custom_call_target="tpu_custom_call" | custom-call | tf_op jit(solution)/shard_map/project/pallas_call | solution.py:312
  6.6 27.2 %all_to_all.35 = bf16[128,8,384]{2,1,0:T(8,128)(2,1)} all-to-all(bf16[128,8,384]{2,1,0:T(8,128)(2,1)} %bitcast.25), channel_id=1, replica_groups=mesh['zx'=16,'core'=2,'rep'=4] {'zx','core','rep'}, dimensions={0} | all-to-all | bytes 1572864 | tf_op jit(solution)/shard_map/all_to_all | solution.py:288
  33.9 4.6 %all-to-all-start.2 = ((bf16[128,8,256]{2,1,0:T(8,128)(2,1)}), bf16[128,8,256]{2,1,0:T(8,128)(2,1)S(1)}, u32[]{:S(2)}, u32[]{:S(2)}) async-start(bf16[128,8,256]{2,1,0:T(8,128)(2,1)} %bitcast.26), calls=%async_computation.2 | async-start | bytes 1048576 | tf_op jit(solution)/shard_map/all_to_all | solution.py:288
  38.5 2.8 compact0.1
  43.5 8.5 %collective-permute-done.1.right = bf16[544,256]{1,0:T(8,128)(2,1)S(1)} collective-permute-done((bf16[544,256]{1,0:T(8,128)(2,1)}, bf16[544,256]{1,0:T(8,128)(2,1)S(1)}, u32[]{:S(2)}, u32[]{:S(2)}) %collective-permute-start.1) | collective-permute-done | bytes 278560 | tf_op jit(solution)/shard_map/ppermute | solution.py:274
  52.0 2.8 collective-permute-start.3
  55.7 5.2 %near0.1 = (bf16[2048,256]{1,0:T(8,128)(2,1)}, f32[3,8,512]{2,1,0:T(8,128)}) custom-call(bf16[544,256]{1,0:T(8,128)(2,1)} %get-tuple-element.29.own, bf16[544,256]{1,0:T(8,128)(2,1)} %copy-done.6, bf16[544,256]{1,0:T(8,128)(2,1)} %copy-done.5), custom_call_target="tpu_custom_call" | custom-call | tf_op jit(solution)/shard_map/near0/pallas_call | solution.py:312
  61.8 6.0 %far0.1 = (bf16[2048,256]{1,0:T(8,128)(2,1)}, bf16[32,128,256]{2,1,0:T(8,128)(2,1)}, f32[8,512]{1,0:T(8,128)}) custom-call(s32[32]{0:T(128)} %get-tuple-element.54.serve, bf16[2048,256]{1,0:T(8,128)(2,1)} %get-tuple-element.30.partial, bf16[256,256]{1,0:T(8,128)(2,1)} %copy-done.18, bf16[288,256]{1,0:T(8,128)(2,1)} %copy-done.17), custom_call_target="tpu_custom_call" | custom-call | tf_op jit(solution)/shard_map/far0/pallas_call | solution.py:312
  68.6 6.8 %all-to-all-start.1 = ((bf16[32,128,256]{2,1,0:T(8,128)(2,1)}), bf16[32,128,256]{2,1,0:T(8,128)(2,1)S(1)}, u32[]{:S(2)}, u32[]{:S(2)}) async-start(bf16[32,128,256]{2,1,0:T(8,128)(2,1)} %get-tuple-element.32), calls=%async_computation.1 | async-start | bytes 4194304 | tf_op jit(solution)/shard_map/all_to_all | solution.py:288
  80.8 6.7 %collective-permute-done.4.left = bf16[512,256]{1,0:T(8,128)(2,1)S(1)} collective-permute-done((bf16[512,256]{1,0:T(8,128)(2,1)}, bf16[512,256]{1,0:T(8,128)(2,1)S(1)}, u32[]{:S(2)}, u32[]{:S(2)}) %collective-permute-start.4) | collective-permute-done | bytes 262176 | tf_op jit(solution)/shard_map/ppermute | solution.py:274
  87.7 3.3 %collective-permute-start.7 = (bf16[256,256]{1,0:T(8,128)(2,1)S(1)}, bf16[256,256]{1,0:T(8,128)(2,1)S(1)}, u32[]{:S(2)}, u32[]{:S(2)}) collective-permute-start(bf16[256,256]{1,0:T(8,128)(2,1)S(1)} %slice.27), channel_id=1, source_target_pairs={{0,3},{1,0},{2,1},{3,2},{4,7},{5,4},{6,5},{7,6},{8,11},{9,8},{10,9... | collective-permute-start | bytes 393224 | tf_op jit(solution)/shard_map/ppermute | solution.py:274
  91.0 5.2 %near1.1.partial = bf16[2048,256]{1,0:T(8,128)(2,1)} custom-call(bf16[512,256]{1,0:T(8,128)(2,1)} %compact1.1.own, bf16[512,256]{1,0:T(8,128)(2,1)} %copy-done.7, bf16[512,256]{1,0:T(8,128)(2,1)} %copy-done.8, f32[3,8,512]{2,1,0:T(8,128)} %get-tuple-element.35.slots.r_5_), custom_call_target="tpu_custom_call" | custom-call | tf_op jit(solution)/shard_map/near1/pallas_call | solution.py:312
  96.9 5.9 %far1.1 = (bf16[2048,256]{1,0:T(8,128)(2,1)}, bf16[32,128,256]{2,1,0:T(8,128)(2,1)}) custom-call(s32[32]{0:T(128)} %get-tuple-element.54.serve, bf16[2048,256]{1,0:T(8,128)(2,1)} %near1.1.partial, bf16[256,256]{1,0:T(8,128)(2,1)} %copy-done.19, bf16[256,256]{1,0:T(8,128)(2,1)} %copy-done.20, f32[8,512]{1,0:T(8,128)} %get-tuple-element.36.slots.r_6_), custom_call_target="tpu_custom_call" | custom-call | tf_op jit(solution)/shard_map/far1/pallas_call | solution.py:312
  106.7 4.9 %all-to-all-start.3 = ((bf16[32,128,256]{2,1,0:T(8,128)(2,1)}), bf16[32,128,256]{2,1,0:T(8,128)(2,1)}, u32[]{:S(2)}, u32[]{:S(2)}) async-start(bf16[32,128,256]{2,1,0:T(8,128)(2,1)} %get-tuple-element.38), calls=%async_computation.3 | async-start | bytes 4194304 | tf_op jit(solution)/shard_map/all_to_all | solution.py:288
  113.0 4.5 %logits.1.begun = f32[16,256,128]{2,1,0:T(8,128)} custom-call(s32[32]{0:T(128)} %fusion.3.need.r_0_, bf16[2048,256]{1,0:T(8,128)(2,1)} %get-tuple-element.31.anchors, bf16[32,128,256]{2,1,0:T(8,128)(2,1)} %copy-done), custom_call_target="tpu_custom_call" | custom-call | tf_op jit(solution)/shard_map/logits/pallas_call | solution.py:312
  117.5 24.1 %all-to-all-done.3.fetched.r_4_ = bf16[32,128,256]{2,1,0:T(8,128)(2,1)} async-done(((bf16[32,128,256]{2,1,0:T(8,128)(2,1)}), bf16[32,128,256]{2,1,0:T(8,128)(2,1)}, u32[]{:S(2)}, u32[]{:S(2)}) %all-to-all-start.3) | async-done | bytes 2097184 | tf_op jit(solution)/shard_map/all_to_all | solution.py:288
  141.6 5.3 %scores.1 = (f32[16,256,128]{2,1,0:T(8,128)}, f32[32,128]{1,0:T(8,128)}) custom-call(s32[32]{0:T(128)} %fusion.3.need.r_0_, s32[16,128]{1,0:T(8,128)} %subtract_bitcast_fusion.column.r_1_, f32[16,256,128]{2,1,0:T(8,128)} %logits.1.begun, bf16[2048,256]{1,0:T(8,128)(2,1)} %get-tuple-element.37.anchors, bf16[32,128,256]{2,1,0:T(8,128)(2,1)} %all-to-all-done.3.fetched.r_4_), custom_call_target="tpu_custom_call" | custom-call | tf_op jit(solution)/shard_map/scores/pallas_call | solution.py:312
  146.8 18.3 %psum.7.r_2_ = f32[32,128]{1,0:T(8,128)} all-reduce(f32[32,128]{1,0:T(8,128)} %get-tuple-element.39), channel_id=1, replica_groups=mesh['zx'=16,'core'=2,'rep'=4] {'rep'}, use_global_device_ids=true, to_apply=%region_1.2 | all-reduce | flops 4096 | bytes 32768 | tf_op jit(solution)/shard_map/psum | solution.py:401
  165.1 6.8 %grads1.1 = (bf16[512,256]{1,0:T(8,128)(2,1)}, bf16[512,256]{1,0:T(8,128)(2,1)}, bf16[512,256]{1,0:T(8,128)(2,1)}, bf16[512,256]{1,0:T(8,128)(2,1)}) custom-call(s32[32]{0:T(128)} %fusion.3.need.r_0_, s32[16,128]{1,0:T(8,128)} %subtract_bitcast_fusion.column.r_1_, f32[32,128]{1,0:T(8,128)} %psum.7.r_2_, f32[16,256,128]{2,1,0:T(8,128)} %get-tuple-element.42.r_3_, ...), custom_call_target="tpu_custom_call" | custom-call | tf_op jit(solution)/shard_map/grads1/pallas_call | solution.py:312
  174.8 3.7 %collective-permute-done.12.b = bf16[512,256]{1,0:T(8,128)(2,1)S(1)} collective-permute-done((bf16[512,256]{1,0:T(8,128)(2,1)}, bf16[512,256]{1,0:T(8,128)(2,1)S(1)}, u32[]{:S(2)}, u32[]{:S(2)}) %collective-permute-start.12) | collective-permute-done | bytes 262176 | tf_op jit(solution)/shard_map/ppermute | solution.py:274
  178.5 4.0 %collective-permute-done.13.c = bf16[512,256]{1,0:T(8,128)(2,1)S(1)} collective-permute-done((bf16[512,256]{1,0:T(8,128)(2,1)}, bf16[512,256]{1,0:T(8,128)(2,1)S(1)}, u32[]{:S(2)}, u32[]{:S(2)}) %collective-permute-start.13) | collective-permute-done | bytes 262176 | tf_op jit(solution)/shard_map/ppermute | solution.py:274
  183.3 2.8 %back1.1 = bf16[1024,256]{1,0:T(8,128)(2,1)} custom-call(bf16[512,256]{1,0:T(8,128)(2,1)} %get-tuple-element.47.a, bf16[512,256]{1,0:T(8,128)(2,1)} %copy-done.14, bf16[512,256]{1,0:T(8,128)(2,1)} %copy-done.15, bf16[512,256]{1,0:T(8,128)(2,1)} %copy-done.16, f32[8,1024]{1,0:T(8,128)} %get-tuple-element.34.place), custom_call_target="tpu_custom_call" | custom-call | tf_op jit(solution)/shard_map/back1/pallas_call | solution.py:312
  186.2 6.1 %all-to-all-start.5 = ((bf16[128,8,256]{2,1,0:T(8,128)(2,1)}), bf16[128,8,256]{2,1,0:T(8,128)(2,1)S(1)}, u32[]{:S(2)}, u32[]{:S(2)}) async-start(bf16[128,8,256]{2,1,0:T(8,128)(2,1)} %bitcast.20), calls=%async_computation.5 | async-start | bytes 1048576 | tf_op jit(solution)/shard_map/all_to_all | solution.py:288
  192.3 6.8 %grads0.1 = (bf16[512,256]{1,0:T(8,128)(2,1)}, bf16[512,256]{1,0:T(8,128)(2,1)}, bf16[512,256]{1,0:T(8,128)(2,1)}, bf16[512,256]{1,0:T(8,128)(2,1)}) custom-call(s32[32]{0:T(128)} %fusion.3.need.r_0_, s32[16,128]{1,0:T(8,128)} %subtract_bitcast_fusion.column.r_1_, f32[32,128]{1,0:T(8,128)} %psum.7.r_2_, f32[16,256,128]{2,1,0:T(8,128)} %get-tuple-element.42.r_3_, ...), custom_call_target="tpu_custom_call" | custom-call | tf_op jit(solution)/shard_map/grads0/pallas_call | solution.py:312
  204.2 3.6 %stripes.1 = (bf16[1024,512]{1,0:T(8,128)(2,1)}, bf16[1024,512]{1,0:T(8,128)(2,1)}) custom-call(s32[1]{0:T(128)} %bitcast.8.core, bf16[512,2048]{1,0:T(8,128)(2,1)} %feat.1), custom_call_target="tpu_custom_call" | custom-call | tf_op jit(solution)/shard_map/stripes/pallas_call | solution.py:312
  208.2 6.7 %collective-permute-done.11.d = bf16[512,256]{1,0:T(8,128)(2,1)S(1)} collective-permute-done((bf16[512,256]{1,0:T(8,128)(2,1)}, bf16[512,256]{1,0:T(8,128)(2,1)S(1)}, u32[]{:S(2)}, u32[]{:S(2)}) %collective-permute-start.11) | collective-permute-done | bytes 262176 | tf_op jit(solution)/shard_map/ppermute | solution.py:274
  215.8 2.8 %back0.1 = bf16[1024,256]{1,0:T(8,128)(2,1)} custom-call(bf16[512,256]{1,0:T(8,128)(2,1)} %get-tuple-element.43.a, bf16[512,256]{1,0:T(8,128)(2,1)} %copy-done.13, bf16[512,256]{1,0:T(8,128)(2,1)} %copy-done.11, bf16[512,256]{1,0:T(8,128)(2,1)} %copy-done.12, f32[8,1024]{1,0:T(8,128)} %get-tuple-element.34.place), custom_call_target="tpu_custom_call" | custom-call | tf_op jit(solution)/shard_map/back0/pallas_call | solution.py:312
  218.6 23.2 %all_to_all.36 = bf16[128,8,256]{2,1,0:T(8,128)(2,1)} all-to-all(bf16[128,8,256]{2,1,0:T(8,128)(2,1)} %bitcast.21), channel_id=1, replica_groups=mesh['zx'=16,'core'=2,'rep'=4] {'zx','core','rep'}, dimensions={0} | all-to-all | bytes 1048576 | tf_op jit(solution)/shard_map/all_to_all | solution.py:288
  241.8 3.5 %unit_grad.1.grad = bf16[512,512]{1,0:T(8,128)(2,1)} custom-call(bf16[1024,256]{1,0:T(8,128)(2,1)} %bitcast.24, bf16[1024,256]{1,0:T(8,128)(2,1)} %bitcast.23, f32[8,512]{1,0:T(8,128)} %get-tuple-element.51.place, f32[512,512]{1,0:T(8,128)} %get-tuple-element.52.unit, f32[512,128]{1,0:T(8,128)} %get-tuple-element.53.norm), custom_call_target="tpu_custom_call" | custom-call | tf_op jit(solution)/shard_map/unit_grad/pallas_call | solution.py:312
  248.2 4.1 %head_grad.1 = bf16[1024,512]{1,0:T(8,128)(2,1)} custom-call(bf16[1024,512]{1,0:T(8,128)(2,1)} %get-tuple-element.40.mine, bf16[1024,512]{1,0:T(8,128)(2,1)} %copy-done.4, bf16[512,512]{1,0:T(8,128)(2,1)} %unit_grad.1.grad, bf16[512,512]{1,0:T(8,128)(2,1)} %copy-done.9), custom_call_target="tpu_custom_call" | custom-call | tf_op jit(solution)/shard_map/head_grad/pallas_call | solution.py:312
  252.3 5.0 %all-to-all-start.6 = ((bf16[64,16,512]{2,1,0:T(8,128)(2,1)}), bf16[64,16,512]{2,1,0:T(8,128)(2,1)S(1)}, u32[]{:S(2)}, u32[]{:S(2)}) async-start(bf16[64,16,512]{2,1,0:T(8,128)(2,1)} %bitcast.18), calls=%async_computation.6 | async-start | bytes 2097152 | tf_op jit(solution)/shard_map/all_to_all | solution.py:288
  257.9 18.6 %all-to-all-done.6.parts = bf16[64,16,512]{2,1,0:T(8,128)(2,1)S(1)} async-done(((bf16[64,16,512]{2,1,0:T(8,128)(2,1)}), bf16[64,16,512]{2,1,0:T(8,128)(2,1)S(1)}, u32[]{:S(2)}, u32[]{:S(2)}) %all-to-all-start.6) | async-done | bytes 1048608 | tf_op jit(solution)/shard_map/all_to_all | solution.py:288
  (88 shorter events, 32.8 us)
Async XLA Ops:
  6.6 48.3 %copy-start.21 = (s32[512,8]{0,1:T(8,128)S(1)}, s32[512,8]{0,1:T(8,128)}, u32[]{:S(2)}) copy-start(s32[512,8]{0,1:T(8,128)} %param.8) | copy-start | bytes 49156
  33.9 33.9 %all-to-all-start.2 = ((bf16[128,8,256]{2,1,0:T(8,128)(2,1)}), bf16[128,8,256]{2,1,0:T(8,128)(2,1)S(1)}, u32[]{:S(2)}, u32[]{:S(2)}) async-start(bf16[128,8,256]{2,1,0:T(8,128)(2,1)} %bitcast.26), calls=%async_computation.2 | async-start | bytes 1048576 | tf_op jit(solution)/shard_map/all_to_all | solution.py:288
  41.3 10.8 %collective-permute-start.1 = (bf16[544,256]{1,0:T(8,128)(2,1)}, bf16[544,256]{1,0:T(8,128)(2,1)S(1)}, u32[]{:S(2)}, u32[]{:S(2)}) collective-permute-start(bf16[544,256]{1,0:T(8,128)(2,1)} %get-tuple-element.29.own), channel_id=1, source_target_pairs={{0,3},{1,0},{2,1},{3,2},{4,7},{5,4},{6,5},{7,6},{8,11},{9,8},{10,9... | collective-permute-start | bytes 835592 | tf_op jit(solution)/shard_map/ppermute | solution.py:274
  43.5 11.3 %collective-permute-start = (bf16[544,256]{1,0:T(8,128)(2,1)}, bf16[544,256]{1,0:T(8,128)(2,1)S(1)}, u32[]{:S(2)}, u32[]{:S(2)}) collective-permute-start(bf16[544,256]{1,0:T(8,128)(2,1)} %get-tuple-element.29.own), channel_id=1, source_target_pairs={{0,1},{1,2},{2,3},{3,0},{4,5},{5,6},{6,7},{7,4},{8,9},{9,10},{10,1... | collective-permute-start | bytes 835592 | tf_op jit(solution)/shard_map/ppermute | solution.py:274
  52.0 3.7 %copy-start.5 = (bf16[544,256]{1,0:T(8,128)(2,1)}, bf16[544,256]{1,0:T(8,128)(2,1)S(1)}, u32[]{:S(2)}) copy-start(bf16[544,256]{1,0:T(8,128)(2,1)S(1)} %collective-permute-done.1.right) | copy-start | bytes 835588
  52.0 9.1 %collective-permute-start.3 = (bf16[288,256]{1,0:T(8,128)(2,1)S(1)}, bf16[288,256]{1,0:T(8,128)(2,1)S(1)}, u32[]{:S(2)}, u32[]{:S(2)}) collective-permute-start(bf16[288,256]{1,0:T(8,128)(2,1)S(1)} %slice.25), channel_id=1, source_target_pairs={{0,3},{1,0},{2,1},{3,2},{4,7},{5,4},{6,5},{7,6},{8,11},{9,8},{10,9... | collective-permute-start | bytes 442376 | tf_op jit(solution)/shard_map/ppermute | solution.py:274
  54.8 6.3 %collective-permute-start.2 = (bf16[256,256]{1,0:T(8,128)(2,1)S(1)}, bf16[256,256]{1,0:T(8,128)(2,1)S(1)}, u32[]{:S(2)}, u32[]{:S(2)}) collective-permute-start(bf16[256,256]{1,0:T(8,128)(2,1)S(1)} %slice.24), channel_id=1, source_target_pairs={{0,1},{1,2},{2,3},{3,0},{4,5},{5,6},{6,7},{7,4},{8,9},{9,10},{10,1... | collective-permute-start | bytes 393224 | tf_op jit(solution)/shard_map/ppermute | solution.py:274
  68.6 36.8 %all-to-all-start.1 = ((bf16[32,128,256]{2,1,0:T(8,128)(2,1)}), bf16[32,128,256]{2,1,0:T(8,128)(2,1)S(1)}, u32[]{:S(2)}, u32[]{:S(2)}) async-start(bf16[32,128,256]{2,1,0:T(8,128)(2,1)} %get-tuple-element.32), calls=%async_computation.1 | async-start | bytes 4194304 | tf_op jit(solution)/shard_map/all_to_all | solution.py:288
  77.6 10.0 %collective-permute-start.4 = (bf16[512,256]{1,0:T(8,128)(2,1)}, bf16[512,256]{1,0:T(8,128)(2,1)S(1)}, u32[]{:S(2)}, u32[]{:S(2)}) collective-permute-start(bf16[512,256]{1,0:T(8,128)(2,1)} %compact1.1.own), channel_id=1, source_target_pairs={{0,1},{1,2},{2,3},{3,0},{4,5},{5,6},{6,7},{7,4},{8,9},{9,10},{10,1... | collective-permute-start | bytes 786440 | tf_op jit(solution)/shard_map/ppermute | solution.py:274
  78.5 9.1 %collective-permute-start.5 = (bf16[512,256]{1,0:T(8,128)(2,1)}, bf16[512,256]{1,0:T(8,128)(2,1)S(1)}, u32[]{:S(2)}, u32[]{:S(2)}) collective-permute-start(bf16[512,256]{1,0:T(8,128)(2,1)} %compact1.1.own), channel_id=1, source_target_pairs={{0,3},{1,0},{2,1},{3,2},{4,7},{5,4},{6,5},{7,6},{8,11},{9,8},{10,9... | collective-permute-start | bytes 786440 | tf_op jit(solution)/shard_map/ppermute | solution.py:274
  87.6 3.4 %copy-start.7 = (bf16[512,256]{1,0:T(8,128)(2,1)}, bf16[512,256]{1,0:T(8,128)(2,1)S(1)}, u32[]{:S(2)}) copy-start(bf16[512,256]{1,0:T(8,128)(2,1)S(1)} %collective-permute-done.4.left) | copy-start | bytes 786436
  87.6 8.6 %collective-permute-start.6 = (bf16[256,256]{1,0:T(8,128)(2,1)S(1)}, bf16[256,256]{1,0:T(8,128)(2,1)S(1)}, u32[]{:S(2)}, u32[]{:S(2)}) collective-permute-start(bf16[256,256]{1,0:T(8,128)(2,1)S(1)} %slice.26), channel_id=1, source_target_pairs={{0,1},{1,2},{2,3},{3,0},{4,5},{5,6},{6,7},{7,4},{8,9},{9,10},{10,1... | collective-permute-start | bytes 393224 | tf_op jit(solution)/shard_map/ppermute | solution.py:274
  87.7 3.3 %copy-start.8 = (bf16[512,256]{1,0:T(8,128)(2,1)}, bf16[512,256]{1,0:T(8,128)(2,1)S(1)}, u32[]{:S(2)}) copy-start(bf16[512,256]{1,0:T(8,128)(2,1)S(1)} %collective-permute-done.5.right) | copy-start | bytes 786436
  87.7 8.5 %collective-permute-start.7 = (bf16[256,256]{1,0:T(8,128)(2,1)S(1)}, bf16[256,256]{1,0:T(8,128)(2,1)S(1)}, u32[]{:S(2)}, u32[]{:S(2)}) collective-permute-start(bf16[256,256]{1,0:T(8,128)(2,1)S(1)} %slice.27), channel_id=1, source_target_pairs={{0,3},{1,0},{2,1},{3,2},{4,7},{5,4},{6,5},{7,6},{8,11},{9,8},{10,9... | collective-permute-start | bytes 393224 | tf_op jit(solution)/shard_map/ppermute | solution.py:274
  105.4 1.3 copy-start
  105.4 7.0 %copy-start.22 = (s32[2048]{0:T(1024)S(1)}, s32[2048]{0:T(1024)}, u32[]{:S(2)}) copy-start(s32[2048]{0:T(1024)} %param.9) | copy-start | bytes 24580
  106.7 34.8 %all-to-all-start.3 = ((bf16[32,128,256]{2,1,0:T(8,128)(2,1)}), bf16[32,128,256]{2,1,0:T(8,128)(2,1)}, u32[]{:S(2)}, u32[]{:S(2)}) async-start(bf16[32,128,256]{2,1,0:T(8,128)(2,1)} %get-tuple-element.38), calls=%async_computation.3 | async-start | bytes 4194304 | tf_op jit(solution)/shard_map/all_to_all | solution.py:288
  171.9 6.6 %collective-permute-start.12 = (bf16[512,256]{1,0:T(8,128)(2,1)}, bf16[512,256]{1,0:T(8,128)(2,1)S(1)}, u32[]{:S(2)}, u32[]{:S(2)}) collective-permute-start(bf16[512,256]{1,0:T(8,128)(2,1)} %get-tuple-element.48), channel_id=1, source_target_pairs={{0,3},{1,0},{2,1},{3,2},{4,7},{5,4},{6,5},{7,6},{8,11},{9,8},{10,9... | collective-permute-start | bytes 786440 | tf_op jit(solution)/shard_map/ppermute | solution.py:274
  171.9 10.6 %collective-permute-start.13 = (bf16[512,256]{1,0:T(8,128)(2,1)}, bf16[512,256]{1,0:T(8,128)(2,1)S(1)}, u32[]{:S(2)}, u32[]{:S(2)}) collective-permute-start(bf16[512,256]{1,0:T(8,128)(2,1)} %get-tuple-element.49), channel_id=1, source_target_pairs={{0,1},{1,2},{2,3},{3,0},{4,5},{5,6},{6,7},{7,4},{8,9},{9,10},{10,1... | collective-permute-start | bytes 786440 | tf_op jit(solution)/shard_map/ppermute | solution.py:274
  173.9 8.6 %collective-permute-start.14 = (bf16[512,256]{1,0:T(8,128)(2,1)}, bf16[512,256]{1,0:T(8,128)(2,1)S(1)}, u32[]{:S(2)}, u32[]{:S(2)}) collective-permute-start(bf16[512,256]{1,0:T(8,128)(2,1)} %get-tuple-element.50), channel_id=1, source_target_pairs={{0,2},{1,3},{2,0},{3,1},{4,6},{5,7},{6,4},{7,5},{8,10},{9,11},{10,... | collective-permute-start | bytes 786440 | tf_op jit(solution)/shard_map/ppermute | solution.py:274
  178.5 4.0 %copy-start.14 = (bf16[512,256]{1,0:T(8,128)(2,1)}, bf16[512,256]{1,0:T(8,128)(2,1)S(1)}, u32[]{:S(2)}) copy-start(bf16[512,256]{1,0:T(8,128)(2,1)S(1)} %collective-permute-done.12.b) | copy-start | bytes 786436
  186.2 32.4 %all-to-all-start.5 = ((bf16[128,8,256]{2,1,0:T(8,128)(2,1)}), bf16[128,8,256]{2,1,0:T(8,128)(2,1)S(1)}, u32[]{:S(2)}, u32[]{:S(2)}) async-start(bf16[128,8,256]{2,1,0:T(8,128)(2,1)} %bitcast.20), calls=%async_computation.5 | async-start | bytes 1048576 | tf_op jit(solution)/shard_map/all_to_all | solution.py:288
  199.1 9.1 %collective-permute-start.10 = (bf16[512,256]{1,0:T(8,128)(2,1)}, bf16[512,256]{1,0:T(8,128)(2,1)S(1)}, u32[]{:S(2)}, u32[]{:S(2)}) collective-permute-start(bf16[512,256]{1,0:T(8,128)(2,1)} %get-tuple-element.45), channel_id=1, source_target_pairs={{0,1},{1,2},{2,3},{3,0},{4,5},{5,6},{6,7},{7,4},{8,9},{9,10},{10,1... | collective-permute-start | bytes 786440 | tf_op jit(solution)/shard_map/ppermute | solution.py:274
  200.1 14.9 %collective-permute-start.11 = (bf16[512,256]{1,0:T(8,128)(2,1)}, bf16[512,256]{1,0:T(8,128)(2,1)S(1)}, u32[]{:S(2)}, u32[]{:S(2)}) collective-permute-start(bf16[512,256]{1,0:T(8,128)(2,1)} %get-tuple-element.46), channel_id=1, source_target_pairs={{0,2},{1,3},{2,0},{3,1},{4,6},{5,7},{6,4},{7,5},{8,10},{9,11},{10,... | collective-permute-start | bytes 786440 | tf_op jit(solution)/shard_map/ppermute | solution.py:274
  202.8 12.2 %collective-permute-start.9 = (bf16[512,256]{1,0:T(8,128)(2,1)}, bf16[512,256]{1,0:T(8,128)(2,1)S(1)}, u32[]{:S(2)}, u32[]{:S(2)}) collective-permute-start(bf16[512,256]{1,0:T(8,128)(2,1)} %get-tuple-element.44), channel_id=1, source_target_pairs={{0,3},{1,0},{2,1},{3,2},{4,7},{5,4},{6,5},{7,6},{8,11},{9,8},{10,9... | collective-permute-start | bytes 786440 | tf_op jit(solution)/shard_map/ppermute | solution.py:274
  207.8 37.4 %collective-permute-start.8 = (bf16[1024,512]{1,0:T(8,128)(2,1)}, bf16[1024,512]{1,0:T(8,128)(2,1)S(1)}, u32[]{:S(2)}, u32[]{:S(2)}) collective-permute-start(bf16[1024,512]{1,0:T(8,128)(2,1)} %get-tuple-element.41), channel_id=1, source_target_pairs={{0,4},{4,0},{1,5},{5,1},{2,6},{6,2},{3,7},{7,3},{8,12},{12,8},{9,1... | collective-permute-start | bytes 3145736 | tf_op jit(solution)/shard_map/ppermute | solution.py:278
  208.2 6.7 %copy-start.11 = (bf16[512,256]{1,0:T(8,128)(2,1)}, bf16[512,256]{1,0:T(8,128)(2,1)S(1)}, u32[]{:S(2)}) copy-start(bf16[512,256]{1,0:T(8,128)(2,1)S(1)} %collective-permute-done.10.c) | copy-start | bytes 786436
  218.6 23.2 %copy-start.3 = (bf16[128,8,256]{2,1,0:T(8,128)(2,1)}, bf16[128,8,256]{2,1,0:T(8,128)(2,1)S(1)}, u32[]{:S(2)}) copy-start(bf16[128,8,256]{2,1,0:T(8,128)(2,1)S(1)} %all-to-all-done.5) | copy-start | bytes 1572868
  245.3 2.1 collective-permute-start.15
  245.3 2.1 copy-start.4
  252.3 5.0 %copy-start.10 = (f32[32,128]{1,0:T(8,128)S(1)}, f32[32,128]{1,0:T(8,128)}, u32[]{:S(2)}) copy-start(f32[32,128]{1,0:T(8,128)} %psum.7.r_2_) | copy-start | bytes 49156
  252.3 24.2 %all-to-all-start.6 = ((bf16[64,16,512]{2,1,0:T(8,128)(2,1)}), bf16[64,16,512]{2,1,0:T(8,128)(2,1)S(1)}, u32[]{:S(2)}, u32[]{:S(2)}) async-start(bf16[64,16,512]{2,1,0:T(8,128)(2,1)} %bitcast.18), calls=%async_computation.6 | async-start | bytes 2097152 | tf_op jit(solution)/shard_map/all_to_all | solution.py:288
  (12 other events, 9.3 us)

commit v3 on v2

v3 whole, which is shorter than its diff:
```python
import math

import jax
import jax.numpy as jnp
from jax import lax
from jax.experimental import pallas as pl
from jax.experimental.pallas import tpu as pltpu
from jax.sharding import PartitionSpec as P

BR = 128
PAIRS_REP = 2
REPS = 4

logit_sharpness = 0.05
objective_factor = 32.0
norm_eps = 1e-06

BF = jnp.bfloat16
F32 = jnp.float32
I32 = jnp.int32
VMEM_BYTES = 24 * 1024 * 1024


def params():
    return pltpu.CompilerParams(vmem_limit_bytes=VMEM_BYTES)


def iota(shape, dim):
    return lax.broadcasted_iota(I32, shape, dim)


def hot(mask):
    return jnp.where(mask, 1.0, 0.0).astype(BF)


def dot(a, b, ca=1, cb=0):
    return lax.dot_general(a, b, (((ca,), (cb,)), ((), ())), preferred_element_type=F32)


def sds(shape, dtype):
    return jax.ShapeDtypeStruct(shape, dtype)


def column_of(rows):
    wide = jnp.concatenate([rows] * (BR // rows.shape[0]), axis=0)
    return wide.T[:, 0:1].astype(I32)


def project_kernel(owner_slots, owners, cap, slot, feat, head, send, unit, norm, place):
    n = feat.shape[0]
    e = head.shape[1]
    projected = dot(feat[...], head[...])
    length = jnp.sqrt(jnp.sum(projected * projected, axis=1, keepdims=True) + norm_eps)
    rows = projected / length
    unit[...] = rows
    norm[...] = jnp.broadcast_to(length, norm.shape)
    descriptor = rows.astype(BF)
    s = slot[...]
    owner = s // owner_slots
    local = s - owner * owner_slots
    mine = iota((owners, n), 0) == owner
    before = dot(hot(mine), hot(iota((n, n), 0) < iota((n, n), 1)))
    rank = jnp.sum(jnp.where(mine, before, 0.0), axis=0, keepdims=True).astype(I32)
    p = (owner * REPS + (rank & (REPS - 1))) * cap + rank // REPS
    place[...] = jnp.broadcast_to(p.astype(F32), place.shape)
    scatter = hot(iota((send.shape[0], n), 0) == p)
    send[:, :e] = dot(scatter, descriptor).astype(BF)
    high = local // BR
    low = local - high * BR
    row = iota((BR, n), 0)
    tags = jnp.where(row == 0, high, jnp.where(row == 1, low, jnp.where(row == 2, 1, 0)))
    send[:, e:] = dot(scatter, tags.astype(F32).astype(BF), 1, 1).astype(BF)


def stripes_kernel(core, feat, mine, other):
    n = feat.shape[0]
    first = core[0] == 0
    half = BR // 2
    for z in range(feat.shape[1] // BR):
        t = feat[:, z * BR : (z + 1) * BR].astype(F32).T
        a, b = t[:half, :], t[half:, :]
        mine[z * half : (z + 1) * half, :] = jnp.where(first, a, b).astype(BF)
        other[z * half : (z + 1) * half, :] = jnp.where(first, b, a).astype(BF)


def compact_kernel(got, packed, place):
    count = got.shape[0]
    e = packed.shape[1]
    rows = packed.shape[0] - 16
    tags = got[:, e:].astype(F32).T
    valid = tags[2:3, :]
    upper = hot(iota((count, count), 0) < iota((count, count), 1))
    before = dot(jnp.broadcast_to(valid, (16, count)).astype(BF), upper)[0:1, :]
    pos = jnp.where(valid > 0.5, before, -1.0)
    place[...] = jnp.broadcast_to(pos, place.shape)
    pick = hot(iota((rows, count), 0) == pos.astype(I32))
    packed[:rows, :] = dot(pick, got[:, :e]).astype(BF)
    packed[rows:, :] = dot(tags[:16, :].astype(BF), pick, 1, 1).astype(BF)


def slot_row(tag):
    tag = tag.astype(F32)
    return tag[0:1, :] * BR + tag[1:2, :]


def near_kernel(own, left, right, partial, slots):
    n = own.shape[0] - 16
    pieces = []
    for k, ref in enumerate((own, left, right)):
        row = slot_row(ref[n:, :])
        slots[k, :, :] = jnp.broadcast_to(row, slots.shape[1:])
        pieces.append((row.astype(I32), ref[:n, :]))
    place_rows(partial, pieces, None)


def place_rows(out, pieces, start):
    step = 256

    def body(i, carry):
        base = pl.multiple_of(i * step, step)
        total = None if start is None else start[pl.ds(base, step), :].astype(F32)
        for ids, rows in pieces:
            at = iota((step, rows.shape[0]), 0) + base
            part = dot(hot(at == ids), rows)
            total = part if total is None else total + part
        out[pl.ds(base, step), :] = total.astype(BF)
        return carry

    lax.fori_loop(0, out.shape[0] // step, body, 0)


def serve_blocks(serve, anchors, served, sems):
    copies = []
    for d in range(served.shape[0]):
        start = pl.multiple_of(serve[d] * BR, BR)
        copies.append(
            pltpu.make_async_copy(anchors.at[pl.ds(start, BR), :], served.at[d], sems.at[d])
        )
    for c in copies:
        c.start()
    for c in copies:
        c.wait()


def far_kernel(serve, partial, far_a, far_b, anchors, served, slots, sems):
    q = far_a.shape[0]
    row = slot_row(far_b[q:, :])
    slots[...] = jnp.broadcast_to(row, slots.shape)
    ids = row.astype(I32)
    place_rows(anchors, [(ids[:, :q], far_a[...]), (ids[:, q:], far_b[:q, :])], partial)
    serve_blocks(serve, anchors, served, sems)


def scores_kernel(need, column, anchors, fetched, weights, stats):
    blocks = weights.shape[0]

    def body(i, carry):
        for j in range(4):
            b = i * 4 + j
            q = anchors[pl.ds(pl.multiple_of(b * BR, BR), BR), :]
            total = jnp.zeros((1, BR), F32)
            positive = jnp.zeros((1, BR), F32)
            want = column[pl.ds(b, 1), :]
            for k in range(PAIRS_REP):
                logits = dot(fetched[need[b * PAIRS_REP + k]], q, 1, 1) / logit_sharpness
                hit = iota((BR, BR), 0) + k * BR == want
                w = jnp.where(hit, 0.0, jnp.exp(logits - 1.0 / logit_sharpness))
                weights[b, k * BR : (k + 1) * BR, :] = w.astype(BF)
                total += jnp.sum(w, axis=0, keepdims=True)
                positive += jnp.sum(jnp.where(hit, logits, 0.0), axis=0, keepdims=True)
            stats[pl.ds(b, 1), :] = total
            stats[pl.ds(blocks + b, 1), :] = positive
        return carry

    lax.fori_loop(0, blocks // 4, body, 0)


def mix_kernel(need, column, weights, fetched, pulled, partner):
    blocks = weights.shape[0]

    def body(i, carry):
        for j in range(4):
            b = i * 4 + j
            want = column[pl.ds(b, 1), :]
            at = pl.ds(pl.multiple_of(b * BR, BR), BR)
            both = jnp.zeros((2 * BR, pulled.shape[1]), F32)
            for k in range(PAIRS_REP):
                hit = hot(iota((BR, BR), 0) + k * BR == want)
                w = weights[b, k * BR : (k + 1) * BR, :]
                both += dot(
                    jnp.concatenate([w.T, hit.T], axis=0), fetched[need[b * PAIRS_REP + k]]
                )
            pulled[at, :] = both[:BR, :].astype(BF)
            partner[at, :] = both[BR:, :].astype(BF)
        return carry

    lax.fori_loop(0, blocks // 4, body, 0)


def pick_rows(out, rows, ids):
    step = 256
    for h in range(out.shape[0] // step):
        pick = hot(iota((step, rows.shape[0]), 1) == ids[h * step : (h + 1) * step, :])
        out[h * step : (h + 1) * step, :] = dot(pick, rows[...]).astype(BF)


def shares_kernel(factor, s0, s1, s2, s3, pulled, partner, slots, far, share, y1, y2, y3):
    blocks = s0.shape[0] // 2
    stats = (s0[...] + s2[...]) + (s1[...] + s3[...])
    rest, matching = stats[:blocks, :], stats[blocks:, :]
    total = rest + jnp.exp(matching - 1.0 / logit_sharpness)
    scale = jnp.concatenate([factor / total, factor * (rest / total)], axis=0)
    scale = jnp.concatenate([scale] * (BR // (2 * blocks)), axis=0).T
    for b in range(blocks):
        at = slice(b * BR, (b + 1) * BR)
        grad = pulled[at, :].astype(F32) * scale[:, b : b + 1]
        grad -= partner[at, :].astype(F32) * scale[:, blocks + b : blocks + b + 1]
        share[at, :] = grad.astype(BF)
    pick_rows(y3, share, column_of(far[...]))
    pick_rows(y1, share, column_of(slots[1, :, :]))
    pick_rows(y2, share, column_of(slots[2, :, :]))


def own_kernel(share, slots, y0):
    pick_rows(y0, share, column_of(slots[0, :, :]))


def back_kernel(a, b, c, d, place, back):
    total = a[...].astype(F32) + b[...].astype(F32) + c[...].astype(F32) + d[...].astype(F32)
    rows = a.shape[0]
    pos = column_of(place[...])
    back[...] = dot(hot(iota((back.shape[0], rows), 1) == pos), total.astype(BF)).astype(BF)


def unit_grad_kernel(got, place, unit, norm, out):
    n = unit.shape[0]
    grad = dot(hot(iota((n, got.shape[0]), 1) == column_of(place[...])), got[...])
    rows = unit[...]
    radial = jnp.sum(rows * grad, axis=1, keepdims=True)
    out[...] = ((grad - rows * radial) / norm[:, 0:1]).astype(BF)


def head_grad_kernel(mine, theirs, grad, partner, out):
    step = 256
    for i in range(out.shape[0] // step):
        at = slice(i * step, (i + 1) * step)
        out[at, :] = (dot(mine[at, :], grad[...]) + dot(theirs[at, :], partner[...])).astype(BF)


def sum_kernel(parts, out):
    out[...] = jnp.sum(parts[...].astype(F32), axis=0)


def turn(x, k):
    return lax.ppermute(x, "rep", [(i, (i + k) % REPS) for i in range(REPS)])


def swap(x):
    return lax.ppermute(x, "core", [(0, 1), (1, 0)])


def exchange(x, axes):
    return lax.all_to_all(x, axes, 0, 0, tiled=True)


def shards(features, head_weight, slot_of_image, candidates, positives):
    owners_axes = ("zx", "core")
    everyone = ("zx", "core", "rep")
    dp = lax.axis_size(owners_axes)
    me = lax.axis_index(owners_axes)
    core = lax.axis_index("core")
    rep = lax.axis_index("rep")
    n, width = features.shape
    e = head_weight.shape[1]
    devices = dp * REPS
    owner_slots = n * REPS
    blocks = owner_slots // BR
    cap = 2 * n // devices
    count = devices * cap
    factor = objective_factor / (logit_sharpness * math.sqrt(n * devices))
    vmem = pl.BlockSpec(memory_space=pltpu.VMEM)
    smem = pl.BlockSpec(memory_space=pltpu.SMEM)
    far_away = pl.BlockSpec(memory_space=pl.ANY)

    def call(kernel, name, shapes, args, **more):
        return pl.pallas_call(
            kernel, out_shape=shapes, compiler_params=params(), name=name, **more
        )(*args)

    send, unit, norm, place = call(
        lambda *r: project_kernel(owner_slots, dp, cap, *r),
        "project",
        (sds((count, e + BR), BF), sds((n, e), F32), sds((n, BR), F32), sds((8, n), F32)),
        (slot_of_image.reshape(1, n), features, head_weight),
    )
    got = exchange(send.reshape(devices, cap, e + BR), everyone).reshape(count, e + BR)

    mine, other = call(
        stripes_kernel,
        "stripes",
        (sds((width // 2, n), BF),) * 2,
        (core.reshape(1), features),
        in_specs=[smem, vmem],
    )
    theirs = swap(other)

    packed, back_place = call(
        compact_kernel, "compact", (sds((n + 16, e), BF), sds((8, count), F32)), (got,)
    )
    left, right = turn(packed, 1), turn(packed, 3)
    far_a, far_b = turn(left[: n // 2], 1), turn(right[n // 2 :], 3)

    table = candidates.reshape(dp, blocks, REPS, PAIRS_REP)
    table = lax.dynamic_index_in_dim(table, rep, axis=2, keepdims=False)
    table = table.reshape(dp, blocks * PAIRS_REP)
    owner = table // blocks
    serve = jnp.sum(jnp.where(owner == me, table - owner * blocks, 0), axis=1)
    need = lax.dynamic_index_in_dim(owner, me, axis=0, keepdims=False)
    column = positives.reshape(blocks, BR) - rep * (PAIRS_REP * BR)

    partial, slots = call(
        near_kernel,
        "near",
        (sds((owner_slots, e), BF), sds((3, 8, n), F32)),
        (packed, left, right),
    )
    anchors, served, far = call(
        far_kernel,
        "far",
        (sds((owner_slots, e), BF), sds((dp, BR, e), BF), sds((8, n), F32)),
        (serve, partial, far_a, far_b),
        in_specs=[smem] + [vmem] * 3,
        out_specs=(vmem, far_away, vmem),
        scratch_shapes=[pltpu.SemaphoreType.DMA((dp,))],
    )
    fetched = exchange(served, owners_axes)
    weights, stats = call(
        scores_kernel,
        "scores",
        (sds((blocks, PAIRS_REP * BR, BR), BF), sds((2 * blocks, BR), F32)),
        (need, column, anchors, fetched),
        in_specs=[smem] + [vmem] * 3,
    )
    spread = (stats, turn(stats, 1), turn(stats, 2), turn(stats, 3))
    pulled, partner = call(
        mix_kernel,
        "mix",
        (sds((owner_slots, e), BF),) * 2,
        (need, column, weights, fetched),
        in_specs=[smem] + [vmem] * 3,
    )
    share, y1, y2, y3 = call(
        lambda *r: shares_kernel(factor, *r),
        "shares",
        (sds((owner_slots, e), BF),) + (sds((n, e), BF),) * 3,
        (*spread, pulled, partner, slots, far),
    )
    y0 = call(own_kernel, "own", sds((n, e), BF), (share, slots))
    shares = (y0, turn(y1, 3), turn(y2, 1), turn(y3, 2))
    back = call(back_kernel, "back", sds((count, e), BF), (*shares, back_place))
    returned = exchange(back.reshape(devices, cap, e), everyone).reshape(count, e)

    both = (spread[0] + spread[2]) + (spread[1] + spread[3])
    rest, matching = both[:blocks], both[blocks:]
    total = rest + jnp.exp(matching - 1.0 / logit_sharpness)
    anchor_row_loss = (jnp.log(total) + 1.0 / logit_sharpness - matching).reshape(owner_slots)

    grad = call(
        unit_grad_kernel, "unit_grad", sds((n, e), BF), (returned, place, unit, norm)
    )
    partial = call(
        head_grad_kernel, "head_grad", sds((width // 2, e), BF), (mine, theirs, grad, swap(grad))
    )
    parts = exchange(partial.reshape(devices // 2, width // devices, e), ("zx", "rep"))
    weight_grad = call(sum_kernel, "add", sds((width // devices, e), F32), (parts,))
    return (anchor_row_loss, weight_grad)


def solution(mesh):
    dp, rep = mesh.devices.shape
    split = jax.sharding.Mesh(mesh.devices.reshape(dp // 2, 2, rep), ("zx", "core", "rep"))
    everyone = ("zx", "core", "rep")
    owners = ("zx", "core")
    placed = (P(everyone, None), P(), P(everyone), P(), P(owners))
    return jax.shard_map(
        shards,
        mesh=split,
        in_specs=placed,
        out_specs=(P(owners), P(everyone, None)),
        check_vma=False,
    )
```

time: 281 us -> 236 us (0.84)
  waiting for transfers between devices: 77.7 us -> 122 us
  blocking collectives: 68.7 us -> 32.5 us
  Pallas kernels: 75.6 us -> 40.2 us
  starting transfers between devices: 47 us -> 30.1 us
    all_to_all x5 -> x3, waiting for transfers between devices: 45.2 us -> 87.9 us  [exchange(): return lax.all_to_all(x, axes, 0, 0, tiled=True)]
    pallas_call x17 -> x13, Pallas kernels: 75.6 us -> 40.2 us  [call(): pl.pallas_call(kernel, out_shape=shapes, compiler_params=params(), name=n...]
    psum x1 -> x0, blocking collectives: 18.3 us -> none  [shards(): stats = lax.psum(stats, 'rep')]
    all_to_all x2 -> x1, blocking collectives: 50.4 us -> 32.5 us  [exchange(): return lax.all_to_all(x, axes, 0, 0, tiled=True)]
    all_to_all x5 -> x3, starting transfers between devices: 27.4 us -> 17.9 us  [exchange(): return lax.all_to_all(x, axes, 0, 0, tiled=True)]
    ppermute x14 -> x10, starting transfers between devices: 19.6 us -> 12 us  [turn(): return lax.ppermute(x, 'rep', [(i, (i + k) % REPS) for i in range(REPS)])]
    ppermute x14 -> x10, waiting for transfers between devices: 30.3 us -> 32.4 us  [turn(): return lax.ppermute(x, 'rep', [(i, (i + k) % REPS) for i in range(REPS)])]
    unnamed x46 -> x22, local copies, waits for them, and re-layouts: 6.98 us -> 8.08 us
  transfers between devices with their start and end apart: 21 -> 15, of which waited for: 11 -> 9; matrix products, arithmetic and copies ran while one was open for 1% -> 1% of each run, Pallas kernels for 17% -> 6%
where the time goes in v3:
time: 236 us; the launch traced here: 235 us
  waiting for transfers between devices  122 us (52%)
  Pallas kernels  40.2 us (17%)
  blocking collectives  32.5 us (14%)
  starting transfers between devices  30.1 us (13%)
  local copies, waits for them, and re-layouts  8.29 us (4%)
    all_to_all x3, waiting for transfers between devices, exchange(): return lax.all_to_all(x, axes, 0, 0, tiled=True)  87.9 us
    pallas_call x13, Pallas kernels, call(): pl.pallas_call(kernel, out_shape=shapes, compiler_params=params(), name=n...  40.2 us
    all_to_all x1, blocking collectives, exchange(): return lax.all_to_all(x, axes, 0, 0, tiled=True)  32.5 us
    ppermute x10, waiting for transfers between devices, turn(): return lax.ppermute(x, 'rep', [(i, (i + k) % REPS) for i in range(REPS)])  32.4 us
    all_to_all x3, starting transfers between devices, exchange(): return lax.all_to_all(x, axes, 0, 0, tiled=True)  17.9 us
    ppermute x10, starting transfers between devices, turn(): return lax.ppermute(x, 'rep', [(i, (i + k) % REPS) for i in range(REPS)])  12 us
    unnamed x22, local copies, waits for them, and re-layouts  8.08 us
  transfers between devices with their start and end apart: 15, of which 9 were waited for; matrix products, arithmetic and copies ran while one was open for 1% of the time, Pallas kernels for 6%

profile of v3, /device:TPU:0, one launch (start us, length us, event | category | flops | bytes accessed | tf_op | source)
XLA Modules:
  0.0 235.0 jit_solution(18356896674012536403)
XLA Ops:
  0.6 1.6 copy-done
  2.2 1.6 copy-done.3
  4.5 2.3 project.1
  6.9 32.5 %all_to_all.20 = bf16[128,8,640]{2,1,0:T(8,128)(2,1)S(1)} all-to-all(bf16[128,8,640]{2,1,0:T(8,128)(2,1)S(1)} %bitcast.16), channel_id=1, replica_groups=mesh['zx'=16,'core'=2,'rep'=4] {'zx','core','rep'}, dimensions={0} | all-to-all | bytes 2621440 | tf_op jit(solution)/shard_map/all_to_all | solution.py:263
  40.5 1.2 collective-permute-start.1
  42.5 12.3 %collective-permute-done.1.right = bf16[528,512]{1,0:T(8,128)(2,1)S(1)} collective-permute-done((bf16[528,512]{1,0:T(8,128)(2,1)S(1)}, bf16[528,512]{1,0:T(8,128)(2,1)S(1)}, u32[]{:S(2)}, u32[]{:S(2)}) %collective-permute-start.1) | collective-permute-done | bytes 540704 | tf_op jit(solution)/shard_map/ppermute | solution.py:255
  54.8 2.2 collective-permute-start.3
  57.4 4.8 %near.1 = (bf16[2048,512]{1,0:T(8,128)(2,1)S(1)}, f32[3,8,512]{2,1,0:T(8,128)S(1)}) custom-call(bf16[528,512]{1,0:T(8,128)(2,1)S(1)} %get-tuple-element.24.own, bf16[528,512]{1,0:T(8,128)(2,1)S(1)} %collective-permute-done.left, bf16[528,512]{1,0:T(8,128)(2,1)S(1)} %collective-permute-done.1.right), custom_call_target="tpu_custom_call" | custom-call | tf_op jit(solution)/shard_map/near/pallas_call | solution.py:286
  62.2 3.0 %collective-permute-done.2.far_a = bf16[256,512]{1,0:T(8,128)(2,1)S(1)} collective-permute-done((bf16[256,512]{1,0:T(8,128)(2,1)S(1)}, bf16[256,512]{1,0:T(8,128)(2,1)S(1)}, u32[]{:S(2)}, u32[]{:S(2)}) %collective-permute-start.2) | collective-permute-done | bytes 262176 | tf_op jit(solution)/shard_map/ppermute | solution.py:255
  65.2 8.9 %far.1 = (bf16[2048,512]{1,0:T(8,128)(2,1)S(1)}, bf16[32,128,512]{2,1,0:T(8,128)(2,1)S(1)}, f32[8,512]{1,0:T(8,128)S(1)}) custom-call(s32[32]{0:T(128)S(1)} %get-tuple-element.44.serve, bf16[2048,512]{1,0:T(8,128)(2,1)S(1)} %get-tuple-element.25.partial, bf16[256,512]{1,0:T(8,128)(2,1)S(1)} %collective-permute-done.2.far_a, ...), custom_call_target="tpu_custom_call" | custom-call | tf_op jit(solution)/shard_map/far/pallas_call | solution.py:286
  74.1 2.0 copy-done.2
  76.1 5.5 %all-to-all-start.1 = ((bf16[32,128,512]{2,1,0:T(8,128)(2,1)}), bf16[32,128,512]{2,1,0:T(8,128)(2,1)}, u32[]{:S(2)}, u32[]{:S(2)}) async-start(bf16[32,128,512]{2,1,0:T(8,128)(2,1)} %copy-done.2), calls=%async_computation.1 | async-start | bytes 8388608 | tf_op jit(solution)/shard_map/all_to_all | solution.py:263
  81.9 53.2 %all-to-all-done.1.fetched = bf16[32,128,512]{2,1,0:T(8,128)(2,1)} async-done(((bf16[32,128,512]{2,1,0:T(8,128)(2,1)}), bf16[32,128,512]{2,1,0:T(8,128)(2,1)}, u32[]{:S(2)}, u32[]{:S(2)}) %all-to-all-start.1) | async-done | bytes 4194336 | tf_op jit(solution)/shard_map/all_to_all | solution.py:263
  135.1 4.0 %scores.1 = (bf16[16,256,128]{2,1,0:T(8,128)(2,1)S(1)}, f32[32,128]{1,0:T(8,128)S(1)}) custom-call(s32[32]{0:T(128)S(1)} %fusion.3.need, s32[16,128]{1,0:T(8,128)S(1)} %subtract_bitcast_fusion.column, bf16[2048,512]{1,0:T(8,128)(2,1)S(1)} %get-tuple-element.26.anchors, bf16[32,128,512]{2,1,0:T(8,128)(2,1)} %all-to-all-done.1.fetched), custom_call_target="tpu_custom_call" | custom-call | tf_op jit(solution)/shard_map/scores/pallas_call | solution.py:286
  139.2 1.4 collective-permute-start.5
  140.6 1.9 collective-permute-start.6
  142.5 5.1 %mix.1 = (bf16[2048,512]{1,0:T(8,128)(2,1)S(1)}, bf16[2048,512]{1,0:T(8,128)(2,1)S(1)}) custom-call(s32[32]{0:T(128)S(1)} %fusion.3.need, s32[16,128]{1,0:T(8,128)S(1)} %subtract_bitcast_fusion.column, bf16[16,256,128]{2,1,0:T(8,128)(2,1)S(1)} %get-tuple-element.31.weights, bf16[32,128,512]{2,1,0:T(8,128)(2,1)} %all-to-all-done.1.fetched), custom_call_target="tpu_custom_call" | custom-call | tf_op jit(solution)/shard_map/mix/pallas_call | solution.py:286
  147.7 4.4 %shares.1 = (bf16[2048,512]{1,0:T(8,128)(2,1)S(1)}, bf16[512,512]{1,0:T(8,128)(2,1)S(1)}, bf16[512,512]{1,0:T(8,128)(2,1)S(1)}, bf16[512,512]{1,0:T(8,128)(2,1)S(1)}) custom-call(f32[32,128]{1,0:T(8,128)S(1)} %get-tuple-element.28.r_0_, f32[32,128]{1,0:T(8,128)S(1)} %collective-permute-done.5.r_1_, f32[32,128]{1,0:T(8,128)S(1)} %collective-permute-done.4.r_2_, ...), custom_call_target="tpu_custom_call" | custom-call | tf_op jit(solution)/shard_map/shares/pallas_call | solution.py:286
  152.1 2.3 collective-permute-start.10
  155.0 1.4 collective-permute-start.9
  156.4 1.6 own.1.a
  158.0 10.5 %collective-permute-done.10.d = bf16[512,512]{1,0:T(8,128)(2,1)S(1)} collective-permute-done((bf16[512,512]{1,0:T(8,128)(2,1)S(1)}, bf16[512,512]{1,0:T(8,128)(2,1)S(1)}, u32[]{:S(2)}, u32[]{:S(2)}) %collective-permute-start.10) | collective-permute-done | bytes 524320 | tf_op jit(solution)/shard_map/ppermute | solution.py:255
  168.5 4.8 %collective-permute-done.8.b = bf16[512,512]{1,0:T(8,128)(2,1)S(1)} collective-permute-done((bf16[512,512]{1,0:T(8,128)(2,1)S(1)}, bf16[512,512]{1,0:T(8,128)(2,1)S(1)}, u32[]{:S(2)}, u32[]{:S(2)}) %collective-permute-start.8) | collective-permute-done | bytes 524320 | tf_op jit(solution)/shard_map/ppermute | solution.py:255
  173.3 1.9 collective-permute-done.9.c
  175.1 2.1 back.1
  177.3 7.5 %all-to-all-start.2 = ((bf16[128,8,512]{2,1,0:T(8,128)(2,1)}), bf16[128,8,512]{2,1,0:T(8,128)(2,1)S(1)}, u32[]{:S(2)}, u32[]{:S(2)}) async-start(bf16[128,8,512]{2,1,0:T(8,128)(2,1)} %bitcast.7), calls=%async_computation.2 | async-start | bytes 2097152 | tf_op jit(solution)/shard_map/all_to_all | solution.py:263
  184.8 1.7 stripes.1
  187.4 16.1 %all-to-all-done.2 = bf16[128,8,512]{2,1,0:T(8,128)(2,1)S(1)} async-done(((bf16[128,8,512]{2,1,0:T(8,128)(2,1)}), bf16[128,8,512]{2,1,0:T(8,128)(2,1)S(1)}, u32[]{:S(2)}, u32[]{:S(2)}) %all-to-all-start.2) | async-done | bytes 1048608 | tf_op jit(solution)/shard_map/all_to_all | solution.py:263
  206.1 1.8 collective-permute-done.11.partner
  207.8 2.2 head_grad.1
  210.1 4.9 %all-to-all-start.3 = ((bf16[64,16,512]{2,1,0:T(8,128)(2,1)}), bf16[64,16,512]{2,1,0:T(8,128)(2,1)S(1)}, u32[]{:S(2)}, u32[]{:S(2)}) async-start(bf16[64,16,512]{2,1,0:T(8,128)(2,1)} %bitcast.9), calls=%async_computation.3 | async-start | bytes 2097152 | tf_op jit(solution)/shard_map/all_to_all | solution.py:263
  215.6 18.6 %all-to-all-done.3.parts = bf16[64,16,512]{2,1,0:T(8,128)(2,1)S(1)} async-done(((bf16[64,16,512]{2,1,0:T(8,128)(2,1)}), bf16[64,16,512]{2,1,0:T(8,128)(2,1)S(1)}, u32[]{:S(2)}, u32[]{:S(2)}) %all-to-all-start.3) | async-done | bytes 1048608 | tf_op jit(solution)/shard_map/all_to_all | solution.py:263
  (45 shorter events, 8.9 us)
Async XLA Ops:
  0.6 1.6 copy-start
  2.2 1.6 copy-start.3
  3.8 0.7 copy-start.8
  6.9 48.0 %copy-start.4 = (f32[512,512]{1,0:T(8,128)}, f32[512,512]{1,0:T(8,128)S(1)}, u32[]{:S(2)}) copy-start(f32[512,512]{1,0:T(8,128)S(1)} %get-tuple-element.42.unit) | copy-start | bytes 3145732
  6.9 50.3 %copy-start.9 = (s32[512,8]{0,1:T(8,128)S(1)}, s32[512,8]{0,1:T(8,128)}, u32[]{:S(2)}) copy-start(s32[512,8]{0,1:T(8,128)} %param.8) | copy-start | bytes 49156
  40.5 14.3 %collective-permute-start.1 = (bf16[528,512]{1,0:T(8,128)(2,1)S(1)}, bf16[528,512]{1,0:T(8,128)(2,1)S(1)}, u32[]{:S(2)}, u32[]{:S(2)}) collective-permute-start(bf16[528,512]{1,0:T(8,128)(2,1)S(1)} %get-tuple-element.24.own), channel_id=1, source_target_pairs={{0,3},{1,0},{2,1},{3,2},{4,7},{5,4},{6,5},{7,6},{8,11},{9,8},{10,9... | collective-permute-start | bytes 1622024 | tf_op jit(solution)/shard_map/ppermute | solution.py:255
  41.7 15.3 %collective-permute-start = (bf16[528,512]{1,0:T(8,128)(2,1)S(1)}, bf16[528,512]{1,0:T(8,128)(2,1)S(1)}, u32[]{:S(2)}, u32[]{:S(2)}) collective-permute-start(bf16[528,512]{1,0:T(8,128)(2,1)S(1)} %get-tuple-element.24.own), channel_id=1, source_target_pairs={{0,1},{1,2},{2,3},{3,0},{4,5},{5,6},{6,7},{7,4},{8,9},{9,10},{10,1... | collective-permute-start | bytes 1622024 | tf_op jit(solution)/shard_map/ppermute | solution.py:255
  54.8 10.3 %collective-permute-start.3 = (bf16[272,512]{1,0:T(8,128)(2,1)S(1)}, bf16[272,512]{1,0:T(8,128)(2,1)S(1)}, u32[]{:S(2)}, u32[]{:S(2)}) collective-permute-start(bf16[272,512]{1,0:T(8,128)(2,1)S(1)} %slice.17), channel_id=1, source_target_pairs={{0,3},{1,0},{2,1},{3,2},{4,7},{5,4},{6,5},{7,6},{8,11},{9,8},{10,9... | collective-permute-start | bytes 835592 | tf_op jit(solution)/shard_map/ppermute | solution.py:255
  57.0 8.1 %collective-permute-start.2 = (bf16[256,512]{1,0:T(8,128)(2,1)S(1)}, bf16[256,512]{1,0:T(8,128)(2,1)S(1)}, u32[]{:S(2)}, u32[]{:S(2)}) collective-permute-start(bf16[256,512]{1,0:T(8,128)(2,1)S(1)} %slice.16), channel_id=1, source_target_pairs={{0,1},{1,2},{2,3},{3,0},{4,5},{5,6},{6,7},{7,4},{8,9},{9,10},{10,1... | collective-permute-start | bytes 786440 | tf_op jit(solution)/shard_map/ppermute | solution.py:255
  74.1 2.0 copy-start.2
  76.1 5.8 %copy-start.10 = (s32[2048]{0:T(1024)S(1)}, s32[2048]{0:T(1024)}, u32[]{:S(2)}) copy-start(s32[2048]{0:T(1024)} %param.9) | copy-start | bytes 24580
  76.1 59.0 %all-to-all-start.1 = ((bf16[32,128,512]{2,1,0:T(8,128)(2,1)}), bf16[32,128,512]{2,1,0:T(8,128)(2,1)}, u32[]{:S(2)}, u32[]{:S(2)}) async-start(bf16[32,128,512]{2,1,0:T(8,128)(2,1)} %copy-done.2), calls=%async_computation.1 | async-start | bytes 8388608 | tf_op jit(solution)/shard_map/all_to_all | solution.py:263
  139.1 8.5 %collective-permute-start.4 = (f32[32,128]{1,0:T(8,128)S(1)}, f32[32,128]{1,0:T(8,128)S(1)}, u32[]{:S(2)}, u32[]{:S(2)}) collective-permute-start(f32[32,128]{1,0:T(8,128)S(1)} %get-tuple-element.28.r_0_), channel_id=1, source_target_pairs={{0,2},{1,3},{2,0},{3,1},{4,6},{5,7},{6,4},{7,5},{8,10},{9,11},{10,... | collective-permute-start | bytes 49160 | tf_op jit(solution)/shard_map/ppermute | solution.py:255
  139.2 8.4 %collective-permute-start.5 = (f32[32,128]{1,0:T(8,128)S(1)}, f32[32,128]{1,0:T(8,128)S(1)}, u32[]{:S(2)}, u32[]{:S(2)}) collective-permute-start(f32[32,128]{1,0:T(8,128)S(1)} %get-tuple-element.28.r_0_), channel_id=1, source_target_pairs={{0,1},{1,2},{2,3},{3,0},{4,5},{5,6},{6,7},{7,4},{8,9},{9,10},{10,1... | collective-permute-start | bytes 49160 | tf_op jit(solution)/shard_map/ppermute | solution.py:255
  140.6 7.1 %collective-permute-start.6 = (f32[32,128]{1,0:T(8,128)S(1)}, f32[32,128]{1,0:T(8,128)S(1)}, u32[]{:S(2)}, u32[]{:S(2)}) collective-permute-start(f32[32,128]{1,0:T(8,128)S(1)} %get-tuple-element.28.r_0_), channel_id=1, source_target_pairs={{0,3},{1,0},{2,1},{3,2},{4,7},{5,4},{6,5},{7,6},{8,11},{9,8},{10,9... | collective-permute-start | bytes 49160 | tf_op jit(solution)/shard_map/ppermute | solution.py:255
  152.1 16.4 %collective-permute-start.10 = (bf16[512,512]{1,0:T(8,128)(2,1)S(1)}, bf16[512,512]{1,0:T(8,128)(2,1)S(1)}, u32[]{:S(2)}, u32[]{:S(2)}) collective-permute-start(bf16[512,512]{1,0:T(8,128)(2,1)S(1)} %get-tuple-element.39), channel_id=1, source_target_pairs={{0,2},{1,3},{2,0},{3,1},{4,6},{5,7},{6,4},{7,5},{8,10},{9,11},{10,... | collective-permute-start | bytes 1572872 | tf_op jit(solution)/shard_map/ppermute | solution.py:255
  154.4 18.9 %collective-permute-start.8 = (bf16[512,512]{1,0:T(8,128)(2,1)S(1)}, bf16[512,512]{1,0:T(8,128)(2,1)S(1)}, u32[]{:S(2)}, u32[]{:S(2)}) collective-permute-start(bf16[512,512]{1,0:T(8,128)(2,1)S(1)} %get-tuple-element.37), channel_id=1, source_target_pairs={{0,3},{1,0},{2,1},{3,2},{4,7},{5,4},{6,5},{7,6},{8,11},{9,8},{10,9... | collective-permute-start | bytes 1572872 | tf_op jit(solution)/shard_map/ppermute | solution.py:255
  155.0 20.1 %collective-permute-start.9 = (bf16[512,512]{1,0:T(8,128)(2,1)S(1)}, bf16[512,512]{1,0:T(8,128)(2,1)S(1)}, u32[]{:S(2)}, u32[]{:S(2)}) collective-permute-start(bf16[512,512]{1,0:T(8,128)(2,1)S(1)} %get-tuple-element.38), channel_id=1, source_target_pairs={{0,1},{1,2},{2,3},{3,0},{4,5},{5,6},{6,7},{7,4},{8,9},{9,10},{10,1... | collective-permute-start | bytes 1572872 | tf_op jit(solution)/shard_map/ppermute | solution.py:255
  175.1 9.6 %copy-start.1 = (bf16[512,2048]{1,0:T(8,128)(2,1)S(1)}, bf16[512,2048]{1,0:T(8,128)(2,1)}, u32[]{:S(2)}) copy-start(bf16[512,2048]{1,0:T(8,128)(2,1)} %feat.1) | copy-start | bytes 6291460
  177.3 26.3 %all-to-all-start.2 = ((bf16[128,8,512]{2,1,0:T(8,128)(2,1)}), bf16[128,8,512]{2,1,0:T(8,128)(2,1)S(1)}, u32[]{:S(2)}, u32[]{:S(2)}) async-start(bf16[128,8,512]{2,1,0:T(8,128)(2,1)} %bitcast.7), calls=%async_computation.2 | async-start | bytes 2097152 | tf_op jit(solution)/shard_map/all_to_all | solution.py:263
  186.5 1.0 copy-start.6
  187.4 18.6 %collective-permute-start.7 = (bf16[1024,512]{1,0:T(8,128)(2,1)}, bf16[1024,512]{1,0:T(8,128)(2,1)S(1)}, u32[]{:S(2)}, u32[]{:S(2)}) collective-permute-start(bf16[1024,512]{1,0:T(8,128)(2,1)} %get-tuple-element.30), channel_id=1, source_target_pairs={{0,4},{4,0},{1,5},{5,1},{2,6},{6,2},{3,7},{7,3},{8,12},{12,8},{9,1... | collective-permute-start | bytes 3145736 | tf_op jit(solution)/shard_map/ppermute | solution.py:259
  203.5 1.2 copy-start.5
  204.8 3.1 %copy-start.7 = (bf16[1024,512]{1,0:T(8,128)(2,1)S(1)}, bf16[1024,512]{1,0:T(8,128)(2,1)}, u32[]{:S(2)}) copy-start(bf16[1024,512]{1,0:T(8,128)(2,1)} %copy-done.6) | copy-start | bytes 3145732
  205.9 2.0 collective-permute-start.11
  210.1 24.1 %all-to-all-start.3 = ((bf16[64,16,512]{2,1,0:T(8,128)(2,1)}), bf16[64,16,512]{2,1,0:T(8,128)(2,1)S(1)}, u32[]{:S(2)}, u32[]{:S(2)}) async-start(bf16[64,16,512]{2,1,0:T(8,128)(2,1)} %bitcast.9), calls=%async_computation.3 | async-start | bytes 2097152 | tf_op jit(solution)/shard_map/all_to_all | solution.py:263

commit v4 on v3

--- a/solution.py
+++ b/solution.py
@@ -23,6 +23,10 @@
 
 def params():
     return pltpu.CompilerParams(vmem_limit_bytes=VMEM_BYTES)
+
+
+def cost(us):
+    return pl.CostEstimate(flops=int(us * 1e9), bytes_accessed=int(us * 1e6), transcendentals=0)
 
 
 def iota(shape, dim):
@@ -61,7 +65,9 @@
     mine = iota((owners, n), 0) == owner
     before = dot(hot(mine), hot(iota((n, n), 0) < iota((n, n), 1)))
     rank = jnp.sum(jnp.where(mine, before, 0.0), axis=0, keepdims=True).astype(I32)
-    p = (owner * REPS + (rank & (REPS - 1))) * cap + rank // REPS
+    member = rank & (REPS - 1)
+    device = (owner // 2) * 8 + (member // 2) * 4 + (owner & 1) * 2 + (member & 1)
+    p = device * cap + rank // REPS
     place[...] = jnp.broadcast_to(p.astype(F32), place.shape)
     scatter = hot(iota((send.shape[0], n), 0) == p)
     send[:, :e] = dot(scatter, descriptor).astype(BF)
@@ -103,18 +109,8 @@
     return tag[0:1, :] * BR + tag[1:2, :]
 
 
-def near_kernel(own, left, right, partial, slots):
-    n = own.shape[0] - 16
-    pieces = []
-    for k, ref in enumerate((own, left, right)):
-        row = slot_row(ref[n:, :])
-        slots[k, :, :] = jnp.broadcast_to(row, slots.shape[1:])
-        pieces.append((row.astype(I32), ref[:n, :]))
-    place_rows(partial, pieces, None)
-
-
-def place_rows(out, pieces, start):
-    step = 256
+def place_rows(out, pieces, start, after=None):
+    step = 2 * BR
 
     def body(i, carry):
         base = pl.multiple_of(i * step, step)
@@ -124,31 +120,53 @@
             part = dot(hot(at == ids), rows)
             total = part if total is None else total + part
         out[pl.ds(base, step), :] = total.astype(BF)
+        if after is not None:
+            after(i)
         return carry
 
     lax.fori_loop(0, out.shape[0] // step, body, 0)
 
 
-def serve_blocks(serve, anchors, served, sems):
-    copies = []
-    for d in range(served.shape[0]):
+def near_kernel(own, beside, partial, slots):
+    n = own.shape[0] - 16
+    pieces = []
+    for k, ref in enumerate((own, beside)):
+        row = slot_row(ref[n:, :])
+        slots[k, :, :] = jnp.broadcast_to(row, slots.shape[1:])
+        pieces.append((row.astype(I32), ref[:n, :]))
+    place_rows(partial, pieces, None)
+
+
+def middle_kernel(begun, across, partial, slots):
+    n = across.shape[0] - 16
+    row = slot_row(across[n:, :])
+    slots[...] = jnp.broadcast_to(row, slots.shape)
+    place_rows(partial, [(row.astype(I32), across[:n, :])], begun)
+
+
+def far_kernel(serve, order, ready, begun, corner, anchors, served, slots, sems):
+    n = corner.shape[0] - 16
+    row = slot_row(corner[n:, :])
+    slots[...] = jnp.broadcast_to(row, slots.shape)
+
+    def copy(d):
         start = pl.multiple_of(serve[d] * BR, BR)
-        copies.append(
-            pltpu.make_async_copy(anchors.at[pl.ds(start, BR), :], served.at[d], sems.at[d])
-        )
-    for c in copies:
-        c.start()
-    for c in copies:
-        c.wait()
-
-
-def far_kernel(serve, partial, far_a, far_b, anchors, served, slots, sems):
-    q = far_a.shape[0]
-    row = slot_row(far_b[q:, :])
-    slots[...] = jnp.broadcast_to(row, slots.shape)
-    ids = row.astype(I32)
-    place_rows(anchors, [(ids[:, :q], far_a[...]), (ids[:, q:], far_b[:q, :])], partial)
-    serve_blocks(serve, anchors, served, sems)
+        return pltpu.make_async_copy(anchors.at[pl.ds(start, BR), :], served.at[d], sems.at[d])
+
+    def begin(j, carry):
+        copy(order[j]).start()
+        return carry
+
+    def after(i):
+        lax.fori_loop(ready[i], ready[i + 1], begin, 0)
+
+    place_rows(anchors, [(row.astype(I32), corner[:n, :])], begun, after)
+
+    def finish(d, carry):
+        copy(d).wait()
+        return carry
+
+    lax.fori_loop(0, served.shape[0], finish, 0)
 
 
 def scores_kernel(need, column, anchors, fetched, weights, stats):
@@ -204,9 +222,9 @@
         out[h * step : (h + 1) * step, :] = dot(pick, rows[...]).astype(BF)
 
 
-def shares_kernel(factor, s0, s1, s2, s3, pulled, partner, slots, far, share, y1, y2, y3):
+def shares_kernel(factor, s0, s1, s2, s3, pulled, partner, slots, share, out):
     blocks = s0.shape[0] // 2
-    stats = (s0[...] + s2[...]) + (s1[...] + s3[...])
+    stats = (s0[...] + s3[...]) + (s1[...] + s2[...])
     rest, matching = stats[:blocks, :], stats[blocks:, :]
     total = rest + jnp.exp(matching - 1.0 / logit_sharpness)
     scale = jnp.concatenate([factor / total, factor * (rest / total)], axis=0)
@@ -216,17 +234,15 @@
         grad = pulled[at, :].astype(F32) * scale[:, b : b + 1]
         grad -= partner[at, :].astype(F32) * scale[:, blocks + b : blocks + b + 1]
         share[at, :] = grad.astype(BF)
-    pick_rows(y3, share, column_of(far[...]))
-    pick_rows(y1, share, column_of(slots[1, :, :]))
-    pick_rows(y2, share, column_of(slots[2, :, :]))
-
-
-def own_kernel(share, slots, y0):
-    pick_rows(y0, share, column_of(slots[0, :, :]))
-
-
-def back_kernel(a, b, c, d, place, back):
-    total = a[...].astype(F32) + b[...].astype(F32) + c[...].astype(F32) + d[...].astype(F32)
+    pick_rows(out, share, column_of(slots[...]))
+
+
+def pick_kernel(share, slots, out):
+    pick_rows(out, share, column_of(slots[...]))
+
+
+def back_kernel(a, b, c, place, back):
+    total = a[...].astype(F32) + b[...].astype(F32) + c[...].astype(F32)
     rows = a.shape[0]
     pos = column_of(place[...])
     back[...] = dot(hot(iota((back.shape[0], rows), 1) == pos), total.astype(BF)).astype(BF)
@@ -251,12 +267,9 @@
     out[...] = jnp.sum(parts[...].astype(F32), axis=0)
 
 
-def turn(x, k):
-    return lax.ppermute(x, "rep", [(i, (i + k) % REPS) for i in range(REPS)])
-
-
-def swap(x):
-    return lax.ppermute(x, "core", [(0, 1), (1, 0)])
+def swap(x, axes=("core",)):
+    size = 2 ** len(axes)
+    return lax.ppermute(x, axes, [(i, size - 1 - i) for i in range(size)])
 
 
 def exchange(x, axes):
@@ -264,12 +277,13 @@
 
 
 def shards(features, head_weight, slot_of_image, candidates, positives):
-    owners_axes = ("zx", "core")
-    everyone = ("zx", "core", "rep")
+    owners_axes = ("zx", "yhi")
+    everyone = ("zx", "core", "yhi", "ylo")
     dp = lax.axis_size(owners_axes)
     me = lax.axis_index(owners_axes)
     core = lax.axis_index("core")
-    rep = lax.axis_index("rep")
+    member = core * 2 + lax.axis_index("ylo")
+    home = core == lax.axis_index("yhi")
     n, width = features.shape
     e = head_weight.shape[1]
     devices = dp * REPS
@@ -307,30 +321,43 @@
     packed, back_place = call(
         compact_kernel, "compact", (sds((n + 16, e), BF), sds((8, count), F32)), (got,)
     )
-    left, right = turn(packed, 1), turn(packed, 3)
-    far_a, far_b = turn(left[: n // 2], 1), turn(right[n // 2 :], 3)
+    beside = swap(packed)
+    across = swap(packed, ("ylo",))
 
     table = candidates.reshape(dp, blocks, REPS, PAIRS_REP)
-    table = lax.dynamic_index_in_dim(table, rep, axis=2, keepdims=False)
+    table = lax.dynamic_index_in_dim(table, member, axis=2, keepdims=False)
     table = table.reshape(dp, blocks * PAIRS_REP)
     owner = table // blocks
     serve = jnp.sum(jnp.where(owner == me, table - owner * blocks, 0), axis=1)
     need = lax.dynamic_index_in_dim(owner, me, axis=0, keepdims=False)
-    column = positives.reshape(blocks, BR) - rep * (PAIRS_REP * BR)
-
+    column = jnp.where(home, positives, swap(positives)).reshape(blocks, BR)
+    column = column - member * (PAIRS_REP * BR)
+    numbers = jnp.arange(dp, dtype=I32)
+    keys = serve * dp + numbers
+    place_of = jnp.sum((keys[None, :] < keys[:, None]).astype(I32), axis=1)
+    order = jnp.sum(jnp.where(place_of[None, :] == numbers[:, None], numbers[None, :], 0), axis=1)
+    bounds = 2 * jnp.arange(blocks // 2 + 1, dtype=I32)
+    ready = jnp.sum((serve[None, :] < bounds[:, None]).astype(I32), axis=1)
+
+    whole = sds((owner_slots, e), BF)
+    ids_shape = sds((8, n), F32)
     partial, slots = call(
         near_kernel,
         "near",
-        (sds((owner_slots, e), BF), sds((3, 8, n), F32)),
-        (packed, left, right),
-    )
-    anchors, served, far = call(
+        (whole, sds((2, 8, n), F32)),
+        (packed, beside),
+        cost_estimate=cost(4),
+    )
+    partial, across = lax.optimization_barrier((partial, across))
+    corner = swap(across)
+    partial, slots_across = call(middle_kernel, "middle", (whole, ids_shape), (partial, across))
+    anchors, served, slots_corner = call(
         far_kernel,
         "far",
-        (sds((owner_slots, e), BF), sds((dp, BR, e), BF), sds((8, n), F32)),
-        (serve, partial, far_a, far_b),
-        in_specs=[smem] + [vmem] * 3,
-        out_specs=(vmem, far_away, vmem),
+        (whole, pltpu.HBM((dp, BR, e), BF), ids_shape),
+        (serve, order, ready, partial, corner),
+        in_specs=[smem] * 3 + [vmem] * 2,
+        out_specs=(vmem, pl.BlockSpec(memory_space=pltpu.HBM), vmem),
         scratch_shapes=[pltpu.SemaphoreType.DMA((dp,))],
     )
     fetched = exchange(served, owners_axes)
@@ -341,7 +368,7 @@
         (need, column, anchors, fetched),
         in_specs=[smem] + [vmem] * 3,
     )
-    spread = (stats, turn(stats, 1), turn(stats, 2), turn(stats, 3))
+    spread = (stats, swap(stats), swap(stats, ("ylo",)), swap(stats, ("core", "ylo")))
     pulled, partner = call(
         mix_kernel,
         "mix",
@@ -349,37 +376,50 @@
         (need, column, weights, fetched),
         in_specs=[smem] + [vmem] * 3,
     )
-    share, y1, y2, y3 = call(
+    share, for_corner = call(
         lambda *r: shares_kernel(factor, *r),
         "shares",
-        (sds((owner_slots, e), BF),) + (sds((n, e), BF),) * 3,
-        (*spread, pulled, partner, slots, far),
-    )
-    y0 = call(own_kernel, "own", sds((n, e), BF), (share, slots))
-    shares = (y0, turn(y1, 3), turn(y2, 1), turn(y3, 2))
-    back = call(back_kernel, "back", sds((count, e), BF), (*shares, back_place))
+        (whole, sds((n, e), BF)),
+        (*spread, pulled, partner, slots_corner),
+    )
+
+    def pick(name, ids):
+        return call(pick_kernel, name, sds((n, e), BF), (share, ids))
+
+    for_across = pick("across", slots_across).astype(F32) + swap(for_corner).astype(F32)
+    from_across = swap(for_across.astype(BF), ("ylo",))
+    from_beside = swap(pick("beside", slots[1]))
+    back = call(
+        back_kernel,
+        "back",
+        pltpu.HBM((count, e), BF),
+        (pick("own", slots[0]), from_beside, from_across, back_place),
+    )
     returned = exchange(back.reshape(devices, cap, e), everyone).reshape(count, e)
 
-    both = (spread[0] + spread[2]) + (spread[1] + spread[3])
+    both = (spread[0] + spread[3]) + (spread[1] + spread[2])
     rest, matching = both[:blocks], both[blocks:]
     total = rest + jnp.exp(matching - 1.0 / logit_sharpness)
-    anchor_row_loss = (jnp.log(total) + 1.0 / logit_sharpness - matching).reshape(owner_slots)
+    loss = (jnp.log(total) + 1.0 / logit_sharpness - matching).reshape(owner_slots)
+    anchor_row_loss = jnp.where(home, loss, swap(loss, ("yhi",)))
 
     grad = call(
         unit_grad_kernel, "unit_grad", sds((n, e), BF), (returned, place, unit, norm)
     )
     partial = call(
-        head_grad_kernel, "head_grad", sds((width // 2, e), BF), (mine, theirs, grad, swap(grad))
-    )
-    parts = exchange(partial.reshape(devices // 2, width // devices, e), ("zx", "rep"))
+        head_grad_kernel, "head_grad", pltpu.HBM((width // 2, e), BF), (mine, theirs, grad, swap(grad))
+    )
+    parts = exchange(partial.reshape(devices // 2, width // devices, e), ("zx", "yhi", "ylo"))
     weight_grad = call(sum_kernel, "add", sds((width // devices, e), F32), (parts,))
     return (anchor_row_loss, weight_grad)
 
 
 def solution(mesh):
     dp, rep = mesh.devices.shape
-    split = jax.sharding.Mesh(mesh.devices.reshape(dp // 2, 2, rep), ("zx", "core", "rep"))
-    everyone = ("zx", "core", "rep")
+    split = jax.sharding.Mesh(
+        mesh.devices.reshape(dp // 2, 2, rep // 2, 2), ("zx", "core", "yhi", "ylo")
+    )
+    everyone = ("zx", "core", "yhi", "ylo")
     owners = ("zx", "core")
     placed = (P(everyone, None), P(), P(everyone), P(), P(owners))
     return jax.shard_map(

time: 236 us -> 226 us (0.958)
  waiting for transfers between devices: 122 us -> 112 us
  starting transfers between devices: 30.1 us -> 33.4 us
    ppermute x12 -> x13, starting transfers between devices: 12.2 us -> 19.1 us  [swap(): return lax.ppermute(x, axes, [(i, size - 1 - i) for i in range(size)])]
    all_to_all x3, waiting for transfers between devices: 87.9 us -> 81 us  [exchange(): return lax.all_to_all(x, axes, 0, 0, tiled=True)]
    ppermute x12 -> x13, waiting for transfers between devices: 34.2 us -> 30.7 us  [swap(): return lax.ppermute(x, axes, [(i, size - 1 - i) for i in range(size)])]
    all_to_all x3, starting transfers between devices: 17.9 us -> 14.4 us  [exchange(): return lax.all_to_all(x, axes, 0, 0, tiled=True)]
    unnamed x22 -> x20, local copies, waits for them, and re-layouts: 8.08 us -> 6.07 us
    pallas_call x13 -> x16, Pallas kernels: 40.2 us -> 38.3 us  [call(): pl.pallas_call(kernel, out_shape=shapes, compiler_params=params(), name=n...]
  transfers between devices with their start and end apart: 15 -> 16, of which waited for: 9 -> 9; matrix products, arithmetic and copies ran while one was open for 1% -> 1% of each run, Pallas kernels for 6% -> 8%
where the time goes in v4:
time: 226 us; the launch traced here: 225 us
  waiting for transfers between devices  112 us (50%)
  Pallas kernels  38.3 us (17%)
  starting transfers between devices  33.4 us (15%)
  blocking collectives  32.5 us (14%)
  local copies, waits for them, and re-layouts  6.24 us (3%)
    all_to_all x3, waiting for transfers between devices, exchange(): return lax.all_to_all(x, axes, 0, 0, tiled=True)  81 us
    pallas_call x16, Pallas kernels, call(): pl.pallas_call(kernel, out_shape=shapes, compiler_params=params(), name=n...  38.3 us
    all_to_all x1, blocking collectives, exchange(): return lax.all_to_all(x, axes, 0, 0, tiled=True)  32.5 us
    ppermute x13, waiting for transfers between devices, swap(): return lax.ppermute(x, axes, [(i, size - 1 - i) for i in range(size)])  30.7 us
    ppermute x13, starting transfers between devices, swap(): return lax.ppermute(x, axes, [(i, size - 1 - i) for i in range(size)])  19.1 us
    all_to_all x3, starting transfers between devices, exchange(): return lax.all_to_all(x, axes, 0, 0, tiled=True)  14.4 us
    unnamed x20, local copies, waits for them, and re-layouts  6.07 us
  transfers between devices with their start and end apart: 16, of which 9 were waited for; matrix products, arithmetic and copies ran while one was open for 1% of the time, Pallas kernels for 8%

profile of v4, /device:TPU:0, one launch (start us, length us, event | category | flops | bytes accessed | tf_op | source)
XLA Modules:
  0.0 224.6 jit_solution(12905528403266617206)
XLA Ops:
  0.6 1.6 copy-done
  2.2 1.6 copy-done.2
  4.5 2.4 %project.1 = (bf16[1024,640]{1,0:T(8,128)(2,1)S(1)}, f32[512,512]{1,0:T(8,128)S(1)}, f32[512,128]{1,0:T(8,128)S(1)}, f32[8,512]{1,0:T(8,128)S(1)}) custom-call(s32[1,512]{1,0:T(1,128)S(1)} %bitcast.23, bf16[512,2048]{1,0:T(8,128)(2,1)S(1)} %copy-done, bf16[2048,512]{1,0:T(8,128)(2,1)S(1)} %copy-done.2), custom_call_target="tpu_custom_call" | custom-call | tf_op jit(solution)/shard_map/project/pallas_call | solution.py:300
  6.9 32.5 %all_to_all.20 = bf16[128,8,640]{2,1,0:T(8,128)(2,1)S(1)} all-to-all(bf16[128,8,640]{2,1,0:T(8,128)(2,1)S(1)} %bitcast.22), channel_id=1, replica_groups=mesh['zx'=16,'core'=2,'yhi'=2,'ylo'=2] {'zx','core','yhi','ylo'}, dimensions={0} | all-to-all | bytes 2621440 | tf_op jit(solution)/shard_map/all_to_all | solution.py:276
  39.4 1.2 compact.1
  42.5 3.6 %near.1 = (bf16[2048,512]{1,0:T(8,128)(2,1)S(1)}, f32[2,8,512]{2,1,0:T(8,128)S(1)}) custom-call(bf16[528,512]{1,0:T(8,128)(2,1)S(1)} %get-tuple-element.26.own, bf16[528,512]{1,0:T(8,128)(2,1)S(1)} %collective-permute-done.1.beside), custom_call_target="tpu_custom_call" | custom-call | flops 4000000000 | bytes 4000000 | tf_op jit(solution)/shard_map/near/pallas_call | solution.py:300
  46.1 9.1 %collective-permute-done.2.across = bf16[528,512]{1,0:T(8,128)(2,1)S(1)} collective-permute-done((bf16[528,512]{1,0:T(8,128)(2,1)S(1)}, bf16[528,512]{1,0:T(8,128)(2,1)S(1)}, u32[]{:S(2)}, u32[]{:S(2)}) %collective-permute-start.2) | collective-permute-done | bytes 540704 | tf_op jit(solution)/shard_map/ppermute | solution.py:272
  55.7 2.5 %middle.1 = (bf16[2048,512]{1,0:T(8,128)(2,1)S(1)}, f32[8,512]{1,0:T(8,128)S(1)}) custom-call(bf16[2048,512]{1,0:T(8,128)(2,1)S(1)} %get-tuple-element.28.begun, bf16[528,512]{1,0:T(8,128)(2,1)S(1)} %collective-permute-done.2.across), custom_call_target="tpu_custom_call" | custom-call | tf_op jit(solution)/shard_map/middle/pallas_call | solution.py:300
  58.3 4.5 %far.1 = (bf16[2048,512]{1,0:T(8,128)(2,1)S(1)}, bf16[32,128,512]{2,1,0:T(8,128)(2,1)}, f32[8,512]{1,0:T(8,128)S(1)}) custom-call(s32[32]{0:T(128)S(1)} %get-tuple-element.48.serve, s32[32]{0:T(128)S(1)} %select_reduce_fusion.1.order, s32[9]{0:T(128)S(1)} %convert_reduce_fusion.1.ready, bf16[2048,512]{1,0:T(8,128)(2,1)S(1)} %get-tuple-element.30.begun, ...), custom_call_target="tpu_custom_call" | custom-call | tf_op jit(solution)/shard_map/far/pallas_call | solution.py:300
  62.8 4.9 %all-to-all-start.1 = ((bf16[32,128,512]{2,1,0:T(8,128)(2,1)}), bf16[32,128,512]{2,1,0:T(8,128)(2,1)}, u32[]{:S(2)}, u32[]{:S(2)}) async-start(bf16[32,128,512]{2,1,0:T(8,128)(2,1)} %get-tuple-element.32), calls=%async_computation.1 | async-start | bytes 8388608 | tf_op jit(solution)/shard_map/all_to_all | solution.py:276
  69.0 57.2 %all-to-all-done.1.fetched = bf16[32,128,512]{2,1,0:T(8,128)(2,1)} async-done(((bf16[32,128,512]{2,1,0:T(8,128)(2,1)}), bf16[32,128,512]{2,1,0:T(8,128)(2,1)}, u32[]{:S(2)}, u32[]{:S(2)}) %all-to-all-start.1) | async-done | bytes 4194336 | tf_op jit(solution)/shard_map/all_to_all | solution.py:276
  126.1 4.0 %scores.1 = (bf16[16,256,128]{2,1,0:T(8,128)(2,1)S(1)}, f32[32,128]{1,0:T(8,128)S(1)}) custom-call(s32[32]{0:T(128)S(1)} %fusion.3.need, s32[16,128]{1,0:T(8,128)S(1)} %subtract_bitcast_fusion.column, bf16[2048,512]{1,0:T(8,128)(2,1)S(1)} %get-tuple-element.31.anchors, bf16[32,128,512]{2,1,0:T(8,128)(2,1)} %all-to-all-done.1.fetched), custom_call_target="tpu_custom_call" | custom-call | tf_op jit(solution)/shard_map/scores/pallas_call | solution.py:300
  130.2 11.0 %collective-permute-start.4 = (f32[32,128]{1,0:T(8,128)S(1)}, f32[32,128]{1,0:T(8,128)S(1)}, u32[]{:S(2)}, u32[]{:S(2)}) collective-permute-start(f32[32,128]{1,0:T(8,128)S(1)} %get-tuple-element.33.r_0_), channel_id=1, source_target_pairs={{0,5},{1,4},{4,1},{5,0},{2,7},{3,6},{6,3},{7,2},{8,13},{9,12},{12,... | collective-permute-start | bytes 49160 | tf_op jit(solution)/shard_map/ppermute | solution.py:272
  142.0 5.1 %mix.1 = (bf16[2048,512]{1,0:T(8,128)(2,1)S(1)}, bf16[2048,512]{1,0:T(8,128)(2,1)S(1)}) custom-call(s32[32]{0:T(128)S(1)} %fusion.3.need, s32[16,128]{1,0:T(8,128)S(1)} %subtract_bitcast_fusion.column, bf16[16,256,128]{2,1,0:T(8,128)(2,1)S(1)} %get-tuple-element.36.weights, bf16[32,128,512]{2,1,0:T(8,128)(2,1)} %all-to-all-done.1.fetched), custom_call_target="tpu_custom_call" | custom-call | tf_op jit(solution)/shard_map/mix/pallas_call | solution.py:300
  147.1 2.1 shares.1
  149.7 1.6 across.1
  151.3 1.6 beside.1
  153.5 2.0 collective-permute-start.11
  155.5 1.6 own.1.a
  157.2 10.5 %collective-permute-done.11.c = bf16[512,512]{1,0:T(8,128)(2,1)S(1)} collective-permute-done((bf16[512,512]{1,0:T(8,128)(2,1)S(1)}, bf16[512,512]{1,0:T(8,128)(2,1)S(1)}, u32[]{:S(2)}, u32[]{:S(2)}) %collective-permute-start.11) | collective-permute-done | bytes 524320 | tf_op jit(solution)/shard_map/ppermute | solution.py:272
  167.7 2.1 back.1
  169.8 4.6 %all-to-all-start.2 = ((bf16[128,8,512]{2,1,0:T(8,128)(2,1)}), bf16[128,8,512]{2,1,0:T(8,128)(2,1)S(1)}, u32[]{:S(2)}, u32[]{:S(2)}) async-start(bf16[128,8,512]{2,1,0:T(8,128)(2,1)} %bitcast.25), calls=%async_computation.2 | async-start | bytes 2097152 | tf_op jit(solution)/shard_map/all_to_all | solution.py:276
  174.4 1.7 stripes.1
  177.1 16.1 %all-to-all-done.2 = bf16[128,8,512]{2,1,0:T(8,128)(2,1)S(1)} async-done(((bf16[128,8,512]{2,1,0:T(8,128)(2,1)}), bf16[128,8,512]{2,1,0:T(8,128)(2,1)S(1)}, u32[]{:S(2)}, u32[]{:S(2)}) %all-to-all-start.2) | async-done | bytes 1048608 | tf_op jit(solution)/shard_map/all_to_all | solution.py:276
  193.1 1.2 copy-done.4
  194.4 1.1 unit_grad.1.grad
  195.7 1.8 collective-permute-done.12.partner
  197.5 2.3 %head_grad.1 = bf16[1024,512]{1,0:T(8,128)(2,1)} custom-call(bf16[1024,512]{1,0:T(8,128)(2,1)S(1)} %copy-done.6, bf16[1024,512]{1,0:T(8,128)(2,1)S(1)} %collective-permute-done.8.theirs, bf16[512,512]{1,0:T(8,128)(2,1)S(1)} %unit_grad.1.grad, bf16[512,512]{1,0:T(8,128)(2,1)S(1)} %collective-permute-done.12.partner), custom_call_target="tpu_custom_call" | custom-call | tf_op jit(solution)/shard_map/head_grad/pallas_call | solution.py:300
  199.7 4.9 %all-to-all-start.3 = ((bf16[64,16,512]{2,1,0:T(8,128)(2,1)}), bf16[64,16,512]{2,1,0:T(8,128)(2,1)S(1)}, u32[]{:S(2)}, u32[]{:S(2)}) async-start(bf16[64,16,512]{2,1,0:T(8,128)(2,1)} %bitcast.24), calls=%async_computation.3 | async-start | bytes 2097152 | tf_op jit(solution)/shard_map/all_to_all | solution.py:276
  204.6 3.2 %collective-permute-start.7 = (f32[2048]{0:T(1024)S(1)}, f32[2048]{0:T(1024)S(1)}, u32[]{:S(2)}, u32[]{:S(2)}) collective-permute-start(f32[2048]{0:T(1024)S(1)} %fusion.9), channel_id=1, source_target_pairs={{0,2},{2,0},{1,3},{3,1},{4,6},{6,4},{5,7},{7,5},{8,10},{10,8},{9,1... | collective-permute-start | bytes 24584 | tf_op jit(solution)/shard_map/ppermute | solution.py:272
  207.8 7.6 %collective-permute-done.7 = f32[2048]{0:T(1024)S(1)} collective-permute-done((f32[2048]{0:T(1024)S(1)}, f32[2048]{0:T(1024)S(1)}, u32[]{:S(2)}, u32[]{:S(2)}) %collective-permute-start.7) | collective-permute-done | bytes 8224 | tf_op jit(solution)/shard_map/ppermute | solution.py:272
  216.1 7.8 %all-to-all-done.3.parts = bf16[64,16,512]{2,1,0:T(8,128)(2,1)S(1)} async-done(((bf16[64,16,512]{2,1,0:T(8,128)(2,1)}), bf16[64,16,512]{2,1,0:T(8,128)(2,1)S(1)}, u32[]{:S(2)}, u32[]{:S(2)}) %all-to-all-start.3) | async-done | bytes 1048608 | tf_op jit(solution)/shard_map/all_to_all | solution.py:276
  (54 shorter events, 8.8 us)
Async XLA Ops:
  0.6 1.6 copy-start
  2.2 1.6 copy-start.2
  3.8 0.7 copy-start.7
  6.9 33.7 %copy-start.3 = (f32[512,512]{1,0:T(8,128)}, f32[512,512]{1,0:T(8,128)S(1)}, u32[]{:S(2)}) copy-start(f32[512,512]{1,0:T(8,128)S(1)} %get-tuple-element.46.unit) | copy-start | bytes 3145732
  6.9 34.4 %copy-start.8 = (s32[512,8]{0,1:T(8,128)S(1)}, s32[512,8]{0,1:T(8,128)}, u32[]{:S(2)}) copy-start(s32[512,8]{0,1:T(8,128)} %param.8) | copy-start | bytes 49156
  40.5 2.0 collective-permute-start.1
  40.7 14.6 %collective-permute-start.2 = (bf16[528,512]{1,0:T(8,128)(2,1)S(1)}, bf16[528,512]{1,0:T(8,128)(2,1)S(1)}, u32[]{:S(2)}, u32[]{:S(2)}) collective-permute-start(bf16[528,512]{1,0:T(8,128)(2,1)S(1)} %get-tuple-element.26.own), channel_id=1, source_target_pairs={{0,1},{1,0},{2,3},{3,2},{4,5},{5,4},{6,7},{7,6},{8,9},{9,8},{10,11... | collective-permute-start | bytes 1622024 | tf_op jit(solution)/shard_map/ppermute | solution.py:272
  55.3 3.0 %collective-permute-start.3 = (bf16[528,512]{1,0:T(8,128)(2,1)S(1)}, bf16[528,512]{1,0:T(8,128)(2,1)S(1)}, u32[]{:S(2)}, u32[]{:S(2)}) collective-permute-start(bf16[528,512]{1,0:T(8,128)(2,1)S(1)} %collective-permute-done.2.across), channel_id=1, source_target_pairs={{0,4},{4,0},{1,5},{5,1},{2,6},{6,2},{3,7},{7,3},{8,12},{12,8},{9,1... | collective-permute-start | bytes 1622024 | tf_op jit(solution)/shard_map/ppermute | solution.py:272
  62.8 4.9 %copy-start.9 = (s32[2048]{0:T(1024)S(1)}, s32[2048]{0:T(1024)}, u32[]{:S(2)}) copy-start(s32[2048]{0:T(1024)} %param.9) | copy-start | bytes 24580
  62.8 63.3 %all-to-all-start.1 = ((bf16[32,128,512]{2,1,0:T(8,128)(2,1)}), bf16[32,128,512]{2,1,0:T(8,128)(2,1)}, u32[]{:S(2)}, u32[]{:S(2)}) async-start(bf16[32,128,512]{2,1,0:T(8,128)(2,1)} %get-tuple-element.32), calls=%async_computation.1 | async-start | bytes 8388608 | tf_op jit(solution)/shard_map/all_to_all | solution.py:276
  67.7 1.3 collective-permute-start
  130.2 16.9 %collective-permute-start.4 = (f32[32,128]{1,0:T(8,128)S(1)}, f32[32,128]{1,0:T(8,128)S(1)}, u32[]{:S(2)}, u32[]{:S(2)}) collective-permute-start(f32[32,128]{1,0:T(8,128)S(1)} %get-tuple-element.33.r_0_), channel_id=1, source_target_pairs={{0,5},{1,4},{4,1},{5,0},{2,7},{3,6},{6,3},{7,2},{8,13},{9,12},{12,... | collective-permute-start | bytes 49160 | tf_op jit(solution)/shard_map/ppermute | solution.py:272
  141.2 6.0 %collective-permute-start.5 = (f32[32,128]{1,0:T(8,128)S(1)}, f32[32,128]{1,0:T(8,128)S(1)}, u32[]{:S(2)}, u32[]{:S(2)}) collective-permute-start(f32[32,128]{1,0:T(8,128)S(1)} %get-tuple-element.33.r_0_), channel_id=1, source_target_pairs={{0,4},{4,0},{1,5},{5,1},{2,6},{6,2},{3,7},{7,3},{8,12},{12,8},{9,1... | collective-permute-start | bytes 49160 | tf_op jit(solution)/shard_map/ppermute | solution.py:272
  141.9 5.2 %collective-permute-start.6 = (f32[32,128]{1,0:T(8,128)S(1)}, f32[32,128]{1,0:T(8,128)S(1)}, u32[]{:S(2)}, u32[]{:S(2)}) collective-permute-start(f32[32,128]{1,0:T(8,128)S(1)} %get-tuple-element.33.r_0_), channel_id=1, source_target_pairs={{0,1},{1,0},{2,3},{3,2},{4,5},{5,4},{6,7},{7,6},{8,9},{9,8},{10,11... | collective-permute-start | bytes 49160 | tf_op jit(solution)/shard_map/ppermute | solution.py:272
  149.3 4.1 %collective-permute-start.10 = (bf16[512,512]{1,0:T(8,128)(2,1)S(1)}, bf16[512,512]{1,0:T(8,128)(2,1)S(1)}, u32[]{:S(2)}, u32[]{:S(2)}) collective-permute-start(bf16[512,512]{1,0:T(8,128)(2,1)S(1)} %get-tuple-element.43), channel_id=1, source_target_pairs={{0,4},{4,0},{1,5},{5,1},{2,6},{6,2},{3,7},{7,3},{8,12},{12,8},{9,1... | collective-permute-start | bytes 1572872 | tf_op jit(solution)/shard_map/ppermute | solution.py:272
  152.9 4.2 %collective-permute-start.9 = (bf16[512,512]{1,0:T(8,128)(2,1)S(1)}, bf16[512,512]{1,0:T(8,128)(2,1)S(1)}, u32[]{:S(2)}, u32[]{:S(2)}) collective-permute-start(bf16[512,512]{1,0:T(8,128)(2,1)S(1)} %beside.1), channel_id=1, source_target_pairs={{0,4},{4,0},{1,5},{5,1},{2,6},{6,2},{3,7},{7,3},{8,12},{12,8},{9,1... | collective-permute-start | bytes 1572872 | tf_op jit(solution)/shard_map/ppermute | solution.py:272
  153.5 14.2 %collective-permute-start.11 = (bf16[512,512]{1,0:T(8,128)(2,1)S(1)}, bf16[512,512]{1,0:T(8,128)(2,1)S(1)}, u32[]{:S(2)}, u32[]{:S(2)}) collective-permute-start(bf16[512,512]{1,0:T(8,128)(2,1)S(1)} %add_convert_fusion), channel_id=1, source_target_pairs={{0,1},{1,0},{2,3},{3,2},{4,5},{5,4},{6,7},{7,6},{8,9},{9,8},{10,11... | collective-permute-start | bytes 1572872 | tf_op jit(solution)/shard_map/ppermute | solution.py:272
  167.7 6.7 %copy-start.1 = (bf16[512,2048]{1,0:T(8,128)(2,1)S(1)}, bf16[512,2048]{1,0:T(8,128)(2,1)}, u32[]{:S(2)}) copy-start(bf16[512,2048]{1,0:T(8,128)(2,1)} %feat.1) | copy-start | bytes 6291460
  169.8 23.4 %all-to-all-start.2 = ((bf16[128,8,512]{2,1,0:T(8,128)(2,1)}), bf16[128,8,512]{2,1,0:T(8,128)(2,1)S(1)}, u32[]{:S(2)}, u32[]{:S(2)}) async-start(bf16[128,8,512]{2,1,0:T(8,128)(2,1)} %bitcast.25), calls=%async_computation.2 | async-start | bytes 2097152 | tf_op jit(solution)/shard_map/all_to_all | solution.py:276
  176.1 1.0 copy-start.5
  177.1 18.6 %collective-permute-start.8 = (bf16[1024,512]{1,0:T(8,128)(2,1)}, bf16[1024,512]{1,0:T(8,128)(2,1)S(1)}, u32[]{:S(2)}, u32[]{:S(2)}) collective-permute-start(bf16[1024,512]{1,0:T(8,128)(2,1)} %get-tuple-element.35), channel_id=1, source_target_pairs={{0,4},{4,0},{1,5},{5,1},{2,6},{6,2},{3,7},{7,3},{8,12},{12,8},{9,1... | collective-permute-start | bytes 3145736 | tf_op jit(solution)/shard_map/ppermute | solution.py:272
  193.1 1.2 copy-start.4
  194.4 3.1 %copy-start.6 = (bf16[1024,512]{1,0:T(8,128)(2,1)S(1)}, bf16[1024,512]{1,0:T(8,128)(2,1)}, u32[]{:S(2)}) copy-start(bf16[1024,512]{1,0:T(8,128)(2,1)} %copy-done.5) | copy-start | bytes 3145732
  195.5 2.0 collective-permute-start.12
  199.7 24.1 %all-to-all-start.3 = ((bf16[64,16,512]{2,1,0:T(8,128)(2,1)}), bf16[64,16,512]{2,1,0:T(8,128)(2,1)S(1)}, u32[]{:S(2)}, u32[]{:S(2)}) async-start(bf16[64,16,512]{2,1,0:T(8,128)(2,1)} %bitcast.24), calls=%async_computation.3 | async-start | bytes 2097152 | tf_op jit(solution)/shard_map/all_to_all | solution.py:276
  204.6 10.8 %collective-permute-start.7 = (f32[2048]{0:T(1024)S(1)}, f32[2048]{0:T(1024)S(1)}, u32[]{:S(2)}, u32[]{:S(2)}) collective-permute-start(f32[2048]{0:T(1024)S(1)} %fusion.9), channel_id=1, source_target_pairs={{0,2},{2,0},{1,3},{3,1},{4,6},{6,4},{5,7},{7,5},{8,10},{10,8},{9,1... | collective-permute-start | bytes 24584 | tf_op jit(solution)/shard_map/ppermute | solution.py:272

commit v5 on v4

--- a/solution.py
+++ b/solution.py
@@ -50,15 +50,20 @@
     return wide.T[:, 0:1].astype(I32)
 
 
-def project_kernel(owner_slots, owners, cap, slot, feat, head, send, unit, norm, place):
+def project_kernel(
+    owner_slots, owners, cap, slot, feat_in, head_in, send, unit, norm, place, feat, head, sems
+):
     n = feat.shape[0]
-    e = head.shape[1]
-    projected = dot(feat[...], head[...])
-    length = jnp.sqrt(jnp.sum(projected * projected, axis=1, keepdims=True) + norm_eps)
-    rows = projected / length
-    unit[...] = rows
-    norm[...] = jnp.broadcast_to(length, norm.shape)
-    descriptor = rows.astype(BF)
+    width, e = head.shape
+    parts = 4
+    copies = []
+    for k in range(parts):
+        at = pl.ds(k * (width // parts), width // parts)
+        copies.append(pltpu.make_async_copy(head_in.at[at, :], head.at[at, :], sems.at[k]))
+        at = pl.ds(k * (n // parts), n // parts)
+        copies.append(pltpu.make_async_copy(feat_in.at[at, :], feat.at[at, :], sems.at[parts + k]))
+    for c in copies:
+        c.start()
     s = slot[...]
     owner = s // owner_slots
     local = s - owner * owner_slots
@@ -66,16 +71,24 @@
     before = dot(hot(mine), hot(iota((n, n), 0) < iota((n, n), 1)))
     rank = jnp.sum(jnp.where(mine, before, 0.0), axis=0, keepdims=True).astype(I32)
     member = rank & (REPS - 1)
-    device = (owner // 2) * 8 + (member // 2) * 4 + (owner & 1) * 2 + (member & 1)
+    slab = member & 1
+    device = (owner // 2) * 8 + (member // 2) * 4 + slab * 2 + ((owner & 1) ^ slab)
     p = device * cap + rank // REPS
     place[...] = jnp.broadcast_to(p.astype(F32), place.shape)
     scatter = hot(iota((send.shape[0], n), 0) == p)
-    send[:, :e] = dot(scatter, descriptor).astype(BF)
     high = local // BR
     low = local - high * BR
     row = iota((BR, n), 0)
     tags = jnp.where(row == 0, high, jnp.where(row == 1, low, jnp.where(row == 2, 1, 0)))
     send[:, e:] = dot(scatter, tags.astype(F32).astype(BF), 1, 1).astype(BF)
+    for c in copies:
+        c.wait()
+    projected = dot(feat[...], head[...])
+    length = jnp.sqrt(jnp.sum(projected * projected, axis=1, keepdims=True) + norm_eps)
+    rows = projected / length
+    unit[...] = rows
+    norm[...] = jnp.broadcast_to(length, norm.shape)
+    send[:, :e] = dot(scatter, rows.astype(BF)).astype(BF)
 
 
 def stripes_kernel(core, feat, mine, other):
@@ -277,13 +290,14 @@
 
 
 def shards(features, head_weight, slot_of_image, candidates, positives):
-    owners_axes = ("zx", "yhi")
+    slab_axes = ("zx", "ylo")
     everyone = ("zx", "core", "yhi", "ylo")
-    dp = lax.axis_size(owners_axes)
-    me = lax.axis_index(owners_axes)
+    dp = lax.axis_size(slab_axes)
+    slab = lax.axis_index("yhi")
+    me = lax.axis_index(slab_axes) ^ slab
     core = lax.axis_index("core")
-    member = core * 2 + lax.axis_index("ylo")
-    home = core == lax.axis_index("yhi")
+    member = core * 2 + slab
+    home = core == (me & 1)
     n, width = features.shape
     e = head_weight.shape[1]
     devices = dp * REPS
@@ -305,7 +319,17 @@
         lambda *r: project_kernel(owner_slots, dp, cap, *r),
         "project",
         (sds((count, e + BR), BF), sds((n, e), F32), sds((n, BR), F32), sds((8, n), F32)),
-        (slot_of_image.reshape(1, n), features, head_weight),
+        (
+            slot_of_image.reshape(1, n),
+            pltpu.with_memory_space_constraint(features, pltpu.HBM),
+            pltpu.with_memory_space_constraint(head_weight, pltpu.HBM),
+        ),
+        in_specs=[vmem, far_away, far_away],
+        scratch_shapes=[
+            pltpu.VMEM((n, width), BF),
+            pltpu.VMEM((width, e), BF),
+            pltpu.SemaphoreType.DMA((8,)),
+        ],
     )
     got = exchange(send.reshape(devices, cap, e + BR), everyone).reshape(count, e + BR)
 
@@ -318,26 +342,28 @@
     )
     theirs = swap(other)
 
-    packed, back_place = call(
-        compact_kernel, "compact", (sds((n + 16, e), BF), sds((8, count), F32)), (got,)
-    )
-    beside = swap(packed)
-    across = swap(packed, ("ylo",))
-
     table = candidates.reshape(dp, blocks, REPS, PAIRS_REP)
     table = lax.dynamic_index_in_dim(table, member, axis=2, keepdims=False)
     table = table.reshape(dp, blocks * PAIRS_REP)
     owner = table // blocks
-    serve = jnp.sum(jnp.where(owner == me, table - owner * blocks, 0), axis=1)
-    need = lax.dynamic_index_in_dim(owner, me, axis=0, keepdims=False)
+    numbers = jnp.arange(dp, dtype=I32)
+    wanted = jnp.sum(jnp.where(owner == me, table - owner * blocks, 0), axis=1)
+    serve = jnp.sum(jnp.where(numbers[None, :] == (numbers ^ slab)[:, None], wanted[None, :], 0), axis=1)
+    need = lax.dynamic_index_in_dim(owner, me, axis=0, keepdims=False) ^ slab
     column = jnp.where(home, positives, swap(positives)).reshape(blocks, BR)
     column = column - member * (PAIRS_REP * BR)
-    numbers = jnp.arange(dp, dtype=I32)
     keys = serve * dp + numbers
     place_of = jnp.sum((keys[None, :] < keys[:, None]).astype(I32), axis=1)
     order = jnp.sum(jnp.where(place_of[None, :] == numbers[:, None], numbers[None, :], 0), axis=1)
     bounds = 2 * jnp.arange(blocks // 2 + 1, dtype=I32)
     ready = jnp.sum((serve[None, :] < bounds[:, None]).astype(I32), axis=1)
+
+    got, serve, order, ready, need = lax.optimization_barrier((got, serve, order, ready, need))
+    packed, back_place = call(
+        compact_kernel, "compact", (sds((n + 16, e), BF), sds((8, count), F32)), (got,)
+    )
+    beside = swap(packed)
+    across = swap(packed, ("yhi", "ylo"))
 
     whole = sds((owner_slots, e), BF)
     ids_shape = sds((8, n), F32)
@@ -360,7 +386,7 @@
         out_specs=(vmem, pl.BlockSpec(memory_space=pltpu.HBM), vmem),
         scratch_shapes=[pltpu.SemaphoreType.DMA((dp,))],
     )
-    fetched = exchange(served, owners_axes)
+    fetched = exchange(served, slab_axes)
     weights, stats = call(
         scores_kernel,
         "scores",
@@ -368,7 +394,7 @@
         (need, column, anchors, fetched),
         in_specs=[smem] + [vmem] * 3,
     )
-    spread = (stats, swap(stats), swap(stats, ("ylo",)), swap(stats, ("core", "ylo")))
+    spread = (stats, swap(stats), swap(stats, ("yhi", "ylo")), swap(stats, ("core", "yhi", "ylo")))
     pulled, partner = call(
         mix_kernel,
         "mix",
@@ -387,7 +413,7 @@
         return call(pick_kernel, name, sds((n, e), BF), (share, ids))
 
     for_across = pick("across", slots_across).astype(F32) + swap(for_corner).astype(F32)
-    from_across = swap(for_across.astype(BF), ("ylo",))
+    from_across = swap(for_across.astype(BF), ("yhi", "ylo"))
     from_beside = swap(pick("beside", slots[1]))
     back = call(
         back_kernel,
@@ -401,7 +427,7 @@
     rest, matching = both[:blocks], both[blocks:]
     total = rest + jnp.exp(matching - 1.0 / logit_sharpness)
     loss = (jnp.log(total) + 1.0 / logit_sharpness - matching).reshape(owner_slots)
-    anchor_row_loss = jnp.where(home, loss, swap(loss, ("yhi",)))
+    anchor_row_loss = jnp.where(home, loss, swap(loss, ("ylo",)))
 
     grad = call(
         unit_grad_kernel, "unit_grad", sds((n, e), BF), (returned, place, unit, norm)

time: 226 us -> 228 us (level)
  blocking collectives: 32.5 us -> 0 us
  waiting for transfers between devices: 112 us -> 138 us
  starting transfers between devices: 33.4 us -> 41.1 us
  Pallas kernels: 38.3 us -> 41.5 us
    all_to_all x1 -> x0, blocking collectives: 32.5 us -> none  [exchange(): return lax.all_to_all(x, axes, 0, 0, tiled=True)]
    all_to_all x3 -> x4, waiting for transfers between devices: 81 us -> 104 us  [exchange(): return lax.all_to_all(x, axes, 0, 0, tiled=True)]
    all_to_all x3 -> x4, starting transfers between devices: 14.4 us -> 33 us  [exchange(): return lax.all_to_all(x, axes, 0, 0, tiled=True)]
    ppermute x13, starting transfers between devices: 19.1 us -> 8.06 us  [swap(): return lax.ppermute(x, axes, [(i, size - 1 - i) for i in range(size)])]
    pallas_call x16, Pallas kernels: 38.3 us -> 41.5 us  [call(): pl.pallas_call(kernel, out_shape=shapes, compiler_params=params(), name=n...]
    ppermute x13, waiting for transfers between devices: 30.7 us -> 33.6 us  [swap(): return lax.ppermute(x, axes, [(i, size - 1 - i) for i in range(size)])]
    unnamed x20 -> x16, local copies, waits for them, and re-layouts: 6.07 us -> 3.94 us
  transfers between devices with their start and end apart: 16 -> 17, of which waited for: 9 -> 10; matrix products, arithmetic and copies ran while one was open for 1% -> 1% of each run, Pallas kernels for 8% -> 8%
where the time goes in v5:
time: 228 us; the launch traced here: 227 us
  waiting for transfers between devices  138 us (61%)
  Pallas kernels  41.5 us (18%)
  starting transfers between devices  41.1 us (18%)
  local copies, waits for them, and re-layouts  4.11 us (2%)
    all_to_all x4, waiting for transfers between devices, exchange(): return lax.all_to_all(x, axes, 0, 0, tiled=True)  104 us
    pallas_call x16, Pallas kernels, call(): pl.pallas_call(kernel, out_shape=shapes, compiler_params=params(), name=n...  41.5 us
    ppermute x13, waiting for transfers between devices, swap(): return lax.ppermute(x, axes, [(i, size - 1 - i) for i in range(size)])  33.6 us
    all_to_all x4, starting transfers between devices, exchange(): return lax.all_to_all(x, axes, 0, 0, tiled=True)  33 us
    ppermute x13, starting transfers between devices, swap(): return lax.ppermute(x, axes, [(i, size - 1 - i) for i in range(size)])  8.06 us
  transfers between devices with their start and end apart: 17, of which 10 were waited for; matrix products, arithmetic and copies ran while one was open for 1% of the time, Pallas kernels for 8%

profile of v5, /device:TPU:0, one launch (start us, length us, event | category | flops | bytes accessed | tf_op | source)
XLA Modules:
  0.0 227.3 jit_solution(4345005126294850442)
XLA Ops:
  1.3 5.5 %project.1 = (bf16[1024,640]{1,0:T(8,128)(2,1)}, f32[512,512]{1,0:T(8,128)S(1)}, f32[512,128]{1,0:T(8,128)S(1)}, f32[8,512]{1,0:T(8,128)S(1)}) custom-call(s32[1,512]{1,0:T(1,128)S(1)} %bitcast.22, bf16[512,2048]{1,0:T(8,128)(2,1)} %feat.1, bf16[2048,512]{1,0:T(8,128)(2,1)} %r_2_.1), custom_call_target="tpu_custom_call" | custom-call | tf_op jit(solution)/shard_map/project/pallas_call | solution.py:314
  6.8 1.0 copy-done.1
  7.9 11.1 %all-to-all-start = ((bf16[128,8,640]{2,1,0:T(8,128)(2,1)}), bf16[128,8,640]{2,1,0:T(8,128)(2,1)S(1)}, u32[]{:S(2)}, u32[]{:S(2)}) async-start(bf16[128,8,640]{2,1,0:T(8,128)(2,1)} %bitcast.1), calls=%async_computation | async-start | bytes 2621440 | tf_op jit(solution)/shard_map/all_to_all | solution.py:289
  20.2 20.4 %all-to-all-done = bf16[128,8,640]{2,1,0:T(8,128)(2,1)S(1)} async-done(((bf16[128,8,640]{2,1,0:T(8,128)(2,1)}), bf16[128,8,640]{2,1,0:T(8,128)(2,1)S(1)}, u32[]{:S(2)}, u32[]{:S(2)}) %all-to-all-start) | async-done | bytes 1310752 | tf_op jit(solution)/shard_map/all_to_all | solution.py:289
  40.6 1.2 compact.1
  41.9 1.1 collective-permute-start.2
  43.7 3.6 %near.1 = (bf16[2048,512]{1,0:T(8,128)(2,1)S(1)}, f32[2,8,512]{2,1,0:T(8,128)S(1)}) custom-call(bf16[528,512]{1,0:T(8,128)(2,1)S(1)} %get-tuple-element.36.own, bf16[528,512]{1,0:T(8,128)(2,1)S(1)} %collective-permute-done.1.beside), custom_call_target="tpu_custom_call" | custom-call | flops 4000000000 | bytes 4000000 | tf_op jit(solution)/shard_map/near/pallas_call | solution.py:314
  47.3 10.3 %collective-permute-done.2.across = bf16[528,512]{1,0:T(8,128)(2,1)S(1)} collective-permute-done((bf16[528,512]{1,0:T(8,128)(2,1)S(1)}, bf16[528,512]{1,0:T(8,128)(2,1)S(1)}, u32[]{:S(2)}, u32[]{:S(2)}) %collective-permute-start.2) | collective-permute-done | bytes 540704 | tf_op jit(solution)/shard_map/ppermute | solution.py:285
  57.7 2.5 %middle.1 = (bf16[2048,512]{1,0:T(8,128)(2,1)S(1)}, f32[8,512]{1,0:T(8,128)S(1)}) custom-call(bf16[2048,512]{1,0:T(8,128)(2,1)S(1)} %get-tuple-element.38.begun, bf16[528,512]{1,0:T(8,128)(2,1)S(1)} %collective-permute-done.2.across), custom_call_target="tpu_custom_call" | custom-call | tf_op jit(solution)/shard_map/middle/pallas_call | solution.py:314
  60.2 4.6 %far.1 = (bf16[2048,512]{1,0:T(8,128)(2,1)S(1)}, bf16[32,128,512]{2,1,0:T(8,128)(2,1)}, f32[8,512]{1,0:T(8,128)S(1)}) custom-call(s32[32]{0:T(128)S(1)} %select_reduce_fusion.2.serve, s32[32]{0:T(128)S(1)} %select_reduce_fusion.1.order, s32[9]{0:T(128)S(1)} %convert_reduce_fusion.1.ready, bf16[2048,512]{1,0:T(8,128)(2,1)S(1)} %get-tuple-element.40.begun, ...), custom_call_target="tpu_custom_call" | custom-call | tf_op jit(solution)/shard_map/far/pallas_call | solution.py:314
  64.9 4.9 %all-to-all-start.1 = ((bf16[32,128,512]{2,1,0:T(8,128)(2,1)}), bf16[32,128,512]{2,1,0:T(8,128)(2,1)}, u32[]{:S(2)}, u32[]{:S(2)}) async-start(bf16[32,128,512]{2,1,0:T(8,128)(2,1)} %get-tuple-element.42), calls=%async_computation.1 | async-start | bytes 8388608 | tf_op jit(solution)/shard_map/all_to_all | solution.py:289
  71.2 57.5 %all-to-all-done.1.fetched = bf16[32,128,512]{2,1,0:T(8,128)(2,1)} async-done(((bf16[32,128,512]{2,1,0:T(8,128)(2,1)}), bf16[32,128,512]{2,1,0:T(8,128)(2,1)}, u32[]{:S(2)}, u32[]{:S(2)}) %all-to-all-start.1) | async-done | bytes 4194336 | tf_op jit(solution)/shard_map/all_to_all | solution.py:289
  128.7 4.0 %scores.1 = (bf16[16,256,128]{2,1,0:T(8,128)(2,1)S(1)}, f32[32,128]{1,0:T(8,128)S(1)}) custom-call(s32[32]{0:T(128)S(1)} %fusion.4.need, s32[16,128]{1,0:T(8,128)S(1)} %subtract_bitcast_fusion.column, bf16[2048,512]{1,0:T(8,128)(2,1)S(1)} %get-tuple-element.41.anchors, bf16[32,128,512]{2,1,0:T(8,128)(2,1)} %all-to-all-done.1.fetched), custom_call_target="tpu_custom_call" | custom-call | tf_op jit(solution)/shard_map/scores/pallas_call | solution.py:314
  132.9 3.2 %collective-permute-start.6 = (f32[32,128]{1,0:T(8,128)S(1)}, f32[32,128]{1,0:T(8,128)S(1)}, u32[]{:S(2)}, u32[]{:S(2)}) collective-permute-start(f32[32,128]{1,0:T(8,128)S(1)} %get-tuple-element.43.r_0_), channel_id=1, source_target_pairs={{0,3},{1,2},{2,1},{3,0},{4,7},{5,6},{6,5},{7,4},{8,11},{9,10},{10,... | collective-permute-start | bytes 49160 | tf_op jit(solution)/shard_map/ppermute | solution.py:285
  136.1 5.1 %mix.1 = (bf16[2048,512]{1,0:T(8,128)(2,1)S(1)}, bf16[2048,512]{1,0:T(8,128)(2,1)S(1)}) custom-call(s32[32]{0:T(128)S(1)} %fusion.4.need, s32[16,128]{1,0:T(8,128)S(1)} %subtract_bitcast_fusion.column, bf16[16,256,128]{2,1,0:T(8,128)(2,1)S(1)} %get-tuple-element.46.weights, bf16[32,128,512]{2,1,0:T(8,128)(2,1)} %all-to-all-done.1.fetched), custom_call_target="tpu_custom_call" | custom-call | tf_op jit(solution)/shard_map/mix/pallas_call | solution.py:314
  141.3 2.1 shares.1
  143.7 1.6 across.1
  145.3 1.6 beside.1
  147.8 1.6 own.1.a
  149.5 13.4 %collective-permute-done.11.c = bf16[512,512]{1,0:T(8,128)(2,1)S(1)} collective-permute-done((bf16[512,512]{1,0:T(8,128)(2,1)S(1)}, bf16[512,512]{1,0:T(8,128)(2,1)S(1)}, u32[]{:S(2)}, u32[]{:S(2)}) %collective-permute-start.11) | collective-permute-done | bytes 524320 | tf_op jit(solution)/shard_map/ppermute | solution.py:285
  162.8 2.1 back.1
  164.9 12.1 %all-to-all-start.2 = ((bf16[128,8,512]{2,1,0:T(8,128)(2,1)}), bf16[128,8,512]{2,1,0:T(8,128)(2,1)S(1)}, u32[]{:S(2)}, u32[]{:S(2)}) async-start(bf16[128,8,512]{2,1,0:T(8,128)(2,1)} %bitcast.24), calls=%async_computation.2 | async-start | bytes 2097152 | tf_op jit(solution)/shard_map/all_to_all | solution.py:289
  177.0 1.7 stripes.1
  179.7 16.1 %all-to-all-done.2 = bf16[128,8,512]{2,1,0:T(8,128)(2,1)S(1)} async-done(((bf16[128,8,512]{2,1,0:T(8,128)(2,1)}), bf16[128,8,512]{2,1,0:T(8,128)(2,1)S(1)}, u32[]{:S(2)}, u32[]{:S(2)}) %all-to-all-start.2) | async-done | bytes 1048608 | tf_op jit(solution)/shard_map/all_to_all | solution.py:289
  195.8 1.2 copy-done.2
  197.0 1.1 unit_grad.1.grad
  198.3 1.8 collective-permute-done.12.partner
  200.1 2.3 head_grad.1
  202.4 4.9 %all-to-all-start.3 = ((bf16[64,16,512]{2,1,0:T(8,128)(2,1)}), bf16[64,16,512]{2,1,0:T(8,128)(2,1)S(1)}, u32[]{:S(2)}, u32[]{:S(2)}) async-start(bf16[64,16,512]{2,1,0:T(8,128)(2,1)} %bitcast.23), calls=%async_computation.3 | async-start | bytes 2097152 | tf_op jit(solution)/shard_map/all_to_all | solution.py:289
  207.3 1.6 collective-permute-start.7
  208.9 6.6 %collective-permute-done.7 = f32[2048]{0:T(1024)S(1)} collective-permute-done((f32[2048]{0:T(1024)S(1)}, f32[2048]{0:T(1024)S(1)}, u32[]{:S(2)}, u32[]{:S(2)}) %collective-permute-start.7) | collective-permute-done | bytes 8224 | tf_op jit(solution)/shard_map/ppermute | solution.py:285
  216.2 10.3 %all-to-all-done.3.parts = bf16[64,16,512]{2,1,0:T(8,128)(2,1)S(1)} async-done(((bf16[64,16,512]{2,1,0:T(8,128)(2,1)}), bf16[64,16,512]{2,1,0:T(8,128)(2,1)S(1)}, u32[]{:S(2)}, u32[]{:S(2)}) %all-to-all-start.3) | async-done | bytes 1048608 | tf_op jit(solution)/shard_map/all_to_all | solution.py:289
  (53 shorter events, 7.9 us)
Async XLA Ops:
  0.6 0.7 copy-start.5
  6.8 1.1 copy-start.1
  7.9 11.2 %copy-start.6 = (s32[512,8]{0,1:T(8,128)S(1)}, s32[512,8]{0,1:T(8,128)}, u32[]{:S(2)}) copy-start(s32[512,8]{0,1:T(8,128)} %param.8) | copy-start | bytes 49156
  7.9 32.7 %all-to-all-start = ((bf16[128,8,640]{2,1,0:T(8,128)(2,1)}), bf16[128,8,640]{2,1,0:T(8,128)(2,1)S(1)}, u32[]{:S(2)}, u32[]{:S(2)}) async-start(bf16[128,8,640]{2,1,0:T(8,128)(2,1)} %bitcast.1), calls=%async_computation | async-start | bytes 2621440 | tf_op jit(solution)/shard_map/all_to_all | solution.py:289
  41.7 2.0 collective-permute-start.1
  41.9 15.8 %collective-permute-start.2 = (bf16[528,512]{1,0:T(8,128)(2,1)S(1)}, bf16[528,512]{1,0:T(8,128)(2,1)S(1)}, u32[]{:S(2)}, u32[]{:S(2)}) collective-permute-start(bf16[528,512]{1,0:T(8,128)(2,1)S(1)} %get-tuple-element.36.own), channel_id=1, source_target_pairs={{0,3},{1,2},{2,1},{3,0},{4,7},{5,6},{6,5},{7,4},{8,11},{9,10},{10,... | collective-permute-start | bytes 1622024 | tf_op jit(solution)/shard_map/ppermute | solution.py:285
  57.7 2.5 %collective-permute-start.3 = (bf16[528,512]{1,0:T(8,128)(2,1)S(1)}, bf16[528,512]{1,0:T(8,128)(2,1)S(1)}, u32[]{:S(2)}, u32[]{:S(2)}) collective-permute-start(bf16[528,512]{1,0:T(8,128)(2,1)S(1)} %collective-permute-done.2.across), channel_id=1, source_target_pairs={{0,4},{4,0},{1,5},{5,1},{2,6},{6,2},{3,7},{7,3},{8,12},{12,8},{9,1... | collective-permute-start | bytes 1622024 | tf_op jit(solution)/shard_map/ppermute | solution.py:285
  64.9 4.9 %copy-start.7 = (s32[2048]{0:T(1024)S(1)}, s32[2048]{0:T(1024)}, u32[]{:S(2)}) copy-start(s32[2048]{0:T(1024)} %param.9) | copy-start | bytes 24580
  64.9 63.8 %all-to-all-start.1 = ((bf16[32,128,512]{2,1,0:T(8,128)(2,1)}), bf16[32,128,512]{2,1,0:T(8,128)(2,1)}, u32[]{:S(2)}, u32[]{:S(2)}) async-start(bf16[32,128,512]{2,1,0:T(8,128)(2,1)} %get-tuple-element.42), calls=%async_computation.1 | async-start | bytes 8388608 | tf_op jit(solution)/shard_map/all_to_all | solution.py:289
  69.8 1.4 collective-permute-start
  132.7 8.6 %collective-permute-start.4 = (f32[32,128]{1,0:T(8,128)S(1)}, f32[32,128]{1,0:T(8,128)S(1)}, u32[]{:S(2)}, u32[]{:S(2)}) collective-permute-start(f32[32,128]{1,0:T(8,128)S(1)} %get-tuple-element.43.r_0_), channel_id=1, source_target_pairs={{0,7},{1,6},{2,5},{3,4},{4,3},{5,2},{6,1},{7,0},{8,15},{9,14},{10,... | collective-permute-start | bytes 49160 | tf_op jit(solution)/shard_map/ppermute | solution.py:285
  132.8 8.5 %collective-permute-start.5 = (f32[32,128]{1,0:T(8,128)S(1)}, f32[32,128]{1,0:T(8,128)S(1)}, u32[]{:S(2)}, u32[]{:S(2)}) collective-permute-start(f32[32,128]{1,0:T(8,128)S(1)} %get-tuple-element.43.r_0_), channel_id=1, source_target_pairs={{0,4},{4,0},{1,5},{5,1},{2,6},{6,2},{3,7},{7,3},{8,12},{12,8},{9,1... | collective-permute-start | bytes 49160 | tf_op jit(solution)/shard_map/ppermute | solution.py:285
  132.9 8.4 %collective-permute-start.6 = (f32[32,128]{1,0:T(8,128)S(1)}, f32[32,128]{1,0:T(8,128)S(1)}, u32[]{:S(2)}, u32[]{:S(2)}) collective-permute-start(f32[32,128]{1,0:T(8,128)S(1)} %get-tuple-element.43.r_0_), channel_id=1, source_target_pairs={{0,3},{1,2},{2,1},{3,0},{4,7},{5,6},{6,5},{7,4},{8,11},{9,10},{10,... | collective-permute-start | bytes 49160 | tf_op jit(solution)/shard_map/ppermute | solution.py:285
  143.4 4.1 %collective-permute-start.10 = (bf16[512,512]{1,0:T(8,128)(2,1)S(1)}, bf16[512,512]{1,0:T(8,128)(2,1)S(1)}, u32[]{:S(2)}, u32[]{:S(2)}) collective-permute-start(bf16[512,512]{1,0:T(8,128)(2,1)S(1)} %get-tuple-element.53), channel_id=1, source_target_pairs={{0,4},{4,0},{1,5},{5,1},{2,6},{6,2},{3,7},{7,3},{8,12},{12,8},{9,1... | collective-permute-start | bytes 1572872 | tf_op jit(solution)/shard_map/ppermute | solution.py:285
  147.0 2.5 %collective-permute-start.9 = (bf16[512,512]{1,0:T(8,128)(2,1)S(1)}, bf16[512,512]{1,0:T(8,128)(2,1)S(1)}, u32[]{:S(2)}, u32[]{:S(2)}) collective-permute-start(bf16[512,512]{1,0:T(8,128)(2,1)S(1)} %beside.1), channel_id=1, source_target_pairs={{0,4},{4,0},{1,5},{5,1},{2,6},{6,2},{3,7},{7,3},{8,12},{12,8},{9,1... | collective-permute-start | bytes 1572872 | tf_op jit(solution)/shard_map/ppermute | solution.py:285
  147.7 15.1 %collective-permute-start.11 = (bf16[512,512]{1,0:T(8,128)(2,1)S(1)}, bf16[512,512]{1,0:T(8,128)(2,1)S(1)}, u32[]{:S(2)}, u32[]{:S(2)}) collective-permute-start(bf16[512,512]{1,0:T(8,128)(2,1)S(1)} %add_convert_fusion), channel_id=1, source_target_pairs={{0,3},{1,2},{2,1},{3,0},{4,7},{5,6},{6,5},{7,4},{8,11},{9,10},{10,... | collective-permute-start | bytes 1572872 | tf_op jit(solution)/shard_map/ppermute | solution.py:285
  162.8 14.2 %copy-start = (bf16[512,2048]{1,0:T(8,128)(2,1)S(1)}, bf16[512,2048]{1,0:T(8,128)(2,1)}, u32[]{:S(2)}) copy-start(bf16[512,2048]{1,0:T(8,128)(2,1)} %feat.1) | copy-start | bytes 6291460
  164.9 30.9 %all-to-all-start.2 = ((bf16[128,8,512]{2,1,0:T(8,128)(2,1)}), bf16[128,8,512]{2,1,0:T(8,128)(2,1)S(1)}, u32[]{:S(2)}, u32[]{:S(2)}) async-start(bf16[128,8,512]{2,1,0:T(8,128)(2,1)} %bitcast.24), calls=%async_computation.2 | async-start | bytes 2097152 | tf_op jit(solution)/shard_map/all_to_all | solution.py:289
  178.7 1.0 copy-start.3
  179.7 18.6 %collective-permute-start.8 = (bf16[1024,512]{1,0:T(8,128)(2,1)}, bf16[1024,512]{1,0:T(8,128)(2,1)S(1)}, u32[]{:S(2)}, u32[]{:S(2)}) collective-permute-start(bf16[1024,512]{1,0:T(8,128)(2,1)} %get-tuple-element.45), channel_id=1, source_target_pairs={{0,4},{4,0},{1,5},{5,1},{2,6},{6,2},{3,7},{7,3},{8,12},{12,8},{9,1... | collective-permute-start | bytes 3145736 | tf_op jit(solution)/shard_map/ppermute | solution.py:285
  195.8 1.2 copy-start.2
  197.0 3.1 %copy-start.4 = (bf16[1024,512]{1,0:T(8,128)(2,1)S(1)}, bf16[1024,512]{1,0:T(8,128)(2,1)}, u32[]{:S(2)}) copy-start(bf16[1024,512]{1,0:T(8,128)(2,1)} %copy-done.3) | copy-start | bytes 3145732
  198.1 2.0 collective-permute-start.12
  202.4 24.1 %all-to-all-start.3 = ((bf16[64,16,512]{2,1,0:T(8,128)(2,1)}), bf16[64,16,512]{2,1,0:T(8,128)(2,1)S(1)}, u32[]{:S(2)}, u32[]{:S(2)}) async-start(bf16[64,16,512]{2,1,0:T(8,128)(2,1)} %bitcast.23), calls=%async_computation.3 | async-start | bytes 2097152 | tf_op jit(solution)/shard_map/all_to_all | solution.py:289
  207.3 8.3 %collective-permute-start.7 = (f32[2048]{0:T(1024)S(1)}, f32[2048]{0:T(1024)S(1)}, u32[]{:S(2)}, u32[]{:S(2)}) collective-permute-start(f32[2048]{0:T(1024)S(1)} %fusion.10), channel_id=1, source_target_pairs={{0,1},{1,0},{2,3},{3,2},{4,5},{5,4},{6,7},{7,6},{8,9},{9,8},{10,11... | collective-permute-start | bytes 24584 | tf_op jit(solution)/shard_map/ppermute | solution.py:285

commit v6 on v5

--- a/solution.py
+++ b/solution.py
@@ -51,17 +51,17 @@
 
 
 def project_kernel(
-    owner_slots, owners, cap, slot, feat_in, head_in, send, unit, norm, place, feat, head, sems
+    owner_slots, owners, cap, slot, feat_in, head_in, send, unit, norm, place, feat, head, kept, sems
 ):
     n = feat.shape[0]
     width, e = head.shape
     parts = 4
+    depth = width // parts
     copies = []
     for k in range(parts):
-        at = pl.ds(k * (width // parts), width // parts)
+        at = pl.ds(k * depth, depth)
         copies.append(pltpu.make_async_copy(head_in.at[at, :], head.at[at, :], sems.at[k]))
-        at = pl.ds(k * (n // parts), n // parts)
-        copies.append(pltpu.make_async_copy(feat_in.at[at, :], feat.at[at, :], sems.at[parts + k]))
+        copies.append(pltpu.make_async_copy(feat_in.at[:, at], feat.at[:, at], sems.at[parts + k]))
     for c in copies:
         c.start()
     s = slot[...]
@@ -81,14 +81,20 @@
     row = iota((BR, n), 0)
     tags = jnp.where(row == 0, high, jnp.where(row == 1, low, jnp.where(row == 2, 1, 0)))
     send[:, e:] = dot(scatter, tags.astype(F32).astype(BF), 1, 1).astype(BF)
-    for c in copies:
-        c.wait()
-    projected = dot(feat[...], head[...])
+    projected = jnp.zeros((n, e), F32)
+    for k in range(parts):
+        copies[2 * k].wait()
+        copies[2 * k + 1].wait()
+        at = slice(k * depth, (k + 1) * depth)
+        projected += dot(feat[:, at], head[at, :])
     length = jnp.sqrt(jnp.sum(projected * projected, axis=1, keepdims=True) + norm_eps)
     rows = projected / length
-    unit[...] = rows
+    kept[...] = rows
+    keep = pltpu.make_async_copy(kept, unit, sems.at[2 * parts])
+    keep.start()
     norm[...] = jnp.broadcast_to(length, norm.shape)
     send[:, :e] = dot(scatter, rows.astype(BF)).astype(BF)
+    keep.wait()
 
 
 def stripes_kernel(core, feat, mine, other):
@@ -182,45 +188,48 @@
     lax.fori_loop(0, served.shape[0], finish, 0)
 
 
-def scores_kernel(need, column, anchors, fetched, weights, stats):
+def scores_kernel(need, column, anchors, fetched, weights, stats, partners, sems):
     blocks = weights.shape[0]
+
+    def copy(b, k):
+        return pltpu.make_async_copy(
+            fetched.at[need[b * PAIRS_REP + k]],
+            partners.at[b, pl.ds(k * BR, BR), :],
+            sems.at[b * PAIRS_REP + k],
+        )
+
+    for b in range(blocks):
+        for k in range(PAIRS_REP):
+            copy(b, k).start()
 
     def body(i, carry):
         for j in range(4):
             b = i * 4 + j
+            for k in range(PAIRS_REP):
+                copy(b, k).wait()
             q = anchors[pl.ds(pl.multiple_of(b * BR, BR), BR), :]
-            total = jnp.zeros((1, BR), F32)
-            positive = jnp.zeros((1, BR), F32)
-            want = column[pl.ds(b, 1), :]
-            for k in range(PAIRS_REP):
-                logits = dot(fetched[need[b * PAIRS_REP + k]], q, 1, 1) / logit_sharpness
-                hit = iota((BR, BR), 0) + k * BR == want
-                w = jnp.where(hit, 0.0, jnp.exp(logits - 1.0 / logit_sharpness))
-                weights[b, k * BR : (k + 1) * BR, :] = w.astype(BF)
-                total += jnp.sum(w, axis=0, keepdims=True)
-                positive += jnp.sum(jnp.where(hit, logits, 0.0), axis=0, keepdims=True)
-            stats[pl.ds(b, 1), :] = total
+            logits = dot(partners[b], q, 1, 1) / logit_sharpness
+            hit = iota(logits.shape, 0) == column[pl.ds(b, 1), :]
+            w = jnp.where(hit, 0.0, jnp.exp(logits - 1.0 / logit_sharpness))
+            weights[b, :, :] = w.astype(BF)
+            stats[pl.ds(b, 1), :] = jnp.sum(w, axis=0, keepdims=True)
+            positive = jnp.sum(jnp.where(hit, logits, 0.0), axis=0, keepdims=True)
             stats[pl.ds(blocks + b, 1), :] = positive
         return carry
 
     lax.fori_loop(0, blocks // 4, body, 0)
 
 
-def mix_kernel(need, column, weights, fetched, pulled, partner):
+def mix_kernel(column, weights, partners, pulled, partner):
     blocks = weights.shape[0]
 
     def body(i, carry):
         for j in range(4):
             b = i * 4 + j
-            want = column[pl.ds(b, 1), :]
+            w = weights[b]
+            hit = hot(iota(w.shape, 0) == column[pl.ds(b, 1), :])
+            both = dot(jnp.concatenate([w, hit], axis=1), partners[b], 0, 0)
             at = pl.ds(pl.multiple_of(b * BR, BR), BR)
-            both = jnp.zeros((2 * BR, pulled.shape[1]), F32)
-            for k in range(PAIRS_REP):
-                hit = hot(iota((BR, BR), 0) + k * BR == want)
-                w = weights[b, k * BR : (k + 1) * BR, :]
-                both += dot(
-                    jnp.concatenate([w.T, hit.T], axis=0), fetched[need[b * PAIRS_REP + k]]
-                )
             pulled[at, :] = both[:BR, :].astype(BF)
             partner[at, :] = both[BR:, :].astype(BF)
         return carry
@@ -261,19 +270,29 @@
     back[...] = dot(hot(iota((back.shape[0], rows), 1) == pos), total.astype(BF)).astype(BF)
 
 
-def unit_grad_kernel(got, place, unit, norm, out):
-    n = unit.shape[0]
+def unit_grad_kernel(got, place, unit, norm, out, kept, sem):
+    fetch = pltpu.make_async_copy(unit, kept, sem)
+    fetch.start()
+    n = norm.shape[0]
     grad = dot(hot(iota((n, got.shape[0]), 1) == column_of(place[...])), got[...])
-    rows = unit[...]
+    fetch.wait()
+    rows = kept[...]
     radial = jnp.sum(rows * grad, axis=1, keepdims=True)
     out[...] = ((grad - rows * radial) / norm[:, 0:1]).astype(BF)
 
 
-def head_grad_kernel(mine, theirs, grad, partner, out):
+def head_begun_kernel(mine, grad, out):
     step = 256
     for i in range(out.shape[0] // step):
         at = slice(i * step, (i + 1) * step)
-        out[at, :] = (dot(mine[at, :], grad[...]) + dot(theirs[at, :], partner[...])).astype(BF)
+        out[at, :] = dot(mine[at, :], grad[...])
+
+
+def head_grad_kernel(begun, theirs, partner, out):
+    step = 256
+    for i in range(out.shape[0] // step):
+        at = slice(i * step, (i + 1) * step)
+        out[at, :] = (begun[at, :] + dot(theirs[at, :], partner[...])).astype(BF)
 
 
 def sum_kernel(parts, out):
@@ -318,17 +337,19 @@
     send, unit, norm, place = call(
         lambda *r: project_kernel(owner_slots, dp, cap, *r),
         "project",
-        (sds((count, e + BR), BF), sds((n, e), F32), sds((n, BR), F32), sds((8, n), F32)),
+        (sds((count, e + BR), BF), pltpu.HBM((n, e), F32), sds((n, BR), F32), sds((8, n), F32)),
         (
             slot_of_image.reshape(1, n),
             pltpu.with_memory_space_constraint(features, pltpu.HBM),
             pltpu.with_memory_space_constraint(head_weight, pltpu.HBM),
         ),
         in_specs=[vmem, far_away, far_away],
+        out_specs=(vmem, far_away, vmem, vmem),
         scratch_shapes=[
             pltpu.VMEM((n, width), BF),
             pltpu.VMEM((width, e), BF),
-            pltpu.SemaphoreType.DMA((8,)),
+            pltpu.VMEM((n, e), F32),
+            pltpu.SemaphoreType.DMA((9,)),
         ],
     )
     got = exchange(send.reshape(devices, cap, e + BR), everyone).reshape(count, e + BR)
@@ -387,20 +408,24 @@
         scratch_shapes=[pltpu.SemaphoreType.DMA((dp,))],
     )
     fetched = exchange(served, slab_axes)
-    weights, stats = call(
+    weights, stats, partners = call(
         scores_kernel,
         "scores",
-        (sds((blocks, PAIRS_REP * BR, BR), BF), sds((2 * blocks, BR), F32)),
+        (
+            sds((blocks, PAIRS_REP * BR, BR), BF),
+            sds((2 * blocks, BR), F32),
+            sds((blocks, PAIRS_REP * BR, e), BF),
+        ),
         (need, column, anchors, fetched),
-        in_specs=[smem] + [vmem] * 3,
+        in_specs=[smem, vmem, vmem, far_away],
+        scratch_shapes=[pltpu.SemaphoreType.DMA((blocks * PAIRS_REP,))],
     )
     spread = (stats, swap(stats), swap(stats, ("yhi", "ylo")), swap(stats, ("core", "yhi", "ylo")))
     pulled, partner = call(
         mix_kernel,
         "mix",
         (sds((owner_slots, e), BF),) * 2,
-        (need, column, weights, fetched),
-        in_specs=[smem] + [vmem] * 3,
+        (column, weights, partners),
     )
     share, for_corner = call(
         lambda *r: shares_kernel(factor, *r),
@@ -409,17 +434,19 @@
         (*spread, pulled, partner, slots_corner),
     )
 
-    def pick(name, ids):
-        return call(pick_kernel, name, sds((n, e), BF), (share, ids))
-
-    for_across = pick("across", slots_across).astype(F32) + swap(for_corner).astype(F32)
+    def pick(name, rows, ids):
+        return call(
+            pick_kernel, name, sds((n, e), BF), (rows, ids), cost_estimate=cost(0.01)
+        )
+
+    for_across = pick("across", share, slots_across).astype(F32) + swap(for_corner).astype(F32)
     from_across = swap(for_across.astype(BF), ("yhi", "ylo"))
-    from_beside = swap(pick("beside", slots[1]))
+    from_beside = swap(pick("beside", share, slots[1]))
     back = call(
         back_kernel,
         "back",
         pltpu.HBM((count, e), BF),
-        (pick("own", slots[0]), from_beside, from_across, back_place),
+        (pick("own", share, slots[0]), from_beside, from_across, back_place),
     )
     returned = exchange(back.reshape(devices, cap, e), everyone).reshape(count, e)
 
@@ -430,10 +457,19 @@
     anchor_row_loss = jnp.where(home, loss, swap(loss, ("ylo",)))
 
     grad = call(
-        unit_grad_kernel, "unit_grad", sds((n, e), BF), (returned, place, unit, norm)
-    )
+        unit_grad_kernel,
+        "unit_grad",
+        sds((n, e), BF),
+        (returned, place, pltpu.with_memory_space_constraint(unit, pltpu.HBM), norm),
+        in_specs=[vmem, vmem, far_away, vmem],
+        scratch_shapes=[pltpu.VMEM((n, e), F32), pltpu.SemaphoreType.DMA],
+    )
+    begun = call(head_begun_kernel, "head_begun", sds((width // 2, e), F32), (mine, grad))
     partial = call(
-        head_grad_kernel, "head_grad", pltpu.HBM((width // 2, e), BF), (mine, theirs, grad, swap(grad))
+        head_grad_kernel,
+        "head_grad",
+        pltpu.HBM((width // 2, e), BF),
+        (begun, theirs, swap(grad)),
     )
     parts = exchange(partial.reshape(devices // 2, width // devices, e), ("zx", "yhi", "ylo"))
     weight_grad = call(sum_kernel, "add", sds((width // devices, e), F32), (parts,))

time: 228 us -> 227 us (level)
    ppermute x13, waiting for transfers between devices: 33.6 us -> 31.3 us  [swap(): return lax.ppermute(x, axes, [(i, size - 1 - i) for i in range(size)])]
    pallas_call x16 -> x17, Pallas kernels: 41.5 us -> 42.9 us  [call(): pl.pallas_call(kernel, out_shape=shapes, compiler_params=params(), name=n...]
  transfers between devices with their start and end apart: 17 -> 17, of which waited for: 10 -> 11; matrix products, arithmetic and copies ran while one was open for 1% -> 1% of each run, Pallas kernels for 8% -> 8%
where the time goes in v6:
time: 227 us; the launch traced here: 225 us
  waiting for transfers between devices  136 us (60%)
  Pallas kernels  42.9 us (19%)
  starting transfers between devices  41.8 us (18%)
    all_to_all x4, waiting for transfers between devices, exchange(): return lax.all_to_all(x, axes, 0, 0, tiled=True)  104 us
    pallas_call x17, Pallas kernels, call(): pl.pallas_call(kernel, out_shape=shapes, compiler_params=params(), name=n...  42.9 us
    all_to_all x4, starting transfers between devices, exchange(): return lax.all_to_all(x, axes, 0, 0, tiled=True)  31.6 us
    ppermute x13, waiting for transfers between devices, swap(): return lax.ppermute(x, axes, [(i, size - 1 - i) for i in range(size)])  31.3 us
    ppermute x13, starting transfers between devices, swap(): return lax.ppermute(x, axes, [(i, size - 1 - i) for i in range(size)])  10.2 us
  transfers between devices with their start and end apart: 17, of which 11 were waited for; matrix products, arithmetic and copies ran while one was open for 1% of the time, Pallas kernels for 8%

profile of v6, /device:TPU:0, one launch (start us, length us, event | category | flops | bytes accessed | tf_op | source)
XLA Modules:
  0.0 224.9 jit_solution(3577910767186069882)
XLA Ops:
  1.3 6.3 %project.1 = (bf16[1024,640]{1,0:T(8,128)(2,1)}, f32[512,512]{1,0:T(8,128)}, f32[512,128]{1,0:T(8,128)S(1)}, f32[8,512]{1,0:T(8,128)S(1)}) custom-call(s32[1,512]{1,0:T(1,128)S(1)} %bitcast.22, bf16[512,2048]{1,0:T(8,128)(2,1)} %feat.1, bf16[2048,512]{1,0:T(8,128)(2,1)} %r_2_.1), custom_call_target="tpu_custom_call" | custom-call | tf_op jit(solution)/shard_map/project/pallas_call | solution.py:333
  7.6 11.2 %all-to-all-start = ((bf16[128,8,640]{2,1,0:T(8,128)(2,1)}), bf16[128,8,640]{2,1,0:T(8,128)(2,1)S(1)}, u32[]{:S(2)}, u32[]{:S(2)}) async-start(bf16[128,8,640]{2,1,0:T(8,128)(2,1)} %bitcast.1), calls=%async_computation | async-start | bytes 2621440 | tf_op jit(solution)/shard_map/all_to_all | solution.py:308
  19.9 20.4 %all-to-all-done = bf16[128,8,640]{2,1,0:T(8,128)(2,1)S(1)} async-done(((bf16[128,8,640]{2,1,0:T(8,128)(2,1)}), bf16[128,8,640]{2,1,0:T(8,128)(2,1)S(1)}, u32[]{:S(2)}, u32[]{:S(2)}) %all-to-all-start) | async-done | bytes 1310752 | tf_op jit(solution)/shard_map/all_to_all | solution.py:308
  40.3 1.2 compact.1
  41.6 1.1 collective-permute-start.2
  43.4 3.6 %near.1 = (bf16[2048,512]{1,0:T(8,128)(2,1)S(1)}, f32[2,8,512]{2,1,0:T(8,128)S(1)}) custom-call(bf16[528,512]{1,0:T(8,128)(2,1)S(1)} %get-tuple-element.37.own, bf16[528,512]{1,0:T(8,128)(2,1)S(1)} %collective-permute-done.1.beside), custom_call_target="tpu_custom_call" | custom-call | flops 4000000000 | bytes 4000000 | tf_op jit(solution)/shard_map/near/pallas_call | solution.py:333
  47.1 10.3 %collective-permute-done.2.across = bf16[528,512]{1,0:T(8,128)(2,1)S(1)} collective-permute-done((bf16[528,512]{1,0:T(8,128)(2,1)S(1)}, bf16[528,512]{1,0:T(8,128)(2,1)S(1)}, u32[]{:S(2)}, u32[]{:S(2)}) %collective-permute-start.2) | collective-permute-done | bytes 540704 | tf_op jit(solution)/shard_map/ppermute | solution.py:304
  57.4 2.5 %middle.1 = (bf16[2048,512]{1,0:T(8,128)(2,1)S(1)}, f32[8,512]{1,0:T(8,128)S(1)}) custom-call(bf16[2048,512]{1,0:T(8,128)(2,1)S(1)} %get-tuple-element.39.begun, bf16[528,512]{1,0:T(8,128)(2,1)S(1)} %collective-permute-done.2.across), custom_call_target="tpu_custom_call" | custom-call | tf_op jit(solution)/shard_map/middle/pallas_call | solution.py:333
  59.9 4.6 %far.1 = (bf16[2048,512]{1,0:T(8,128)(2,1)S(1)}, bf16[32,128,512]{2,1,0:T(8,128)(2,1)}, f32[8,512]{1,0:T(8,128)S(1)}) custom-call(s32[32]{0:T(128)S(1)} %select_reduce_fusion.2.serve, s32[32]{0:T(128)S(1)} %select_reduce_fusion.1.order, s32[9]{0:T(128)S(1)} %convert_reduce_fusion.1.ready, bf16[2048,512]{1,0:T(8,128)(2,1)S(1)} %get-tuple-element.41.begun, ...), custom_call_target="tpu_custom_call" | custom-call | tf_op jit(solution)/shard_map/far/pallas_call | solution.py:333
  64.6 4.9 %all-to-all-start.1 = ((bf16[32,128,512]{2,1,0:T(8,128)(2,1)}), bf16[32,128,512]{2,1,0:T(8,128)(2,1)}, u32[]{:S(2)}, u32[]{:S(2)}) async-start(bf16[32,128,512]{2,1,0:T(8,128)(2,1)} %get-tuple-element.43), calls=%async_computation.1 | async-start | bytes 8388608 | tf_op jit(solution)/shard_map/all_to_all | solution.py:308
  70.7 57.6 %all-to-all-done.1.fetched = bf16[32,128,512]{2,1,0:T(8,128)(2,1)} async-done(((bf16[32,128,512]{2,1,0:T(8,128)(2,1)}), bf16[32,128,512]{2,1,0:T(8,128)(2,1)}, u32[]{:S(2)}, u32[]{:S(2)}) %all-to-all-start.1) | async-done | bytes 4194336 | tf_op jit(solution)/shard_map/all_to_all | solution.py:308
  128.4 6.6 %scores.1 = (bf16[16,256,128]{2,1,0:T(8,128)(2,1)S(1)}, f32[32,128]{1,0:T(8,128)S(1)}, bf16[16,256,512]{2,1,0:T(8,128)(2,1)S(1)}) custom-call(s32[32]{0:T(128)S(1)} %fusion.4.need, s32[16,128]{1,0:T(8,128)S(1)} %subtract_bitcast_fusion.column, bf16[2048,512]{1,0:T(8,128)(2,1)S(1)} %get-tuple-element.42.anchors, bf16[32,128,512]{2,1,0:T(8,128)(2,1)} %all-to-all-done.1.fetched), custom_call_target="tpu_custom_call" | custom-call | tf_op jit(solution)/shard_map/scores/pallas_call | solution.py:333
  136.0 2.4 %collective-permute-start.6 = (f32[32,128]{1,0:T(8,128)S(1)}, f32[32,128]{1,0:T(8,128)S(1)}, u32[]{:S(2)}, u32[]{:S(2)}) collective-permute-start(f32[32,128]{1,0:T(8,128)S(1)} %get-tuple-element.44.r_0_), channel_id=1, source_target_pairs={{0,3},{1,2},{2,1},{3,0},{4,7},{5,6},{6,5},{7,4},{8,11},{9,10},{10,... | collective-permute-start | bytes 49160 | tf_op jit(solution)/shard_map/ppermute | solution.py:304
  138.4 1.9 mix.1
  141.0 2.1 shares.1
  143.4 1.6 beside.1
  145.6 1.6 across.1
  147.4 2.5 %collective-permute-start.10 = (bf16[512,512]{1,0:T(8,128)(2,1)S(1)}, bf16[512,512]{1,0:T(8,128)(2,1)S(1)}, u32[]{:S(2)}, u32[]{:S(2)}) collective-permute-start(bf16[512,512]{1,0:T(8,128)(2,1)S(1)} %add_convert_fusion), channel_id=1, source_target_pairs={{0,3},{1,2},{2,1},{3,0},{4,7},{5,6},{6,5},{7,4},{8,11},{9,10},{10,... | collective-permute-start | bytes 1572872 | tf_op jit(solution)/shard_map/ppermute | solution.py:304
  149.8 1.6 own.1.a
  151.5 11.0 %collective-permute-done.10.c = bf16[512,512]{1,0:T(8,128)(2,1)S(1)} collective-permute-done((bf16[512,512]{1,0:T(8,128)(2,1)S(1)}, bf16[512,512]{1,0:T(8,128)(2,1)S(1)}, u32[]{:S(2)}, u32[]{:S(2)}) %collective-permute-start.10) | collective-permute-done | bytes 524320 | tf_op jit(solution)/shard_map/ppermute | solution.py:304
  162.5 2.1 back.1
  164.6 10.7 %all-to-all-start.2 = ((bf16[128,8,512]{2,1,0:T(8,128)(2,1)}), bf16[128,8,512]{2,1,0:T(8,128)(2,1)S(1)}, u32[]{:S(2)}, u32[]{:S(2)}) async-start(bf16[128,8,512]{2,1,0:T(8,128)(2,1)} %bitcast.24), calls=%async_computation.2 | async-start | bytes 2097152 | tf_op jit(solution)/shard_map/all_to_all | solution.py:308
  175.3 1.7 stripes.1
  177.0 1.0 copy-done.1
  178.0 16.1 %all-to-all-done.2 = bf16[128,8,512]{2,1,0:T(8,128)(2,1)S(1)} async-done(((bf16[128,8,512]{2,1,0:T(8,128)(2,1)}), bf16[128,8,512]{2,1,0:T(8,128)(2,1)S(1)}, u32[]{:S(2)}, u32[]{:S(2)}) %all-to-all-start.2) | async-done | bytes 1048608 | tf_op jit(solution)/shard_map/all_to_all | solution.py:308
  194.0 2.2 unit_grad.1.grad
  197.2 1.1 collective-permute-done.12.partner
  198.2 1.7 head_grad.1
  199.9 4.9 %all-to-all-start.3 = ((bf16[64,16,512]{2,1,0:T(8,128)(2,1)}), bf16[64,16,512]{2,1,0:T(8,128)(2,1)S(1)}, u32[]{:S(2)}, u32[]{:S(2)}) async-start(bf16[64,16,512]{2,1,0:T(8,128)(2,1)} %bitcast.23), calls=%async_computation.3 | async-start | bytes 2097152 | tf_op jit(solution)/shard_map/all_to_all | solution.py:308
  204.9 1.6 collective-permute-start.7
  206.5 6.6 %collective-permute-done.7 = f32[2048]{0:T(1024)S(1)} collective-permute-done((f32[2048]{0:T(1024)S(1)}, f32[2048]{0:T(1024)S(1)}, u32[]{:S(2)}, u32[]{:S(2)}) %collective-permute-start.7) | collective-permute-done | bytes 8224 | tf_op jit(solution)/shard_map/ppermute | solution.py:304
  213.7 10.3 %all-to-all-done.3.parts = bf16[64,16,512]{2,1,0:T(8,128)(2,1)S(1)} async-done(((bf16[64,16,512]{2,1,0:T(8,128)(2,1)}), bf16[64,16,512]{2,1,0:T(8,128)(2,1)S(1)}, u32[]{:S(2)}, u32[]{:S(2)}) %all-to-all-start.3) | async-done | bytes 1048608 | tf_op jit(solution)/shard_map/all_to_all | solution.py:308
  (50 shorter events, 8.9 us)
Async XLA Ops:
  0.6 0.7 copy-start.3
  7.6 11.2 %copy-start.4 = (s32[512,8]{0,1:T(8,128)S(1)}, s32[512,8]{0,1:T(8,128)}, u32[]{:S(2)}) copy-start(s32[512,8]{0,1:T(8,128)} %param.8) | copy-start | bytes 49156
  7.6 32.7 %all-to-all-start = ((bf16[128,8,640]{2,1,0:T(8,128)(2,1)}), bf16[128,8,640]{2,1,0:T(8,128)(2,1)S(1)}, u32[]{:S(2)}, u32[]{:S(2)}) async-start(bf16[128,8,640]{2,1,0:T(8,128)(2,1)} %bitcast.1), calls=%async_computation | async-start | bytes 2621440 | tf_op jit(solution)/shard_map/all_to_all | solution.py:308
  41.5 2.0 collective-permute-start.1
  41.6 15.8 %collective-permute-start.2 = (bf16[528,512]{1,0:T(8,128)(2,1)S(1)}, bf16[528,512]{1,0:T(8,128)(2,1)S(1)}, u32[]{:S(2)}, u32[]{:S(2)}) collective-permute-start(bf16[528,512]{1,0:T(8,128)(2,1)S(1)} %get-tuple-element.37.own), channel_id=1, source_target_pairs={{0,3},{1,2},{2,1},{3,0},{4,7},{5,6},{6,5},{7,4},{8,11},{9,10},{10,... | collective-permute-start | bytes 1622024 | tf_op jit(solution)/shard_map/ppermute | solution.py:304
  57.4 2.5 %collective-permute-start.3 = (bf16[528,512]{1,0:T(8,128)(2,1)S(1)}, bf16[528,512]{1,0:T(8,128)(2,1)S(1)}, u32[]{:S(2)}, u32[]{:S(2)}) collective-permute-start(bf16[528,512]{1,0:T(8,128)(2,1)S(1)} %collective-permute-done.2.across), channel_id=1, source_target_pairs={{0,4},{4,0},{1,5},{5,1},{2,6},{6,2},{3,7},{7,3},{8,12},{12,8},{9,1... | collective-permute-start | bytes 1622024 | tf_op jit(solution)/shard_map/ppermute | solution.py:304
  64.6 4.9 %copy-start.5 = (s32[2048]{0:T(1024)S(1)}, s32[2048]{0:T(1024)}, u32[]{:S(2)}) copy-start(s32[2048]{0:T(1024)} %param.9) | copy-start | bytes 24580
  64.6 63.8 %all-to-all-start.1 = ((bf16[32,128,512]{2,1,0:T(8,128)(2,1)}), bf16[32,128,512]{2,1,0:T(8,128)(2,1)}, u32[]{:S(2)}, u32[]{:S(2)}) async-start(bf16[32,128,512]{2,1,0:T(8,128)(2,1)} %get-tuple-element.43), calls=%async_computation.1 | async-start | bytes 8388608 | tf_op jit(solution)/shard_map/all_to_all | solution.py:308
  69.5 1.3 collective-permute-start
  135.0 5.3 %collective-permute-start.4 = (f32[32,128]{1,0:T(8,128)S(1)}, f32[32,128]{1,0:T(8,128)S(1)}, u32[]{:S(2)}, u32[]{:S(2)}) collective-permute-start(f32[32,128]{1,0:T(8,128)S(1)} %get-tuple-element.44.r_0_), channel_id=1, source_target_pairs={{0,7},{1,6},{2,5},{3,4},{4,3},{5,2},{6,1},{7,0},{8,15},{9,14},{10,... | collective-permute-start | bytes 49160 | tf_op jit(solution)/shard_map/ppermute | solution.py:304
  135.2 5.1 %collective-permute-start.5 = (f32[32,128]{1,0:T(8,128)S(1)}, f32[32,128]{1,0:T(8,128)S(1)}, u32[]{:S(2)}, u32[]{:S(2)}) collective-permute-start(f32[32,128]{1,0:T(8,128)S(1)} %get-tuple-element.44.r_0_), channel_id=1, source_target_pairs={{0,4},{4,0},{1,5},{5,1},{2,6},{6,2},{3,7},{7,3},{8,12},{12,8},{9,1... | collective-permute-start | bytes 49160 | tf_op jit(solution)/shard_map/ppermute | solution.py:304
  136.0 4.9 %collective-permute-start.6 = (f32[32,128]{1,0:T(8,128)S(1)}, f32[32,128]{1,0:T(8,128)S(1)}, u32[]{:S(2)}, u32[]{:S(2)}) collective-permute-start(f32[32,128]{1,0:T(8,128)S(1)} %get-tuple-element.44.r_0_), channel_id=1, source_target_pairs={{0,3},{1,2},{2,1},{3,0},{4,7},{5,6},{6,5},{7,4},{8,11},{9,10},{10,... | collective-permute-start | bytes 49160 | tf_op jit(solution)/shard_map/ppermute | solution.py:304
  143.1 4.1 %collective-permute-start.9 = (bf16[512,512]{1,0:T(8,128)(2,1)S(1)}, bf16[512,512]{1,0:T(8,128)(2,1)S(1)}, u32[]{:S(2)}, u32[]{:S(2)}) collective-permute-start(bf16[512,512]{1,0:T(8,128)(2,1)S(1)} %get-tuple-element.54), channel_id=1, source_target_pairs={{0,4},{4,0},{1,5},{5,1},{2,6},{6,2},{3,7},{7,3},{8,12},{12,8},{9,1... | collective-permute-start | bytes 1572872 | tf_op jit(solution)/shard_map/ppermute | solution.py:304
  145.0 6.4 %collective-permute-start.8 = (bf16[512,512]{1,0:T(8,128)(2,1)S(1)}, bf16[512,512]{1,0:T(8,128)(2,1)S(1)}, u32[]{:S(2)}, u32[]{:S(2)}) collective-permute-start(bf16[512,512]{1,0:T(8,128)(2,1)S(1)} %beside.1), channel_id=1, source_target_pairs={{0,4},{4,0},{1,5},{5,1},{2,6},{6,2},{3,7},{7,3},{8,12},{12,8},{9,1... | collective-permute-start | bytes 1572872 | tf_op jit(solution)/shard_map/ppermute | solution.py:304
  147.4 15.2 %collective-permute-start.10 = (bf16[512,512]{1,0:T(8,128)(2,1)S(1)}, bf16[512,512]{1,0:T(8,128)(2,1)S(1)}, u32[]{:S(2)}, u32[]{:S(2)}) collective-permute-start(bf16[512,512]{1,0:T(8,128)(2,1)S(1)} %add_convert_fusion), channel_id=1, source_target_pairs={{0,3},{1,2},{2,1},{3,0},{4,7},{5,6},{6,5},{7,4},{8,11},{9,10},{10,... | collective-permute-start | bytes 1572872 | tf_op jit(solution)/shard_map/ppermute | solution.py:304
  162.5 12.8 %copy-start = (bf16[512,2048]{1,0:T(8,128)(2,1)S(1)}, bf16[512,2048]{1,0:T(8,128)(2,1)}, u32[]{:S(2)}) copy-start(bf16[512,2048]{1,0:T(8,128)(2,1)} %feat.1) | copy-start | bytes 6291460
  164.6 29.4 %all-to-all-start.2 = ((bf16[128,8,512]{2,1,0:T(8,128)(2,1)}), bf16[128,8,512]{2,1,0:T(8,128)(2,1)S(1)}, u32[]{:S(2)}, u32[]{:S(2)}) async-start(bf16[128,8,512]{2,1,0:T(8,128)(2,1)} %bitcast.24), calls=%async_computation.2 | async-start | bytes 2097152 | tf_op jit(solution)/shard_map/all_to_all | solution.py:308
  177.0 1.0 copy-start.1
  178.0 18.5 %copy-start.2 = (bf16[1024,512]{1,0:T(8,128)(2,1)S(1)}, bf16[1024,512]{1,0:T(8,128)(2,1)}, u32[]{:S(2)}) copy-start(bf16[1024,512]{1,0:T(8,128)(2,1)} %copy-done.1) | copy-start | bytes 3145732
  178.0 19.2 %collective-permute-start.11 = (bf16[1024,512]{1,0:T(8,128)(2,1)}, bf16[1024,512]{1,0:T(8,128)(2,1)S(1)}, u32[]{:S(2)}, u32[]{:S(2)}) collective-permute-start(bf16[1024,512]{1,0:T(8,128)(2,1)} %get-tuple-element.59), channel_id=1, source_target_pairs={{0,4},{4,0},{1,5},{5,1},{2,6},{6,2},{3,7},{7,3},{8,12},{12,8},{9,1... | collective-permute-start | bytes 3145736 | tf_op jit(solution)/shard_map/ppermute | solution.py:304
  196.2 2.0 collective-permute-start.12
  199.9 24.1 %all-to-all-start.3 = ((bf16[64,16,512]{2,1,0:T(8,128)(2,1)}), bf16[64,16,512]{2,1,0:T(8,128)(2,1)S(1)}, u32[]{:S(2)}, u32[]{:S(2)}) async-start(bf16[64,16,512]{2,1,0:T(8,128)(2,1)} %bitcast.23), calls=%async_computation.3 | async-start | bytes 2097152 | tf_op jit(solution)/shard_map/all_to_all | solution.py:308
  204.9 8.3 %collective-permute-start.7 = (f32[2048]{0:T(1024)S(1)}, f32[2048]{0:T(1024)S(1)}, u32[]{:S(2)}, u32[]{:S(2)}) collective-permute-start(f32[2048]{0:T(1024)S(1)} %fusion.10), channel_id=1, source_target_pairs={{0,1},{1,0},{2,3},{3,2},{4,5},{5,4},{6,7},{7,6},{8,9},{9,8},{10,11... | collective-permute-start | bytes 24584 | tf_op jit(solution)/shard_map/ppermute | solution.py:304

commit v7 on v6

--- a/solution.py
+++ b/solution.py
@@ -21,6 +21,19 @@
 VMEM_BYTES = 24 * 1024 * 1024
 
 
+AXES = ("z", "x", "core", "yhi", "ylo")
+DISPATCH = ("core", "x", "yhi", "ylo", "z")
+FETCH = ("ylo", "x", "z")
+REDUCE = ("x", "yhi", "ylo", "z")
+
+
+def position(order, sizes, place):
+    at = 0
+    for axis in order:
+        at = at * sizes[axis] + place[axis]
+    return at
+
+
 def params():
     return pltpu.CompilerParams(vmem_limit_bytes=VMEM_BYTES)
 
@@ -51,7 +64,7 @@
 
 
 def project_kernel(
-    owner_slots, owners, cap, slot, feat_in, head_in, send, unit, norm, place, feat, head, kept, sems
+    owner_slots, sizes, cap, slot, feat_in, head_in, send, unit, norm, place, feat, head, kept, sems
 ):
     n = feat.shape[0]
     width, e = head.shape
@@ -67,12 +80,18 @@
     s = slot[...]
     owner = s // owner_slots
     local = s - owner * owner_slots
+    owners = sizes["z"] * sizes["x"] * 2
     mine = iota((owners, n), 0) == owner
     before = dot(hot(mine), hot(iota((n, n), 0) < iota((n, n), 1)))
     rank = jnp.sum(jnp.where(mine, before, 0.0), axis=0, keepdims=True).astype(I32)
     member = rank & (REPS - 1)
     slab = member & 1
-    device = (owner // 2) * 8 + (member // 2) * 4 + slab * 2 + ((owner & 1) ^ slab)
+    column = owner // 2
+    z = column // sizes["x"]
+    place_of = dict(
+        z=z, x=column - z * sizes["x"], core=member // 2, yhi=slab, ylo=(owner & 1) ^ slab
+    )
+    device = position(DISPATCH, sizes, place_of)
     p = device * cap + rank // REPS
     place[...] = jnp.broadcast_to(p.astype(F32), place.shape)
     scatter = hot(iota((send.shape[0], n), 0) == p)
@@ -97,15 +116,19 @@
     keep.wait()
 
 
-def stripes_kernel(core, feat, mine, other):
-    n = feat.shape[0]
+def stripes_kernel(sizes, core, feat, mine, other):
     first = core[0] == 0
     half = BR // 2
-    for z in range(feat.shape[1] // BR):
-        t = feat[:, z * BR : (z + 1) * BR].astype(F32).T
+    rows = half // REPS
+    for column in range(feat.shape[1] // BR):
+        t = feat[:, column * BR : (column + 1) * BR].astype(F32).T
         a, b = t[:half, :], t[half:, :]
-        mine[z * half : (z + 1) * half, :] = jnp.where(first, a, b).astype(BF)
-        other[z * half : (z + 1) * half, :] = jnp.where(first, b, a).astype(BF)
+        here, there = jnp.where(first, a, b).astype(BF), jnp.where(first, b, a).astype(BF)
+        z, x = divmod(column, sizes["x"])
+        for y in range(REPS):
+            at = position(REDUCE, sizes, dict(z=z, x=x, yhi=y // 2, ylo=y % 2)) * rows
+            mine[at : at + rows, :] = here[y * rows : (y + 1) * rows, :]
+            other[at : at + rows, :] = there[y * rows : (y + 1) * rows, :]
 
 
 def compact_kernel(got, packed, place):
@@ -188,39 +211,34 @@
     lax.fori_loop(0, served.shape[0], finish, 0)
 
 
-def scores_kernel(need, column, anchors, fetched, weights, stats, partners, sems):
+def scores_kernel(need, column, anchors, fetched, weights, stats, partners, sem):
+    load = pltpu.make_async_copy(fetched, partners, sem)
+    load.start()
     blocks = weights.shape[0]
-
-    def copy(b, k):
-        return pltpu.make_async_copy(
-            fetched.at[need[b * PAIRS_REP + k]],
-            partners.at[b, pl.ds(k * BR, BR), :],
-            sems.at[b * PAIRS_REP + k],
-        )
-
-    for b in range(blocks):
-        for k in range(PAIRS_REP):
-            copy(b, k).start()
+    load.wait()
 
     def body(i, carry):
         for j in range(4):
             b = i * 4 + j
+            q = anchors[pl.ds(pl.multiple_of(b * BR, BR), BR), :]
+            total = jnp.zeros((1, BR), F32)
+            positive = jnp.zeros((1, BR), F32)
+            want = column[pl.ds(b, 1), :]
             for k in range(PAIRS_REP):
-                copy(b, k).wait()
-            q = anchors[pl.ds(pl.multiple_of(b * BR, BR), BR), :]
-            logits = dot(partners[b], q, 1, 1) / logit_sharpness
-            hit = iota(logits.shape, 0) == column[pl.ds(b, 1), :]
-            w = jnp.where(hit, 0.0, jnp.exp(logits - 1.0 / logit_sharpness))
-            weights[b, :, :] = w.astype(BF)
-            stats[pl.ds(b, 1), :] = jnp.sum(w, axis=0, keepdims=True)
-            positive = jnp.sum(jnp.where(hit, logits, 0.0), axis=0, keepdims=True)
+                logits = dot(partners[need[b * PAIRS_REP + k]], q, 1, 1) / logit_sharpness
+                hit = iota((BR, BR), 0) + k * BR == want
+                w = jnp.where(hit, 0.0, jnp.exp(logits - 1.0 / logit_sharpness))
+                weights[b, k * BR : (k + 1) * BR, :] = w.astype(BF)
+                total += jnp.sum(w, axis=0, keepdims=True)
+                positive += jnp.sum(jnp.where(hit, logits, 0.0), axis=0, keepdims=True)
+            stats[pl.ds(b, 1), :] = total
             stats[pl.ds(blocks + b, 1), :] = positive
         return carry
 
     lax.fori_loop(0, blocks // 4, body, 0)
 
 
-def mix_kernel(column, weights, partners, pulled, partner):
+def mix_kernel(need, column, weights, partners, pulled, partner):
     blocks = weights.shape[0]
 
     def body(i, carry):
@@ -228,7 +246,8 @@
             b = i * 4 + j
             w = weights[b]
             hit = hot(iota(w.shape, 0) == column[pl.ds(b, 1), :])
-            both = dot(jnp.concatenate([w, hit], axis=1), partners[b], 0, 0)
+            pair = [partners[need[b * PAIRS_REP + k]] for k in range(PAIRS_REP)]
+            both = dot(jnp.concatenate([w, hit], axis=1), jnp.concatenate(pair, axis=0), 0, 0)
             at = pl.ds(pl.multiple_of(b * BR, BR), BR)
             pulled[at, :] = both[:BR, :].astype(BF)
             partner[at, :] = both[BR:, :].astype(BF)
@@ -309,11 +328,11 @@
 
 
 def shards(features, head_weight, slot_of_image, candidates, positives):
-    slab_axes = ("zx", "ylo")
-    everyone = ("zx", "core", "yhi", "ylo")
-    dp = lax.axis_size(slab_axes)
+    sizes = {axis: lax.axis_size(axis) for axis in AXES}
+    dp = sizes["z"] * sizes["x"] * 2
     slab = lax.axis_index("yhi")
-    me = lax.axis_index(slab_axes) ^ slab
+    me = (lax.axis_index("z") * sizes["x"] + lax.axis_index("x")) * 2
+    me = me + (lax.axis_index("ylo") ^ slab)
     core = lax.axis_index("core")
     member = core * 2 + slab
     home = core == (me & 1)
@@ -335,7 +354,7 @@
         )(*args)
 
     send, unit, norm, place = call(
-        lambda *r: project_kernel(owner_slots, dp, cap, *r),
+        lambda *r: project_kernel(owner_slots, sizes, cap, *r),
         "project",
         (sds((count, e + BR), BF), pltpu.HBM((n, e), F32), sds((n, BR), F32), sds((8, n), F32)),
         (
@@ -352,10 +371,10 @@
             pltpu.SemaphoreType.DMA((9,)),
         ],
     )
-    got = exchange(send.reshape(devices, cap, e + BR), everyone).reshape(count, e + BR)
+    got = exchange(send.reshape(devices, cap, e + BR), DISPATCH).reshape(count, e + BR)
 
     mine, other = call(
-        stripes_kernel,
+        lambda *r: stripes_kernel(sizes, *r),
         "stripes",
         (sds((width // 2, n), BF),) * 2,
         (core.reshape(1), features),
@@ -369,8 +388,17 @@
     owner = table // blocks
     numbers = jnp.arange(dp, dtype=I32)
     wanted = jnp.sum(jnp.where(owner == me, table - owner * blocks, 0), axis=1)
-    serve = jnp.sum(jnp.where(numbers[None, :] == (numbers ^ slab)[:, None], wanted[None, :], 0), axis=1)
-    need = lax.dynamic_index_in_dim(owner, me, axis=0, keepdims=False) ^ slab
+
+    def fetch_place(number):
+        column = number // 2
+        z = column // sizes["x"]
+        x = column - z * sizes["x"]
+        return position(FETCH, sizes, dict(z=z, x=x, ylo=(number & 1) ^ slab))
+
+    serve = jnp.sum(
+        jnp.where(fetch_place(numbers)[None, :] == numbers[:, None], wanted[None, :], 0), axis=1
+    )
+    need = fetch_place(lax.dynamic_index_in_dim(owner, me, axis=0, keepdims=False))
     column = jnp.where(home, positives, swap(positives)).reshape(blocks, BR)
     column = column - member * (PAIRS_REP * BR)
     keys = serve * dp + numbers
@@ -407,25 +435,26 @@
         out_specs=(vmem, pl.BlockSpec(memory_space=pltpu.HBM), vmem),
         scratch_shapes=[pltpu.SemaphoreType.DMA((dp,))],
     )
-    fetched = exchange(served, slab_axes)
+    fetched = exchange(served, FETCH)
     weights, stats, partners = call(
         scores_kernel,
         "scores",
         (
             sds((blocks, PAIRS_REP * BR, BR), BF),
             sds((2 * blocks, BR), F32),
-            sds((blocks, PAIRS_REP * BR, e), BF),
+            sds((dp, BR, e), BF),
         ),
         (need, column, anchors, fetched),
         in_specs=[smem, vmem, vmem, far_away],
-        scratch_shapes=[pltpu.SemaphoreType.DMA((blocks * PAIRS_REP,))],
+        scratch_shapes=[pltpu.SemaphoreType.DMA],
     )
     spread = (stats, swap(stats), swap(stats, ("yhi", "ylo")), swap(stats, ("core", "yhi", "ylo")))
     pulled, partner = call(
         mix_kernel,
         "mix",
         (sds((owner_slots, e), BF),) * 2,
-        (column, weights, partners),
+        (need, column, weights, partners),
+        in_specs=[smem] + [vmem] * 3,
     )
     share, for_corner = call(
         lambda *r: shares_kernel(factor, *r),
@@ -448,7 +477,7 @@
         pltpu.HBM((count, e), BF),
         (pick("own", share, slots[0]), from_beside, from_across, back_place),
     )
-    returned = exchange(back.reshape(devices, cap, e), everyone).reshape(count, e)
+    returned = exchange(back.reshape(devices, cap, e), DISPATCH).reshape(count, e)
 
     both = (spread[0] + spread[3]) + (spread[1] + spread[2])
     rest, matching = both[:blocks], both[blocks:]
@@ -471,23 +500,21 @@
         pltpu.HBM((width // 2, e), BF),
         (begun, theirs, swap(grad)),
     )
-    parts = exchange(partial.reshape(devices // 2, width // devices, e), ("zx", "yhi", "ylo"))
+    parts = exchange(partial.reshape(devices // 2, width // devices, e), REDUCE)
     weight_grad = call(sum_kernel, "add", sds((width // devices, e), F32), (parts,))
     return (anchor_row_loss, weight_grad)
 
 
 def solution(mesh):
     dp, rep = mesh.devices.shape
-    split = jax.sharding.Mesh(
-        mesh.devices.reshape(dp // 2, 2, rep // 2, 2), ("zx", "core", "yhi", "ylo")
-    )
-    everyone = ("zx", "core", "yhi", "ylo")
-    owners = ("zx", "core")
-    placed = (P(everyone, None), P(), P(everyone), P(), P(owners))
+    z = x = math.isqrt(dp // 2)
+    split = jax.sharding.Mesh(mesh.devices.reshape(z, x, 2, rep // 2, 2), AXES)
+    owners = ("z", "x", "core")
+    placed = (P(AXES, None), P(), P(AXES), P(), P(owners))
     return jax.shard_map(
         shards,
         mesh=split,
         in_specs=placed,
-        out_specs=(P(owners), P(everyone, None)),
+        out_specs=(P(owners), P(AXES, None)),
         check_vma=False,
     )

time: 227 us -> 227 us (level)
  waiting for transfers between devices: 136 us -> 139 us
    all_to_all x4, waiting for transfers between devices: 104 us -> 111 us  [exchange(): return lax.all_to_all(x, axes, 0, 0, tiled=True)]
    ppermute x13, waiting for transfers between devices: 31.3 us -> 28.7 us  [swap(): return lax.ppermute(x, axes, [(i, size - 1 - i) for i in range(size)])]
  transfers between devices with their start and end apart: 17 -> 17, of which waited for: 11 -> 10; matrix products, arithmetic and copies ran while one was open for 1% -> 1% of each run, Pallas kernels for 8% -> 8%
where the time goes in v7:
time: 227 us
  waiting for transfers between devices  139 us (61%)
  starting transfers between devices  41.8 us (18%)
  Pallas kernels  41.3 us (18%)
    all_to_all x4, waiting for transfers between devices, exchange(): return lax.all_to_all(x, axes, 0, 0, tiled=True)  111 us
    pallas_call x17, Pallas kernels, call(): pl.pallas_call(kernel, out_shape=shapes, compiler_params=params(), name=n...  41.3 us
    all_to_all x4, starting transfers between devices, exchange(): return lax.all_to_all(x, axes, 0, 0, tiled=True)  30.6 us
    ppermute x13, waiting for transfers between devices, swap(): return lax.ppermute(x, axes, [(i, size - 1 - i) for i in range(size)])  28.7 us
    ppermute x13, starting transfers between devices, swap(): return lax.ppermute(x, axes, [(i, size - 1 - i) for i in range(size)])  11.1 us
  transfers between devices with their start and end apart: 17, of which 10 were waited for; matrix products, arithmetic and copies ran while one was open for 1% of the time, Pallas kernels for 8%

profile of v7, /device:TPU:0, one launch (start us, length us, event | category | flops | bytes accessed | tf_op | source)
XLA Modules:
  0.0 227.0 jit_solution(7328337464539342072)
XLA Ops:
  1.3 6.3 %project.1 = (bf16[1024,640]{1,0:T(8,128)(2,1)}, f32[512,512]{1,0:T(8,128)}, f32[512,128]{1,0:T(8,128)S(1)}, f32[8,512]{1,0:T(8,128)S(1)}) custom-call(s32[1,512]{1,0:T(1,128)S(1)} %bitcast.22, bf16[512,2048]{1,0:T(8,128)(2,1)} %r_1_.3, bf16[2048,512]{1,0:T(8,128)(2,1)} %r_2_.1), custom_call_target="tpu_custom_call" | custom-call | tf_op jit(solution)/shard_map/project/pallas_call | solution.py:352
  7.6 11.2 %all-to-all-start = ((bf16[128,8,640]{2,1,0:T(8,128)(2,1)}), bf16[128,8,640]{2,1,0:T(8,128)(2,1)S(1)}, u32[]{:S(2)}, u32[]{:S(2)}) async-start(bf16[128,8,640]{2,1,0:T(8,128)(2,1)} %bitcast.1), calls=%async_computation | async-start | bytes 2621440 | tf_op jit(solution)/shard_map/all_to_all | solution.py:327
  19.9 19.2 %all-to-all-done = bf16[128,8,640]{2,1,0:T(8,128)(2,1)S(1)} async-done(((bf16[128,8,640]{2,1,0:T(8,128)(2,1)}), bf16[128,8,640]{2,1,0:T(8,128)(2,1)S(1)}, u32[]{:S(2)}, u32[]{:S(2)}) %all-to-all-start) | async-done | bytes 1310752 | tf_op jit(solution)/shard_map/all_to_all | solution.py:327
  39.1 1.2 compact.1
  40.3 1.9 collective-permute-start.2
  42.3 3.6 %near.1 = (bf16[2048,512]{1,0:T(8,128)(2,1)S(1)}, f32[2,8,512]{2,1,0:T(8,128)S(1)}) custom-call(bf16[528,512]{1,0:T(8,128)(2,1)S(1)} %get-tuple-element.37.own, bf16[528,512]{1,0:T(8,128)(2,1)S(1)} %collective-permute-done.1.beside), custom_call_target="tpu_custom_call" | custom-call | flops 4000000000 | bytes 4000000 | tf_op jit(solution)/shard_map/near/pallas_call | solution.py:352
  45.9 10.3 %collective-permute-done.2.across = bf16[528,512]{1,0:T(8,128)(2,1)S(1)} collective-permute-done((bf16[528,512]{1,0:T(8,128)(2,1)S(1)}, bf16[528,512]{1,0:T(8,128)(2,1)S(1)}, u32[]{:S(2)}, u32[]{:S(2)}) %collective-permute-start.2) | collective-permute-done | bytes 540704 | tf_op jit(solution)/shard_map/ppermute | solution.py:323
  56.2 2.5 %middle.1 = (bf16[2048,512]{1,0:T(8,128)(2,1)S(1)}, f32[8,512]{1,0:T(8,128)S(1)}) custom-call(bf16[2048,512]{1,0:T(8,128)(2,1)S(1)} %get-tuple-element.39.begun, bf16[528,512]{1,0:T(8,128)(2,1)S(1)} %collective-permute-done.2.across), custom_call_target="tpu_custom_call" | custom-call | tf_op jit(solution)/shard_map/middle/pallas_call | solution.py:352
  58.8 4.5 %far.1 = (bf16[2048,512]{1,0:T(8,128)(2,1)S(1)}, bf16[32,128,512]{2,1,0:T(8,128)(2,1)}, f32[8,512]{1,0:T(8,128)S(1)}) custom-call(s32[32]{0:T(128)S(1)} %select_reduce_fusion.2.serve, s32[32]{0:T(128)S(1)} %select_reduce_fusion.1.order, s32[9]{0:T(128)S(1)} %convert_reduce_fusion.1.ready, bf16[2048,512]{1,0:T(8,128)(2,1)S(1)} %get-tuple-element.41.begun, ...), custom_call_target="tpu_custom_call" | custom-call | tf_op jit(solution)/shard_map/far/pallas_call | solution.py:352
  63.3 4.9 %all-to-all-start.1 = ((bf16[32,128,512]{2,1,0:T(8,128)(2,1)}), bf16[32,128,512]{2,1,0:T(8,128)(2,1)}, u32[]{:S(2)}, u32[]{:S(2)}) async-start(bf16[32,128,512]{2,1,0:T(8,128)(2,1)} %get-tuple-element.43), calls=%async_computation.1 | async-start | bytes 8388608 | tf_op jit(solution)/shard_map/all_to_all | solution.py:327
  69.6 65.0 %all-to-all-done.1.fetched = bf16[32,128,512]{2,1,0:T(8,128)(2,1)} async-done(((bf16[32,128,512]{2,1,0:T(8,128)(2,1)}), bf16[32,128,512]{2,1,0:T(8,128)(2,1)}, u32[]{:S(2)}, u32[]{:S(2)}) %all-to-all-start.1) | async-done | bytes 4194336 | tf_op jit(solution)/shard_map/all_to_all | solution.py:327
  134.6 4.6 %scores.1 = (bf16[16,256,128]{2,1,0:T(8,128)(2,1)S(1)}, f32[32,128]{1,0:T(8,128)S(1)}, bf16[32,128,512]{2,1,0:T(8,128)(2,1)S(1)}) custom-call(s32[32]{0:T(128)S(1)} %get-tuple-element.32.need, s32[16,128]{1,0:T(8,128)S(1)} %subtract_bitcast_fusion.column, bf16[2048,512]{1,0:T(8,128)(2,1)S(1)} %get-tuple-element.42.anchors, ...), custom_call_target="tpu_custom_call" | custom-call | tf_op jit(solution)/shard_map/scores/pallas_call | solution.py:352
  139.4 3.2 %collective-permute-start.6 = (f32[32,128]{1,0:T(8,128)S(1)}, f32[32,128]{1,0:T(8,128)S(1)}, u32[]{:S(2)}, u32[]{:S(2)}) collective-permute-start(f32[32,128]{1,0:T(8,128)S(1)} %get-tuple-element.44.r_0_), channel_id=1, source_target_pairs={{0,3},{1,2},{2,1},{3,0},{4,7},{5,6},{6,5},{7,4},{8,11},{9,10},{10,... | collective-permute-start | bytes 49160 | tf_op jit(solution)/shard_map/ppermute | solution.py:323
  142.7 2.4 %mix.1 = (bf16[2048,512]{1,0:T(8,128)(2,1)S(1)}, bf16[2048,512]{1,0:T(8,128)(2,1)S(1)}) custom-call(s32[32]{0:T(128)S(1)} %get-tuple-element.32.need, s32[16,128]{1,0:T(8,128)S(1)} %subtract_bitcast_fusion.column, bf16[16,256,128]{2,1,0:T(8,128)(2,1)S(1)} %get-tuple-element.46.weights, bf16[32,128,512]{2,1,0:T(8,128)(2,1)S(1)} %get-tuple-element.47.partners), custom_call_target="tpu_custom_call" | custom-call | tf_op jit(solution)/shard_map/mix/pallas_call | solution.py:352
  145.1 2.1 shares.1
  147.5 1.6 beside.1
  149.7 1.6 across.1
  151.5 2.6 %collective-permute-start.10 = (bf16[512,512]{1,0:T(8,128)(2,1)S(1)}, bf16[512,512]{1,0:T(8,128)(2,1)S(1)}, u32[]{:S(2)}, u32[]{:S(2)}) collective-permute-start(bf16[512,512]{1,0:T(8,128)(2,1)S(1)} %add_convert_fusion), channel_id=1, source_target_pairs={{0,3},{1,2},{2,1},{3,0},{4,7},{5,6},{6,5},{7,4},{8,11},{9,10},{10,... | collective-permute-start | bytes 1572872 | tf_op jit(solution)/shard_map/ppermute | solution.py:323
  154.1 1.6 own.1.a
  155.7 10.9 %collective-permute-done.10.c = bf16[512,512]{1,0:T(8,128)(2,1)S(1)} collective-permute-done((bf16[512,512]{1,0:T(8,128)(2,1)S(1)}, bf16[512,512]{1,0:T(8,128)(2,1)S(1)}, u32[]{:S(2)}, u32[]{:S(2)}) %collective-permute-start.10) | collective-permute-done | bytes 524320 | tf_op jit(solution)/shard_map/ppermute | solution.py:323
  166.7 2.1 back.1
  168.7 9.0 %all-to-all-start.2 = ((bf16[128,8,512]{2,1,0:T(8,128)(2,1)}), bf16[128,8,512]{2,1,0:T(8,128)(2,1)S(1)}, u32[]{:S(2)}, u32[]{:S(2)}) async-start(bf16[128,8,512]{2,1,0:T(8,128)(2,1)} %bitcast.24), calls=%async_computation.2 | async-start | bytes 2097152 | tf_op jit(solution)/shard_map/all_to_all | solution.py:327
  177.8 1.7 stripes.1
  179.5 1.0 copy-done.1
  180.5 15.4 %all-to-all-done.2 = bf16[128,8,512]{2,1,0:T(8,128)(2,1)S(1)} async-done(((bf16[128,8,512]{2,1,0:T(8,128)(2,1)}), bf16[128,8,512]{2,1,0:T(8,128)(2,1)S(1)}, u32[]{:S(2)}, u32[]{:S(2)}) %all-to-all-start.2) | async-done | bytes 1048608 | tf_op jit(solution)/shard_map/all_to_all | solution.py:327
  195.9 2.2 unit_grad.1.grad
  198.9 1.2 collective-permute-done.12.partner
  200.1 1.7 head_grad.1
  201.8 5.6 %all-to-all-start.3 = ((bf16[64,16,512]{2,1,0:T(8,128)(2,1)}), bf16[64,16,512]{2,1,0:T(8,128)(2,1)S(1)}, u32[]{:S(2)}, u32[]{:S(2)}) async-start(bf16[64,16,512]{2,1,0:T(8,128)(2,1)} %bitcast.23), calls=%async_computation.3 | async-start | bytes 2097152 | tf_op jit(solution)/shard_map/all_to_all | solution.py:327
  207.4 1.7 collective-permute-start.7
  209.1 5.4 %collective-permute-done.7 = f32[2048]{0:T(1024)S(1)} collective-permute-done((f32[2048]{0:T(1024)S(1)}, f32[2048]{0:T(1024)S(1)}, u32[]{:S(2)}, u32[]{:S(2)}) %collective-permute-start.7) | collective-permute-done | bytes 8224 | tf_op jit(solution)/shard_map/ppermute | solution.py:323
  215.1 11.2 %all-to-all-done.3.parts = bf16[64,16,512]{2,1,0:T(8,128)(2,1)S(1)} async-done(((bf16[64,16,512]{2,1,0:T(8,128)(2,1)}), bf16[64,16,512]{2,1,0:T(8,128)(2,1)S(1)}, u32[]{:S(2)}, u32[]{:S(2)}) %all-to-all-start.3) | async-done | bytes 1048608 | tf_op jit(solution)/shard_map/all_to_all | solution.py:327
  (50 shorter events, 6.7 us)
Async XLA Ops:
  0.6 0.7 copy-start.3
  7.6 11.2 %copy-start.4 = (s32[512,8]{0,1:T(8,128)S(1)}, s32[512,8]{0,1:T(8,128)}, u32[]{:S(2)}) copy-start(s32[512,8]{0,1:T(8,128)} %param.8) | copy-start | bytes 49156
  7.6 31.5 %all-to-all-start = ((bf16[128,8,640]{2,1,0:T(8,128)(2,1)}), bf16[128,8,640]{2,1,0:T(8,128)(2,1)S(1)}, u32[]{:S(2)}, u32[]{:S(2)}) async-start(bf16[128,8,640]{2,1,0:T(8,128)(2,1)} %bitcast.1), calls=%async_computation | async-start | bytes 2621440 | tf_op jit(solution)/shard_map/all_to_all | solution.py:327
  40.3 2.0 collective-permute-start.1
  40.3 15.9 %collective-permute-start.2 = (bf16[528,512]{1,0:T(8,128)(2,1)S(1)}, bf16[528,512]{1,0:T(8,128)(2,1)S(1)}, u32[]{:S(2)}, u32[]{:S(2)}) collective-permute-start(bf16[528,512]{1,0:T(8,128)(2,1)S(1)} %get-tuple-element.37.own), channel_id=1, source_target_pairs={{0,3},{1,2},{2,1},{3,0},{4,7},{5,6},{6,5},{7,4},{8,11},{9,10},{10,... | collective-permute-start | bytes 1622024 | tf_op jit(solution)/shard_map/ppermute | solution.py:323
  56.2 2.5 %collective-permute-start.3 = (bf16[528,512]{1,0:T(8,128)(2,1)S(1)}, bf16[528,512]{1,0:T(8,128)(2,1)S(1)}, u32[]{:S(2)}, u32[]{:S(2)}) collective-permute-start(bf16[528,512]{1,0:T(8,128)(2,1)S(1)} %collective-permute-done.2.across), channel_id=1, source_target_pairs={{0,4},{4,0},{1,5},{5,1},{2,6},{6,2},{3,7},{7,3},{8,12},{12,8},{9,1... | collective-permute-start | bytes 1622024 | tf_op jit(solution)/shard_map/ppermute | solution.py:323
  63.3 4.9 %copy-start.5 = (s32[2048]{0:T(1024)S(1)}, s32[2048]{0:T(1024)}, u32[]{:S(2)}) copy-start(s32[2048]{0:T(1024)} %param.9) | copy-start | bytes 24580
  63.3 71.3 %all-to-all-start.1 = ((bf16[32,128,512]{2,1,0:T(8,128)(2,1)}), bf16[32,128,512]{2,1,0:T(8,128)(2,1)}, u32[]{:S(2)}, u32[]{:S(2)}) async-start(bf16[32,128,512]{2,1,0:T(8,128)(2,1)} %get-tuple-element.43), calls=%async_computation.1 | async-start | bytes 8388608 | tf_op jit(solution)/shard_map/all_to_all | solution.py:327
  68.2 1.5 collective-permute-start
  139.3 5.8 %collective-permute-start.4 = (f32[32,128]{1,0:T(8,128)S(1)}, f32[32,128]{1,0:T(8,128)S(1)}, u32[]{:S(2)}, u32[]{:S(2)}) collective-permute-start(f32[32,128]{1,0:T(8,128)S(1)} %get-tuple-element.44.r_0_), channel_id=1, source_target_pairs={{0,7},{1,6},{2,5},{3,4},{4,3},{5,2},{6,1},{7,0},{8,15},{9,14},{10,... | collective-permute-start | bytes 49160 | tf_op jit(solution)/shard_map/ppermute | solution.py:323
  139.3 5.8 %collective-permute-start.5 = (f32[32,128]{1,0:T(8,128)S(1)}, f32[32,128]{1,0:T(8,128)S(1)}, u32[]{:S(2)}, u32[]{:S(2)}) collective-permute-start(f32[32,128]{1,0:T(8,128)S(1)} %get-tuple-element.44.r_0_), channel_id=1, source_target_pairs={{0,4},{4,0},{1,5},{5,1},{2,6},{6,2},{3,7},{7,3},{8,12},{12,8},{9,1... | collective-permute-start | bytes 49160 | tf_op jit(solution)/shard_map/ppermute | solution.py:323
  139.4 5.7 %collective-permute-start.6 = (f32[32,128]{1,0:T(8,128)S(1)}, f32[32,128]{1,0:T(8,128)S(1)}, u32[]{:S(2)}, u32[]{:S(2)}) collective-permute-start(f32[32,128]{1,0:T(8,128)S(1)} %get-tuple-element.44.r_0_), channel_id=1, source_target_pairs={{0,3},{1,2},{2,1},{3,0},{4,7},{5,6},{6,5},{7,4},{8,11},{9,10},{10,... | collective-permute-start | bytes 49160 | tf_op jit(solution)/shard_map/ppermute | solution.py:323
  147.3 4.1 %collective-permute-start.9 = (bf16[512,512]{1,0:T(8,128)(2,1)S(1)}, bf16[512,512]{1,0:T(8,128)(2,1)S(1)}, u32[]{:S(2)}, u32[]{:S(2)}) collective-permute-start(bf16[512,512]{1,0:T(8,128)(2,1)S(1)} %get-tuple-element.54), channel_id=1, source_target_pairs={{0,4},{4,0},{1,5},{5,1},{2,6},{6,2},{3,7},{7,3},{8,12},{12,8},{9,1... | collective-permute-start | bytes 1572872 | tf_op jit(solution)/shard_map/ppermute | solution.py:323
  149.2 6.5 %collective-permute-start.8 = (bf16[512,512]{1,0:T(8,128)(2,1)S(1)}, bf16[512,512]{1,0:T(8,128)(2,1)S(1)}, u32[]{:S(2)}, u32[]{:S(2)}) collective-permute-start(bf16[512,512]{1,0:T(8,128)(2,1)S(1)} %beside.1), channel_id=1, source_target_pairs={{0,4},{4,0},{1,5},{5,1},{2,6},{6,2},{3,7},{7,3},{8,12},{12,8},{9,1... | collective-permute-start | bytes 1572872 | tf_op jit(solution)/shard_map/ppermute | solution.py:323
  151.5 15.1 %collective-permute-start.10 = (bf16[512,512]{1,0:T(8,128)(2,1)S(1)}, bf16[512,512]{1,0:T(8,128)(2,1)S(1)}, u32[]{:S(2)}, u32[]{:S(2)}) collective-permute-start(bf16[512,512]{1,0:T(8,128)(2,1)S(1)} %add_convert_fusion), channel_id=1, source_target_pairs={{0,3},{1,2},{2,1},{3,0},{4,7},{5,6},{6,5},{7,4},{8,11},{9,10},{10,... | collective-permute-start | bytes 1572872 | tf_op jit(solution)/shard_map/ppermute | solution.py:323
  166.7 11.1 %copy-start = (bf16[512,2048]{1,0:T(8,128)(2,1)S(1)}, bf16[512,2048]{1,0:T(8,128)(2,1)}, u32[]{:S(2)}) copy-start(bf16[512,2048]{1,0:T(8,128)(2,1)} %r_1_.3) | copy-start | bytes 6291460
  168.7 27.2 %all-to-all-start.2 = ((bf16[128,8,512]{2,1,0:T(8,128)(2,1)}), bf16[128,8,512]{2,1,0:T(8,128)(2,1)S(1)}, u32[]{:S(2)}, u32[]{:S(2)}) async-start(bf16[128,8,512]{2,1,0:T(8,128)(2,1)} %bitcast.24), calls=%async_computation.2 | async-start | bytes 2097152 | tf_op jit(solution)/shard_map/all_to_all | solution.py:327
  179.5 1.0 copy-start.1
  180.5 17.8 %copy-start.2 = (bf16[1024,512]{1,0:T(8,128)(2,1)S(1)}, bf16[1024,512]{1,0:T(8,128)(2,1)}, u32[]{:S(2)}) copy-start(bf16[1024,512]{1,0:T(8,128)(2,1)} %copy-done.1) | copy-start | bytes 3145732
  180.5 18.5 %collective-permute-start.11 = (bf16[1024,512]{1,0:T(8,128)(2,1)}, bf16[1024,512]{1,0:T(8,128)(2,1)S(1)}, u32[]{:S(2)}, u32[]{:S(2)}) collective-permute-start(bf16[1024,512]{1,0:T(8,128)(2,1)} %get-tuple-element.59), channel_id=1, source_target_pairs={{0,4},{4,0},{1,5},{5,1},{2,6},{6,2},{3,7},{7,3},{8,12},{12,8},{9,1... | collective-permute-start | bytes 3145736 | tf_op jit(solution)/shard_map/ppermute | solution.py:323
  198.1 2.0 collective-permute-start.12
  201.8 24.4 %all-to-all-start.3 = ((bf16[64,16,512]{2,1,0:T(8,128)(2,1)}), bf16[64,16,512]{2,1,0:T(8,128)(2,1)S(1)}, u32[]{:S(2)}, u32[]{:S(2)}) async-start(bf16[64,16,512]{2,1,0:T(8,128)(2,1)} %bitcast.23), calls=%async_computation.3 | async-start | bytes 2097152 | tf_op jit(solution)/shard_map/all_to_all | solution.py:327
  207.4 7.0 %collective-permute-start.7 = (f32[2048]{0:T(1024)S(1)}, f32[2048]{0:T(1024)S(1)}, u32[]{:S(2)}, u32[]{:S(2)}) collective-permute-start(f32[2048]{0:T(1024)S(1)} %fusion.9), channel_id=1, source_target_pairs={{0,1},{1,0},{2,3},{3,2},{4,5},{5,4},{6,7},{7,6},{8,9},{9,8},{10,11... | collective-permute-start | bytes 24584 | tf_op jit(solution)/shard_map/ppermute | solution.py:323

commit v8 on v7

--- a/solution.py
+++ b/solution.py
@@ -131,7 +131,7 @@
             other[at : at + rows, :] = there[y * rows : (y + 1) * rows, :]
 
 
-def compact_kernel(got, packed, place):
+def compact_kernel(got, positives, packed, place):
     count = got.shape[0]
     e = packed.shape[1]
     rows = packed.shape[0] - 16
@@ -143,7 +143,11 @@
     place[...] = jnp.broadcast_to(pos, place.shape)
     pick = hot(iota((rows, count), 0) == pos.astype(I32))
     packed[:rows, :] = dot(pick, got[:, :e]).astype(BF)
-    packed[rows:, :] = dot(tags[:16, :].astype(BF), pick, 1, 1).astype(BF)
+    slot = dot(tags[:16, :].astype(BF), pick, 1, 1)
+    high = positives[...] // BR
+    low = positives[...] - high * BR
+    spare = [slot[:4, :], high.astype(F32), low.astype(F32), jnp.zeros((4, e), F32)]
+    packed[rows:, :] = jnp.concatenate(spare, axis=0).astype(BF)
 
 
 def slot_row(tag):
@@ -169,7 +173,7 @@
     lax.fori_loop(0, out.shape[0] // step, body, 0)
 
 
-def near_kernel(own, beside, partial, slots):
+def near_kernel(own, beside, partial, slots, positives):
     n = own.shape[0] - 16
     pieces = []
     for k, ref in enumerate((own, beside)):
@@ -177,6 +181,12 @@
         slots[k, :, :] = jnp.broadcast_to(row, slots.shape[1:])
         pieces.append((row.astype(I32), ref[:n, :]))
     place_rows(partial, pieces, None)
+    spare = beside[n:, :].astype(F32)
+    digits = (spare[4:8, :] * BR + spare[8:12, :]).astype(I32)
+    lanes = digits.shape[1] // BR
+    for i in range(positives.shape[0]):
+        at = slice((i % lanes) * BR, (i % lanes + 1) * BR)
+        positives[i : i + 1, :] = digits[i // lanes : i // lanes + 1, at]
 
 
 def middle_kernel(begun, across, partial, slots):
@@ -399,8 +409,6 @@
         jnp.where(fetch_place(numbers)[None, :] == numbers[:, None], wanted[None, :], 0), axis=1
     )
     need = fetch_place(lax.dynamic_index_in_dim(owner, me, axis=0, keepdims=False))
-    column = jnp.where(home, positives, swap(positives)).reshape(blocks, BR)
-    column = column - member * (PAIRS_REP * BR)
     keys = serve * dp + numbers
     place_of = jnp.sum((keys[None, :] < keys[:, None]).astype(I32), axis=1)
     order = jnp.sum(jnp.where(place_of[None, :] == numbers[:, None], numbers[None, :], 0), axis=1)
@@ -409,21 +417,23 @@
 
     got, serve, order, ready, need = lax.optimization_barrier((got, serve, order, ready, need))
     packed, back_place = call(
-        compact_kernel, "compact", (sds((n + 16, e), BF), sds((8, count), F32)), (got,)
+        compact_kernel, "compact", (sds((n + 16, e), BF), sds((8, count), F32)), (got, positives.reshape(4, e))
     )
     beside = swap(packed)
     across = swap(packed, ("yhi", "ylo"))
 
     whole = sds((owner_slots, e), BF)
     ids_shape = sds((8, n), F32)
-    partial, slots = call(
+    partial, slots, other_positives = call(
         near_kernel,
         "near",
-        (whole, sds((2, 8, n), F32)),
+        (whole, sds((2, 8, n), F32), sds((blocks, BR), I32)),
         (packed, beside),
         cost_estimate=cost(4),
     )
     partial, across = lax.optimization_barrier((partial, across))
+    column = jnp.where(home, positives.reshape(blocks, BR), other_positives)
+    column = column - member * (PAIRS_REP * BR)
     corner = swap(across)
     partial, slots_across = call(middle_kernel, "middle", (whole, ids_shape), (partial, across))
     anchors, served, slots_corner = call(

time: 227 us -> 225 us (level); the launches traced: 227 us -> 222 us
  waiting for transfers between devices: 139 us -> 136 us
    all_to_all x4, waiting for transfers between devices: 111 us -> 108 us  [exchange(): return lax.all_to_all(x, axes, 0, 0, tiled=True)]
    ppermute x13 -> x12, starting transfers between devices: 11.1 us -> 10.4 us  [swap(): return lax.ppermute(x, axes, [(i, size - 1 - i) for i in range(size)])]
    ppermute x13 -> x12, waiting for transfers between devices: 28.7 us -> 28.1 us  [swap(): return lax.ppermute(x, axes, [(i, size - 1 - i) for i in range(size)])]
  transfers between devices with their start and end apart: 17 -> 16, of which waited for: 10 -> 10; matrix products, arithmetic and copies ran while one was open for 1% -> 1% of each run, Pallas kernels for 8% -> 8%
where the time goes in v8:
time: 225 us; the launch traced here: 222 us
  waiting for transfers between devices  136 us (60%)
  Pallas kernels  41.4 us (18%)
  starting transfers between devices  40.3 us (18%)
    all_to_all x4, waiting for transfers between devices, exchange(): return lax.all_to_all(x, axes, 0, 0, tiled=True)  108 us
    pallas_call x17, Pallas kernels, call(): pl.pallas_call(kernel, out_shape=shapes, compiler_params=params(), name=n...  41.4 us
    all_to_all x4, starting transfers between devices, exchange(): return lax.all_to_all(x, axes, 0, 0, tiled=True)  29.9 us
    ppermute x12, waiting for transfers between devices, swap(): return lax.ppermute(x, axes, [(i, size - 1 - i) for i in range(size)])  28.1 us
    ppermute x12, starting transfers between devices, swap(): return lax.ppermute(x, axes, [(i, size - 1 - i) for i in range(size)])  10.4 us
  transfers between devices with their start and end apart: 16, of which 10 were waited for; matrix products, arithmetic and copies ran while one was open for 1% of the time, Pallas kernels for 8%

profile of v8, /device:TPU:0, one launch (start us, length us, event | category | flops | bytes accessed | tf_op | source)
XLA Modules:
  0.0 222.5 jit_solution(1424178769242214878)
XLA Ops:
  1.3 6.3 %project.1 = (bf16[1024,640]{1,0:T(8,128)(2,1)}, f32[512,512]{1,0:T(8,128)}, f32[512,128]{1,0:T(8,128)S(1)}, f32[8,512]{1,0:T(8,128)S(1)}) custom-call(s32[1,512]{1,0:T(1,128)S(1)} %bitcast.24, bf16[512,2048]{1,0:T(8,128)(2,1)} %r_1_.3, bf16[2048,512]{1,0:T(8,128)(2,1)} %r_2_.1), custom_call_target="tpu_custom_call" | custom-call | tf_op jit(solution)/shard_map/project/pallas_call | solution.py:362
  7.6 11.2 %all-to-all-start = ((bf16[128,8,640]{2,1,0:T(8,128)(2,1)}), bf16[128,8,640]{2,1,0:T(8,128)(2,1)S(1)}, u32[]{:S(2)}, u32[]{:S(2)}) async-start(bf16[128,8,640]{2,1,0:T(8,128)(2,1)} %bitcast.1), calls=%async_computation | async-start | bytes 2621440 | tf_op jit(solution)/shard_map/all_to_all | solution.py:337
  20.0 19.2 %all-to-all-done = bf16[128,8,640]{2,1,0:T(8,128)(2,1)S(1)} async-done(((bf16[128,8,640]{2,1,0:T(8,128)(2,1)}), bf16[128,8,640]{2,1,0:T(8,128)(2,1)S(1)}, u32[]{:S(2)}, u32[]{:S(2)}) %all-to-all-start) | async-done | bytes 1310752 | tf_op jit(solution)/shard_map/all_to_all | solution.py:337
  39.2 1.2 compact.1
  40.3 1.9 collective-permute-start.1
  42.3 3.6 %near.1 = (bf16[2048,512]{1,0:T(8,128)(2,1)S(1)}, f32[2,8,512]{2,1,0:T(8,128)S(1)}, s32[16,128]{1,0:T(8,128)S(1)}) custom-call(bf16[528,512]{1,0:T(8,128)(2,1)S(1)} %get-tuple-element.35.own, bf16[528,512]{1,0:T(8,128)(2,1)S(1)} %collective-permute-done.beside), custom_call_target="tpu_custom_call" | custom-call | flops 4000000000 | bytes 4000000 | tf_op jit(solution)/shard_map/near/pallas_call | solution.py:362
  45.9 10.3 %collective-permute-done.1.across = bf16[528,512]{1,0:T(8,128)(2,1)S(1)} collective-permute-done((bf16[528,512]{1,0:T(8,128)(2,1)S(1)}, bf16[528,512]{1,0:T(8,128)(2,1)S(1)}, u32[]{:S(2)}, u32[]{:S(2)}) %collective-permute-start.1) | collective-permute-done | bytes 540704 | tf_op jit(solution)/shard_map/ppermute | solution.py:333
  56.3 2.5 %middle.1 = (bf16[2048,512]{1,0:T(8,128)(2,1)S(1)}, f32[8,512]{1,0:T(8,128)S(1)}) custom-call(bf16[2048,512]{1,0:T(8,128)(2,1)S(1)} %get-tuple-element.41.begun, bf16[528,512]{1,0:T(8,128)(2,1)S(1)} %collective-permute-done.1.across), custom_call_target="tpu_custom_call" | custom-call | tf_op jit(solution)/shard_map/middle/pallas_call | solution.py:362
  58.8 4.6 %far.1 = (bf16[2048,512]{1,0:T(8,128)(2,1)S(1)}, bf16[32,128,512]{2,1,0:T(8,128)(2,1)}, f32[8,512]{1,0:T(8,128)S(1)}) custom-call(s32[32]{0:T(128)S(1)} %select_reduce_fusion.2.serve, s32[32]{0:T(128)S(1)} %select_reduce_fusion.1.order, s32[9]{0:T(128)S(1)} %convert_reduce_fusion.1.ready, bf16[2048,512]{1,0:T(8,128)(2,1)S(1)} %get-tuple-element.43.begun, ...), custom_call_target="tpu_custom_call" | custom-call | tf_op jit(solution)/shard_map/far/pallas_call | solution.py:362
  63.4 4.9 %all-to-all-start.1 = ((bf16[32,128,512]{2,1,0:T(8,128)(2,1)}), bf16[32,128,512]{2,1,0:T(8,128)(2,1)}, u32[]{:S(2)}, u32[]{:S(2)}) async-start(bf16[32,128,512]{2,1,0:T(8,128)(2,1)} %get-tuple-element.45), calls=%async_computation.1 | async-start | bytes 8388608 | tf_op jit(solution)/shard_map/all_to_all | solution.py:337
  68.3 62.4 %all-to-all-done.1.fetched = bf16[32,128,512]{2,1,0:T(8,128)(2,1)} async-done(((bf16[32,128,512]{2,1,0:T(8,128)(2,1)}), bf16[32,128,512]{2,1,0:T(8,128)(2,1)}, u32[]{:S(2)}, u32[]{:S(2)}) %all-to-all-start.1) | async-done | bytes 4194336 | tf_op jit(solution)/shard_map/all_to_all | solution.py:337
  130.7 4.6 %scores.1 = (bf16[16,256,128]{2,1,0:T(8,128)(2,1)S(1)}, f32[32,128]{1,0:T(8,128)S(1)}, bf16[32,128,512]{2,1,0:T(8,128)(2,1)S(1)}) custom-call(s32[32]{0:T(128)S(1)} %get-tuple-element.33.need, s32[16,128]{1,0:T(8,128)S(1)} %fusion.10.column, bf16[2048,512]{1,0:T(8,128)(2,1)S(1)} %get-tuple-element.44.anchors, bf16[32,128,512]{2,1,0:T(8,128)(2,1)} %all-to-all-done.1.fetched), custom_call_target="tpu_custom_call" | custom-call | tf_op jit(solution)/shard_map/scores/pallas_call | solution.py:362
  136.4 2.4 %collective-permute-start.5 = (f32[32,128]{1,0:T(8,128)S(1)}, f32[32,128]{1,0:T(8,128)S(1)}, u32[]{:S(2)}, u32[]{:S(2)}) collective-permute-start(f32[32,128]{1,0:T(8,128)S(1)} %get-tuple-element.46.r_0_), channel_id=1, source_target_pairs={{0,3},{1,2},{2,1},{3,0},{4,7},{5,6},{6,5},{7,4},{8,11},{9,10},{10,... | collective-permute-start | bytes 49160 | tf_op jit(solution)/shard_map/ppermute | solution.py:333
  138.8 2.4 %mix.1 = (bf16[2048,512]{1,0:T(8,128)(2,1)S(1)}, bf16[2048,512]{1,0:T(8,128)(2,1)S(1)}) custom-call(s32[32]{0:T(128)S(1)} %get-tuple-element.33.need, s32[16,128]{1,0:T(8,128)S(1)} %fusion.10.column, bf16[16,256,128]{2,1,0:T(8,128)(2,1)S(1)} %get-tuple-element.48.weights, bf16[32,128,512]{2,1,0:T(8,128)(2,1)S(1)} %get-tuple-element.49.partners), custom_call_target="tpu_custom_call" | custom-call | tf_op jit(solution)/shard_map/mix/pallas_call | solution.py:362
  141.3 2.1 shares.1
  143.5 1.6 beside.1
  145.9 1.6 across.1
  147.7 2.5 %collective-permute-start.9 = (bf16[512,512]{1,0:T(8,128)(2,1)S(1)}, bf16[512,512]{1,0:T(8,128)(2,1)S(1)}, u32[]{:S(2)}, u32[]{:S(2)}) collective-permute-start(bf16[512,512]{1,0:T(8,128)(2,1)S(1)} %add_convert_fusion), channel_id=1, source_target_pairs={{0,3},{1,2},{2,1},{3,0},{4,7},{5,6},{6,5},{7,4},{8,11},{9,10},{10,... | collective-permute-start | bytes 1572872 | tf_op jit(solution)/shard_map/ppermute | solution.py:333
  150.2 1.6 own.1.a
  151.8 11.0 %collective-permute-done.9.c = bf16[512,512]{1,0:T(8,128)(2,1)S(1)} collective-permute-done((bf16[512,512]{1,0:T(8,128)(2,1)S(1)}, bf16[512,512]{1,0:T(8,128)(2,1)S(1)}, u32[]{:S(2)}, u32[]{:S(2)}) %collective-permute-start.9) | collective-permute-done | bytes 524320 | tf_op jit(solution)/shard_map/ppermute | solution.py:333
  162.8 2.1 back.1
  164.9 8.3 %all-to-all-start.2 = ((bf16[128,8,512]{2,1,0:T(8,128)(2,1)}), bf16[128,8,512]{2,1,0:T(8,128)(2,1)S(1)}, u32[]{:S(2)}, u32[]{:S(2)}) async-start(bf16[128,8,512]{2,1,0:T(8,128)(2,1)} %bitcast.26), calls=%async_computation.2 | async-start | bytes 2097152 | tf_op jit(solution)/shard_map/all_to_all | solution.py:337
  173.2 1.7 stripes.1
  174.9 1.0 copy-done.1
  175.9 15.4 %all-to-all-done.2 = bf16[128,8,512]{2,1,0:T(8,128)(2,1)S(1)} async-done(((bf16[128,8,512]{2,1,0:T(8,128)(2,1)}), bf16[128,8,512]{2,1,0:T(8,128)(2,1)S(1)}, u32[]{:S(2)}, u32[]{:S(2)}) %all-to-all-start.2) | async-done | bytes 1048608 | tf_op jit(solution)/shard_map/all_to_all | solution.py:337
  191.3 2.2 unit_grad.1.grad
  194.4 1.2 collective-permute-done.11.partner
  195.5 1.7 head_grad.1
  197.2 5.6 %all-to-all-start.3 = ((bf16[64,16,512]{2,1,0:T(8,128)(2,1)}), bf16[64,16,512]{2,1,0:T(8,128)(2,1)S(1)}, u32[]{:S(2)}, u32[]{:S(2)}) async-start(bf16[64,16,512]{2,1,0:T(8,128)(2,1)} %bitcast.25), calls=%async_computation.3 | async-start | bytes 2097152 | tf_op jit(solution)/shard_map/all_to_all | solution.py:337
  202.9 1.7 collective-permute-start.6
  204.5 5.4 %collective-permute-done.6 = f32[2048]{0:T(1024)S(1)} collective-permute-done((f32[2048]{0:T(1024)S(1)}, f32[2048]{0:T(1024)S(1)}, u32[]{:S(2)}, u32[]{:S(2)}) %collective-permute-start.6) | collective-permute-done | bytes 8224 | tf_op jit(solution)/shard_map/ppermute | solution.py:333
  210.5 11.2 %all-to-all-done.3.parts = bf16[64,16,512]{2,1,0:T(8,128)(2,1)S(1)} async-done(((bf16[64,16,512]{2,1,0:T(8,128)(2,1)}), bf16[64,16,512]{2,1,0:T(8,128)(2,1)S(1)}, u32[]{:S(2)}, u32[]{:S(2)}) %all-to-all-start.3) | async-done | bytes 1048608 | tf_op jit(solution)/shard_map/all_to_all | solution.py:337
  (49 shorter events, 6.2 us)
Async XLA Ops:
  0.6 0.7 copy-start.3
  7.6 11.2 %copy-start.5 = (s32[512,8]{0,1:T(8,128)S(1)}, s32[512,8]{0,1:T(8,128)}, u32[]{:S(2)}) copy-start(s32[512,8]{0,1:T(8,128)} %param.8) | copy-start | bytes 49156
  7.6 11.5 %copy-start.4 = (s32[2048]{0:T(1024)S(1)}, s32[2048]{0:T(1024)}, u32[]{:S(2)}) copy-start(s32[2048]{0:T(1024)} %param.9) | copy-start | bytes 24580
  7.6 31.5 %all-to-all-start = ((bf16[128,8,640]{2,1,0:T(8,128)(2,1)}), bf16[128,8,640]{2,1,0:T(8,128)(2,1)S(1)}, u32[]{:S(2)}, u32[]{:S(2)}) async-start(bf16[128,8,640]{2,1,0:T(8,128)(2,1)} %bitcast.1), calls=%async_computation | async-start | bytes 2621440 | tf_op jit(solution)/shard_map/all_to_all | solution.py:337
  40.3 1.9 collective-permute-start
  40.3 15.9 %collective-permute-start.1 = (bf16[528,512]{1,0:T(8,128)(2,1)S(1)}, bf16[528,512]{1,0:T(8,128)(2,1)S(1)}, u32[]{:S(2)}, u32[]{:S(2)}) collective-permute-start(bf16[528,512]{1,0:T(8,128)(2,1)S(1)} %get-tuple-element.35.own), channel_id=1, source_target_pairs={{0,3},{1,2},{2,1},{3,0},{4,7},{5,6},{6,5},{7,4},{8,11},{9,10},{10,... | collective-permute-start | bytes 1622024 | tf_op jit(solution)/shard_map/ppermute | solution.py:333
  56.2 2.5 %collective-permute-start.2 = (bf16[528,512]{1,0:T(8,128)(2,1)S(1)}, bf16[528,512]{1,0:T(8,128)(2,1)S(1)}, u32[]{:S(2)}, u32[]{:S(2)}) collective-permute-start(bf16[528,512]{1,0:T(8,128)(2,1)S(1)} %collective-permute-done.1.across), channel_id=1, source_target_pairs={{0,4},{4,0},{1,5},{5,1},{2,6},{6,2},{3,7},{7,3},{8,12},{12,8},{9,1... | collective-permute-start | bytes 1622024 | tf_op jit(solution)/shard_map/ppermute | solution.py:333
  63.4 67.3 %all-to-all-start.1 = ((bf16[32,128,512]{2,1,0:T(8,128)(2,1)}), bf16[32,128,512]{2,1,0:T(8,128)(2,1)}, u32[]{:S(2)}, u32[]{:S(2)}) async-start(bf16[32,128,512]{2,1,0:T(8,128)(2,1)} %get-tuple-element.45), calls=%async_computation.1 | async-start | bytes 8388608 | tf_op jit(solution)/shard_map/all_to_all | solution.py:337
  135.3 5.8 %collective-permute-start.3 = (f32[32,128]{1,0:T(8,128)S(1)}, f32[32,128]{1,0:T(8,128)S(1)}, u32[]{:S(2)}, u32[]{:S(2)}) collective-permute-start(f32[32,128]{1,0:T(8,128)S(1)} %get-tuple-element.46.r_0_), channel_id=1, source_target_pairs={{0,7},{1,6},{2,5},{3,4},{4,3},{5,2},{6,1},{7,0},{8,15},{9,14},{10,... | collective-permute-start | bytes 49160 | tf_op jit(solution)/shard_map/ppermute | solution.py:333
  135.4 5.8 %collective-permute-start.4 = (f32[32,128]{1,0:T(8,128)S(1)}, f32[32,128]{1,0:T(8,128)S(1)}, u32[]{:S(2)}, u32[]{:S(2)}) collective-permute-start(f32[32,128]{1,0:T(8,128)S(1)} %get-tuple-element.46.r_0_), channel_id=1, source_target_pairs={{0,4},{4,0},{1,5},{5,1},{2,6},{6,2},{3,7},{7,3},{8,12},{12,8},{9,1... | collective-permute-start | bytes 49160 | tf_op jit(solution)/shard_map/ppermute | solution.py:333
  136.4 4.9 %collective-permute-start.5 = (f32[32,128]{1,0:T(8,128)S(1)}, f32[32,128]{1,0:T(8,128)S(1)}, u32[]{:S(2)}, u32[]{:S(2)}) collective-permute-start(f32[32,128]{1,0:T(8,128)S(1)} %get-tuple-element.46.r_0_), channel_id=1, source_target_pairs={{0,3},{1,2},{2,1},{3,0},{4,7},{5,6},{6,5},{7,4},{8,11},{9,10},{10,... | collective-permute-start | bytes 49160 | tf_op jit(solution)/shard_map/ppermute | solution.py:333
  143.4 4.1 %collective-permute-start.8 = (bf16[512,512]{1,0:T(8,128)(2,1)S(1)}, bf16[512,512]{1,0:T(8,128)(2,1)S(1)}, u32[]{:S(2)}, u32[]{:S(2)}) collective-permute-start(bf16[512,512]{1,0:T(8,128)(2,1)S(1)} %get-tuple-element.56), channel_id=1, source_target_pairs={{0,4},{4,0},{1,5},{5,1},{2,6},{6,2},{3,7},{7,3},{8,12},{12,8},{9,1... | collective-permute-start | bytes 1572872 | tf_op jit(solution)/shard_map/ppermute | solution.py:333
  145.2 6.6 %collective-permute-start.7 = (bf16[512,512]{1,0:T(8,128)(2,1)S(1)}, bf16[512,512]{1,0:T(8,128)(2,1)S(1)}, u32[]{:S(2)}, u32[]{:S(2)}) collective-permute-start(bf16[512,512]{1,0:T(8,128)(2,1)S(1)} %beside.1), channel_id=1, source_target_pairs={{0,4},{4,0},{1,5},{5,1},{2,6},{6,2},{3,7},{7,3},{8,12},{12,8},{9,1... | collective-permute-start | bytes 1572872 | tf_op jit(solution)/shard_map/ppermute | solution.py:333
  147.7 15.1 %collective-permute-start.9 = (bf16[512,512]{1,0:T(8,128)(2,1)S(1)}, bf16[512,512]{1,0:T(8,128)(2,1)S(1)}, u32[]{:S(2)}, u32[]{:S(2)}) collective-permute-start(bf16[512,512]{1,0:T(8,128)(2,1)S(1)} %add_convert_fusion), channel_id=1, source_target_pairs={{0,3},{1,2},{2,1},{3,0},{4,7},{5,6},{6,5},{7,4},{8,11},{9,10},{10,... | collective-permute-start | bytes 1572872 | tf_op jit(solution)/shard_map/ppermute | solution.py:333
  162.8 10.4 %copy-start = (bf16[512,2048]{1,0:T(8,128)(2,1)S(1)}, bf16[512,2048]{1,0:T(8,128)(2,1)}, u32[]{:S(2)}) copy-start(bf16[512,2048]{1,0:T(8,128)(2,1)} %r_1_.3) | copy-start | bytes 6291460
  164.9 26.4 %all-to-all-start.2 = ((bf16[128,8,512]{2,1,0:T(8,128)(2,1)}), bf16[128,8,512]{2,1,0:T(8,128)(2,1)S(1)}, u32[]{:S(2)}, u32[]{:S(2)}) async-start(bf16[128,8,512]{2,1,0:T(8,128)(2,1)} %bitcast.26), calls=%async_computation.2 | async-start | bytes 2097152 | tf_op jit(solution)/shard_map/all_to_all | solution.py:337
  174.9 1.0 copy-start.1
  175.9 17.7 %copy-start.2 = (bf16[1024,512]{1,0:T(8,128)(2,1)S(1)}, bf16[1024,512]{1,0:T(8,128)(2,1)}, u32[]{:S(2)}) copy-start(bf16[1024,512]{1,0:T(8,128)(2,1)} %copy-done.1) | copy-start | bytes 3145732
  175.9 18.5 %collective-permute-start.10 = (bf16[1024,512]{1,0:T(8,128)(2,1)}, bf16[1024,512]{1,0:T(8,128)(2,1)S(1)}, u32[]{:S(2)}, u32[]{:S(2)}) collective-permute-start(bf16[1024,512]{1,0:T(8,128)(2,1)} %get-tuple-element.61), channel_id=1, source_target_pairs={{0,4},{4,0},{1,5},{5,1},{2,6},{6,2},{3,7},{7,3},{8,12},{12,8},{9,1... | collective-permute-start | bytes 3145736 | tf_op jit(solution)/shard_map/ppermute | solution.py:333
  193.5 2.0 collective-permute-start.11
  197.2 24.4 %all-to-all-start.3 = ((bf16[64,16,512]{2,1,0:T(8,128)(2,1)}), bf16[64,16,512]{2,1,0:T(8,128)(2,1)S(1)}, u32[]{:S(2)}, u32[]{:S(2)}) async-start(bf16[64,16,512]{2,1,0:T(8,128)(2,1)} %bitcast.25), calls=%async_computation.3 | async-start | bytes 2097152 | tf_op jit(solution)/shard_map/all_to_all | solution.py:337
  202.9 7.0 %collective-permute-start.6 = (f32[2048]{0:T(1024)S(1)}, f32[2048]{0:T(1024)S(1)}, u32[]{:S(2)}, u32[]{:S(2)}) collective-permute-start(f32[2048]{0:T(1024)S(1)} %fusion.9), channel_id=1, source_target_pairs={{0,1},{1,0},{2,3},{3,2},{4,5},{5,4},{6,7},{7,6},{8,9},{9,8},{10,11... | collective-permute-start | bytes 24584 | tf_op jit(solution)/shard_map/ppermute | solution.py:333

commit v9 on v8

--- a/solution.py
+++ b/solution.py
@@ -381,15 +381,15 @@
             pltpu.SemaphoreType.DMA((9,)),
         ],
     )
-    got = exchange(send.reshape(devices, cap, e + BR), DISPATCH).reshape(count, e + BR)
-
+    send, late_features = lax.optimization_barrier((send, features))
     mine, other = call(
         lambda *r: stripes_kernel(sizes, *r),
         "stripes",
         (sds((width // 2, n), BF),) * 2,
-        (core.reshape(1), features),
+        (core.reshape(1), late_features),
         in_specs=[smem, vmem],
     )
+    got = exchange(send.reshape(devices, cap, e + BR), DISPATCH).reshape(count, e + BR)
     theirs = swap(other)
 
     table = candidates.reshape(dp, blocks, REPS, PAIRS_REP)
@@ -415,7 +415,9 @@
     bounds = 2 * jnp.arange(blocks // 2 + 1, dtype=I32)
     ready = jnp.sum((serve[None, :] < bounds[:, None]).astype(I32), axis=1)
 
-    got, serve, order, ready, need = lax.optimization_barrier((got, serve, order, ready, need))
+    got, serve, order, ready, need, mine, theirs = lax.optimization_barrier(
+        (got, serve, order, ready, need, mine, theirs)
+    )
     packed, back_place = call(
         compact_kernel, "compact", (sds((n + 16, e), BF), sds((8, count), F32)), (got, positives.reshape(4, e))
     )
@@ -431,9 +433,9 @@
         (packed, beside),
         cost_estimate=cost(4),
     )
-    partial, across = lax.optimization_barrier((partial, across))
     column = jnp.where(home, positives.reshape(blocks, BR), other_positives)
     column = column - member * (PAIRS_REP * BR)
+    partial, across, column = lax.optimization_barrier((partial, across, column))
     corner = swap(across)
     partial, slots_across = call(middle_kernel, "middle", (whole, ids_shape), (partial, across))
     anchors, served, slots_corner = call(
@@ -480,20 +482,23 @@
 
     for_across = pick("across", share, slots_across).astype(F32) + swap(for_corner).astype(F32)
     from_across = swap(for_across.astype(BF), ("yhi", "ylo"))
+    own = pick("own", share, slots[0])
     from_beside = swap(pick("beside", share, slots[1]))
-    back = call(
-        back_kernel,
-        "back",
-        pltpu.HBM((count, e), BF),
-        (pick("own", share, slots[0]), from_beside, from_across, back_place),
-    )
-    returned = exchange(back.reshape(devices, cap, e), DISPATCH).reshape(count, e)
-
     both = (spread[0] + spread[3]) + (spread[1] + spread[2])
     rest, matching = both[:blocks], both[blocks:]
     total = rest + jnp.exp(matching - 1.0 / logit_sharpness)
     loss = (jnp.log(total) + 1.0 / logit_sharpness - matching).reshape(owner_slots)
     anchor_row_loss = jnp.where(home, loss, swap(loss, ("ylo",)))
+    own, from_beside, anchor_row_loss = lax.optimization_barrier(
+        (own, from_beside, anchor_row_loss)
+    )
+    back = call(
+        back_kernel,
+        "back",
+        pltpu.HBM((count, e), BF),
+        (own, from_beside, from_across, back_place),
+    )
+    returned = exchange(back.reshape(devices, cap, e), DISPATCH).reshape(count, e)
 
     grad = call(
         unit_grad_kernel,

time: 225 us -> 209 us (0.929)
  blocking collectives: 0 us -> 106 us
  waiting for transfers between devices: 136 us -> 39.3 us
  starting transfers between devices: 40.3 us -> 18.8 us
  Pallas kernels: 41.4 us -> 38 us
    all_to_all x0 -> x3, blocking collectives: none -> 106 us  [exchange(): return lax.all_to_all(x, axes, 0, 0, tiled=True)]
    all_to_all x4 -> x1, waiting for transfers between devices: 108 us -> 14.8 us  [exchange(): return lax.all_to_all(x, axes, 0, 0, tiled=True)]
    all_to_all x4 -> x1, starting transfers between devices: 29.9 us -> 11.1 us  [exchange(): return lax.all_to_all(x, axes, 0, 0, tiled=True)]
    ppermute x12, waiting for transfers between devices: 28.1 us -> 24.5 us  [swap(): return lax.ppermute(x, axes, [(i, size - 1 - i) for i in range(size)])]
    pallas_call x17, Pallas kernels: 41.4 us -> 38 us  [call(): pl.pallas_call(kernel, out_shape=shapes, compiler_params=params(), name=n...]
    ppermute x12, starting transfers between devices: 10.4 us -> 7.61 us  [swap(): return lax.ppermute(x, axes, [(i, size - 1 - i) for i in range(size)])]
  transfers between devices with their start and end apart: 16 -> 13, of which waited for: 10 -> 7; matrix products, arithmetic and copies ran while one was open for 1% -> 1% of each run, Pallas kernels for 8% -> 8%
where the time goes in v9:
time: 209 us
  blocking collectives  106 us (51%)
  waiting for transfers between devices  39.3 us (19%)
  Pallas kernels  38 us (18%)
  starting transfers between devices  18.8 us (9%)
  local copies, waits for them, and re-layouts  3.66 us (2%)
    all_to_all x3, blocking collectives, exchange(): return lax.all_to_all(x, axes, 0, 0, tiled=True)  106 us
    pallas_call x17, Pallas kernels, call(): pl.pallas_call(kernel, out_shape=shapes, compiler_params=params(), name=n...  38 us
    ppermute x12, waiting for transfers between devices, swap(): return lax.ppermute(x, axes, [(i, size - 1 - i) for i in range(size)])  24.5 us
    all_to_all x1, waiting for transfers between devices, exchange(): return lax.all_to_all(x, axes, 0, 0, tiled=True)  14.8 us
    all_to_all x1, starting transfers between devices, exchange(): return lax.all_to_all(x, axes, 0, 0, tiled=True)  11.1 us
    ppermute x12, starting transfers between devices, swap(): return lax.ppermute(x, axes, [(i, size - 1 - i) for i in range(size)])  7.61 us
  transfers between devices with their start and end apart: 13, of which 7 were waited for; matrix products, arithmetic and copies ran while one was open for 1% of the time, Pallas kernels for 8%

profile of v9, /device:TPU:0, one launch (start us, length us, event | category | flops | bytes accessed | tf_op | source)
XLA Modules:
  0.0 208.5 jit_solution(2598897954485045732)
XLA Ops:
  1.3 5.0 %project.1 = (bf16[1024,640]{1,0:T(8,128)(2,1)S(1)}, f32[512,512]{1,0:T(8,128)}, f32[512,128]{1,0:T(8,128)S(1)}, f32[8,512]{1,0:T(8,128)S(1)}) custom-call(s32[1,512]{1,0:T(1,128)S(1)} %bitcast.25, bf16[512,2048]{1,0:T(8,128)(2,1)} %r_1_.2, bf16[2048,512]{1,0:T(8,128)(2,1)} %r_2_.1), custom_call_target="tpu_custom_call" | custom-call | tf_op jit(solution)/shard_map/project/pallas_call | solution.py:362
  6.3 1.1 copy-done.1
  8.1 11.1 %all-to-all-start = ((bf16[128,8,640]{2,1,0:T(8,128)(2,1)}), bf16[128,8,640]{2,1,0:T(8,128)(2,1)S(1)}, u32[]{:S(2)}, u32[]{:S(2)}) async-start(bf16[128,8,640]{2,1,0:T(8,128)(2,1)} %bitcast.24), calls=%async_computation | async-start | bytes 2621440 | tf_op jit(solution)/shard_map/all_to_all | solution.py:337
  19.3 1.7 stripes.1
  20.9 1.0 copy-done.2
  23.1 1.7 collective-permute-done.theirs
  24.8 14.8 %all-to-all-done = bf16[128,8,640]{2,1,0:T(8,128)(2,1)S(1)} async-done(((bf16[128,8,640]{2,1,0:T(8,128)(2,1)}), bf16[128,8,640]{2,1,0:T(8,128)(2,1)S(1)}, u32[]{:S(2)}, u32[]{:S(2)}) %all-to-all-start) | async-done | bytes 1310752 | tf_op jit(solution)/shard_map/all_to_all | solution.py:337
  39.6 1.2 compact.1
  40.8 1.9 collective-permute-start.2
  42.7 3.6 %near.1 = (bf16[2048,512]{1,0:T(8,128)(2,1)S(1)}, f32[2,8,512]{2,1,0:T(8,128)S(1)}, s32[16,128]{1,0:T(8,128)S(1)}) custom-call(bf16[528,512]{1,0:T(8,128)(2,1)S(1)} %get-tuple-element.47.own, bf16[528,512]{1,0:T(8,128)(2,1)S(1)} %collective-permute-done.1.beside), custom_call_target="tpu_custom_call" | custom-call | flops 4000000000 | bytes 4000000 | tf_op jit(solution)/shard_map/near/pallas_call | solution.py:362
  46.4 10.3 %collective-permute-done.2.across = bf16[528,512]{1,0:T(8,128)(2,1)S(1)} collective-permute-done((bf16[528,512]{1,0:T(8,128)(2,1)S(1)}, bf16[528,512]{1,0:T(8,128)(2,1)S(1)}, u32[]{:S(2)}, u32[]{:S(2)}) %collective-permute-start.2) | collective-permute-done | bytes 540704 | tf_op jit(solution)/shard_map/ppermute | solution.py:333
  56.7 2.5 %middle.1 = (bf16[2048,512]{1,0:T(8,128)(2,1)S(1)}, f32[8,512]{1,0:T(8,128)S(1)}) custom-call(bf16[2048,512]{1,0:T(8,128)(2,1)S(1)} %get-tuple-element.54.begun, bf16[528,512]{1,0:T(8,128)(2,1)S(1)} %collective-permute-done.2.across), custom_call_target="tpu_custom_call" | custom-call | tf_op jit(solution)/shard_map/middle/pallas_call | solution.py:362
  59.3 4.5 %far.1 = (bf16[2048,512]{1,0:T(8,128)(2,1)S(1)}, bf16[32,128,512]{2,1,0:T(8,128)(2,1)}, f32[8,512]{1,0:T(8,128)S(1)}) custom-call(s32[32]{0:T(128)S(1)} %select_reduce_fusion.2.serve, s32[32]{0:T(128)S(1)} %select_reduce_fusion.1.order, s32[9]{0:T(128)S(1)} %convert_reduce_fusion.1.ready, bf16[2048,512]{1,0:T(8,128)(2,1)S(1)} %get-tuple-element.56.begun, ...), custom_call_target="tpu_custom_call" | custom-call | tf_op jit(solution)/shard_map/far/pallas_call | solution.py:362
  63.8 56.6 %all_to_all.20.fetched = bf16[32,128,512]{2,1,0:T(8,128)(2,1)S(1)} all-to-all(bf16[32,128,512]{2,1,0:T(8,128)(2,1)} %get-tuple-element.58), channel_id=1, replica_groups=mesh['z'=4,'x'=4,'core'=2,'yhi'=2,'ylo'=2] {'ylo','x','z'}, dimensions={0} | all-to-all | bytes 8388608 | tf_op jit(solution)/shard_map/all_to_all | solution.py:337
  120.4 2.7 %scores.1 = (bf16[16,256,128]{2,1,0:T(8,128)(2,1)S(1)}, f32[32,128]{1,0:T(8,128)S(1)}, bf16[32,128,512]{2,1,0:T(8,128)(2,1)S(1)}) custom-call(s32[32]{0:T(128)S(1)} %get-tuple-element.45.need, s32[16,128]{1,0:T(8,128)S(1)} %fusion.10.column, bf16[2048,512]{1,0:T(8,128)(2,1)S(1)} %get-tuple-element.57.anchors, bf16[32,128,512]{2,1,0:T(8,128)(2,1)S(1)} %all_to_all.20.fetched), custom_call_target="tpu_custom_call" | custom-call | tf_op jit(solution)/shard_map/scores/pallas_call | solution.py:362
  123.2 1.7 collective-permute-start.5
  124.8 1.4 collective-permute-start.4
  126.2 2.4 %mix.1 = (bf16[2048,512]{1,0:T(8,128)(2,1)S(1)}, bf16[2048,512]{1,0:T(8,128)(2,1)S(1)}) custom-call(s32[32]{0:T(128)S(1)} %get-tuple-element.45.need, s32[16,128]{1,0:T(8,128)S(1)} %fusion.10.column, bf16[16,256,128]{2,1,0:T(8,128)(2,1)S(1)} %get-tuple-element.60.weights, bf16[32,128,512]{2,1,0:T(8,128)(2,1)S(1)} %get-tuple-element.61.partners), custom_call_target="tpu_custom_call" | custom-call | tf_op jit(solution)/shard_map/mix/pallas_call | solution.py:362
  128.6 2.1 shares.1
  131.0 1.6 beside.1
  133.2 1.6 across.1
  135.0 1.6 collective-permute-start.10
  136.7 1.6 own.1.a
  138.3 2.0 collective-permute-done.8
  141.0 9.2 %collective-permute-done.10.c = bf16[512,512]{1,0:T(8,128)(2,1)S(1)} collective-permute-done((bf16[512,512]{1,0:T(8,128)(2,1)S(1)}, bf16[512,512]{1,0:T(8,128)(2,1)S(1)}, u32[]{:S(2)}, u32[]{:S(2)}) %collective-permute-start.10) | collective-permute-done | bytes 524320 | tf_op jit(solution)/shard_map/ppermute | solution.py:333
  150.1 2.1 %back.1 = bf16[1024,512]{1,0:T(8,128)(2,1)} custom-call(bf16[512,512]{1,0:T(8,128)(2,1)S(1)} %own.1.a, bf16[512,512]{1,0:T(8,128)(2,1)S(1)} %collective-permute-done.7.b, bf16[512,512]{1,0:T(8,128)(2,1)S(1)} %collective-permute-done.10.c, f32[8,1024]{1,0:T(8,128)S(1)} %get-tuple-element.73.place), custom_call_target="tpu_custom_call" | custom-call | tf_op jit(solution)/shard_map/back/pallas_call | solution.py:362
  152.2 25.2 %all_to_all.21 = bf16[128,8,512]{2,1,0:T(8,128)(2,1)S(1)} all-to-all(bf16[128,8,512]{2,1,0:T(8,128)(2,1)} %bitcast.26), channel_id=1, replica_groups=mesh['z'=4,'x'=4,'core'=2,'yhi'=2,'ylo'=2] {'core','x','yhi','ylo','z'}, dimensions={0} | all-to-all | bytes 2097152 | tf_op jit(solution)/shard_map/all_to_all | solution.py:337
  177.4 2.2 %unit_grad.1.grad = bf16[512,512]{1,0:T(8,128)(2,1)S(1)} custom-call(bf16[1024,512]{1,0:T(8,128)(2,1)S(1)} %bitcast.23, f32[8,512]{1,0:T(8,128)S(1)} %get-tuple-element.74.place, f32[512,512]{1,0:T(8,128)} %get-tuple-element.75.unit, f32[512,128]{1,0:T(8,128)S(1)} %copy-done.5), custom_call_target="tpu_custom_call" | custom-call | tf_op jit(solution)/shard_map/unit_grad/pallas_call | solution.py:362
  180.4 1.2 collective-permute-done.11.partner
  181.6 1.7 head_grad.1
  183.3 24.4 %all_to_all.22.parts = bf16[64,16,512]{2,1,0:T(8,128)(2,1)S(1)} all-to-all(bf16[64,16,512]{2,1,0:T(8,128)(2,1)} %bitcast.27), channel_id=1, replica_groups=mesh['z'=4,'x'=4,'core'=2,'yhi'=2,'ylo'=2] {'x','yhi','ylo','z'}, dimensions={0} | all-to-all | bytes 2097152 | tf_op jit(solution)/shard_map/all_to_all | solution.py:337
  207.7 0.8 add.126
  (52 shorter events, 5.2 us)
Async XLA Ops:
  0.6 0.7 copy-start.6
  6.3 1.1 copy-start.1
  7.4 0.7 copy-start.4
  8.1 11.2 %copy-start = (bf16[512,2048]{1,0:T(8,128)(2,1)S(1)}, bf16[512,2048]{1,0:T(8,128)(2,1)}, u32[]{:S(2)}) copy-start(bf16[512,2048]{1,0:T(8,128)(2,1)} %r_1_.2) | copy-start | bytes 6291460
  8.1 13.8 %copy-start.8 = (s32[512,8]{0,1:T(8,128)S(1)}, s32[512,8]{0,1:T(8,128)}, u32[]{:S(2)}) copy-start(s32[512,8]{0,1:T(8,128)} %param.8) | copy-start | bytes 49156
  8.1 14.2 %copy-start.7 = (s32[2048]{0:T(1024)S(1)}, s32[2048]{0:T(1024)}, u32[]{:S(2)}) copy-start(s32[2048]{0:T(1024)} %param.9) | copy-start | bytes 24580
  8.1 31.5 %all-to-all-start = ((bf16[128,8,640]{2,1,0:T(8,128)(2,1)}), bf16[128,8,640]{2,1,0:T(8,128)(2,1)S(1)}, u32[]{:S(2)}, u32[]{:S(2)}) async-start(bf16[128,8,640]{2,1,0:T(8,128)(2,1)} %bitcast.24), calls=%async_computation | async-start | bytes 2621440 | tf_op jit(solution)/shard_map/all_to_all | solution.py:337
  20.9 1.0 copy-start.2
  21.9 2.9 %collective-permute-start = (bf16[1024,512]{1,0:T(8,128)(2,1)}, bf16[1024,512]{1,0:T(8,128)(2,1)S(1)}, u32[]{:S(2)}, u32[]{:S(2)}) collective-permute-start(bf16[1024,512]{1,0:T(8,128)(2,1)} %get-tuple-element.44), channel_id=1, source_target_pairs={{0,4},{4,0},{1,5},{5,1},{2,6},{6,2},{3,7},{7,3},{8,12},{12,8},{9,1... | collective-permute-start | bytes 3145736 | tf_op jit(solution)/shard_map/ppermute | solution.py:333
  40.8 1.9 collective-permute-start.1
  40.8 15.9 %collective-permute-start.2 = (bf16[528,512]{1,0:T(8,128)(2,1)S(1)}, bf16[528,512]{1,0:T(8,128)(2,1)S(1)}, u32[]{:S(2)}, u32[]{:S(2)}) collective-permute-start(bf16[528,512]{1,0:T(8,128)(2,1)S(1)} %get-tuple-element.47.own), channel_id=1, source_target_pairs={{0,3},{1,2},{2,1},{3,0},{4,7},{5,6},{6,5},{7,4},{8,11},{9,10},{10,... | collective-permute-start | bytes 1622024 | tf_op jit(solution)/shard_map/ppermute | solution.py:333
  56.7 2.5 %collective-permute-start.3 = (bf16[528,512]{1,0:T(8,128)(2,1)S(1)}, bf16[528,512]{1,0:T(8,128)(2,1)S(1)}, u32[]{:S(2)}, u32[]{:S(2)}) collective-permute-start(bf16[528,512]{1,0:T(8,128)(2,1)S(1)} %collective-permute-done.2.across), channel_id=1, source_target_pairs={{0,4},{4,0},{1,5},{5,1},{2,6},{6,2},{3,7},{7,3},{8,12},{12,8},{9,1... | collective-permute-start | bytes 1622024 | tf_op jit(solution)/shard_map/ppermute | solution.py:333
  123.1 5.6 %collective-permute-start.6 = (f32[32,128]{1,0:T(8,128)S(1)}, f32[32,128]{1,0:T(8,128)S(1)}, u32[]{:S(2)}, u32[]{:S(2)}) collective-permute-start(f32[32,128]{1,0:T(8,128)S(1)} %get-tuple-element.59.r_0_), channel_id=1, source_target_pairs={{0,7},{1,6},{2,5},{3,4},{4,3},{5,2},{6,1},{7,0},{8,15},{9,14},{10,... | collective-permute-start | bytes 49160 | tf_op jit(solution)/shard_map/ppermute | solution.py:333
  123.2 5.5 %collective-permute-start.5 = (f32[32,128]{1,0:T(8,128)S(1)}, f32[32,128]{1,0:T(8,128)S(1)}, u32[]{:S(2)}, u32[]{:S(2)}) collective-permute-start(f32[32,128]{1,0:T(8,128)S(1)} %get-tuple-element.59.r_0_), channel_id=1, source_target_pairs={{0,3},{1,2},{2,1},{3,0},{4,7},{5,6},{6,5},{7,4},{8,11},{9,10},{10,... | collective-permute-start | bytes 49160 | tf_op jit(solution)/shard_map/ppermute | solution.py:333
  124.8 3.8 %collective-permute-start.4 = (f32[32,128]{1,0:T(8,128)S(1)}, f32[32,128]{1,0:T(8,128)S(1)}, u32[]{:S(2)}, u32[]{:S(2)}) collective-permute-start(f32[32,128]{1,0:T(8,128)S(1)} %get-tuple-element.59.r_0_), channel_id=1, source_target_pairs={{0,4},{4,0},{1,5},{5,1},{2,6},{6,2},{3,7},{7,3},{8,12},{12,8},{9,1... | collective-permute-start | bytes 49160 | tf_op jit(solution)/shard_map/ppermute | solution.py:333
  130.7 4.1 %collective-permute-start.9 = (bf16[512,512]{1,0:T(8,128)(2,1)S(1)}, bf16[512,512]{1,0:T(8,128)(2,1)S(1)}, u32[]{:S(2)}, u32[]{:S(2)}) collective-permute-start(bf16[512,512]{1,0:T(8,128)(2,1)S(1)} %get-tuple-element.72), channel_id=1, source_target_pairs={{0,4},{4,0},{1,5},{5,1},{2,6},{6,2},{3,7},{7,3},{8,12},{12,8},{9,1... | collective-permute-start | bytes 1572872 | tf_op jit(solution)/shard_map/ppermute | solution.py:333
  132.6 8.3 %collective-permute-start.7 = (bf16[512,512]{1,0:T(8,128)(2,1)S(1)}, bf16[512,512]{1,0:T(8,128)(2,1)S(1)}, u32[]{:S(2)}, u32[]{:S(2)}) collective-permute-start(bf16[512,512]{1,0:T(8,128)(2,1)S(1)} %beside.1), channel_id=1, source_target_pairs={{0,4},{4,0},{1,5},{5,1},{2,6},{6,2},{3,7},{7,3},{8,12},{12,8},{9,1... | collective-permute-start | bytes 1572872 | tf_op jit(solution)/shard_map/ppermute | solution.py:333
  135.0 15.1 %collective-permute-start.10 = (bf16[512,512]{1,0:T(8,128)(2,1)S(1)}, bf16[512,512]{1,0:T(8,128)(2,1)S(1)}, u32[]{:S(2)}, u32[]{:S(2)}) collective-permute-start(bf16[512,512]{1,0:T(8,128)(2,1)S(1)} %add_convert_fusion), channel_id=1, source_target_pairs={{0,3},{1,2},{2,1},{3,0},{4,7},{5,6},{6,5},{7,4},{8,11},{9,10},{10,... | collective-permute-start | bytes 1572872 | tf_op jit(solution)/shard_map/ppermute | solution.py:333
  136.6 3.7 %collective-permute-start.8 = (f32[2048]{0:T(1024)S(1)}, f32[2048]{0:T(1024)S(1)}, u32[]{:S(2)}, u32[]{:S(2)}) collective-permute-start(f32[2048]{0:T(1024)S(1)} %fusion.9), channel_id=1, source_target_pairs={{0,1},{1,0},{2,3},{3,2},{4,5},{5,4},{6,7},{7,6},{8,9},{9,8},{10,11... | collective-permute-start | bytes 24584 | tf_op jit(solution)/shard_map/ppermute | solution.py:333
  150.1 27.3 %copy-start.5 = (f32[512,128]{1,0:T(8,128)S(1)}, f32[512,128]{1,0:T(8,128)}, u32[]{:S(2)}) copy-start(f32[512,128]{1,0:T(8,128)} %copy-done.4) | copy-start | bytes 786436
  152.2 27.5 %copy-start.3 = (bf16[1024,512]{1,0:T(8,128)(2,1)S(1)}, bf16[1024,512]{1,0:T(8,128)(2,1)}, u32[]{:S(2)}) copy-start(bf16[1024,512]{1,0:T(8,128)(2,1)} %copy-done.2) | copy-start | bytes 3145732
  179.6 2.0 collective-permute-start.11

commit v10 on v9

--- a/solution.py
+++ b/solution.py
@@ -59,12 +59,16 @@
 
 
 def column_of(rows):
+    return float_column_of(rows).astype(I32)
+
+
+def float_column_of(rows):
     wide = jnp.concatenate([rows] * (BR // rows.shape[0]), axis=0)
-    return wide.T[:, 0:1].astype(I32)
+    return wide.T[:, 0:1]
 
 
 def project_kernel(
-    owner_slots, sizes, cap, slot, feat_in, head_in, send, unit, norm, place, feat, head, kept, sems
+    owner_slots, sizes, cap, slot, feat_in, head_in, sent, unit, place, feat, head, kept, send, sems
 ):
     n = feat.shape[0]
     width, e = head.shape
@@ -93,7 +97,7 @@
     )
     device = position(DISPATCH, sizes, place_of)
     p = device * cap + rank // REPS
-    place[...] = jnp.broadcast_to(p.astype(F32), place.shape)
+    place[:8, :] = jnp.broadcast_to(p.astype(F32), (8, n))
     scatter = hot(iota((send.shape[0], n), 0) == p)
     high = local // BR
     low = local - high * BR
@@ -111,9 +115,21 @@
     kept[...] = rows
     keep = pltpu.make_async_copy(kept, unit, sems.at[2 * parts])
     keep.start()
-    norm[...] = jnp.broadcast_to(length, norm.shape)
-    send[:, :e] = dot(scatter, rows.astype(BF)).astype(BF)
+    place[8:, :] = jnp.broadcast_to(length, (n, BR)).T[:8, :]
+    descriptor = rows.astype(BF)
+    step = send.shape[0] // parts
+    leave = []
+    for k in range(parts):
+        at = slice(k * step, (k + 1) * step)
+        send[at, :e] = dot(scatter[at, :], descriptor).astype(BF)
+        at = pl.ds(k * step, step)
+        leave.append(
+            pltpu.make_async_copy(send.at[at, :], sent.at[at, :], sems.at[2 * parts + 1 + k])
+        )
+        leave[-1].start()
     keep.wait()
+    for c in leave:
+        c.wait()
 
 
 def stripes_kernel(sizes, core, feat, mine, other):
@@ -221,11 +237,8 @@
     lax.fori_loop(0, served.shape[0], finish, 0)
 
 
-def scores_kernel(need, column, anchors, fetched, weights, stats, partners, sem):
-    load = pltpu.make_async_copy(fetched, partners, sem)
-    load.start()
+def scores_kernel(need, column, anchors, partners, weights, stats):
     blocks = weights.shape[0]
-    load.wait()
 
     def body(i, carry):
         for j in range(4):
@@ -292,22 +305,25 @@
     pick_rows(out, share, column_of(slots[...]))
 
 
-def back_kernel(a, b, c, place, back):
-    total = a[...].astype(F32) + b[...].astype(F32) + c[...].astype(F32)
-    rows = a.shape[0]
-    pos = column_of(place[...])
-    back[...] = dot(hot(iota((back.shape[0], rows), 1) == pos), total.astype(BF)).astype(BF)
-
-
-def unit_grad_kernel(got, place, unit, norm, out, kept, sem):
+def chip_kernel(own, beside, place, total, pick):
+    total[...] = own[...].astype(F32) + beside[...].astype(F32)
+    pick[...] = hot(iota(pick.shape, 1) == column_of(place[...]))
+
+
+def back_kernel(chip, across, pick, back):
+    total = chip[...] + across[...].astype(F32)
+    back[...] = dot(pick[...], total.astype(BF)).astype(BF)
+
+
+def unit_grad_kernel(got, place, unit, out, kept, sem):
     fetch = pltpu.make_async_copy(unit, kept, sem)
     fetch.start()
-    n = norm.shape[0]
-    grad = dot(hot(iota((n, got.shape[0]), 1) == column_of(place[...])), got[...])
+    n = out.shape[0]
+    grad = dot(hot(iota((n, got.shape[0]), 1) == column_of(place[:8, :])), got[...])
     fetch.wait()
     rows = kept[...]
     radial = jnp.sum(rows * grad, axis=1, keepdims=True)
-    out[...] = ((grad - rows * radial) / norm[:, 0:1]).astype(BF)
+    out[...] = ((grad - rows * radial) / float_column_of(place[8:, :])).astype(BF)
 
 
 def head_begun_kernel(mine, grad, out):
@@ -363,22 +379,23 @@
             kernel, out_shape=shapes, compiler_params=params(), name=name, **more
         )(*args)
 
-    send, unit, norm, place = call(
+    send, unit, place = call(
         lambda *r: project_kernel(owner_slots, sizes, cap, *r),
         "project",
-        (sds((count, e + BR), BF), pltpu.HBM((n, e), F32), sds((n, BR), F32), sds((8, n), F32)),
+        (pltpu.HBM((count, e + BR), BF), pltpu.HBM((n, e), F32), pltpu.HBM((16, n), F32)),
         (
             slot_of_image.reshape(1, n),
             pltpu.with_memory_space_constraint(features, pltpu.HBM),
             pltpu.with_memory_space_constraint(head_weight, pltpu.HBM),
         ),
         in_specs=[vmem, far_away, far_away],
-        out_specs=(vmem, far_away, vmem, vmem),
+        out_specs=(far_away, far_away, vmem),
         scratch_shapes=[
             pltpu.VMEM((n, width), BF),
             pltpu.VMEM((width, e), BF),
             pltpu.VMEM((n, e), F32),
-            pltpu.SemaphoreType.DMA((9,)),
+            pltpu.VMEM((count, e + BR), BF),
+            pltpu.SemaphoreType.DMA((13,)),
         ],
     )
     send, late_features = lax.optimization_barrier((send, features))
@@ -448,24 +465,22 @@
         scratch_shapes=[pltpu.SemaphoreType.DMA((dp,))],
     )
     fetched = exchange(served, FETCH)
-    weights, stats, partners = call(
+    weights, stats = call(
         scores_kernel,
         "scores",
         (
             sds((blocks, PAIRS_REP * BR, BR), BF),
             sds((2 * blocks, BR), F32),
-            sds((dp, BR, e), BF),
         ),
         (need, column, anchors, fetched),
-        in_specs=[smem, vmem, vmem, far_away],
-        scratch_shapes=[pltpu.SemaphoreType.DMA],
+        in_specs=[smem] + [vmem] * 3,
     )
     spread = (stats, swap(stats), swap(stats, ("yhi", "ylo")), swap(stats, ("core", "yhi", "ylo")))
     pulled, partner = call(
         mix_kernel,
         "mix",
         (sds((owner_slots, e), BF),) * 2,
-        (need, column, weights, partners),
+        (need, column, weights, fetched),
         in_specs=[smem] + [vmem] * 3,
     )
     share, for_corner = call(
@@ -489,14 +504,15 @@
     total = rest + jnp.exp(matching - 1.0 / logit_sharpness)
     loss = (jnp.log(total) + 1.0 / logit_sharpness - matching).reshape(owner_slots)
     anchor_row_loss = jnp.where(home, loss, swap(loss, ("ylo",)))
-    own, from_beside, anchor_row_loss = lax.optimization_barrier(
-        (own, from_beside, anchor_row_loss)
-    )
+    chip, back_pick = call(
+        chip_kernel, "chip", (sds((n, e), F32), sds((count, n), BF)), (own, from_beside, back_place)
+    )
+    chip, back_pick, anchor_row_loss = lax.optimization_barrier((chip, back_pick, anchor_row_loss))
     back = call(
         back_kernel,
         "back",
         pltpu.HBM((count, e), BF),
-        (own, from_beside, from_across, back_place),
+        (chip, from_across, back_pick),
     )
     returned = exchange(back.reshape(devices, cap, e), DISPATCH).reshape(count, e)
 
@@ -504,8 +520,8 @@
         unit_grad_kernel,
         "unit_grad",
         sds((n, e), BF),
-        (returned, place, pltpu.with_memory_space_constraint(unit, pltpu.HBM), norm),
-        in_specs=[vmem, vmem, far_away, vmem],
+        (returned, place, pltpu.with_memory_space_constraint(unit, pltpu.HBM)),
+        in_specs=[vmem, vmem, far_away],
         scratch_shapes=[pltpu.VMEM((n, e), F32), pltpu.SemaphoreType.DMA],
     )
     begun = call(head_begun_kernel, "head_begun", sds((width // 2, e), F32), (mine, grad))

time: 209 us -> 208 us (level)
    pallas_call x17 -> x18, Pallas kernels: 38 us -> 39.5 us  [call(): pl.pallas_call(kernel, out_shape=shapes, compiler_params=params(), name=n...]
where the time goes in v10:
time: 208 us
  blocking collectives  106 us (51%)
  Pallas kernels  39.5 us (19%)
  waiting for transfers between devices  38.5 us (19%)
  starting transfers between devices  19.3 us (9%)
    all_to_all x3, blocking collectives, exchange(): return lax.all_to_all(x, axes, 0, 0, tiled=True)  106 us
    pallas_call x18, Pallas kernels, call(): pl.pallas_call(kernel, out_shape=shapes, compiler_params=params(), name=n...  39.5 us
    ppermute x12, waiting for transfers between devices, swap(): return lax.ppermute(x, axes, [(i, size - 1 - i) for i in range(size)])  23.8 us
    all_to_all x1, waiting for transfers between devices, exchange(): return lax.all_to_all(x, axes, 0, 0, tiled=True)  14.8 us
    all_to_all x1, starting transfers between devices, exchange(): return lax.all_to_all(x, axes, 0, 0, tiled=True)  11.1 us
    ppermute x12, starting transfers between devices, swap(): return lax.ppermute(x, axes, [(i, size - 1 - i) for i in range(size)])  8.18 us
  transfers between devices with their start and end apart: 13, of which 7 were waited for; matrix products, arithmetic and copies ran while one was open for 1% of the time, Pallas kernels for 8%

profile of v10, /device:TPU:0, one launch (start us, length us, event | category | flops | bytes accessed | tf_op | source)
XLA Modules:
  0.0 207.6 jit_solution(8389105813624577676)
XLA Ops:
  1.3 6.4 %project.1 = (bf16[1024,640]{1,0:T(8,128)(2,1)}, f32[512,512]{1,0:T(8,128)}, f32[16,512]{1,0:T(8,128)}) custom-call(s32[1,512]{1,0:T(1,128)S(1)} %bitcast.24, bf16[512,2048]{1,0:T(8,128)(2,1)} %r_1_.2, bf16[2048,512]{1,0:T(8,128)(2,1)} %r_2_.1), custom_call_target="tpu_custom_call" | custom-call | tf_op jit(solution)/shard_map/project/pallas_call | solution.py:378
  7.8 11.1 %all-to-all-start = ((bf16[128,8,640]{2,1,0:T(8,128)(2,1)}), bf16[128,8,640]{2,1,0:T(8,128)(2,1)S(1)}, u32[]{:S(2)}, u32[]{:S(2)}) async-start(bf16[128,8,640]{2,1,0:T(8,128)(2,1)} %bitcast.27), calls=%async_computation | async-start | bytes 2621440 | tf_op jit(solution)/shard_map/all_to_all | solution.py:353
  18.9 1.7 stripes.1
  20.6 1.0 copy-done.1
  22.8 1.7 collective-permute-done.theirs
  24.5 14.8 %all-to-all-done = bf16[128,8,640]{2,1,0:T(8,128)(2,1)S(1)} async-done(((bf16[128,8,640]{2,1,0:T(8,128)(2,1)}), bf16[128,8,640]{2,1,0:T(8,128)(2,1)S(1)}, u32[]{:S(2)}, u32[]{:S(2)}) %all-to-all-start) | async-done | bytes 1310752 | tf_op jit(solution)/shard_map/all_to_all | solution.py:353
  39.3 1.2 compact.1
  40.4 1.9 collective-permute-start.2
  42.4 3.6 %near.1 = (bf16[2048,512]{1,0:T(8,128)(2,1)S(1)}, f32[2,8,512]{2,1,0:T(8,128)S(1)}, s32[16,128]{1,0:T(8,128)S(1)}) custom-call(bf16[528,512]{1,0:T(8,128)(2,1)S(1)} %get-tuple-element.47.own, bf16[528,512]{1,0:T(8,128)(2,1)S(1)} %collective-permute-done.1.beside), custom_call_target="tpu_custom_call" | custom-call | flops 4000000000 | bytes 4000000 | tf_op jit(solution)/shard_map/near/pallas_call | solution.py:378
  46.1 10.3 %collective-permute-done.2.across = bf16[528,512]{1,0:T(8,128)(2,1)S(1)} collective-permute-done((bf16[528,512]{1,0:T(8,128)(2,1)S(1)}, bf16[528,512]{1,0:T(8,128)(2,1)S(1)}, u32[]{:S(2)}, u32[]{:S(2)}) %collective-permute-start.2) | collective-permute-done | bytes 540704 | tf_op jit(solution)/shard_map/ppermute | solution.py:349
  56.4 2.5 %middle.1 = (bf16[2048,512]{1,0:T(8,128)(2,1)S(1)}, f32[8,512]{1,0:T(8,128)S(1)}) custom-call(bf16[2048,512]{1,0:T(8,128)(2,1)S(1)} %get-tuple-element.54.begun, bf16[528,512]{1,0:T(8,128)(2,1)S(1)} %collective-permute-done.2.across), custom_call_target="tpu_custom_call" | custom-call | tf_op jit(solution)/shard_map/middle/pallas_call | solution.py:378
  58.9 4.6 %far.1 = (bf16[2048,512]{1,0:T(8,128)(2,1)S(1)}, bf16[32,128,512]{2,1,0:T(8,128)(2,1)}, f32[8,512]{1,0:T(8,128)S(1)}) custom-call(s32[32]{0:T(128)S(1)} %select_reduce_fusion.2.serve, s32[32]{0:T(128)S(1)} %select_reduce_fusion.1.order, s32[9]{0:T(128)S(1)} %convert_reduce_fusion.1.ready, bf16[2048,512]{1,0:T(8,128)(2,1)S(1)} %get-tuple-element.56.begun, ...), custom_call_target="tpu_custom_call" | custom-call | tf_op jit(solution)/shard_map/far/pallas_call | solution.py:378
  63.5 56.0 %all_to_all.20.partners = bf16[32,128,512]{2,1,0:T(8,128)(2,1)S(1)} all-to-all(bf16[32,128,512]{2,1,0:T(8,128)(2,1)} %get-tuple-element.58), channel_id=1, replica_groups=mesh['z'=4,'x'=4,'core'=2,'yhi'=2,'ylo'=2] {'ylo','x','z'}, dimensions={0} | all-to-all | bytes 8388608 | tf_op jit(solution)/shard_map/all_to_all | solution.py:353
  119.5 2.4 %scores.1 = (bf16[16,256,128]{2,1,0:T(8,128)(2,1)S(1)}, f32[32,128]{1,0:T(8,128)S(1)}) custom-call(s32[32]{0:T(128)S(1)} %get-tuple-element.45.need, s32[16,128]{1,0:T(8,128)S(1)} %fusion.10.column, bf16[2048,512]{1,0:T(8,128)(2,1)S(1)} %get-tuple-element.57.anchors, bf16[32,128,512]{2,1,0:T(8,128)(2,1)S(1)} %all_to_all.20.partners), custom_call_target="tpu_custom_call" | custom-call | tf_op jit(solution)/shard_map/scores/pallas_call | solution.py:378
  122.4 1.7 collective-permute-start.5
  124.1 0.9 collective-permute-start.4
  125.0 2.4 %mix.1 = (bf16[2048,512]{1,0:T(8,128)(2,1)S(1)}, bf16[2048,512]{1,0:T(8,128)(2,1)S(1)}) custom-call(s32[32]{0:T(128)S(1)} %get-tuple-element.45.need, s32[16,128]{1,0:T(8,128)S(1)} %fusion.10.column, bf16[16,256,128]{2,1,0:T(8,128)(2,1)S(1)} %get-tuple-element.60.weights, bf16[32,128,512]{2,1,0:T(8,128)(2,1)S(1)} %all_to_all.20.partners), custom_call_target="tpu_custom_call" | custom-call | tf_op jit(solution)/shard_map/mix/pallas_call | solution.py:378
  127.4 2.1 %shares.1 = (bf16[2048,512]{1,0:T(8,128)(2,1)S(1)}, bf16[512,512]{1,0:T(8,128)(2,1)S(1)}) custom-call(f32[32,128]{1,0:T(8,128)S(1)} %get-tuple-element.59.r_0_, f32[32,128]{1,0:T(8,128)S(1)} %collective-permute-done.4.r_1_, f32[32,128]{1,0:T(8,128)S(1)} %collective-permute-done.5.r_2_, f32[32,128]{1,0:T(8,128)S(1)} %collective-permute-done.6.r_3_, ...), custom_call_target="tpu_custom_call" | custom-call | tf_op jit(solution)/shard_map/shares/pallas_call | solution.py:378
  129.5 0.7 collective-permute-start.9
  130.3 1.6 beside.1
  132.0 1.6 across.1
  133.8 2.1 %collective-permute-start.10 = (bf16[512,512]{1,0:T(8,128)(2,1)S(1)}, bf16[512,512]{1,0:T(8,128)(2,1)S(1)}, u32[]{:S(2)}, u32[]{:S(2)}) collective-permute-start(bf16[512,512]{1,0:T(8,128)(2,1)S(1)} %add_convert_fusion), channel_id=1, source_target_pairs={{0,3},{1,2},{2,1},{3,0},{4,7},{5,6},{6,5},{7,4},{8,11},{9,10},{10,... | collective-permute-start | bytes 1572872 | tf_op jit(solution)/shard_map/ppermute | solution.py:349
  136.0 1.6 own.1
  137.7 2.0 collective-permute-done.8
  140.9 8.5 %collective-permute-done.10.across = bf16[512,512]{1,0:T(8,128)(2,1)S(1)} collective-permute-done((bf16[512,512]{1,0:T(8,128)(2,1)S(1)}, bf16[512,512]{1,0:T(8,128)(2,1)S(1)}, u32[]{:S(2)}, u32[]{:S(2)}) %collective-permute-start.10) | collective-permute-done | bytes 524320 | tf_op jit(solution)/shard_map/ppermute | solution.py:349
  149.4 1.7 back.1
  151.1 25.3 %all_to_all.21 = bf16[128,8,512]{2,1,0:T(8,128)(2,1)S(1)} all-to-all(bf16[128,8,512]{2,1,0:T(8,128)(2,1)} %bitcast.25), channel_id=1, replica_groups=mesh['z'=4,'x'=4,'core'=2,'yhi'=2,'ylo'=2] {'core','x','yhi','ylo','z'}, dimensions={0} | all-to-all | bytes 2097152 | tf_op jit(solution)/shard_map/all_to_all | solution.py:353
  176.4 2.3 %unit_grad.1.grad = bf16[512,512]{1,0:T(8,128)(2,1)S(1)} custom-call(bf16[1024,512]{1,0:T(8,128)(2,1)S(1)} %bitcast.23, f32[16,512]{1,0:T(8,128)S(1)} %copy-done.3, f32[512,512]{1,0:T(8,128)} %get-tuple-element.76.unit), custom_call_target="tpu_custom_call" | custom-call | tf_op jit(solution)/shard_map/unit_grad/pallas_call | solution.py:378
  179.5 1.2 collective-permute-done.11.partner
  180.7 1.7 head_grad.1
  182.4 24.4 %all_to_all.22.parts = bf16[64,16,512]{2,1,0:T(8,128)(2,1)S(1)} all-to-all(bf16[64,16,512]{2,1,0:T(8,128)(2,1)} %bitcast.26), channel_id=1, replica_groups=mesh['z'=4,'x'=4,'core'=2,'yhi'=2,'ylo'=2] {'x','yhi','ylo','z'}, dimensions={0} | all-to-all | bytes 2097152 | tf_op jit(solution)/shard_map/all_to_all | solution.py:353
  206.8 0.8 add.126
  (49 shorter events, 4.8 us)
Async XLA Ops:
  0.6 0.7 copy-start.4
  7.7 11.2 %copy-start = (bf16[512,2048]{1,0:T(8,128)(2,1)S(1)}, bf16[512,2048]{1,0:T(8,128)(2,1)}, u32[]{:S(2)}) copy-start(bf16[512,2048]{1,0:T(8,128)(2,1)} %r_1_.2) | copy-start | bytes 6291460
  7.7 13.9 %copy-start.6 = (s32[512,8]{0,1:T(8,128)S(1)}, s32[512,8]{0,1:T(8,128)}, u32[]{:S(2)}) copy-start(s32[512,8]{0,1:T(8,128)} %param.8) | copy-start | bytes 49156
  7.7 14.2 %copy-start.5 = (s32[2048]{0:T(1024)S(1)}, s32[2048]{0:T(1024)}, u32[]{:S(2)}) copy-start(s32[2048]{0:T(1024)} %param.9) | copy-start | bytes 24580
  7.8 31.5 %all-to-all-start = ((bf16[128,8,640]{2,1,0:T(8,128)(2,1)}), bf16[128,8,640]{2,1,0:T(8,128)(2,1)S(1)}, u32[]{:S(2)}, u32[]{:S(2)}) async-start(bf16[128,8,640]{2,1,0:T(8,128)(2,1)} %bitcast.27), calls=%async_computation | async-start | bytes 2621440 | tf_op jit(solution)/shard_map/all_to_all | solution.py:353
  20.6 1.0 copy-start.1
  21.6 2.9 %collective-permute-start = (bf16[1024,512]{1,0:T(8,128)(2,1)}, bf16[1024,512]{1,0:T(8,128)(2,1)S(1)}, u32[]{:S(2)}, u32[]{:S(2)}) collective-permute-start(bf16[1024,512]{1,0:T(8,128)(2,1)} %get-tuple-element.44), channel_id=1, source_target_pairs={{0,4},{4,0},{1,5},{5,1},{2,6},{6,2},{3,7},{7,3},{8,12},{12,8},{9,1... | collective-permute-start | bytes 3145736 | tf_op jit(solution)/shard_map/ppermute | solution.py:349
  40.4 1.9 collective-permute-start.1
  40.4 15.9 %collective-permute-start.2 = (bf16[528,512]{1,0:T(8,128)(2,1)S(1)}, bf16[528,512]{1,0:T(8,128)(2,1)S(1)}, u32[]{:S(2)}, u32[]{:S(2)}) collective-permute-start(bf16[528,512]{1,0:T(8,128)(2,1)S(1)} %get-tuple-element.47.own), channel_id=1, source_target_pairs={{0,3},{1,2},{2,1},{3,0},{4,7},{5,6},{6,5},{7,4},{8,11},{9,10},{10,... | collective-permute-start | bytes 1622024 | tf_op jit(solution)/shard_map/ppermute | solution.py:349
  56.4 2.5 %collective-permute-start.3 = (bf16[528,512]{1,0:T(8,128)(2,1)S(1)}, bf16[528,512]{1,0:T(8,128)(2,1)S(1)}, u32[]{:S(2)}, u32[]{:S(2)}) collective-permute-start(bf16[528,512]{1,0:T(8,128)(2,1)S(1)} %collective-permute-done.2.across), channel_id=1, source_target_pairs={{0,4},{4,0},{1,5},{5,1},{2,6},{6,2},{3,7},{7,3},{8,12},{12,8},{9,1... | collective-permute-start | bytes 1622024 | tf_op jit(solution)/shard_map/ppermute | solution.py:349
  121.8 5.6 %collective-permute-start.6 = (f32[32,128]{1,0:T(8,128)S(1)}, f32[32,128]{1,0:T(8,128)S(1)}, u32[]{:S(2)}, u32[]{:S(2)}) collective-permute-start(f32[32,128]{1,0:T(8,128)S(1)} %get-tuple-element.59.r_0_), channel_id=1, source_target_pairs={{0,7},{1,6},{2,5},{3,4},{4,3},{5,2},{6,1},{7,0},{8,15},{9,14},{10,... | collective-permute-start | bytes 49160 | tf_op jit(solution)/shard_map/ppermute | solution.py:349
  122.4 5.1 %collective-permute-start.5 = (f32[32,128]{1,0:T(8,128)S(1)}, f32[32,128]{1,0:T(8,128)S(1)}, u32[]{:S(2)}, u32[]{:S(2)}) collective-permute-start(f32[32,128]{1,0:T(8,128)S(1)} %get-tuple-element.59.r_0_), channel_id=1, source_target_pairs={{0,3},{1,2},{2,1},{3,0},{4,7},{5,6},{6,5},{7,4},{8,11},{9,10},{10,... | collective-permute-start | bytes 49160 | tf_op jit(solution)/shard_map/ppermute | solution.py:349
  124.1 3.4 %collective-permute-start.4 = (f32[32,128]{1,0:T(8,128)S(1)}, f32[32,128]{1,0:T(8,128)S(1)}, u32[]{:S(2)}, u32[]{:S(2)}) collective-permute-start(f32[32,128]{1,0:T(8,128)S(1)} %get-tuple-element.59.r_0_), channel_id=1, source_target_pairs={{0,4},{4,0},{1,5},{5,1},{2,6},{6,2},{3,7},{7,3},{8,12},{12,8},{9,1... | collective-permute-start | bytes 49160 | tf_op jit(solution)/shard_map/ppermute | solution.py:349
  129.5 4.1 %collective-permute-start.9 = (bf16[512,512]{1,0:T(8,128)(2,1)S(1)}, bf16[512,512]{1,0:T(8,128)(2,1)S(1)}, u32[]{:S(2)}, u32[]{:S(2)}) collective-permute-start(bf16[512,512]{1,0:T(8,128)(2,1)S(1)} %get-tuple-element.73), channel_id=1, source_target_pairs={{0,4},{4,0},{1,5},{5,1},{2,6},{6,2},{3,7},{7,3},{8,12},{12,8},{9,1... | collective-permute-start | bytes 1572872 | tf_op jit(solution)/shard_map/ppermute | solution.py:349
  131.9 8.4 %collective-permute-start.7 = (bf16[512,512]{1,0:T(8,128)(2,1)S(1)}, bf16[512,512]{1,0:T(8,128)(2,1)S(1)}, u32[]{:S(2)}, u32[]{:S(2)}) collective-permute-start(bf16[512,512]{1,0:T(8,128)(2,1)S(1)} %beside.1), channel_id=1, source_target_pairs={{0,4},{4,0},{1,5},{5,1},{2,6},{6,2},{3,7},{7,3},{8,12},{12,8},{9,1... | collective-permute-start | bytes 1572872 | tf_op jit(solution)/shard_map/ppermute | solution.py:349
  133.8 15.6 %collective-permute-start.10 = (bf16[512,512]{1,0:T(8,128)(2,1)S(1)}, bf16[512,512]{1,0:T(8,128)(2,1)S(1)}, u32[]{:S(2)}, u32[]{:S(2)}) collective-permute-start(bf16[512,512]{1,0:T(8,128)(2,1)S(1)} %add_convert_fusion), channel_id=1, source_target_pairs={{0,3},{1,2},{2,1},{3,0},{4,7},{5,6},{6,5},{7,4},{8,11},{9,10},{10,... | collective-permute-start | bytes 1572872 | tf_op jit(solution)/shard_map/ppermute | solution.py:349
  135.9 3.7 %collective-permute-start.8 = (f32[2048]{0:T(1024)S(1)}, f32[2048]{0:T(1024)S(1)}, u32[]{:S(2)}, u32[]{:S(2)}) collective-permute-start(f32[2048]{0:T(1024)S(1)} %fusion.9), channel_id=1, source_target_pairs={{0,1},{1,0},{2,3},{3,2},{4,5},{5,4},{6,7},{7,6},{8,9},{9,8},{10,11... | collective-permute-start | bytes 24584 | tf_op jit(solution)/shard_map/ppermute | solution.py:349
  140.9 35.5 %copy-start.3 = (f32[16,512]{1,0:T(8,128)S(1)}, f32[16,512]{1,0:T(8,128)}, u32[]{:S(2)}) copy-start(f32[16,512]{1,0:T(8,128)} %get-tuple-element.75.place) | copy-start | bytes 98308
  151.1 27.7 %copy-start.2 = (bf16[1024,512]{1,0:T(8,128)(2,1)S(1)}, bf16[1024,512]{1,0:T(8,128)(2,1)}, u32[]{:S(2)}) copy-start(bf16[1024,512]{1,0:T(8,128)(2,1)} %copy-done.1) | copy-start | bytes 3145732
  178.7 2.0 collective-permute-start.11

commit v11 on v10

--- a/solution.py
+++ b/solution.py
@@ -212,29 +212,20 @@
     place_rows(partial, [(row.astype(I32), across[:n, :])], begun)
 
 
-def far_kernel(serve, order, ready, begun, corner, anchors, served, slots, sems):
+def far_kernel(serve, order, ready, begun, corner, anchors, served, slots):
     n = corner.shape[0] - 16
     row = slot_row(corner[n:, :])
     slots[...] = jnp.broadcast_to(row, slots.shape)
 
-    def copy(d):
-        start = pl.multiple_of(serve[d] * BR, BR)
-        return pltpu.make_async_copy(anchors.at[pl.ds(start, BR), :], served.at[d], sems.at[d])
-
     def begin(j, carry):
-        copy(order[j]).start()
+        d = order[j]
+        served[d] = anchors[pl.ds(pl.multiple_of(serve[d] * BR, BR), BR), :]
         return carry
 
     def after(i):
         lax.fori_loop(ready[i], ready[i + 1], begin, 0)
 
     place_rows(anchors, [(row.astype(I32), corner[:n, :])], begun, after)
-
-    def finish(d, carry):
-        copy(d).wait()
-        return carry
-
-    lax.fori_loop(0, served.shape[0], finish, 0)
 
 
 def scores_kernel(need, column, anchors, partners, weights, stats):
@@ -458,11 +449,9 @@
     anchors, served, slots_corner = call(
         far_kernel,
         "far",
-        (whole, pltpu.HBM((dp, BR, e), BF), ids_shape),
+        (whole, sds((dp, BR, e), BF), ids_shape),
         (serve, order, ready, partial, corner),
         in_specs=[smem] * 3 + [vmem] * 2,
-        out_specs=(vmem, pl.BlockSpec(memory_space=pltpu.HBM), vmem),
-        scratch_shapes=[pltpu.SemaphoreType.DMA((dp,))],
     )
     fetched = exchange(served, FETCH)
     weights, stats = call(
@@ -511,7 +500,7 @@
     back = call(
         back_kernel,
         "back",
-        pltpu.HBM((count, e), BF),
+        sds((count, e), BF),
         (chip, from_across, back_pick),
     )
     returned = exchange(back.reshape(devices, cap, e), DISPATCH).reshape(count, e)
@@ -528,7 +517,7 @@
     partial = call(
         head_grad_kernel,
         "head_grad",
-        pltpu.HBM((width // 2, e), BF),
+        sds((width // 2, e), BF),
         (begun, theirs, swap(grad)),
     )
     parts = exchange(partial.reshape(devices // 2, width // devices, e), REDUCE)

time: 208 us -> 205 us (0.986)
  Pallas kernels: 39.5 us -> 36.6 us
    pallas_call x18, Pallas kernels: 39.5 us -> 36.6 us  [call(): pl.pallas_call(kernel, out_shape=shapes, compiler_params=params(), name=n...]
where the time goes in v11:
time: 205 us
  blocking collectives  106 us (52%)
  waiting for transfers between devices  38.6 us (19%)
  Pallas kernels  36.6 us (18%)
  starting transfers between devices  18.9 us (9%)
    all_to_all x3, blocking collectives, exchange(): return lax.all_to_all(x, axes, 0, 0, tiled=True)  106 us
    pallas_call x18, Pallas kernels, call(): pl.pallas_call(kernel, out_shape=shapes, compiler_params=params(), name=n...  36.6 us
    ppermute x12, waiting for transfers between devices, swap(): return lax.ppermute(x, axes, [(i, size - 1 - i) for i in range(size)])  23.8 us
    all_to_all x1, waiting for transfers between devices, exchange(): return lax.all_to_all(x, axes, 0, 0, tiled=True)  14.8 us
    all_to_all x1, starting transfers between devices, exchange(): return lax.all_to_all(x, axes, 0, 0, tiled=True)  11.1 us
    ppermute x12, starting transfers between devices, swap(): return lax.ppermute(x, axes, [(i, size - 1 - i) for i in range(size)])  7.76 us
  transfers between devices with their start and end apart: 13, of which 7 were waited for; matrix products, arithmetic and copies ran while one was open for 1% of the time, Pallas kernels for 8%

profile of v11, /device:TPU:0, one launch (start us, length us, event | category | flops | bytes accessed | tf_op | source)
XLA Modules:
  0.0 205.0 jit_solution(5989723634778502481)
XLA Ops:
  1.3 6.4 %project.1 = (bf16[1024,640]{1,0:T(8,128)(2,1)}, f32[512,512]{1,0:T(8,128)}, f32[16,512]{1,0:T(8,128)}) custom-call(s32[1,512]{1,0:T(1,128)S(1)} %bitcast.26, bf16[512,2048]{1,0:T(8,128)(2,1)} %r_1_.2, bf16[2048,512]{1,0:T(8,128)(2,1)} %r_2_.1), custom_call_target="tpu_custom_call" | custom-call | tf_op jit(solution)/shard_map/project/pallas_call | solution.py:369
  7.8 11.1 %all-to-all-start = ((bf16[128,8,640]{2,1,0:T(8,128)(2,1)}), bf16[128,8,640]{2,1,0:T(8,128)(2,1)S(1)}, u32[]{:S(2)}, u32[]{:S(2)}) async-start(bf16[128,8,640]{2,1,0:T(8,128)(2,1)} %bitcast.27), calls=%async_computation | async-start | bytes 2621440 | tf_op jit(solution)/shard_map/all_to_all | solution.py:344
  18.9 1.7 stripes.1
  20.6 1.0 copy-done.1
  22.7 1.7 collective-permute-done.theirs
  24.4 14.8 %all-to-all-done = bf16[128,8,640]{2,1,0:T(8,128)(2,1)S(1)} async-done(((bf16[128,8,640]{2,1,0:T(8,128)(2,1)}), bf16[128,8,640]{2,1,0:T(8,128)(2,1)S(1)}, u32[]{:S(2)}, u32[]{:S(2)}) %all-to-all-start) | async-done | bytes 1310752 | tf_op jit(solution)/shard_map/all_to_all | solution.py:344
  39.3 1.2 compact.1
  40.4 1.9 collective-permute-start.2
  42.4 3.6 %near.1 = (bf16[2048,512]{1,0:T(8,128)(2,1)S(1)}, f32[2,8,512]{2,1,0:T(8,128)S(1)}, s32[16,128]{1,0:T(8,128)S(1)}) custom-call(bf16[528,512]{1,0:T(8,128)(2,1)S(1)} %get-tuple-element.47.own, bf16[528,512]{1,0:T(8,128)(2,1)S(1)} %collective-permute-done.1.beside), custom_call_target="tpu_custom_call" | custom-call | flops 4000000000 | bytes 4000000 | tf_op jit(solution)/shard_map/near/pallas_call | solution.py:369
  46.1 10.3 %collective-permute-done.2.across = bf16[528,512]{1,0:T(8,128)(2,1)S(1)} collective-permute-done((bf16[528,512]{1,0:T(8,128)(2,1)S(1)}, bf16[528,512]{1,0:T(8,128)(2,1)S(1)}, u32[]{:S(2)}, u32[]{:S(2)}) %collective-permute-start.2) | collective-permute-done | bytes 540704 | tf_op jit(solution)/shard_map/ppermute | solution.py:340
  56.4 2.5 %middle.1 = (bf16[2048,512]{1,0:T(8,128)(2,1)S(1)}, f32[8,512]{1,0:T(8,128)S(1)}) custom-call(bf16[2048,512]{1,0:T(8,128)(2,1)S(1)} %get-tuple-element.54.begun, bf16[528,512]{1,0:T(8,128)(2,1)S(1)} %collective-permute-done.2.across), custom_call_target="tpu_custom_call" | custom-call | tf_op jit(solution)/shard_map/middle/pallas_call | solution.py:369
  58.9 3.7 %far.1 = (bf16[2048,512]{1,0:T(8,128)(2,1)S(1)}, bf16[32,128,512]{2,1,0:T(8,128)(2,1)S(1)}, f32[8,512]{1,0:T(8,128)S(1)}) custom-call(s32[32]{0:T(128)S(1)} %select_reduce_fusion.2.serve, s32[32]{0:T(128)S(1)} %select_reduce_fusion.1.order, s32[9]{0:T(128)S(1)} %convert_reduce_fusion.1.ready, bf16[2048,512]{1,0:T(8,128)(2,1)S(1)} %get-tuple-element.56.begun, ...), custom_call_target="tpu_custom_call" | custom-call | tf_op jit(solution)/shard_map/far/pallas_call | solution.py:369
  62.6 56.2 %all_to_all.20.partners = bf16[32,128,512]{2,1,0:T(8,128)(2,1)S(1)} all-to-all(bf16[32,128,512]{2,1,0:T(8,128)(2,1)S(1)} %get-tuple-element.58), channel_id=1, replica_groups=mesh['z'=4,'x'=4,'core'=2,'yhi'=2,'ylo'=2] {'ylo','x','z'}, dimensions={0} | all-to-all | bytes 8388608 | tf_op jit(solution)/shard_map/all_to_all | solution.py:344
  118.8 2.4 %scores.1 = (bf16[16,256,128]{2,1,0:T(8,128)(2,1)S(1)}, f32[32,128]{1,0:T(8,128)S(1)}) custom-call(s32[32]{0:T(128)S(1)} %get-tuple-element.45.need, s32[16,128]{1,0:T(8,128)S(1)} %fusion.10.column, bf16[2048,512]{1,0:T(8,128)(2,1)S(1)} %get-tuple-element.57.anchors, bf16[32,128,512]{2,1,0:T(8,128)(2,1)S(1)} %all_to_all.20.partners), custom_call_target="tpu_custom_call" | custom-call | tf_op jit(solution)/shard_map/scores/pallas_call | solution.py:369
  121.5 1.5 collective-permute-start.5
  123.0 1.3 collective-permute-start.4
  124.3 2.4 %mix.1 = (bf16[2048,512]{1,0:T(8,128)(2,1)S(1)}, bf16[2048,512]{1,0:T(8,128)(2,1)S(1)}) custom-call(s32[32]{0:T(128)S(1)} %get-tuple-element.45.need, s32[16,128]{1,0:T(8,128)S(1)} %fusion.10.column, bf16[16,256,128]{2,1,0:T(8,128)(2,1)S(1)} %get-tuple-element.60.weights, bf16[32,128,512]{2,1,0:T(8,128)(2,1)S(1)} %all_to_all.20.partners), custom_call_target="tpu_custom_call" | custom-call | tf_op jit(solution)/shard_map/mix/pallas_call | solution.py:369
  126.8 2.1 %shares.1 = (bf16[2048,512]{1,0:T(8,128)(2,1)S(1)}, bf16[512,512]{1,0:T(8,128)(2,1)S(1)}) custom-call(f32[32,128]{1,0:T(8,128)S(1)} %get-tuple-element.59.r_0_, f32[32,128]{1,0:T(8,128)S(1)} %collective-permute-done.4.r_1_, f32[32,128]{1,0:T(8,128)S(1)} %collective-permute-done.5.r_2_, f32[32,128]{1,0:T(8,128)S(1)} %collective-permute-done.6.r_3_, ...), custom_call_target="tpu_custom_call" | custom-call | tf_op jit(solution)/shard_map/shares/pallas_call | solution.py:369
  129.2 1.6 beside.1
  131.3 1.6 across.1
  133.1 1.7 collective-permute-start.10
  134.9 1.6 own.1
  136.5 2.0 collective-permute-done.8
  139.8 8.5 %collective-permute-done.10.across = bf16[512,512]{1,0:T(8,128)(2,1)S(1)} collective-permute-done((bf16[512,512]{1,0:T(8,128)(2,1)S(1)}, bf16[512,512]{1,0:T(8,128)(2,1)S(1)}, u32[]{:S(2)}, u32[]{:S(2)}) %collective-permute-start.10) | collective-permute-done | bytes 524320 | tf_op jit(solution)/shard_map/ppermute | solution.py:340
  148.3 0.7 back.1
  149.0 26.0 %all_to_all.21 = bf16[128,8,512]{2,1,0:T(8,128)(2,1)S(1)} all-to-all(bf16[128,8,512]{2,1,0:T(8,128)(2,1)S(1)} %bitcast.23), channel_id=1, replica_groups=mesh['z'=4,'x'=4,'core'=2,'yhi'=2,'ylo'=2] {'core','x','yhi','ylo','z'}, dimensions={0} | all-to-all | bytes 2097152 | tf_op jit(solution)/shard_map/all_to_all | solution.py:344
  175.0 2.3 %unit_grad.1.grad = bf16[512,512]{1,0:T(8,128)(2,1)S(1)} custom-call(bf16[1024,512]{1,0:T(8,128)(2,1)S(1)} %bitcast.24, f32[16,512]{1,0:T(8,128)S(1)} %copy-done.3, f32[512,512]{1,0:T(8,128)} %get-tuple-element.76.unit), custom_call_target="tpu_custom_call" | custom-call | tf_op jit(solution)/shard_map/unit_grad/pallas_call | solution.py:369
  177.4 0.7 head_begun.1.begun
  178.1 1.2 collective-permute-done.11.partner
  179.3 0.7 head_grad.1
  180.0 24.2 %all_to_all.22.parts = bf16[64,16,512]{2,1,0:T(8,128)(2,1)S(1)} all-to-all(bf16[64,16,512]{2,1,0:T(8,128)(2,1)S(1)} %bitcast.25), channel_id=1, replica_groups=mesh['z'=4,'x'=4,'core'=2,'yhi'=2,'ylo'=2] {'x','yhi','ylo','z'}, dimensions={0} | all-to-all | bytes 2097152 | tf_op jit(solution)/shard_map/all_to_all | solution.py:344
  204.2 0.8 add.126
  (49 shorter events, 4.6 us)
Async XLA Ops:
  0.6 0.7 copy-start.4
  7.7 11.2 %copy-start = (bf16[512,2048]{1,0:T(8,128)(2,1)S(1)}, bf16[512,2048]{1,0:T(8,128)(2,1)}, u32[]{:S(2)}) copy-start(bf16[512,2048]{1,0:T(8,128)(2,1)} %r_1_.2) | copy-start | bytes 6291460
  7.7 13.9 %copy-start.6 = (s32[512,8]{0,1:T(8,128)S(1)}, s32[512,8]{0,1:T(8,128)}, u32[]{:S(2)}) copy-start(s32[512,8]{0,1:T(8,128)} %param.8) | copy-start | bytes 49156
  7.7 14.2 %copy-start.5 = (s32[2048]{0:T(1024)S(1)}, s32[2048]{0:T(1024)}, u32[]{:S(2)}) copy-start(s32[2048]{0:T(1024)} %param.9) | copy-start | bytes 24580
  7.8 31.5 %all-to-all-start = ((bf16[128,8,640]{2,1,0:T(8,128)(2,1)}), bf16[128,8,640]{2,1,0:T(8,128)(2,1)S(1)}, u32[]{:S(2)}, u32[]{:S(2)}) async-start(bf16[128,8,640]{2,1,0:T(8,128)(2,1)} %bitcast.27), calls=%async_computation | async-start | bytes 2621440 | tf_op jit(solution)/shard_map/all_to_all | solution.py:344
  20.6 1.0 copy-start.1
  21.6 2.9 %collective-permute-start = (bf16[1024,512]{1,0:T(8,128)(2,1)}, bf16[1024,512]{1,0:T(8,128)(2,1)S(1)}, u32[]{:S(2)}, u32[]{:S(2)}) collective-permute-start(bf16[1024,512]{1,0:T(8,128)(2,1)} %get-tuple-element.44), channel_id=1, source_target_pairs={{0,4},{4,0},{1,5},{5,1},{2,6},{6,2},{3,7},{7,3},{8,12},{12,8},{9,1... | collective-permute-start | bytes 3145736 | tf_op jit(solution)/shard_map/ppermute | solution.py:340
  40.4 1.9 collective-permute-start.1
  40.4 15.9 %collective-permute-start.2 = (bf16[528,512]{1,0:T(8,128)(2,1)S(1)}, bf16[528,512]{1,0:T(8,128)(2,1)S(1)}, u32[]{:S(2)}, u32[]{:S(2)}) collective-permute-start(bf16[528,512]{1,0:T(8,128)(2,1)S(1)} %get-tuple-element.47.own), channel_id=1, source_target_pairs={{0,3},{1,2},{2,1},{3,0},{4,7},{5,6},{6,5},{7,4},{8,11},{9,10},{10,... | collective-permute-start | bytes 1622024 | tf_op jit(solution)/shard_map/ppermute | solution.py:340
  56.4 2.5 %collective-permute-start.3 = (bf16[528,512]{1,0:T(8,128)(2,1)S(1)}, bf16[528,512]{1,0:T(8,128)(2,1)S(1)}, u32[]{:S(2)}, u32[]{:S(2)}) collective-permute-start(bf16[528,512]{1,0:T(8,128)(2,1)S(1)} %collective-permute-done.2.across), channel_id=1, source_target_pairs={{0,4},{4,0},{1,5},{5,1},{2,6},{6,2},{3,7},{7,3},{8,12},{12,8},{9,1... | collective-permute-start | bytes 1622024 | tf_op jit(solution)/shard_map/ppermute | solution.py:340
  121.2 5.6 %collective-permute-start.6 = (f32[32,128]{1,0:T(8,128)S(1)}, f32[32,128]{1,0:T(8,128)S(1)}, u32[]{:S(2)}, u32[]{:S(2)}) collective-permute-start(f32[32,128]{1,0:T(8,128)S(1)} %get-tuple-element.59.r_0_), channel_id=1, source_target_pairs={{0,7},{1,6},{2,5},{3,4},{4,3},{5,2},{6,1},{7,0},{8,15},{9,14},{10,... | collective-permute-start | bytes 49160 | tf_op jit(solution)/shard_map/ppermute | solution.py:340
  121.5 5.3 %collective-permute-start.5 = (f32[32,128]{1,0:T(8,128)S(1)}, f32[32,128]{1,0:T(8,128)S(1)}, u32[]{:S(2)}, u32[]{:S(2)}) collective-permute-start(f32[32,128]{1,0:T(8,128)S(1)} %get-tuple-element.59.r_0_), channel_id=1, source_target_pairs={{0,3},{1,2},{2,1},{3,0},{4,7},{5,6},{6,5},{7,4},{8,11},{9,10},{10,... | collective-permute-start | bytes 49160 | tf_op jit(solution)/shard_map/ppermute | solution.py:340
  123.0 3.8 %collective-permute-start.4 = (f32[32,128]{1,0:T(8,128)S(1)}, f32[32,128]{1,0:T(8,128)S(1)}, u32[]{:S(2)}, u32[]{:S(2)}) collective-permute-start(f32[32,128]{1,0:T(8,128)S(1)} %get-tuple-element.59.r_0_), channel_id=1, source_target_pairs={{0,4},{4,0},{1,5},{5,1},{2,6},{6,2},{3,7},{7,3},{8,12},{12,8},{9,1... | collective-permute-start | bytes 49160 | tf_op jit(solution)/shard_map/ppermute | solution.py:340
  128.9 4.1 %collective-permute-start.9 = (bf16[512,512]{1,0:T(8,128)(2,1)S(1)}, bf16[512,512]{1,0:T(8,128)(2,1)S(1)}, u32[]{:S(2)}, u32[]{:S(2)}) collective-permute-start(bf16[512,512]{1,0:T(8,128)(2,1)S(1)} %get-tuple-element.73), channel_id=1, source_target_pairs={{0,4},{4,0},{1,5},{5,1},{2,6},{6,2},{3,7},{7,3},{8,12},{12,8},{9,1... | collective-permute-start | bytes 1572872 | tf_op jit(solution)/shard_map/ppermute | solution.py:340
  130.8 8.4 %collective-permute-start.7 = (bf16[512,512]{1,0:T(8,128)(2,1)S(1)}, bf16[512,512]{1,0:T(8,128)(2,1)S(1)}, u32[]{:S(2)}, u32[]{:S(2)}) collective-permute-start(bf16[512,512]{1,0:T(8,128)(2,1)S(1)} %beside.1), channel_id=1, source_target_pairs={{0,4},{4,0},{1,5},{5,1},{2,6},{6,2},{3,7},{7,3},{8,12},{12,8},{9,1... | collective-permute-start | bytes 1572872 | tf_op jit(solution)/shard_map/ppermute | solution.py:340
  133.1 15.2 %collective-permute-start.10 = (bf16[512,512]{1,0:T(8,128)(2,1)S(1)}, bf16[512,512]{1,0:T(8,128)(2,1)S(1)}, u32[]{:S(2)}, u32[]{:S(2)}) collective-permute-start(bf16[512,512]{1,0:T(8,128)(2,1)S(1)} %add_convert_fusion), channel_id=1, source_target_pairs={{0,3},{1,2},{2,1},{3,0},{4,7},{5,6},{6,5},{7,4},{8,11},{9,10},{10,... | collective-permute-start | bytes 1572872 | tf_op jit(solution)/shard_map/ppermute | solution.py:340
  134.8 3.7 %collective-permute-start.8 = (f32[2048]{0:T(1024)S(1)}, f32[2048]{0:T(1024)S(1)}, u32[]{:S(2)}, u32[]{:S(2)}) collective-permute-start(f32[2048]{0:T(1024)S(1)} %fusion.9), channel_id=1, source_target_pairs={{0,1},{1,0},{2,3},{3,2},{4,5},{5,4},{6,7},{7,6},{8,9},{9,8},{10,11... | collective-permute-start | bytes 24584 | tf_op jit(solution)/shard_map/ppermute | solution.py:340
  139.8 35.2 %copy-start.3 = (f32[16,512]{1,0:T(8,128)S(1)}, f32[16,512]{1,0:T(8,128)}, u32[]{:S(2)}) copy-start(f32[16,512]{1,0:T(8,128)} %get-tuple-element.75.place) | copy-start | bytes 98308
  149.0 28.4 %copy-start.2 = (bf16[1024,512]{1,0:T(8,128)(2,1)S(1)}, bf16[1024,512]{1,0:T(8,128)(2,1)}, u32[]{:S(2)}) copy-start(bf16[1024,512]{1,0:T(8,128)(2,1)} %copy-done.1) | copy-start | bytes 3145732
  177.3 2.0 collective-permute-start.11

commit v12 on v11

--- a/solution.py
+++ b/solution.py
@@ -68,7 +68,7 @@
 
 
 def project_kernel(
-    owner_slots, sizes, cap, slot, feat_in, head_in, sent, unit, place, feat, head, kept, send, sems
+    owner_slots, sizes, cap, slot, feat_in, head_in, send, unit, place, feat, head, kept, sems
 ):
     n = feat.shape[0]
     width, e = head.shape
@@ -116,20 +116,8 @@
     keep = pltpu.make_async_copy(kept, unit, sems.at[2 * parts])
     keep.start()
     place[8:, :] = jnp.broadcast_to(length, (n, BR)).T[:8, :]
-    descriptor = rows.astype(BF)
-    step = send.shape[0] // parts
-    leave = []
-    for k in range(parts):
-        at = slice(k * step, (k + 1) * step)
-        send[at, :e] = dot(scatter[at, :], descriptor).astype(BF)
-        at = pl.ds(k * step, step)
-        leave.append(
-            pltpu.make_async_copy(send.at[at, :], sent.at[at, :], sems.at[2 * parts + 1 + k])
-        )
-        leave[-1].start()
+    send[:, :e] = dot(scatter, rows.astype(BF)).astype(BF)
     keep.wait()
-    for c in leave:
-        c.wait()
 
 
 def stripes_kernel(sizes, core, feat, mine, other):
@@ -373,61 +361,25 @@
     send, unit, place = call(
         lambda *r: project_kernel(owner_slots, sizes, cap, *r),
         "project",
-        (pltpu.HBM((count, e + BR), BF), pltpu.HBM((n, e), F32), pltpu.HBM((16, n), F32)),
+        (sds((count, e + BR), BF), pltpu.HBM((n, e), F32), pltpu.HBM((16, n), F32)),
         (
             slot_of_image.reshape(1, n),
             pltpu.with_memory_space_constraint(features, pltpu.HBM),
             pltpu.with_memory_space_constraint(head_weight, pltpu.HBM),
         ),
         in_specs=[vmem, far_away, far_away],
-        out_specs=(far_away, far_away, vmem),
+        out_specs=(vmem, far_away, vmem),
         scratch_shapes=[
             pltpu.VMEM((n, width), BF),
             pltpu.VMEM((width, e), BF),
             pltpu.VMEM((n, e), F32),
-            pltpu.VMEM((count, e + BR), BF),
-            pltpu.SemaphoreType.DMA((13,)),
+            pltpu.SemaphoreType.DMA((9,)),
         ],
     )
-    send, late_features = lax.optimization_barrier((send, features))
-    mine, other = call(
-        lambda *r: stripes_kernel(sizes, *r),
-        "stripes",
-        (sds((width // 2, n), BF),) * 2,
-        (core.reshape(1), late_features),
-        in_specs=[smem, vmem],
-    )
+    send, own_positives = lax.optimization_barrier((send, positives.reshape(4, e)))
     got = exchange(send.reshape(devices, cap, e + BR), DISPATCH).reshape(count, e + BR)
-    theirs = swap(other)
-
-    table = candidates.reshape(dp, blocks, REPS, PAIRS_REP)
-    table = lax.dynamic_index_in_dim(table, member, axis=2, keepdims=False)
-    table = table.reshape(dp, blocks * PAIRS_REP)
-    owner = table // blocks
-    numbers = jnp.arange(dp, dtype=I32)
-    wanted = jnp.sum(jnp.where(owner == me, table - owner * blocks, 0), axis=1)
-
-    def fetch_place(number):
-        column = number // 2
-        z = column // sizes["x"]
-        x = column - z * sizes["x"]
-        return position(FETCH, sizes, dict(z=z, x=x, ylo=(number & 1) ^ slab))
-
-    serve = jnp.sum(
-        jnp.where(fetch_place(numbers)[None, :] == numbers[:, None], wanted[None, :], 0), axis=1
-    )
-    need = fetch_place(lax.dynamic_index_in_dim(owner, me, axis=0, keepdims=False))
-    keys = serve * dp + numbers
-    place_of = jnp.sum((keys[None, :] < keys[:, None]).astype(I32), axis=1)
-    order = jnp.sum(jnp.where(place_of[None, :] == numbers[:, None], numbers[None, :], 0), axis=1)
-    bounds = 2 * jnp.arange(blocks // 2 + 1, dtype=I32)
-    ready = jnp.sum((serve[None, :] < bounds[:, None]).astype(I32), axis=1)
-
-    got, serve, order, ready, need, mine, theirs = lax.optimization_barrier(
-        (got, serve, order, ready, need, mine, theirs)
-    )
     packed, back_place = call(
-        compact_kernel, "compact", (sds((n + 16, e), BF), sds((8, count), F32)), (got, positives.reshape(4, e))
+        compact_kernel, "compact", (sds((n + 16, e), BF), sds((8, count), F32)), (got, own_positives)
     )
     beside = swap(packed)
     across = swap(packed, ("yhi", "ylo"))
@@ -441,9 +393,45 @@
         (packed, beside),
         cost_estimate=cost(4),
     )
+    partial, late_features, late_candidates = lax.optimization_barrier(
+        (partial, features, candidates)
+    )
+    mine, other = call(
+        lambda *r: stripes_kernel(sizes, *r),
+        "stripes",
+        (sds((width // 2, n), BF),) * 2,
+        (core.reshape(1), late_features),
+        in_specs=[smem, vmem],
+    )
+    theirs = swap(other)
+    table = late_candidates.reshape(dp, blocks, REPS, PAIRS_REP)
+    table = lax.dynamic_index_in_dim(table, member, axis=2, keepdims=False)
+    table = table.reshape(dp, blocks * PAIRS_REP)
+    owner = table // blocks
+    numbers = jnp.arange(dp, dtype=I32)
+    wanted = jnp.sum(jnp.where(owner == me, table - owner * blocks, 0), axis=1)
+
+    def fetch_place(number):
+        column = number // 2
+        z = column // sizes["x"]
+        x = column - z * sizes["x"]
+        return position(FETCH, sizes, dict(z=z, x=x, ylo=(number & 1) ^ slab))
+
+    serve = jnp.sum(
+        jnp.where(fetch_place(numbers)[None, :] == numbers[:, None], wanted[None, :], 0), axis=1
+    )
+    need = fetch_place(lax.dynamic_index_in_dim(owner, me, axis=0, keepdims=False))
+    keys = serve * dp + numbers
+    place_of = jnp.sum((keys[None, :] < keys[:, None]).astype(I32), axis=1)
+    order = jnp.sum(jnp.where(place_of[None, :] == numbers[:, None], numbers[None, :], 0), axis=1)
+    bounds = 2 * jnp.arange(blocks // 2 + 1, dtype=I32)
+    ready = jnp.sum((serve[None, :] < bounds[:, None]).astype(I32), axis=1)
+
     column = jnp.where(home, positives.reshape(blocks, BR), other_positives)
     column = column - member * (PAIRS_REP * BR)
-    partial, across, column = lax.optimization_barrier((partial, across, column))
+    partial, across, column, mine, theirs, serve, order, ready, need = lax.optimization_barrier(
+        (partial, across, column, mine, theirs, serve, order, ready, need)
+    )
     corner = swap(across)
     partial, slots_across = call(middle_kernel, "middle", (whole, ids_shape), (partial, across))
     anchors, served, slots_corner = call(

time: 205 us -> 205 us (level)
  blocking collectives: 106 us -> 138 us
  waiting for transfers between devices: 38.6 us -> 17.7 us
  starting transfers between devices: 18.9 us -> 8.12 us
    all_to_all x3 -> x4, blocking collectives: 106 us -> 138 us  [exchange(): return lax.all_to_all(x, axes, 0, 0, tiled=True)]
    all_to_all x1 -> x0, waiting for transfers between devices: 14.8 us -> none  [exchange(): return lax.all_to_all(x, axes, 0, 0, tiled=True)]
    all_to_all x1 -> x0, starting transfers between devices: 11.1 us -> none  [exchange(): return lax.all_to_all(x, axes, 0, 0, tiled=True)]
    ppermute x12, waiting for transfers between devices: 23.8 us -> 17.7 us  [swap(): return lax.ppermute(x, axes, [(i, size - 1 - i) for i in range(size)])]
  transfers between devices with their start and end apart: 13 -> 12, of which waited for: 7 -> 5; matrix products, arithmetic and copies ran while one was open for 1% -> 1% of each run, Pallas kernels for 8% -> 8%
where the time goes in v12:
time: 205 us
  blocking collectives  138 us (67%)
  Pallas kernels  35.9 us (18%)
  waiting for transfers between devices  17.7 us (9%)
  starting transfers between devices  8.12 us (4%)
  local copies, waits for them, and re-layouts  2.9 us (1%)
    all_to_all x4, blocking collectives, exchange(): return lax.all_to_all(x, axes, 0, 0, tiled=True)  138 us
    pallas_call x18, Pallas kernels, call(): pl.pallas_call(kernel, out_shape=shapes, compiler_params=params(), name=n...  35.9 us
    ppermute x12, waiting for transfers between devices, swap(): return lax.ppermute(x, axes, [(i, size - 1 - i) for i in range(size)])  17.7 us
    ppermute x12, starting transfers between devices, swap(): return lax.ppermute(x, axes, [(i, size - 1 - i) for i in range(size)])  8.12 us
  transfers between devices with their start and end apart: 12, of which 5 were waited for; matrix products, arithmetic and copies ran while one was open for 1% of the time, Pallas kernels for 8%

profile of v12, /device:TPU:0, one launch (start us, length us, event | category | flops | bytes accessed | tf_op | source)
XLA Modules:
  0.0 204.9 jit_solution(16806925081888243742)
XLA Ops:
  0.6 0.7 reshape.98.positives
  1.3 0.7 copy-done.4
  2.0 5.6 %project.1 = (bf16[1024,640]{1,0:T(8,128)(2,1)S(1)}, f32[512,512]{1,0:T(8,128)}, f32[16,512]{1,0:T(8,128)}) custom-call(s32[1,512]{1,0:T(1,128)S(1)} %bitcast.27, bf16[512,2048]{1,0:T(8,128)(2,1)} %r_1_.2, bf16[2048,512]{1,0:T(8,128)(2,1)} %r_2_.1), custom_call_target="tpu_custom_call" | custom-call | tf_op jit(solution)/shard_map/project/pallas_call | solution.py:357
  7.6 31.3 %all_to_all.20 = bf16[128,8,640]{2,1,0:T(8,128)(2,1)S(1)} all-to-all(bf16[128,8,640]{2,1,0:T(8,128)(2,1)S(1)} %bitcast.26), channel_id=1, replica_groups=mesh['z'=4,'x'=4,'core'=2,'yhi'=2,'ylo'=2] {'core','x','yhi','ylo','z'}, dimensions={0} | all-to-all | bytes 2621440 | tf_op jit(solution)/shard_map/all_to_all | solution.py:332
  38.9 1.2 compact.1
  40.2 1.9 collective-permute-start.1
  42.2 4.6 %near.1 = (bf16[2048,512]{1,0:T(8,128)(2,1)S(1)}, f32[2,8,512]{2,1,0:T(8,128)S(1)}, s32[16,128]{1,0:T(8,128)S(1)}) custom-call(bf16[528,512]{1,0:T(8,128)(2,1)S(1)} %get-tuple-element.45.own, bf16[528,512]{1,0:T(8,128)(2,1)} %collective-permute-done.beside), custom_call_target="tpu_custom_call" | custom-call | flops 4000000000 | bytes 4000000 | tf_op jit(solution)/shard_map/near/pallas_call | solution.py:357
  46.8 1.3 copy-done.1
  48.5 0.7 stripes.1
  50.2 5.9 %collective-permute-done.1.across = bf16[528,512]{1,0:T(8,128)(2,1)S(1)} collective-permute-done((bf16[528,512]{1,0:T(8,128)(2,1)S(1)}, bf16[528,512]{1,0:T(8,128)(2,1)S(1)}, u32[]{:S(2)}, u32[]{:S(2)}) %collective-permute-start.1) | collective-permute-done | bytes 540704 | tf_op jit(solution)/shard_map/ppermute | solution.py:328
  56.2 2.5 %middle.1 = (bf16[2048,512]{1,0:T(8,128)(2,1)S(1)}, f32[8,512]{1,0:T(8,128)S(1)}) custom-call(bf16[2048,512]{1,0:T(8,128)(2,1)S(1)} %copy-done.2, bf16[528,512]{1,0:T(8,128)(2,1)S(1)} %collective-permute-done.1.across), custom_call_target="tpu_custom_call" | custom-call | tf_op jit(solution)/shard_map/middle/pallas_call | solution.py:357
  58.7 3.7 %far.1 = (bf16[2048,512]{1,0:T(8,128)(2,1)S(1)}, bf16[32,128,512]{2,1,0:T(8,128)(2,1)S(1)}, f32[8,512]{1,0:T(8,128)S(1)}) custom-call(s32[32]{0:T(128)S(1)} %select_reduce_fusion.2.serve, s32[32]{0:T(128)S(1)} %select_reduce_fusion.1.order, s32[9]{0:T(128)S(1)} %convert_reduce_fusion.1.ready, bf16[2048,512]{1,0:T(8,128)(2,1)S(1)} %get-tuple-element.60.begun, ...), custom_call_target="tpu_custom_call" | custom-call | tf_op jit(solution)/shard_map/far/pallas_call | solution.py:357
  62.4 56.1 %all_to_all.21.partners = bf16[32,128,512]{2,1,0:T(8,128)(2,1)S(1)} all-to-all(bf16[32,128,512]{2,1,0:T(8,128)(2,1)S(1)} %get-tuple-element.62), channel_id=1, replica_groups=mesh['z'=4,'x'=4,'core'=2,'yhi'=2,'ylo'=2] {'ylo','x','z'}, dimensions={0} | all-to-all | bytes 8388608 | tf_op jit(solution)/shard_map/all_to_all | solution.py:332
  118.5 2.4 %scores.1 = (bf16[16,256,128]{2,1,0:T(8,128)(2,1)S(1)}, f32[32,128]{1,0:T(8,128)S(1)}) custom-call(s32[32]{0:T(128)S(1)} %multiply_add_fusion.need, s32[16,128]{1,0:T(8,128)S(1)} %fusion.10.column, bf16[2048,512]{1,0:T(8,128)(2,1)S(1)} %get-tuple-element.61.anchors, bf16[32,128,512]{2,1,0:T(8,128)(2,1)S(1)} %all_to_all.21.partners), custom_call_target="tpu_custom_call" | custom-call | tf_op jit(solution)/shard_map/scores/pallas_call | solution.py:357
  121.3 1.5 collective-permute-start.5
  122.9 1.3 collective-permute-start.4
  124.1 2.4 %mix.1 = (bf16[2048,512]{1,0:T(8,128)(2,1)S(1)}, bf16[2048,512]{1,0:T(8,128)(2,1)S(1)}) custom-call(s32[32]{0:T(128)S(1)} %multiply_add_fusion.need, s32[16,128]{1,0:T(8,128)S(1)} %fusion.10.column, bf16[16,256,128]{2,1,0:T(8,128)(2,1)S(1)} %get-tuple-element.64.weights, bf16[32,128,512]{2,1,0:T(8,128)(2,1)S(1)} %all_to_all.21.partners), custom_call_target="tpu_custom_call" | custom-call | tf_op jit(solution)/shard_map/mix/pallas_call | solution.py:357
  126.5 2.1 %shares.1 = (bf16[2048,512]{1,0:T(8,128)(2,1)S(1)}, bf16[512,512]{1,0:T(8,128)(2,1)S(1)}) custom-call(f32[32,128]{1,0:T(8,128)S(1)} %get-tuple-element.63.r_0_, f32[32,128]{1,0:T(8,128)S(1)} %collective-permute-done.4.r_1_, f32[32,128]{1,0:T(8,128)S(1)} %collective-permute-done.5.r_2_, f32[32,128]{1,0:T(8,128)S(1)} %collective-permute-done.6.r_3_, ...), custom_call_target="tpu_custom_call" | custom-call | tf_op jit(solution)/shard_map/shares/pallas_call | solution.py:357
  129.0 1.6 beside.1
  131.1 1.6 across.1
  132.9 1.8 collective-permute-start.10
  134.8 1.6 own.1
  136.4 2.0 collective-permute-done.8
  139.7 8.5 %collective-permute-done.10.across = bf16[512,512]{1,0:T(8,128)(2,1)S(1)} collective-permute-done((bf16[512,512]{1,0:T(8,128)(2,1)S(1)}, bf16[512,512]{1,0:T(8,128)(2,1)S(1)}, u32[]{:S(2)}, u32[]{:S(2)}) %collective-permute-start.10) | collective-permute-done | bytes 524320 | tf_op jit(solution)/shard_map/ppermute | solution.py:328
  148.1 0.7 back.1
  148.9 26.0 %all_to_all.22 = bf16[128,8,512]{2,1,0:T(8,128)(2,1)S(1)} all-to-all(bf16[128,8,512]{2,1,0:T(8,128)(2,1)S(1)} %bitcast.23), channel_id=1, replica_groups=mesh['z'=4,'x'=4,'core'=2,'yhi'=2,'ylo'=2] {'core','x','yhi','ylo','z'}, dimensions={0} | all-to-all | bytes 2097152 | tf_op jit(solution)/shard_map/all_to_all | solution.py:332
  174.8 2.3 %unit_grad.1.grad = bf16[512,512]{1,0:T(8,128)(2,1)S(1)} custom-call(bf16[1024,512]{1,0:T(8,128)(2,1)S(1)} %bitcast.24, f32[16,512]{1,0:T(8,128)S(1)} %copy-done.3, f32[512,512]{1,0:T(8,128)} %get-tuple-element.80.unit), custom_call_target="tpu_custom_call" | custom-call | tf_op jit(solution)/shard_map/unit_grad/pallas_call | solution.py:357
  177.2 0.7 head_begun.1.begun
  177.9 1.2 collective-permute-done.11.partner
  179.1 0.7 head_grad.1
  179.8 24.2 %all_to_all.23.parts = bf16[64,16,512]{2,1,0:T(8,128)(2,1)S(1)} all-to-all(bf16[64,16,512]{2,1,0:T(8,128)(2,1)S(1)} %bitcast.25), channel_id=1, replica_groups=mesh['z'=4,'x'=4,'core'=2,'yhi'=2,'ylo'=2] {'x','yhi','ylo','z'}, dimensions={0} | all-to-all | bytes 2097152 | tf_op jit(solution)/shard_map/all_to_all | solution.py:332
  204.1 0.8 add.126
  (49 shorter events, 4.2 us)
Async XLA Ops:
  1.3 0.7 copy-start.4
  40.1 2.1 %collective-permute-start = (bf16[528,512]{1,0:T(8,128)(2,1)S(1)}, bf16[528,512]{1,0:T(8,128)(2,1)}, u32[]{:S(2)}, u32[]{:S(2)}) collective-permute-start(bf16[528,512]{1,0:T(8,128)(2,1)S(1)} %get-tuple-element.45.own), channel_id=1, source_target_pairs={{0,4},{4,0},{1,5},{5,1},{2,6},{6,2},{3,7},{7,3},{8,12},{12,8},{9,1... | collective-permute-start | bytes 1622024 | tf_op jit(solution)/shard_map/ppermute | solution.py:328
  40.2 8.0 %copy-start.6 = (s32[512,8]{0,1:T(8,128)S(1)}, s32[512,8]{0,1:T(8,128)}, u32[]{:S(2)}) copy-start(s32[512,8]{0,1:T(8,128)} %param.8) | copy-start | bytes 49156
  40.2 8.3 %copy-start = (bf16[512,2048]{1,0:T(8,128)(2,1)S(1)}, bf16[512,2048]{1,0:T(8,128)(2,1)}, u32[]{:S(2)}) copy-start(bf16[512,2048]{1,0:T(8,128)(2,1)} %r_1_.2) | copy-start | bytes 6291460
  40.2 16.0 %collective-permute-start.1 = (bf16[528,512]{1,0:T(8,128)(2,1)S(1)}, bf16[528,512]{1,0:T(8,128)(2,1)S(1)}, u32[]{:S(2)}, u32[]{:S(2)}) collective-permute-start(bf16[528,512]{1,0:T(8,128)(2,1)S(1)} %get-tuple-element.45.own), channel_id=1, source_target_pairs={{0,3},{1,2},{2,1},{3,0},{4,7},{5,6},{6,5},{7,4},{8,11},{9,10},{10,... | collective-permute-start | bytes 1622024 | tf_op jit(solution)/shard_map/ppermute | solution.py:328
  46.8 1.3 copy-start.1
  48.2 2.0 %copy-start.5 = (s32[2048]{0:T(1024)S(1)}, s32[2048]{0:T(1024)}, u32[]{:S(2)}) copy-start(s32[2048]{0:T(1024)} %param.9) | copy-start | bytes 24580
  48.5 7.7 %copy-start.2 = (bf16[2048,512]{1,0:T(8,128)(2,1)S(1)}, bf16[2048,512]{1,0:T(8,128)(2,1)}, u32[]{:S(2)}) copy-start(bf16[2048,512]{1,0:T(8,128)(2,1)} %copy-done.1) | copy-start | bytes 6291460
  49.2 6.9 %collective-permute-start.2 = (bf16[1024,512]{1,0:T(8,128)(2,1)S(1)}, bf16[1024,512]{1,0:T(8,128)(2,1)S(1)}, u32[]{:S(2)}, u32[]{:S(2)}) collective-permute-start(bf16[1024,512]{1,0:T(8,128)(2,1)S(1)} %get-tuple-element.51), channel_id=1, source_target_pairs={{0,4},{4,0},{1,5},{5,1},{2,6},{6,2},{3,7},{7,3},{8,12},{12,8},{9,1... | collective-permute-start | bytes 3145736 | tf_op jit(solution)/shard_map/ppermute | solution.py:328
  56.2 2.5 %collective-permute-start.3 = (bf16[528,512]{1,0:T(8,128)(2,1)S(1)}, bf16[528,512]{1,0:T(8,128)(2,1)S(1)}, u32[]{:S(2)}, u32[]{:S(2)}) collective-permute-start(bf16[528,512]{1,0:T(8,128)(2,1)S(1)} %collective-permute-done.1.across), channel_id=1, source_target_pairs={{0,4},{4,0},{1,5},{5,1},{2,6},{6,2},{3,7},{7,3},{8,12},{12,8},{9,1... | collective-permute-start | bytes 1622024 | tf_op jit(solution)/shard_map/ppermute | solution.py:328
  120.9 5.6 %collective-permute-start.6 = (f32[32,128]{1,0:T(8,128)S(1)}, f32[32,128]{1,0:T(8,128)S(1)}, u32[]{:S(2)}, u32[]{:S(2)}) collective-permute-start(f32[32,128]{1,0:T(8,128)S(1)} %get-tuple-element.63.r_0_), channel_id=1, source_target_pairs={{0,7},{1,6},{2,5},{3,4},{4,3},{5,2},{6,1},{7,0},{8,15},{9,14},{10,... | collective-permute-start | bytes 49160 | tf_op jit(solution)/shard_map/ppermute | solution.py:328
  121.3 5.2 %collective-permute-start.5 = (f32[32,128]{1,0:T(8,128)S(1)}, f32[32,128]{1,0:T(8,128)S(1)}, u32[]{:S(2)}, u32[]{:S(2)}) collective-permute-start(f32[32,128]{1,0:T(8,128)S(1)} %get-tuple-element.63.r_0_), channel_id=1, source_target_pairs={{0,3},{1,2},{2,1},{3,0},{4,7},{5,6},{6,5},{7,4},{8,11},{9,10},{10,... | collective-permute-start | bytes 49160 | tf_op jit(solution)/shard_map/ppermute | solution.py:328
  122.9 3.7 %collective-permute-start.4 = (f32[32,128]{1,0:T(8,128)S(1)}, f32[32,128]{1,0:T(8,128)S(1)}, u32[]{:S(2)}, u32[]{:S(2)}) collective-permute-start(f32[32,128]{1,0:T(8,128)S(1)} %get-tuple-element.63.r_0_), channel_id=1, source_target_pairs={{0,4},{4,0},{1,5},{5,1},{2,6},{6,2},{3,7},{7,3},{8,12},{12,8},{9,1... | collective-permute-start | bytes 49160 | tf_op jit(solution)/shard_map/ppermute | solution.py:328
  128.6 4.1 %collective-permute-start.9 = (bf16[512,512]{1,0:T(8,128)(2,1)S(1)}, bf16[512,512]{1,0:T(8,128)(2,1)S(1)}, u32[]{:S(2)}, u32[]{:S(2)}) collective-permute-start(bf16[512,512]{1,0:T(8,128)(2,1)S(1)} %get-tuple-element.77), channel_id=1, source_target_pairs={{0,4},{4,0},{1,5},{5,1},{2,6},{6,2},{3,7},{7,3},{8,12},{12,8},{9,1... | collective-permute-start | bytes 1572872 | tf_op jit(solution)/shard_map/ppermute | solution.py:328
  130.7 8.4 %collective-permute-start.7 = (bf16[512,512]{1,0:T(8,128)(2,1)S(1)}, bf16[512,512]{1,0:T(8,128)(2,1)S(1)}, u32[]{:S(2)}, u32[]{:S(2)}) collective-permute-start(bf16[512,512]{1,0:T(8,128)(2,1)S(1)} %beside.1), channel_id=1, source_target_pairs={{0,4},{4,0},{1,5},{5,1},{2,6},{6,2},{3,7},{7,3},{8,12},{12,8},{9,1... | collective-permute-start | bytes 1572872 | tf_op jit(solution)/shard_map/ppermute | solution.py:328
  132.9 15.3 %collective-permute-start.10 = (bf16[512,512]{1,0:T(8,128)(2,1)S(1)}, bf16[512,512]{1,0:T(8,128)(2,1)S(1)}, u32[]{:S(2)}, u32[]{:S(2)}) collective-permute-start(bf16[512,512]{1,0:T(8,128)(2,1)S(1)} %add_convert_fusion), channel_id=1, source_target_pairs={{0,3},{1,2},{2,1},{3,0},{4,7},{5,6},{6,5},{7,4},{8,11},{9,10},{10,... | collective-permute-start | bytes 1572872 | tf_op jit(solution)/shard_map/ppermute | solution.py:328
  134.7 3.7 %collective-permute-start.8 = (f32[2048]{0:T(1024)S(1)}, f32[2048]{0:T(1024)S(1)}, u32[]{:S(2)}, u32[]{:S(2)}) collective-permute-start(f32[2048]{0:T(1024)S(1)} %fusion.9), channel_id=1, source_target_pairs={{0,1},{1,0},{2,3},{3,2},{4,5},{5,4},{6,7},{7,6},{8,9},{9,8},{10,11... | collective-permute-start | bytes 24584 | tf_op jit(solution)/shard_map/ppermute | solution.py:328
  139.7 35.2 %copy-start.3 = (f32[16,512]{1,0:T(8,128)S(1)}, f32[16,512]{1,0:T(8,128)}, u32[]{:S(2)}) copy-start(f32[16,512]{1,0:T(8,128)} %get-tuple-element.79.place) | copy-start | bytes 98308
  177.1 2.0 collective-permute-start.11

commit v13 on v12

--- a/solution.py
+++ b/solution.py
@@ -393,8 +393,8 @@
         (packed, beside),
         cost_estimate=cost(4),
     )
-    partial, late_features, late_candidates = lax.optimization_barrier(
-        (partial, features, candidates)
+    partial, late_features, late_candidates, slab, me = lax.optimization_barrier(
+        (partial, features, candidates, slab, me)
     )
     mine, other = call(
         lambda *r: stripes_kernel(sizes, *r),

time: 205 us -> 209 us (1.020)
  Pallas kernels: 35.9 us -> 38.7 us
    pallas_call x18, Pallas kernels: 35.9 us -> 38.7 us  [call(): pl.pallas_call(kernel, out_shape=shapes, compiler_params=params(), name=n...]
  transfers between devices with their start and end apart: 12 -> 12, of which waited for: 5 -> 5; matrix products, arithmetic and copies ran while one was open for 1% -> 1% of each run, Pallas kernels for 8% -> 9%
where the time goes in v13:
time: 209 us
  blocking collectives  138 us (66%)
  Pallas kernels  38.7 us (19%)
  waiting for transfers between devices  17.1 us (8%)
  starting transfers between devices  7.93 us (4%)
  local copies, waits for them, and re-layouts  4.5 us (2%)
    all_to_all x4, blocking collectives, exchange(): return lax.all_to_all(x, axes, 0, 0, tiled=True)  138 us
    pallas_call x18, Pallas kernels, call(): pl.pallas_call(kernel, out_shape=shapes, compiler_params=params(), name=n...  38.7 us
    ppermute x12, waiting for transfers between devices, swap(): return lax.ppermute(x, axes, [(i, size - 1 - i) for i in range(size)])  17.1 us
    ppermute x12, starting transfers between devices, swap(): return lax.ppermute(x, axes, [(i, size - 1 - i) for i in range(size)])  7.93 us
  transfers between devices with their start and end apart: 12, of which 5 were waited for; matrix products, arithmetic and copies ran while one was open for 1% of the time, Pallas kernels for 9%

profile of v13, /device:TPU:0, one launch (start us, length us, event | category | flops | bytes accessed | tf_op | source)
XLA Modules:
  0.0 208.6 jit_solution(339182696179693991)
XLA Ops:
  0.6 0.7 reshape.98.positives
  2.0 5.6 %project.1 = (bf16[1024,640]{1,0:T(8,128)(2,1)S(1)}, f32[512,512]{1,0:T(8,128)}, f32[16,512]{1,0:T(8,128)}) custom-call(s32[1,512]{1,0:T(1,128)S(1)} %bitcast.27, bf16[512,2048]{1,0:T(8,128)(2,1)} %r_1_.2, bf16[2048,512]{1,0:T(8,128)(2,1)} %r_2_.1), custom_call_target="tpu_custom_call" | custom-call | tf_op jit(solution)/shard_map/project/pallas_call | solution.py:357
  7.6 31.3 %all_to_all.20 = bf16[128,8,640]{2,1,0:T(8,128)(2,1)S(1)} all-to-all(bf16[128,8,640]{2,1,0:T(8,128)(2,1)S(1)} %bitcast.26), channel_id=1, replica_groups=mesh['z'=4,'x'=4,'core'=2,'yhi'=2,'ylo'=2] {'core','x','yhi','ylo','z'}, dimensions={0} | all-to-all | bytes 2621440 | tf_op jit(solution)/shard_map/all_to_all | solution.py:332
  38.9 2.0 compact.1
  40.9 1.9 collective-permute-start.1
  43.1 4.6 %near.1 = (bf16[2048,512]{1,0:T(8,128)(2,1)S(1)}, f32[2,8,512]{2,1,0:T(8,128)S(1)}, s32[16,128]{1,0:T(8,128)S(1)}) custom-call(bf16[528,512]{1,0:T(8,128)(2,1)} %get-tuple-element.47.own, bf16[528,512]{1,0:T(8,128)(2,1)S(1)} %collective-permute-done.beside), custom_call_target="tpu_custom_call" | custom-call | flops 4000000000 | bytes 4000000 | tf_op jit(solution)/shard_map/near/pallas_call | solution.py:357
  47.7 1.3 copy-done.1
  49.4 1.7 stripes.1
  52.0 5.1 %collective-permute-done.1.across = bf16[528,512]{1,0:T(8,128)(2,1)} collective-permute-done((bf16[528,512]{1,0:T(8,128)(2,1)}, bf16[528,512]{1,0:T(8,128)(2,1)}, u32[]{:S(2)}, u32[]{:S(2)}) %collective-permute-start.1) | collective-permute-done | bytes 540704 | tf_op jit(solution)/shard_map/ppermute | solution.py:328
  57.2 1.6 copy-done.2
  58.8 3.6 %middle.1 = (bf16[2048,512]{1,0:T(8,128)(2,1)S(1)}, f32[8,512]{1,0:T(8,128)S(1)}) custom-call(bf16[2048,512]{1,0:T(8,128)(2,1)S(1)} %copy-done.2, bf16[528,512]{1,0:T(8,128)(2,1)} %collective-permute-done.1.across), custom_call_target="tpu_custom_call" | custom-call | tf_op jit(solution)/shard_map/middle/pallas_call | solution.py:357
  62.4 3.7 %far.1 = (bf16[2048,512]{1,0:T(8,128)(2,1)S(1)}, bf16[32,128,512]{2,1,0:T(8,128)(2,1)S(1)}, f32[8,512]{1,0:T(8,128)S(1)}) custom-call(s32[32]{0:T(128)S(1)} %select_reduce_fusion.2.serve, s32[32]{0:T(128)S(1)} %select_reduce_fusion.1.order, s32[9]{0:T(128)S(1)} %convert_reduce_fusion.1.ready, bf16[2048,512]{1,0:T(8,128)(2,1)S(1)} %get-tuple-element.64.begun, ...), custom_call_target="tpu_custom_call" | custom-call | tf_op jit(solution)/shard_map/far/pallas_call | solution.py:357
  66.0 56.2 %all_to_all.21.partners = bf16[32,128,512]{2,1,0:T(8,128)(2,1)S(1)} all-to-all(bf16[32,128,512]{2,1,0:T(8,128)(2,1)S(1)} %get-tuple-element.66), channel_id=1, replica_groups=mesh['z'=4,'x'=4,'core'=2,'yhi'=2,'ylo'=2] {'ylo','x','z'}, dimensions={0} | all-to-all | bytes 8388608 | tf_op jit(solution)/shard_map/all_to_all | solution.py:332
  122.2 2.4 %scores.1 = (bf16[16,256,128]{2,1,0:T(8,128)(2,1)S(1)}, f32[32,128]{1,0:T(8,128)S(1)}) custom-call(s32[32]{0:T(128)S(1)} %get-tuple-element.57.need, s32[16,128]{1,0:T(8,128)S(1)} %fusion.10.column, bf16[2048,512]{1,0:T(8,128)(2,1)S(1)} %get-tuple-element.65.anchors, bf16[32,128,512]{2,1,0:T(8,128)(2,1)S(1)} %all_to_all.21.partners), custom_call_target="tpu_custom_call" | custom-call | tf_op jit(solution)/shard_map/scores/pallas_call | solution.py:357
  125.0 1.5 collective-permute-start.5
  126.5 1.3 collective-permute-start.4
  127.8 2.4 %mix.1 = (bf16[2048,512]{1,0:T(8,128)(2,1)S(1)}, bf16[2048,512]{1,0:T(8,128)(2,1)S(1)}) custom-call(s32[32]{0:T(128)S(1)} %get-tuple-element.57.need, s32[16,128]{1,0:T(8,128)S(1)} %fusion.10.column, bf16[16,256,128]{2,1,0:T(8,128)(2,1)S(1)} %get-tuple-element.68.weights, bf16[32,128,512]{2,1,0:T(8,128)(2,1)S(1)} %all_to_all.21.partners), custom_call_target="tpu_custom_call" | custom-call | tf_op jit(solution)/shard_map/mix/pallas_call | solution.py:357
  130.2 2.1 shares.1
  132.7 1.6 beside.1
  134.8 1.6 across.1
  136.6 1.8 collective-permute-start.10
  138.5 1.6 own.1
  140.1 2.0 collective-permute-done.8
  143.3 8.5 %collective-permute-done.10.across = bf16[512,512]{1,0:T(8,128)(2,1)S(1)} collective-permute-done((bf16[512,512]{1,0:T(8,128)(2,1)S(1)}, bf16[512,512]{1,0:T(8,128)(2,1)S(1)}, u32[]{:S(2)}, u32[]{:S(2)}) %collective-permute-start.10) | collective-permute-done | bytes 524320 | tf_op jit(solution)/shard_map/ppermute | solution.py:328
  151.8 0.7 back.1
  152.5 26.0 %all_to_all.22 = bf16[128,8,512]{2,1,0:T(8,128)(2,1)S(1)} all-to-all(bf16[128,8,512]{2,1,0:T(8,128)(2,1)S(1)} %bitcast.23), channel_id=1, replica_groups=mesh['z'=4,'x'=4,'core'=2,'yhi'=2,'ylo'=2] {'core','x','yhi','ylo','z'}, dimensions={0} | all-to-all | bytes 2097152 | tf_op jit(solution)/shard_map/all_to_all | solution.py:332
  178.5 2.3 %unit_grad.1.grad = bf16[512,512]{1,0:T(8,128)(2,1)S(1)} custom-call(bf16[1024,512]{1,0:T(8,128)(2,1)S(1)} %bitcast.24, f32[16,512]{1,0:T(8,128)S(1)} %copy-done.3, f32[512,512]{1,0:T(8,128)} %get-tuple-element.84.unit), custom_call_target="tpu_custom_call" | custom-call | tf_op jit(solution)/shard_map/unit_grad/pallas_call | solution.py:357
  180.9 0.7 head_begun.1.begun
  181.6 1.2 collective-permute-done.11.partner
  182.8 0.7 head_grad.1
  183.5 24.2 %all_to_all.23.parts = bf16[64,16,512]{2,1,0:T(8,128)(2,1)S(1)} all-to-all(bf16[64,16,512]{2,1,0:T(8,128)(2,1)S(1)} %bitcast.25), channel_id=1, replica_groups=mesh['z'=4,'x'=4,'core'=2,'yhi'=2,'ylo'=2] {'x','yhi','ylo','z'}, dimensions={0} | all-to-all | bytes 2097152 | tf_op jit(solution)/shard_map/all_to_all | solution.py:332
  207.8 0.8 add.126
  (48 shorter events, 4.9 us)
Async XLA Ops:
  1.3 0.7 copy-start.4
  40.9 2.1 %collective-permute-start = (bf16[528,512]{1,0:T(8,128)(2,1)}, bf16[528,512]{1,0:T(8,128)(2,1)S(1)}, u32[]{:S(2)}, u32[]{:S(2)}) collective-permute-start(bf16[528,512]{1,0:T(8,128)(2,1)} %get-tuple-element.47.own), channel_id=1, source_target_pairs={{0,4},{4,0},{1,5},{5,1},{2,6},{6,2},{3,7},{7,3},{8,12},{12,8},{9,1... | collective-permute-start | bytes 1622024 | tf_op jit(solution)/shard_map/ppermute | solution.py:328
  40.9 8.1 %copy-start.6 = (s32[512,8]{0,1:T(8,128)S(1)}, s32[512,8]{0,1:T(8,128)}, u32[]{:S(2)}) copy-start(s32[512,8]{0,1:T(8,128)} %param.8) | copy-start | bytes 49156
  40.9 8.5 %copy-start = (bf16[512,2048]{1,0:T(8,128)(2,1)S(1)}, bf16[512,2048]{1,0:T(8,128)(2,1)}, u32[]{:S(2)}) copy-start(bf16[512,2048]{1,0:T(8,128)(2,1)} %r_1_.2) | copy-start | bytes 6291460
  40.9 16.2 %collective-permute-start.1 = (bf16[528,512]{1,0:T(8,128)(2,1)}, bf16[528,512]{1,0:T(8,128)(2,1)}, u32[]{:S(2)}, u32[]{:S(2)}) collective-permute-start(bf16[528,512]{1,0:T(8,128)(2,1)} %get-tuple-element.47.own), channel_id=1, source_target_pairs={{0,3},{1,2},{2,1},{3,0},{4,7},{5,6},{6,5},{7,4},{8,11},{9,10},{10,... | collective-permute-start | bytes 1622024 | tf_op jit(solution)/shard_map/ppermute | solution.py:328
  47.7 1.3 copy-start.1
  49.1 2.9 %copy-start.5 = (s32[2048]{0:T(1024)S(1)}, s32[2048]{0:T(1024)}, u32[]{:S(2)}) copy-start(s32[2048]{0:T(1024)} %param.9) | copy-start | bytes 24580
  51.1 6.1 %collective-permute-start.2 = (bf16[1024,512]{1,0:T(8,128)(2,1)}, bf16[1024,512]{1,0:T(8,128)(2,1)S(1)}, u32[]{:S(2)}, u32[]{:S(2)}) collective-permute-start(bf16[1024,512]{1,0:T(8,128)(2,1)} %get-tuple-element.53), channel_id=1, source_target_pairs={{0,4},{4,0},{1,5},{5,1},{2,6},{6,2},{3,7},{7,3},{8,12},{12,8},{9,1... | collective-permute-start | bytes 3145736 | tf_op jit(solution)/shard_map/ppermute | solution.py:328
  57.2 5.2 %collective-permute-start.3 = (bf16[528,512]{1,0:T(8,128)(2,1)}, bf16[528,512]{1,0:T(8,128)(2,1)S(1)}, u32[]{:S(2)}, u32[]{:S(2)}) collective-permute-start(bf16[528,512]{1,0:T(8,128)(2,1)} %collective-permute-done.1.across), channel_id=1, source_target_pairs={{0,4},{4,0},{1,5},{5,1},{2,6},{6,2},{3,7},{7,3},{8,12},{12,8},{9,1... | collective-permute-start | bytes 1622024 | tf_op jit(solution)/shard_map/ppermute | solution.py:328
  57.2 1.6 copy-start.2
  124.7 5.5 %collective-permute-start.6 = (f32[32,128]{1,0:T(8,128)S(1)}, f32[32,128]{1,0:T(8,128)S(1)}, u32[]{:S(2)}, u32[]{:S(2)}) collective-permute-start(f32[32,128]{1,0:T(8,128)S(1)} %get-tuple-element.67.r_0_), channel_id=1, source_target_pairs={{0,7},{1,6},{2,5},{3,4},{4,3},{5,2},{6,1},{7,0},{8,15},{9,14},{10,... | collective-permute-start | bytes 49160 | tf_op jit(solution)/shard_map/ppermute | solution.py:328
  125.0 5.2 %collective-permute-start.5 = (f32[32,128]{1,0:T(8,128)S(1)}, f32[32,128]{1,0:T(8,128)S(1)}, u32[]{:S(2)}, u32[]{:S(2)}) collective-permute-start(f32[32,128]{1,0:T(8,128)S(1)} %get-tuple-element.67.r_0_), channel_id=1, source_target_pairs={{0,3},{1,2},{2,1},{3,0},{4,7},{5,6},{6,5},{7,4},{8,11},{9,10},{10,... | collective-permute-start | bytes 49160 | tf_op jit(solution)/shard_map/ppermute | solution.py:328
  126.5 3.7 %collective-permute-start.4 = (f32[32,128]{1,0:T(8,128)S(1)}, f32[32,128]{1,0:T(8,128)S(1)}, u32[]{:S(2)}, u32[]{:S(2)}) collective-permute-start(f32[32,128]{1,0:T(8,128)S(1)} %get-tuple-element.67.r_0_), channel_id=1, source_target_pairs={{0,4},{4,0},{1,5},{5,1},{2,6},{6,2},{3,7},{7,3},{8,12},{12,8},{9,1... | collective-permute-start | bytes 49160 | tf_op jit(solution)/shard_map/ppermute | solution.py:328
  132.3 4.1 %collective-permute-start.9 = (bf16[512,512]{1,0:T(8,128)(2,1)S(1)}, bf16[512,512]{1,0:T(8,128)(2,1)S(1)}, u32[]{:S(2)}, u32[]{:S(2)}) collective-permute-start(bf16[512,512]{1,0:T(8,128)(2,1)S(1)} %get-tuple-element.81), channel_id=1, source_target_pairs={{0,4},{4,0},{1,5},{5,1},{2,6},{6,2},{3,7},{7,3},{8,12},{12,8},{9,1... | collective-permute-start | bytes 1572872 | tf_op jit(solution)/shard_map/ppermute | solution.py:328
  134.3 8.4 %collective-permute-start.7 = (bf16[512,512]{1,0:T(8,128)(2,1)S(1)}, bf16[512,512]{1,0:T(8,128)(2,1)S(1)}, u32[]{:S(2)}, u32[]{:S(2)}) collective-permute-start(bf16[512,512]{1,0:T(8,128)(2,1)S(1)} %beside.1), channel_id=1, source_target_pairs={{0,4},{4,0},{1,5},{5,1},{2,6},{6,2},{3,7},{7,3},{8,12},{12,8},{9,1... | collective-permute-start | bytes 1572872 | tf_op jit(solution)/shard_map/ppermute | solution.py:328
  136.6 15.2 %collective-permute-start.10 = (bf16[512,512]{1,0:T(8,128)(2,1)S(1)}, bf16[512,512]{1,0:T(8,128)(2,1)S(1)}, u32[]{:S(2)}, u32[]{:S(2)}) collective-permute-start(bf16[512,512]{1,0:T(8,128)(2,1)S(1)} %add_convert_fusion), channel_id=1, source_target_pairs={{0,3},{1,2},{2,1},{3,0},{4,7},{5,6},{6,5},{7,4},{8,11},{9,10},{10,... | collective-permute-start | bytes 1572872 | tf_op jit(solution)/shard_map/ppermute | solution.py:328
  138.4 3.7 %collective-permute-start.8 = (f32[2048]{0:T(1024)S(1)}, f32[2048]{0:T(1024)S(1)}, u32[]{:S(2)}, u32[]{:S(2)}) collective-permute-start(f32[2048]{0:T(1024)S(1)} %fusion.9), channel_id=1, source_target_pairs={{0,1},{1,0},{2,3},{3,2},{4,5},{5,4},{6,7},{7,6},{8,9},{9,8},{10,11... | collective-permute-start | bytes 24584 | tf_op jit(solution)/shard_map/ppermute | solution.py:328
  143.3 35.2 %copy-start.3 = (f32[16,512]{1,0:T(8,128)S(1)}, f32[16,512]{1,0:T(8,128)}, u32[]{:S(2)}) copy-start(f32[16,512]{1,0:T(8,128)} %get-tuple-element.83.place) | copy-start | bytes 98308
  180.8 2.0 collective-permute-start.11
